TPU v7x, 32 devices: a whole 2x2x4 slice. The times are simulated.
32 devices in a mesh: lon: 16 (over z, y, core), head: 2 (over x).
Axes of the slice: x: 2, y: 2, z: 4, core: 2. Of those that a mesh axis runs over, the one named last changes fastest.
Arguments:
- pixels: bfloat16 [48, 32, 4096], P(None, None, 'lon'), may hold values from -6 to 6
- crop_starts: int32 [4, 8], replicated, may hold values from 0 to 30
- crop_shifts: int32 [4, 8], replicated, may hold values from -1 to 1, as said below
- slot_crops: int32 [4, 2048], P(None, 'lon'), may hold values from 0 to 7, as said below
- occupied: int32 [4, 2048], P(None, 'lon'), may hold values from 0 to 1, as said below
- lead_hours: int32 [4, 8], replicated, may hold values from 6 to 168
- patch_weight: bfloat16 [48, 4, 1024], P(None, None, ('lon', 'head')), may hold values from -3 to 3
- variable_embed: bfloat16 [48, 1024], P(None, ('lon', 'head')), may hold values from -3 to 3
- mixer_query: bfloat16 [16, 64], P('head', 'lon'), may hold values from -9 to 9
- mixer_keys: bfloat16 [1024, 1024], P('lon', 'head'), may hold values from -0.1875 to 0.1875
- mixer_values: bfloat16 [1024, 1024], P('lon', 'head'), may hold values from -0.1875 to 0.1875
- mixer_output: bfloat16 [1024, 1024], P('head', 'lon'), may hold values from -0.5 to 0.5
- lead_embed: bfloat16 [2, 1024], P(None, ('lon', 'head')), may hold values from -6 to 6
- first_gain: bfloat16 [1024], P(('lon', 'head')), may hold values from 0.5 to 1.5
- first_bias: bfloat16 [1024], P(('lon', 'head')), may hold values from -3 to 3
- attention_in: bfloat16 [3, 1024, 1024], P(None, 'lon', 'head'), may hold values from -0.25 to 0.25
- attention_out: bfloat16 [1024, 1024], P('head', 'lon'), may hold values from -0.75 to 0.75
- second_gain: bfloat16 [1024], P(('lon', 'head')), may hold values from 0.5 to 1.5
- second_bias: bfloat16 [1024], P(('lon', 'head')), may hold values from -3 to 3
- expand_weight: bfloat16 [1024, 4096], P('lon', 'head'), may hold values from -0.1875 to 0.1875
- expand_bias: bfloat16 [64, 64], P('head', 'lon'), may hold values from -3 to 3
- reduce_weight: bfloat16 [4096, 1024], P('head', 'lon'), may hold values from -0.125 to 0.125
- output_weight: bfloat16 [1024, 192], P('lon', 'head'), may hold values from -0.1875 to 0.1875
- cotangent: bfloat16 [4, 2048, 192], P(None, 'lon', 'head'), may hold values from -6 to 6
Outputs:
- predicted: bfloat16 [4, 2048, 192], P(None, 'lon', 'head')
- pixel_grad: float32 [48, 32, 4096], P(None, None, 'lon')
- grad_patch_weight: float32 [48, 4, 1024], P(None, None, ('lon', 'head'))
- grad_variable_embed: float32 [48, 1024], P(None, ('lon', 'head'))
- grad_mixer_query: float32 [16, 64], P('head', 'lon')
- grad_mixer_keys: float32 [1024, 1024], P('lon', 'head')
- grad_mixer_values: float32 [1024, 1024], P('lon', 'head')
- grad_mixer_output: float32 [1024, 1024], P('head', 'lon')
- grad_lead_embed: float32 [2, 1024], P(None, ('lon', 'head'))
- grad_first_gain: float32 [1024], P(('lon', 'head'))
- grad_first_bias: float32 [1024], P(('lon', 'head'))
- grad_attention_in: float32 [3, 1024, 1024], P(None, 'lon', 'head')
- grad_attention_out: float32 [1024, 1024], P('head', 'lon')
- grad_second_gain: float32 [1024], P(('lon', 'head'))
- grad_second_bias: float32 [1024], P(('lon', 'head'))
- grad_expand_weight: float32 [1024, 4096], P('lon', 'head')
- grad_expand_bias: float32 [64, 64], P('head', 'lon')
- grad_reduce_weight: float32 [4096, 1024], P('head', 'lon')
- grad_output_weight: float32 [1024, 192], P('lon', 'head')
Inputs may be any that keep to these rules, and one draw needn't show every extreme that they name: `crop_shifts`: each is -1 or +1. `slot_crops`: crop numbers start at 0 and never fall along a row; a row's padded slots lie in its last crop. `occupied`: the padded slots of a row form its tail.
All inputs are finite; a program needn't handle non-finite values.
Results may differ from a plain program's by a relative error of at most 0.035.
Values may be sent and summed in bfloat16 or wider, within the bound.
A program may use at most 192 MiB of HBM per device.

v0:
```python
from functools import partial

import jax
import jax.numpy as jnp
from jax import lax
from jax.sharding import PartitionSpec as P

HEAD_DIM = 64


epsilon = 1e-05
masked_score = -1e30
highest = lax.Precision.HIGHEST


def extended(array, sides, width):
    for axis, dim in sides:
        count, length = (lax.axis_size(axis), array.shape[dim])
        up = [(i, (i + 1) % count) for i in range(count)]
        down = [(j, i) for i, j in up]
        last = lax.slice_in_dim(array, length - width, length, axis=dim)
        leading = lax.slice_in_dim(array, 0, width, axis=dim)
        before = lax.ppermute(last, axis, up)
        after = lax.ppermute(leading, axis, down)
        array = jnp.concatenate([before, array, after], axis=dim)
    return array


def layer_norm(values, gain_vector, shift_vector):
    center = values - jnp.mean(values, axis=-1, keepdims=True)
    spread = jnp.mean(center * center, axis=-1, keepdims=True)
    return center * lax.rsqrt(spread + epsilon) * gain_vector + shift_vector


def head_total(partial_sum):
    return lax.psum(partial_sum.astype(jnp.bfloat16), "head").astype(jnp.float32)


def head_share(partial_sum):
    return lax.psum_scatter(
        partial_sum.astype(jnp.bfloat16), "head", scatter_dimension=0, tiled=True
    ).astype(jnp.float32)


def head_rows(values):
    return lax.all_gather(values, "head", axis=0, tiled=True)


def reduce_rows(partial_sum):
    return head_share(partial_sum)


def spread_rows(values):
    return head_rows(values)


def crop_lookup(crop_table, slot_numbers):
    numbers = jnp.arange(crop_table.shape[1], dtype=jnp.int32)
    picked = slot_numbers[:, :, None] == numbers[None, None, :]
    return jnp.sum(jnp.where(picked, crop_table[:, None, :], 0), axis=2)


def outer_sum(left_rows, right_rows):
    return jnp.einsum("ti,tj->ij", left_rows, right_rows, preferred_element_type=jnp.float32)


def block_slice(values, block_index, block_width, axis_number):
    return lax.dynamic_slice_in_dim(values, block_index * block_width, block_width, axis_number)


def block_scores(queries, query_crops, key_block, key_tags):
    scores = jnp.einsum(
        "rqhd,rkhd->rhqk", queries, key_block, preferred_element_type=jnp.float32
    ) * HEAD_DIM ** (-0.5)
    matched = query_crops[:, None, :, None] == key_tags[:, None, None, :]
    return (jnp.where(matched, scores, masked_score), matched)


def key_stats(queries, query_crops, key_rows, key_tags, block_width):
    row_count, slot_count, head_count, head_size = queries.shape

    def key_step(carried, block_index):
        largest, totals = carried
        scores, matched = block_scores(
            queries,
            query_crops,
            block_slice(key_rows, block_index, block_width, 1),
            block_slice(key_tags, block_index, block_width, 1),
        )
        raised = jnp.maximum(largest, jnp.max(scores, axis=-1))
        totals = totals * jnp.exp(largest - raised) + jnp.sum(
            jnp.where(matched, jnp.exp(scores - raised[..., None]), 0.0), axis=-1
        )
        return ((raised, totals), None)

    initial = (
        jnp.full((row_count, head_count, slot_count), masked_score, jnp.float32),
        jnp.zeros((row_count, head_count, slot_count), jnp.float32),
    )
    (largest, totals), _ = lax.scan(key_step, initial, jnp.arange(key_rows.shape[1] // block_width))
    return largest + jnp.log(totals)


def attend(queries, query_crops, key_rows, value_rows, key_tags, log_totals, block_width):

    def attend_step(running, block_index):
        scores, matched = block_scores(
            queries,
            query_crops,
            block_slice(key_rows, block_index, block_width, 1),
            block_slice(key_tags, block_index, block_width, 1),
        )
        weights = jnp.where(matched, jnp.exp(scores - log_totals[..., None]), 0.0).astype(
            jnp.bfloat16
        )
        value_block = block_slice(value_rows, block_index, block_width, 1)
        return (
            running
            + jnp.einsum(
                "rhqk,rkhd->rqhd", weights, value_block, preferred_element_type=jnp.float32
            ),
            None,
        )

    outputs, _ = lax.scan(
        attend_step,
        jnp.zeros(queries.shape, jnp.float32),
        jnp.arange(key_rows.shape[1] // block_width),
    )
    return outputs


def score_grads(
    queries, query_crops, out_grads, log_totals, deltas, key_block, value_block, key_tags
):
    scores, matched = block_scores(queries, query_crops, key_block, key_tags)
    weights = jnp.where(matched, jnp.exp(scores - log_totals[..., None]), 0.0)
    weight_grads = jnp.einsum(
        "rqhd,rkhd->rhqk", out_grads, value_block, preferred_element_type=jnp.float32
    )
    score_delta = (weights * (weight_grads - deltas[..., None])).astype(jnp.bfloat16)
    return (score_delta, weights.astype(jnp.bfloat16))


def mixer_row(patch_row, full_patch, full_variable, pair_weight, head_query):
    embedded = jnp.einsum(
        "svk,vkd->svd", patch_row, full_patch, preferred_element_type=jnp.float32
    ) + full_variable.astype(jnp.float32)
    embedded = embedded.astype(jnp.bfloat16)
    slot_count, var_count, model_width = embedded.shape
    head_count, head_size = head_query.shape
    local_width = head_count * head_size
    paired = jnp.dot(
        embedded.reshape(slot_count * var_count, model_width),
        pair_weight,
        preferred_element_type=jnp.float32,
    ).astype(jnp.bfloat16)
    key_rows = paired[:, :local_width].reshape(slot_count, var_count, head_count, head_size)
    value_rows = paired[:, local_width:].reshape(slot_count, var_count, head_count, head_size)
    scores = jnp.einsum(
        "svhd,hd->shv", key_rows, head_query, preferred_element_type=jnp.float32
    ) * HEAD_DIM ** (-0.5)
    weights = jax.nn.softmax(scores, axis=-1)
    return (embedded, key_rows, value_rows, weights)


def mixer_back(carried, inputs, full_patch, full_variable, pair_weight, head_query):
    patch_row, mixed_grad = inputs
    embedded, key_rows, value_rows, weights = mixer_row(
        patch_row, full_patch, full_variable, pair_weight, head_query
    )
    slot_count, var_count, model_width = embedded.shape
    local_width = key_rows.shape[2] * key_rows.shape[3]
    mixed_wide = mixed_grad.astype(jnp.float32)
    value_grads = jnp.einsum("shv,shd->svhd", weights, mixed_wide, precision=highest).astype(
        jnp.bfloat16
    )
    weight_grads = jnp.einsum(
        "shd,svhd->shv", mixed_wide, value_rows.astype(jnp.float32), precision=highest
    )
    score_delta = (
        weights
        * (weight_grads - jnp.sum(weights * weight_grads, axis=-1, keepdims=True))
        * HEAD_DIM ** (-0.5)
    )
    key_grads = jnp.einsum(
        "shv,hd->svhd", score_delta, head_query.astype(jnp.float32), precision=highest
    ).astype(jnp.bfloat16)
    query_grad = jnp.einsum(
        "shv,svhd->hd", score_delta, key_rows.astype(jnp.float32), precision=highest
    )
    pair_grads = jnp.concatenate(
        [
            key_grads.reshape(slot_count * var_count, local_width),
            value_grads.reshape(slot_count * var_count, local_width),
        ],
        axis=1,
    )
    embed_grad = jnp.einsum(
        "ne,de->nd", pair_grads, pair_weight, preferred_element_type=jnp.float32
    )
    pair_weight_grad = outer_sum(embedded.reshape(slot_count * var_count, model_width), pair_grads)
    embed_grad = embed_grad.reshape(slot_count, var_count, model_width)
    patch_grad = jnp.einsum(
        "svk,svd->vkd", patch_row.astype(jnp.float32), embed_grad, precision=highest
    )
    variable_grad = jnp.sum(embed_grad, axis=0)
    slot_grad = jnp.einsum(
        "svd,vkd->svk", embed_grad, full_patch.astype(jnp.float32), precision=highest
    )
    patch_acc, variable_acc, query_acc, pair_acc = carried
    return (
        (
            patch_acc + patch_grad,
            variable_acc + variable_grad,
            query_acc + query_grad,
            pair_acc + pair_weight_grad,
        ),
        slot_grad,
    )


def local(
    pixels,
    crop_starts,
    crop_shifts,
    slot_crops,
    occupied,
    lead_hours,
    patch_weight,
    variable_embed,
    mixer_query,
    mixer_keys,
    mixer_values,
    mixer_output,
    lead_embed,
    first_gain,
    first_bias,
    attention_in,
    attention_out,
    second_gain,
    second_bias,
    expand_weight,
    expand_bias,
    reduce_weight,
    output_weight,
    cotangent,
):
    shared = (
        lax.all_gather(patch_weight, ("lon", "head"), axis=2, tiled=True),
        lax.all_gather(variable_embed, ("lon", "head"), axis=1, tiled=True),
        lax.all_gather(lead_embed, ("lon", "head"), axis=1, tiled=True),
        lax.all_gather(first_gain, ("lon", "head"), axis=0, tiled=True),
        lax.all_gather(first_bias, ("lon", "head"), axis=0, tiled=True),
        lax.all_gather(second_gain, ("lon", "head"), axis=0, tiled=True),
        lax.all_gather(second_bias, ("lon", "head"), axis=0, tiled=True),
    )
    full_patch, full_variable, full_lead, gain_first, shift_first, gain_second, shift_second = (
        shared
    )
    sector = (
        lax.all_gather(mixer_query, "lon", axis=1, tiled=True),
        lax.all_gather(mixer_keys, "lon", axis=0, tiled=True),
        lax.all_gather(mixer_values, "lon", axis=0, tiled=True),
        lax.all_gather(mixer_output, "lon", axis=1, tiled=True),
        lax.all_gather(attention_in, "lon", axis=1, tiled=True),
        lax.all_gather(attention_out, "lon", axis=1, tiled=True),
        lax.all_gather(expand_weight, "lon", axis=0, tiled=True),
        lax.all_gather(expand_bias, "lon", axis=1, tiled=True),
        lax.all_gather(reduce_weight, "lon", axis=1, tiled=True),
        lax.all_gather(output_weight, "lon", axis=0, tiled=True),
    )
    (
        head_query,
        key_weight,
        value_weight,
        mixer_weight,
        input_weight,
        output_proj,
        up_weight,
        up_bias,
        down_weight,
        final_weight,
    ) = sector
    row_count, slot_width = slot_crops.shape
    token_count = row_count * slot_width
    local_width = key_weight.shape[1]
    head_count = local_width // HEAD_DIM
    pair_weight = jnp.concatenate([key_weight, value_weight], axis=1)
    gain_one = gain_first.astype(jnp.float32)
    shift_one = shift_first.astype(jnp.float32)
    gain_two = gain_second.astype(jnp.float32)
    shift_two = shift_second.astype(jnp.float32)
    lat_slot = crop_lookup(crop_starts, slot_crops)
    shift_slot = crop_lookup(crop_shifts, slot_crops)
    lead_slot = crop_lookup(lead_hours, slot_crops).astype(jnp.float32).reshape(token_count) / 100.0
    share_count = token_count // lax.axis_size("head")
    lead_rows = lax.dynamic_slice_in_dim(
        lead_slot, lax.axis_index("head") * share_count, share_count
    )
    padded = extended(pixels, (("lon", 2),), 1)
    var_count, lat_count = (pixels.shape[0], pixels.shape[1])
    west_pairs = padded[:, :, : 2 * slot_width].reshape(var_count, lat_count, slot_width, 2)
    east_pairs = padded[:, :, 2:].reshape(var_count, lat_count, slot_width, 2)
    side_pairs = jnp.stack([west_pairs, east_pairs])
    tables = jnp.stack([side_pairs[:, :, :-1], side_pairs[:, :, 1:]], axis=3)
    lat_index = jnp.arange(lat_count - 1, dtype=jnp.int32)
    side_shift = 2 * jnp.arange(2, dtype=jnp.int32) - 1
    chosen = (lat_slot[:, :, None, None] == lat_index[None, None, None, :]) & (
        shift_slot[:, :, None, None] == side_shift[None, None, :, None]
    )
    patches = jnp.einsum(
        "rjsa,svapjx->rjvpx",
        chosen.astype(jnp.bfloat16),
        tables,
        preferred_element_type=jnp.float32,
    )
    patches = patches.astype(jnp.bfloat16).reshape(row_count, slot_width, var_count, 4)

    def mixer_forward(patch_row):
        embedded, key_rows, value_rows, weights = mixer_row(
            patch_row, full_patch, full_variable, pair_weight, head_query
        )
        return jnp.einsum(
            "shv,svhd->shd", weights, value_rows.astype(jnp.float32), precision=highest
        ).astype(jnp.bfloat16)

    mixed_low = lax.map(mixer_forward, patches).reshape(token_count, local_width)
    start_sum = reduce_rows(jnp.dot(mixed_low, mixer_weight, preferred_element_type=jnp.float32))
    start_sum = (
        start_sum
        + lead_rows[:, None] * full_lead[0].astype(jnp.float32)
        + full_lead[1].astype(jnp.float32)
    )
    first_low = spread_rows(layer_norm(start_sum, gain_one, shift_one).astype(jnp.bfloat16))
    projected = jnp.einsum(
        "td,kde->kte", first_low, input_weight, preferred_element_type=jnp.float32
    ).astype(jnp.bfloat16)
    projected = projected.reshape(3, row_count, slot_width, head_count, HEAD_DIM)
    queries, key_local, value_local = (projected[0], projected[1], projected[2])
    query_crops = slot_crops.astype(jnp.float32)
    key_tags = jnp.where(occupied == 1, slot_crops, -1).astype(jnp.bfloat16)
    key_all, value_all, tag_all = (
        lax.all_gather(key_local, "lon", axis=1, tiled=True),
        lax.all_gather(value_local, "lon", axis=1, tiled=True),
        lax.all_gather(key_tags, "lon", axis=1, tiled=True),
    )
    block_width = min(512, key_all.shape[1])
    tag_wide = tag_all.astype(jnp.float32)
    log_totals = key_stats(queries, query_crops, key_all, tag_wide, block_width)
    attended = attend(queries, query_crops, key_all, value_all, tag_wide, log_totals, block_width)
    attended_low = attended.astype(jnp.bfloat16).reshape(token_count, local_width)
    middle = start_sum + reduce_rows(
        jnp.dot(attended_low, output_proj, preferred_element_type=jnp.float32)
    )
    second_low = spread_rows(layer_norm(middle, gain_two, shift_two).astype(jnp.bfloat16))
    hidden = jnp.dot(second_low, up_weight, preferred_element_type=jnp.float32) + up_bias.reshape(
        -1
    ).astype(jnp.float32)
    active = jax.nn.gelu(hidden, approximate=False).astype(jnp.bfloat16)
    final_sum = middle + reduce_rows(
        jnp.dot(active, down_weight, preferred_element_type=jnp.float32)
    )
    final_low = spread_rows(final_sum.astype(jnp.bfloat16))
    keep_mask = occupied.reshape(token_count, 1)
    predicted = (
        jnp.dot(final_low, final_weight, preferred_element_type=jnp.float32)
        * keep_mask.astype(jnp.float32)
    ).astype(jnp.bfloat16)
    predicted = predicted.reshape(row_count, slot_width, -1)
    masked_grad = (cotangent * occupied[:, :, None].astype(jnp.bfloat16)).reshape(token_count, -1)
    grad_final_weight = outer_sum(final_low, masked_grad)
    part_top = jnp.einsum(
        "to,do->td", masked_grad, final_weight, preferred_element_type=jnp.float32
    )
    final_grad = reduce_rows(part_top)
    final_grad_low = spread_rows(final_grad.astype(jnp.bfloat16))
    grad_down = outer_sum(active, final_grad_low)
    active_grad = jnp.einsum(
        "td,fd->tf", final_grad_low, down_weight, preferred_element_type=jnp.float32
    )
    _, gelu_back = jax.vjp(partial(jax.nn.gelu, approximate=False), hidden)
    hidden_grad = gelu_back(active_grad)[0].astype(jnp.bfloat16)
    grad_up = outer_sum(second_low, hidden_grad)
    grad_up_bias = jnp.sum(hidden_grad.astype(jnp.float32), axis=0).reshape(up_bias.shape)
    second_grad = jnp.einsum(
        "tf,df->td", hidden_grad, up_weight, preferred_element_type=jnp.float32
    )
    second_in = head_share(second_grad)
    _, second_back = jax.vjp(layer_norm, middle, gain_two, shift_two)
    part_mid, grad_gain_two, grad_shift_two = second_back(second_in)
    middle_grad = final_grad + part_mid
    middle_low = spread_rows(middle_grad.astype(jnp.bfloat16))
    grad_proj = outer_sum(attended_low, middle_low)
    out_grads = jnp.einsum(
        "td,ed->te", middle_low, output_proj, preferred_element_type=jnp.float32
    ).astype(jnp.bfloat16)
    out_grads = out_grads.reshape(row_count, slot_width, head_count, HEAD_DIM)
    deltas = jnp.transpose(jnp.sum(out_grads.astype(jnp.float32) * attended, axis=-1), (0, 2, 1))
    back_keys, back_values, back_raw = (
        lax.all_gather(key_local, "lon", axis=1, tiled=True),
        lax.all_gather(value_local, "lon", axis=1, tiled=True),
        lax.all_gather(key_tags, "lon", axis=1, tiled=True),
    )
    back_tags = back_raw.astype(jnp.float32)
    scale = HEAD_DIM ** (-0.5)
    key_count = back_keys.shape[1] // block_width
    local_zeros = jnp.zeros(queries.shape, jnp.float32)
    whole_zeros = jnp.zeros(back_keys.shape, jnp.float32)

    def both_step(running, block_index):
        query_acc, key_acc, value_acc = running
        key_block = block_slice(back_keys, block_index, block_width, 1)
        score_delta, weights_low = score_grads(
            queries,
            query_crops,
            out_grads,
            log_totals,
            deltas,
            key_block,
            block_slice(back_values, block_index, block_width, 1),
            block_slice(back_tags, block_index, block_width, 1),
        )
        query_acc = (
            query_acc
            + jnp.einsum(
                "rhqk,rkhd->rqhd", score_delta, key_block, preferred_element_type=jnp.float32
            )
            * scale
        )
        key_piece = (
            jnp.einsum("rhqk,rqhd->rkhd", score_delta, queries, preferred_element_type=jnp.float32)
            * scale
        )
        value_piece = jnp.einsum(
            "rhqk,rqhd->rkhd", weights_low, out_grads, preferred_element_type=jnp.float32
        )
        key_acc = lax.dynamic_update_slice_in_dim(key_acc, key_piece, block_index * block_width, 1)
        value_acc = lax.dynamic_update_slice_in_dim(
            value_acc, value_piece, block_index * block_width, 1
        )
        return ((query_acc, key_acc, value_acc), None)

    (query_grad, key_part, value_part), _ = lax.scan(
        both_step, (local_zeros, whole_zeros, whole_zeros), jnp.arange(key_count)
    )
    key_grad, value_grad = (
        lax.psum_scatter(
            key_part.astype(jnp.bfloat16), "lon", scatter_dimension=1, tiled=True
        ).astype(jnp.float32),
        lax.psum_scatter(
            value_part.astype(jnp.bfloat16), "lon", scatter_dimension=1, tiled=True
        ).astype(jnp.float32),
    )
    stacked = (
        jnp.stack([query_grad, key_grad, value_grad])
        .astype(jnp.bfloat16)
        .reshape(3, token_count, local_width)
    )
    first_grad = jnp.einsum(
        "kte,kde->td", stacked, input_weight, preferred_element_type=jnp.float32
    )
    grad_input = jnp.einsum("td,kte->kde", first_low, stacked, preferred_element_type=jnp.float32)
    first_in = head_share(first_grad)
    _, first_back = jax.vjp(layer_norm, start_sum, gain_one, shift_one)
    part_low, grad_gain_one, grad_shift_one = first_back(first_in)
    start_grad = middle_grad + part_low
    grad_lead = jnp.stack(
        [jnp.sum(start_grad * lead_rows[:, None], axis=0), jnp.sum(start_grad, axis=0)]
    )
    start_low = spread_rows(start_grad.astype(jnp.bfloat16))
    grad_mixer = outer_sum(mixed_low, start_low)
    mixed_grad = jnp.einsum(
        "td,ed->te", start_low, mixer_weight, preferred_element_type=jnp.float32
    ).astype(jnp.bfloat16)
    mixed_grad = mixed_grad.reshape(row_count, slot_width, head_count, HEAD_DIM)
    initial = (
        jnp.zeros(full_patch.shape, jnp.float32),
        jnp.zeros(full_variable.shape, jnp.float32),
        jnp.zeros(head_query.shape, jnp.float32),
        jnp.zeros(pair_weight.shape, jnp.float32),
    )
    mixer_step = partial(
        mixer_back,
        full_patch=full_patch,
        full_variable=full_variable,
        pair_weight=pair_weight,
        head_query=head_query,
    )
    (grad_patch, grad_variable, grad_query, grad_pair), slot_grads = lax.scan(
        mixer_step, initial, (patches, mixed_grad)
    )
    slot_total = head_total(slot_grads).reshape(row_count, slot_width, var_count, 2, 2)
    table_grads = jnp.einsum(
        "rjsa,rjvpx->svapjx", chosen.astype(jnp.float32), slot_total, precision=highest
    )
    side_grads = jnp.pad(
        table_grads[:, :, :, 0], ((0, 0), (0, 0), (0, 1), (0, 0), (0, 0))
    ) + jnp.pad(table_grads[:, :, :, 1], ((0, 0), (0, 0), (1, 0), (0, 0), (0, 0)))
    west_grad = side_grads[0].reshape(var_count, lat_count, 2 * slot_width)
    east_grad = side_grads[1].reshape(var_count, lat_count, 2 * slot_width)
    padded_grad = jnp.pad(west_grad, ((0, 0), (0, 0), (0, 2))) + jnp.pad(
        east_grad, ((0, 0), (0, 0), (2, 0))
    )
    rim_values = jnp.stack([padded_grad[:, :, 0], padded_grad[:, :, -1]], axis=2)
    returned = extended(rim_values, (("lon", 2),), 1)
    pixel_grad = (
        padded_grad[:, :, 1:-1]
        + jnp.pad(returned[:, :, 0:1], ((0, 0), (0, 0), (0, 2 * slot_width - 1)))
        + jnp.pad(returned[:, :, 3:4], ((0, 0), (0, 0), (2 * slot_width - 1, 0)))
    )
    sector_out = (
        lax.psum_scatter(
            grad_query.astype(jnp.bfloat16), "lon", scatter_dimension=1, tiled=True
        ).astype(jnp.float32),
        lax.psum_scatter(
            grad_pair[:, :local_width].astype(jnp.bfloat16), "lon", scatter_dimension=0, tiled=True
        ).astype(jnp.float32),
        lax.psum_scatter(
            grad_pair[:, local_width:].astype(jnp.bfloat16), "lon", scatter_dimension=0, tiled=True
        ).astype(jnp.float32),
        lax.psum_scatter(
            grad_mixer.astype(jnp.bfloat16), "lon", scatter_dimension=1, tiled=True
        ).astype(jnp.float32),
        lax.psum_scatter(
            grad_input.astype(jnp.bfloat16), "lon", scatter_dimension=1, tiled=True
        ).astype(jnp.float32),
        lax.psum_scatter(
            grad_proj.astype(jnp.bfloat16), "lon", scatter_dimension=1, tiled=True
        ).astype(jnp.float32),
        lax.psum_scatter(
            grad_up.astype(jnp.bfloat16), "lon", scatter_dimension=0, tiled=True
        ).astype(jnp.float32),
        lax.psum_scatter(
            grad_up_bias.astype(jnp.bfloat16), "lon", scatter_dimension=1, tiled=True
        ).astype(jnp.float32),
        lax.psum_scatter(
            grad_down.astype(jnp.bfloat16), "lon", scatter_dimension=1, tiled=True
        ).astype(jnp.float32),
        lax.psum_scatter(
            grad_final_weight.astype(jnp.bfloat16), "lon", scatter_dimension=0, tiled=True
        ).astype(jnp.float32),
    )
    shared_out = (
        lax.psum_scatter(grad_patch, ("lon", "head"), scatter_dimension=2, tiled=True),
        lax.psum_scatter(grad_variable, ("lon", "head"), scatter_dimension=1, tiled=True),
        lax.psum_scatter(grad_lead, ("lon", "head"), scatter_dimension=1, tiled=True),
        lax.psum_scatter(grad_gain_one, ("lon", "head"), scatter_dimension=0, tiled=True),
        lax.psum_scatter(grad_shift_one, ("lon", "head"), scatter_dimension=0, tiled=True),
        lax.psum_scatter(grad_gain_two, ("lon", "head"), scatter_dimension=0, tiled=True),
        lax.psum_scatter(grad_shift_two, ("lon", "head"), scatter_dimension=0, tiled=True),
    )
    return (
        predicted,
        pixel_grad,
        shared_out[0],
        shared_out[1],
        sector_out[0],
        sector_out[1],
        sector_out[2],
        sector_out[3],
        shared_out[2],
        shared_out[3],
        shared_out[4],
        sector_out[4],
        sector_out[5],
        shared_out[5],
        shared_out[6],
        sector_out[6],
        sector_out[7],
        sector_out[8],
        sector_out[9],
    )


def solution(mesh):
    placed = (
        P(None, None, "lon"),
        P(),
        P(),
        P(None, "lon"),
        P(None, "lon"),
        P(),
        P(None, None, ("lon", "head")),
        P(None, ("lon", "head")),
        P("head", "lon"),
        P("lon", "head"),
        P("lon", "head"),
        P("head", "lon"),
        P(None, ("lon", "head")),
        P(("lon", "head")),
        P(("lon", "head")),
        P(None, "lon", "head"),
        P("head", "lon"),
        P(("lon", "head")),
        P(("lon", "head")),
        P("lon", "head"),
        P("head", "lon"),
        P("head", "lon"),
        P("lon", "head"),
        P(None, "lon", "head"),
    )
    return jax.shard_map(
        local,
        mesh=mesh,
        in_specs=placed,
        out_specs=(
            P(None, "lon", "head"),
            P(None, None, "lon"),
            P(None, None, ("lon", "head")),
            P(None, ("lon", "head")),
            P("head", "lon"),
            P("lon", "head"),
            P("lon", "head"),
            P("head", "lon"),
            P(None, ("lon", "head")),
            P(("lon", "head")),
            P(("lon", "head")),
            P(None, "lon", "head"),
            P("head", "lon"),
            P(("lon", "head")),
            P(("lon", "head")),
            P("lon", "head"),
            P("head", "lon"),
            P("head", "lon"),
            P("lon", "head"),
        ),
        check_vma=False,
    )
```

profile of v0, /device:TPU:0, one launch (start us, length us, event | category | flops | bytes accessed | tf_op | source)
XLA Modules:
  0.0 3484.2 jit_solution(15301932357770188999)
XLA Ops:
  18.9 72.4 %all_gather.81 = bf16[48,4,1024]{0,1,2:T(4,128)(2,1)S(1)} all-gather(bf16[48,4,32]{0,1,2:T(4,128)(2,1)S(1)} %copy.328), channel_id=1, replica_groups=mesh['lon'=16,'head'=2] {'lon','head'}, dimensions={2}, use_global_device_ids=true | all-gather | bytes 405504 | tf_op jit(solution)/shard_map/all_gather | solution.py:250
  91.5 65.5 %all_gather.82 = bf16[48,1024]{0,1:T(8,128)(2,1)S(1)} all-gather(bf16[48,32]{0,1:T(8,128)(2,1)} %param.41), channel_id=1, replica_groups=mesh['lon'=16,'head'=2] {'lon','head'}, dimensions={1}, use_global_device_ids=true | all-gather | bytes 101376 | tf_op jit(solution)/shard_map/all_gather | solution.py:251
  203.5 447.5 %while.68 = (s32[]{:T(128)}, bf16[4,128,8,64]{3,2,1,0:T(8,128)(2,1)}, bf16[4,128,48,4]{1,3,2,0:T(4,128)(2,1)}, bf16[48,4,1024]{2,1,0:T(4,128)(2,1)S(1)}, bf16[48...) while((s32[]{:T(128)}, bf16[4,128,8,64]{3,2,1,0:T(8,128)(2,1)}, ...), condition=%wide.region_5.6_spmd, body=%wide.region_2.5_spmd.sunk | while | flops 13001555968 | bytes 131626088 | solution.py:328
  657.3 39.0 %all-reduce.18 = (bf16[1024]{0:T(1024)(128)(2,1)}, bf16[1024]{0:T(1024)(128)(2,1)S(1)}, bf16[1024]{0:T(1024)(128)(2,1)S(1)}, bf16[1024]{0:T(1024)(128)(2,1)S(1)}) all-reduce(bf16[1024]{0:T(1024)(128)(2,1)S(1)} %dynamic-update-slice.3, bf16[1024]{0:T(1024)(128)(2,1)S(1)} %dynamic-update-slice.2, ...), channel_id=1, replica_groups=mesh['lon'=16,'head'=2] {'lon','head'}, use_global_device_ids=true, to_apply=%add.9 | all-reduce | flops 4096 | bytes 16384
  696.4 65.7 %all-gather.1 = bf16[32,32,2]{1,2,0:T(2,128)(2,1)S(1)} all-gather(bf16[1,32,2]{1,2,0:T(2,128)(2,1)S(1)} %bitcast.487), channel_id=1, replica_groups=mesh['lon'=16,'head'=2] {'lon','head'}, dimensions={0}, use_global_device_ids=true | all-gather | bytes 4224 | tf_op jit(solution)/shard_map/all_gather | solution.py:252
  784.8 47.5 %all-gather.27.cloned.1.call-done = bf16[3,1024,512]{2,1,0:T(8,128)(2,1)} async-done(((bf16[3,64,512]{2,1,0:T(8,128)(2,1)}), bf16[3,1024,512]{2,1,0:T(8,128)(2,1)}) %all-gather.27.cloned.1.call-update) | async-done | bytes 3145744 | tf_op jit(solution)/shard_map/all_gather | solution.py:266
  860.7 80.3 %all-gather.31.cloned.1.call-done = bf16[4,2048,8,64]{1,0,3,2:T(4,128)(2,1)} async-done(((bf16[4,128,8,64]{1,0,3,2:T(4,128)(2,1)}), bf16[4,2048,8,64]{1,0,3,2:T(4,128)(2,1)}) %all-gather.31.cloned.1.call-update) | async-done | bytes 8388624 | tf_op jit(solution)/shard_map/all_gather | solution.py:344
  952.3 28.8 while.69
  981.1 65.2 %all-gather.29.cloned.1.call-done = bf16[4,2048,8,64]{1,0,3,2:T(4,128)(2,1)} async-done(((bf16[4,128,8,64]{1,0,3,2:T(4,128)(2,1)}), bf16[4,2048,8,64]{1,0,3,2:T(4,128)(2,1)}) %all-gather.29.cloned.1.call-update) | async-done | bytes 8388624 | tf_op jit(solution)/shard_map/all_gather | solution.py:345
  1057.7 29.0 while.70
  1153.9 30.7 all-gather.37.cloned.1.call-done
  1229.4 52.8 %all-gather.39.cloned.1.call-done = bf16[2048,1024]{0,1:T(8,128)(2,1)} async-done(((bf16[2048,64]{0,1:T(8,128)(2,1)}), bf16[2048,1024]{0,1:T(8,128)(2,1)}) %all-gather.39.cloned.1.call-update) | async-done | bytes 4194320 | tf_op jit(solution)/shard_map/all_gather | solution.py:270
  1384.8 79.8 %while.71 = (s32[]{:T(128)}, f32[4,128,8,64]{1,3,2,0:T(8,128)S(1)}, bf16[4,2048,8,64]{1,3,2,0:T(8,128)(2,1)}, bf16[4,2048,8,64]{1,3,2,0:T(8,128)(2,1)}, s32[4]{0...) while((s32[]{:T(128)}, f32[4,128,8,64]{1,3,2,0:T(8,128)S(1)}, ...), condition=%wide.region_26.27_spmd.clone, body=%wide.region_25.26_spmd.clone.sunk | while | flops 1369440256 | bytes 57485568 | solution.py:444
  1464.6 23.9 copy.416
  1512.0 24.7 copy.414
  1536.7 23.7 reshape.319
  1562.5 54.2 %reduce-scatter.58.cloned.1.call-done = bf16[128,2048]{1,0:T(8,128)(2,1)} async-done(((bf16[2048,2048]{1,0:T(8,128)(2,1)}), bf16[128,2048]{1,0:T(8,128)(2,1)}) %reduce-scatter.58.cloned.1.call-update) | async-done | bytes 524304
  1619.6 106.0 %reduce-scatter.56.cloned.1.call-done = bf16[128,2048]{1,0:T(8,128)(2,1)} async-done(((bf16[2048,2048]{1,0:T(8,128)(2,1)}), bf16[128,2048]{1,0:T(8,128)(2,1)}) %reduce-scatter.56.cloned.1.call-update) | async-done | bytes 524304
  1810.9 1180.9 %while.72 = (s32[]{:T(128)}, f32[48,4,1024]{2,1,0:T(4,128)}, f32[48,1024]{1,0:T(8,128)}, f32[8,64]{1,0:T(8,128)S(1)}, f32[1024,1024]{1,0:T(8,128)}, /*index=5*/b...) while((s32[]{:T(128)}, f32[48,4,1024]{2,1,0:T(4,128)}, ...), condition=%wide.region_37.38_spmd.clone, body=%wide.region_32.37_spmd.clone.sunk | while | flops 39374934016 | bytes 432913920 | solution.py:490
  2034.8 31.1 fusion.355
  2075.3 28.4 fusion.354
  2328.4 31.0 fusion.355
  2368.7 28.2 fusion.354
  2621.0 31.1 fusion.355
  2661.4 28.5 fusion.354
  2914.0 31.0 fusion.355
  2954.3 28.2 fusion.354
  3014.6 39.6 %all-reduce.17 = (f32[1024]{0:T(1024)S(1)}, f32[1024]{0:T(1024)S(1)}, f32[1024]{0:T(1024)S(1)}, f32[1024]{0:T(1024)S(1)}) all-reduce(f32[1024]{0:T(1024)S(1)} %copy-done.53, f32[1024]{0:T(1024)S(1)} %copy-done.52, f32[1024]{0:T(1024)S(1)} %copy-done.50, f32[1024]{0:T(1024)S(1)} %copy-done.51), channel_id=17, replica_groups=mesh['lon'=16,'head'=2] {'lon','head'}, use_global_device_ids=true, to_apply=%region_49.50.clone | all-reduce | flops 4096 | bytes 32768
  3059.8 60.4 %all-reduce.19 = (bf16[8,64]{0,1:T(8,128)(2,1)S(1)}, bf16[32,64]{1,0:T(8,128)(2,1)S(1)}) all-reduce(bf16[8,64]{0,1:T(8,128)(2,1)S(1)} %copy.368, bf16[32,64]{1,0:T(8,128)(2,1)S(1)} %convert_element_type.350), channel_id=12, replica_groups=mesh['lon'=16,'head'=2] {'lon'}, use_global_device_ids=true, to_apply=%region_41.42.clone | all-reduce | flops 2560 | bytes 10240
  3163.6 41.4 %reduce-scatter.44.cloned.1.call-done = bf16[64,512]{1,0:T(8,128)(2,1)} async-done(((bf16[1024,512]{1,0:T(8,128)(2,1)}), bf16[64,512]{1,0:T(8,128)(2,1)}) %reduce-scatter.44.cloned.1.call-update) | async-done | bytes 65552 | tf_op jit(solution)/shard_map/reduce_scatter | solution.py:519
  3206.5 134.3 %reduce-scatter.40.cloned.1.call-done = f32[48,32]{0,1:T(8,128)} async-done(((f32[48,1024]{0,1:T(8,128)}), f32[48,32]{0,1:T(8,128)}) %reduce-scatter.40.cloned.1.call-update) | async-done | bytes 6160 | tf_op jit(solution)/shard_map/reduce_scatter | solution.py:546
  3340.8 136.6 %reduce-scatter.38.cloned.1.call-done = f32[48,4,32]{0,2,1:T(8,128)} async-done(((f32[48,4,1024]{0,2,1:T(8,128)}), f32[48,4,32]{0,2,1:T(8,128)}) %reduce-scatter.38.cloned.1.call-update) | async-done | bytes 24592 | tf_op jit(solution)/shard_map/reduce_scatter | solution.py:545
  (743 shorter events, 2034.1 us)
Async XLA Ops:
  7.2 191.7 %all-gather.19.cloned.1.call-start = ((), (), s32[]{:S(2)}) async-start(), calls=%async_computation.18 | async-start | bytes 1114112 | tf_op jit(solution)/shard_map/all_gather | solution.py:263
  7.9 193.3 %all-gather.21.cloned.1.call-start = ((), (), s32[]{:S(2)}) async-start(), calls=%async_computation.19 | async-start | bytes 1114112 | tf_op jit(solution)/shard_map/all_gather | solution.py:264
  8.7 644.5 %all-gather.23.cloned.1.call-start = ((), (), s32[]{:S(2)}) async-start(), calls=%async_computation.20 | async-start | bytes 1114112 | tf_op jit(solution)/shard_map/all_gather | solution.py:265
  10.8 165.9 %collective-permute-start = (bf16[48,32,1]{2,1,0:T(8,128)(2,1)}, bf16[48,32,1]{2,1,0:T(8,128)(2,1)S(1)}, u32[]{:S(2)}, u32[]{:S(2)}) collective-permute-start(bf16[48,32,1]{2,1,0:T(8,128)(2,1)} %get-tuple-element.993), channel_id=1, source_target_pairs={{0,2},{2,4},{4,6},{6,8},{8,10},{10,12},{12,14},{14,16},{16,18},{18... | collective-permute-start | bytes 9224 | tf_op jit(solution)/shard_map/ppermute | solution.py:23
  11.2 166.2 %collective-permute-start.1 = (bf16[48,32,1]{2,1,0:T(8,128)(2,1)S(1)}, bf16[48,32,1]{2,1,0:T(8,128)(2,1)}, u32[]{:S(2)}, u32[]{:S(2)}) collective-permute-start(bf16[48,32,1]{2,1,0:T(8,128)(2,1)S(1)} %get-tuple-element.994), channel_id=1, source_target_pairs={{2,0},{4,2},{6,4},{8,6},{10,8},{12,10},{14,12},{16,14},{18,16},{20... | collective-permute-start | bytes 9224 | tf_op jit(solution)/shard_map/ppermute | solution.py:24
  16.2 746.1 %reduce-scatter.26.cloned.1.call-start = ((), (), s32[]{:S(2)}) async-start(), calls=%async_computation.21 | async-start | bytes 1572864 | tf_op jit(solution)/shard_map/reduce_scatter | solution.py:40
  656.3 128.5 %all-gather.25.cloned.1.call-start = ((), (), s32[]{:S(2)}) async-start(), calls=%async_computation.22 | async-start | bytes 1572864 | tf_op jit(solution)/shard_map/all_gather | solution.py:46
  768.1 172.9 %all-gather.31.cloned.1.call-start = ((), (), s32[]{:S(2)}) async-start(), calls=%async_computation.25 | async-start | bytes 8912896 | tf_op jit(solution)/shard_map/all_gather | solution.py:344
  837.7 208.7 %all-gather.29.cloned.1.call-start = ((), (), s32[]{:S(2)}) async-start(), calls=%async_computation.24 | async-start | bytes 8912896 | tf_op jit(solution)/shard_map/all_gather | solution.py:345
  838.9 248.4 %all-gather.33.cloned.1.call-start = ((), (), s32[]{:S(2)}) async-start(), calls=%async_computation.26 | async-start | bytes 1114112 | tf_op jit(solution)/shard_map/all_gather | solution.py:267
  839.6 272.5 %reduce-scatter.28.cloned.1.call-start = ((), (), s32[]{:S(2)}) async-start(), calls=%async_computation.27 | async-start | bytes 1572864 | tf_op jit(solution)/shard_map/reduce_scatter | solution.py:40
  1111.4 73.2 %all-gather.37.cloned.1.call-start = ((), (), s32[]{:S(2)}) async-start(), calls=%async_computation.29 | async-start | bytes 4456448 | tf_op jit(solution)/shard_map/all_gather | solution.py:268
  1112.0 94.6 %all-gather.35.cloned.1.call-start = ((), (), s32[]{:S(2)}) async-start(), calls=%async_computation.28 | async-start | bytes 1572864 | tf_op jit(solution)/shard_map/all_gather | solution.py:46
  1117.5 111.9 %all-gather.43.cloned.1.call-start = ((), (), s32[]{:S(2)}) async-start(), calls=%async_computation.34 | async-start | bytes 1572864 | tf_op jit(solution)/shard_map/all_gather | solution.py:46
  1131.7 150.5 %all-gather.39.cloned.1.call-start = ((), (), s32[]{:S(2)}) async-start(), calls=%async_computation.30 | async-start | bytes 4456448 | tf_op jit(solution)/shard_map/all_gather | solution.py:270
  1132.3 189.8 %reduce-scatter.34.cloned.1.call-start = ((), (), s32[]{:S(2)}) async-start(), calls=%async_computation.35 | async-start | bytes 1572864 | tf_op jit(solution)/shard_map/reduce_scatter | solution.py:40
  1349.4 267.3 %reduce-scatter.58.cloned.1.call-start = ((), (), s32[]{:S(2)}) async-start(), calls=%async_computation.50 | async-start | bytes 8912896
  1511.9 213.6 %reduce-scatter.56.cloned.1.call-start = ((), (), s32[]{:S(2)}) async-start(), calls=%async_computation.49 | async-start | bytes 8912896
  1560.4 195.3 %reduce-scatter.36.cloned.1.call-start = ((), (), s32[]{:S(2)}) async-start(), calls=%async_computation.37 | async-start | bytes 1572864 | tf_op jit(solution)/shard_map/reduce_scatter | solution.py:40
  1736.2 71.2 %all-gather.47.cloned.1.call-start = ((), (), s32[]{:S(2)}) async-start(), calls=%async_computation.38 | async-start | bytes 1572864 | tf_op jit(solution)/shard_map/all_gather | solution.py:46
  1762.9 1243.4 %reduce-scatter.54.cloned.1.call-start = ((), (), s32[]{:S(2)}) async-start(), calls=%async_computation.48 | async-start | bytes 278528 | tf_op jit(solution)/shard_map/reduce_scatter | solution.py:540
  1781.5 1226.1 %reduce-scatter.48.cloned.1.call-start = ((), (), s32[]{:S(2)}) async-start(), calls=%async_computation.45 | async-start | bytes 1114112 | tf_op jit(solution)/shard_map/reduce_scatter | solution.py:528
  1784.6 1224.6 %reduce-scatter.52.cloned.1.call-start = ((), (), s32[]{:S(2)}) async-start(), calls=%async_computation.47 | async-start | bytes 4456448 | tf_op jit(solution)/shard_map/reduce_scatter | solution.py:537
  1790.5 1220.5 %reduce-scatter.50.cloned.1.call-start = ((), (), s32[]{:S(2)}) async-start(), calls=%async_computation.46 | async-start | bytes 4456448 | tf_op jit(solution)/shard_map/reduce_scatter | solution.py:531
  1796.8 1216.0 %all-reduce.25.cloned.1.call-start = ((), (), s32[]{:S(2)}) async-start(), calls=%async_computation.52 | async-start | bytes 8388608
  1806.2 1250.4 %reduce-scatter.60.cloned.1.call-start = ((), (), s32[]{:S(2)}) async-start(), calls=%async_computation.51 | async-start | bytes 540672
  1807.3 1313.0 %all-reduce.23.cloned.1.call-start = ((), (), s32[]{:S(2)}) async-start(), calls=%async_computation.39 | async-start | bytes 1048576 | tf_op jit(solution)/shard_map/psum | solution.py:36
  2994.0 166.6 %reduce-scatter.46.cloned.1.call-start = ((), (), s32[]{:S(2)}) async-start(), calls=%async_computation.44 | async-start | bytes 1114112 | tf_op jit(solution)/shard_map/reduce_scatter | solution.py:522
  2997.2 164.9 %reduce-scatter.42.cloned.1.call-start = ((), (), s32[]{:S(2)}) async-start(), calls=%async_computation.42 | async-start | bytes 1114112 | tf_op jit(solution)/shard_map/reduce_scatter | solution.py:516
  3001.4 203.5 %reduce-scatter.44.cloned.1.call-start = ((), (), s32[]{:S(2)}) async-start(), calls=%async_computation.43 | async-start | bytes 1114112 | tf_op jit(solution)/shard_map/reduce_scatter | solution.py:519
  3002.0 338.8 %reduce-scatter.40.cloned.1.call-start = ((), (), s32[]{:S(2)}) async-start(), calls=%async_computation.41 | async-start | bytes 540672 | tf_op jit(solution)/shard_map/reduce_scatter | solution.py:546
  3005.1 472.3 %reduce-scatter.38.cloned.1.call-start = ((), (), s32[]{:S(2)}) async-start(), calls=%async_computation.40 | async-start | bytes 2162688 | tf_op jit(solution)/shard_map/reduce_scatter | solution.py:545
  (122 other events, 5180.4 us)
Sparse Core Ops, SparseCore 0:
  10.2 41.9 all-gather.18
  54.3 37.0 all-gather.20
  93.6 37.2 all-gather.22
  656.4 19.8 reduce-scatter.25
  787.1 45.2 all-gather.26
  837.8 103.1 all-gather.30
  943.9 102.4 all-gather.28
  1048.8 36.1 all-gather.32
  1111.5 20.1 reduce-scatter.31
  1134.0 50.5 all-gather.36
  1186.8 19.7 all-gather.34
  1208.1 21.2 all-gather.42
  1231.6 50.5 all-gather.38
  1324.3 20.3 reduce-scatter.29
  1349.5 21.2 all-gather.44
  1512.1 104.6 reduce-scatter.57
  1621.2 104.3 reduce-scatter.55
  1735.5 20.0 reduce-scatter.35
  1757.7 21.2 all-gather.40
  1781.2 21.2 all-gather.46
  1805.9 55.3 reduce-scatter.53
  1864.9 56.3 reduce-scatter.47
  1925.5 71.4 reduce-scatter.51
  2000.7 71.5 reduce-scatter.49
  2076.4 110.5 all-reduce.24
  2189.2 132.9 reduce-scatter.59
  2994.1 28.9 all-reduce.22
  3026.7 57.7 reduce-scatter.45
  3088.6 56.4 reduce-scatter.41
  3148.5 56.3 reduce-scatter.43
  3207.9 132.8 reduce-scatter.39
  3343.7 133.7 reduce-scatter.37
  (3 shorter events, 54.3 us)
where the time goes:
time: 3510 us; the launch traced here: 3480 us
  waiting for transfers between devices  910 us (26%)
  local copies, waits for them, and re-layouts  903 us (26%)
  matrix products  846 us (24%)
  blocking collectives  420 us (12%)
  other arithmetic  345 us (10%)
    convert_element_type x8, local copies, waits for them, and re-layouts, mixer_row(): embedded = embedded.astype(jnp.bfloat16)  177 us
    unnamed x39, waiting for transfers between devices  165 us
    unnamed x177, local copies, waits for them, and re-layouts  151 us
    unnamed x3, blocking collectives  139 us
    reduce_scatter x1, waiting for transfers between devices, local(): lax.psum_scatter(grad_patch, ('lon', 'head'), scatter_dimension=2, tiled=...  137 us
    dot_general x8, matrix products, mixer_row(): jnp.dot(embedded.reshape(slot_count * var_count, model_width), pair_weigh...  135 us
    reduce_scatter x1, waiting for transfers between devices, local(): lax.psum_scatter(grad_variable, ('lon', 'head'), scatter_dimension=1, til...  134 us
    reshape x8, local copies, waits for them, and re-layouts, mixer_row(): paired[:, local_width:]  130 us
  transfers between devices with their start and end apart: 39, of which 20 were waited for; matrix products, arithmetic and copies ran while one was open for 54% of the time, Pallas kernels for 0%

commit v1 on v0

--- a/solution.py
+++ b/solution.py
@@ -3,9 +3,12 @@
 import jax
 import jax.numpy as jnp
 from jax import lax
+from jax.experimental import pallas as pl
+from jax.experimental.pallas import tpu as pltpu
 from jax.sharding import PartitionSpec as P
 
 HEAD_DIM = 64
+LON, HEAD = "lon", "head"
 
 
 epsilon = 1e-05
@@ -33,17 +36,17 @@
 
 
 def head_total(partial_sum):
-    return lax.psum(partial_sum.astype(jnp.bfloat16), "head").astype(jnp.float32)
+    return lax.psum(partial_sum.astype(jnp.bfloat16), HEAD).astype(jnp.float32)
 
 
 def head_share(partial_sum):
     return lax.psum_scatter(
-        partial_sum.astype(jnp.bfloat16), "head", scatter_dimension=0, tiled=True
+        partial_sum.astype(jnp.bfloat16), HEAD, scatter_dimension=0, tiled=True
     ).astype(jnp.float32)
 
 
 def head_rows(values):
-    return lax.all_gather(values, "head", axis=0, tiled=True)
+    return lax.all_gather(values, HEAD, axis=0, tiled=True)
 
 
 def reduce_rows(partial_sum):
@@ -247,28 +250,28 @@
     cotangent,
 ):
     shared = (
-        lax.all_gather(patch_weight, ("lon", "head"), axis=2, tiled=True),
-        lax.all_gather(variable_embed, ("lon", "head"), axis=1, tiled=True),
-        lax.all_gather(lead_embed, ("lon", "head"), axis=1, tiled=True),
-        lax.all_gather(first_gain, ("lon", "head"), axis=0, tiled=True),
-        lax.all_gather(first_bias, ("lon", "head"), axis=0, tiled=True),
-        lax.all_gather(second_gain, ("lon", "head"), axis=0, tiled=True),
-        lax.all_gather(second_bias, ("lon", "head"), axis=0, tiled=True),
+        lax.all_gather(patch_weight, (LON, HEAD), axis=2, tiled=True),
+        lax.all_gather(variable_embed, (LON, HEAD), axis=1, tiled=True),
+        lax.all_gather(lead_embed, (LON, HEAD), axis=1, tiled=True),
+        lax.all_gather(first_gain, (LON, HEAD), axis=0, tiled=True),
+        lax.all_gather(first_bias, (LON, HEAD), axis=0, tiled=True),
+        lax.all_gather(second_gain, (LON, HEAD), axis=0, tiled=True),
+        lax.all_gather(second_bias, (LON, HEAD), axis=0, tiled=True),
     )
     full_patch, full_variable, full_lead, gain_first, shift_first, gain_second, shift_second = (
         shared
     )
     sector = (
-        lax.all_gather(mixer_query, "lon", axis=1, tiled=True),
-        lax.all_gather(mixer_keys, "lon", axis=0, tiled=True),
-        lax.all_gather(mixer_values, "lon", axis=0, tiled=True),
-        lax.all_gather(mixer_output, "lon", axis=1, tiled=True),
-        lax.all_gather(attention_in, "lon", axis=1, tiled=True),
-        lax.all_gather(attention_out, "lon", axis=1, tiled=True),
-        lax.all_gather(expand_weight, "lon", axis=0, tiled=True),
-        lax.all_gather(expand_bias, "lon", axis=1, tiled=True),
-        lax.all_gather(reduce_weight, "lon", axis=1, tiled=True),
-        lax.all_gather(output_weight, "lon", axis=0, tiled=True),
+        lax.all_gather(mixer_query, LON, axis=1, tiled=True),
+        lax.all_gather(mixer_keys, LON, axis=0, tiled=True),
+        lax.all_gather(mixer_values, LON, axis=0, tiled=True),
+        lax.all_gather(mixer_output, LON, axis=1, tiled=True),
+        lax.all_gather(attention_in, LON, axis=1, tiled=True),
+        lax.all_gather(attention_out, LON, axis=1, tiled=True),
+        lax.all_gather(expand_weight, LON, axis=0, tiled=True),
+        lax.all_gather(expand_bias, LON, axis=1, tiled=True),
+        lax.all_gather(reduce_weight, LON, axis=1, tiled=True),
+        lax.all_gather(output_weight, LON, axis=0, tiled=True),
     )
     (
         head_query,
@@ -294,11 +297,11 @@
     lat_slot = crop_lookup(crop_starts, slot_crops)
     shift_slot = crop_lookup(crop_shifts, slot_crops)
     lead_slot = crop_lookup(lead_hours, slot_crops).astype(jnp.float32).reshape(token_count) / 100.0
-    share_count = token_count // lax.axis_size("head")
+    share_count = token_count // lax.axis_size(HEAD)
     lead_rows = lax.dynamic_slice_in_dim(
-        lead_slot, lax.axis_index("head") * share_count, share_count
-    )
-    padded = extended(pixels, (("lon", 2),), 1)
+        lead_slot, lax.axis_index(HEAD) * share_count, share_count
+    )
+    padded = extended(pixels, ((LON, 2),), 1)
     var_count, lat_count = (pixels.shape[0], pixels.shape[1])
     west_pairs = padded[:, :, : 2 * slot_width].reshape(var_count, lat_count, slot_width, 2)
     east_pairs = padded[:, :, 2:].reshape(var_count, lat_count, slot_width, 2)
@@ -341,9 +344,9 @@
     query_crops = slot_crops.astype(jnp.float32)
     key_tags = jnp.where(occupied == 1, slot_crops, -1).astype(jnp.bfloat16)
     key_all, value_all, tag_all = (
-        lax.all_gather(key_local, "lon", axis=1, tiled=True),
-        lax.all_gather(value_local, "lon", axis=1, tiled=True),
-        lax.all_gather(key_tags, "lon", axis=1, tiled=True),
+        lax.all_gather(key_local, LON, axis=1, tiled=True),
+        lax.all_gather(value_local, LON, axis=1, tiled=True),
+        lax.all_gather(key_tags, LON, axis=1, tiled=True),
     )
     block_width = min(512, key_all.shape[1])
     tag_wide = tag_all.astype(jnp.float32)
@@ -398,9 +401,9 @@
     out_grads = out_grads.reshape(row_count, slot_width, head_count, HEAD_DIM)
     deltas = jnp.transpose(jnp.sum(out_grads.astype(jnp.float32) * attended, axis=-1), (0, 2, 1))
     back_keys, back_values, back_raw = (
-        lax.all_gather(key_local, "lon", axis=1, tiled=True),
-        lax.all_gather(value_local, "lon", axis=1, tiled=True),
-        lax.all_gather(key_tags, "lon", axis=1, tiled=True),
+        lax.all_gather(key_local, LON, axis=1, tiled=True),
+        lax.all_gather(value_local, LON, axis=1, tiled=True),
+        lax.all_gather(key_tags, LON, axis=1, tiled=True),
     )
     back_tags = back_raw.astype(jnp.float32)
     scale = HEAD_DIM ** (-0.5)
@@ -446,10 +449,10 @@
     )
     key_grad, value_grad = (
         lax.psum_scatter(
-            key_part.astype(jnp.bfloat16), "lon", scatter_dimension=1, tiled=True
+            key_part.astype(jnp.bfloat16), LON, scatter_dimension=1, tiled=True
         ).astype(jnp.float32),
         lax.psum_scatter(
-            value_part.astype(jnp.bfloat16), "lon", scatter_dimension=1, tiled=True
+            value_part.astype(jnp.bfloat16), LON, scatter_dimension=1, tiled=True
         ).astype(jnp.float32),
     )
     stacked = (
@@ -503,7 +506,7 @@
         east_grad, ((0, 0), (0, 0), (2, 0))
     )
     rim_values = jnp.stack([padded_grad[:, :, 0], padded_grad[:, :, -1]], axis=2)
-    returned = extended(rim_values, (("lon", 2),), 1)
+    returned = extended(rim_values, ((LON, 2),), 1)
     pixel_grad = (
         padded_grad[:, :, 1:-1]
         + jnp.pad(returned[:, :, 0:1], ((0, 0), (0, 0), (0, 2 * slot_width - 1)))
@@ -511,44 +514,44 @@
     )
     sector_out = (
         lax.psum_scatter(
-            grad_query.astype(jnp.bfloat16), "lon", scatter_dimension=1, tiled=True
+            grad_query.astype(jnp.bfloat16), LON, scatter_dimension=1, tiled=True
         ).astype(jnp.float32),
         lax.psum_scatter(
-            grad_pair[:, :local_width].astype(jnp.bfloat16), "lon", scatter_dimension=0, tiled=True
+            grad_pair[:, :local_width].astype(jnp.bfloat16), LON, scatter_dimension=0, tiled=True
         ).astype(jnp.float32),
         lax.psum_scatter(
-            grad_pair[:, local_width:].astype(jnp.bfloat16), "lon", scatter_dimension=0, tiled=True
+            grad_pair[:, local_width:].astype(jnp.bfloat16), LON, scatter_dimension=0, tiled=True
         ).astype(jnp.float32),
         lax.psum_scatter(
-            grad_mixer.astype(jnp.bfloat16), "lon", scatter_dimension=1, tiled=True
+            grad_mixer.astype(jnp.bfloat16), LON, scatter_dimension=1, tiled=True
         ).astype(jnp.float32),
         lax.psum_scatter(
-            grad_input.astype(jnp.bfloat16), "lon", scatter_dimension=1, tiled=True
+            grad_input.astype(jnp.bfloat16), LON, scatter_dimension=1, tiled=True
         ).astype(jnp.float32),
         lax.psum_scatter(
-            grad_proj.astype(jnp.bfloat16), "lon", scatter_dimension=1, tiled=True
+            grad_proj.astype(jnp.bfloat16), LON, scatter_dimension=1, tiled=True
         ).astype(jnp.float32),
         lax.psum_scatter(
-            grad_up.astype(jnp.bfloat16), "lon", scatter_dimension=0, tiled=True
+            grad_up.astype(jnp.bfloat16), LON, scatter_dimension=0, tiled=True
         ).astype(jnp.float32),
         lax.psum_scatter(
-            grad_up_bias.astype(jnp.bfloat16), "lon", scatter_dimension=1, tiled=True
+            grad_up_bias.astype(jnp.bfloat16), LON, scatter_dimension=1, tiled=True
         ).astype(jnp.float32),
         lax.psum_scatter(
-            grad_down.astype(jnp.bfloat16), "lon", scatter_dimension=1, tiled=True
+            grad_down.astype(jnp.bfloat16), LON, scatter_dimension=1, tiled=True
         ).astype(jnp.float32),
         lax.psum_scatter(
-            grad_final_weight.astype(jnp.bfloat16), "lon", scatter_dimension=0, tiled=True
+            grad_final_weight.astype(jnp.bfloat16), LON, scatter_dimension=0, tiled=True
         ).astype(jnp.float32),
     )
     shared_out = (
-        lax.psum_scatter(grad_patch, ("lon", "head"), scatter_dimension=2, tiled=True),
-        lax.psum_scatter(grad_variable, ("lon", "head"), scatter_dimension=1, tiled=True),
-        lax.psum_scatter(grad_lead, ("lon", "head"), scatter_dimension=1, tiled=True),
-        lax.psum_scatter(grad_gain_one, ("lon", "head"), scatter_dimension=0, tiled=True),
-        lax.psum_scatter(grad_shift_one, ("lon", "head"), scatter_dimension=0, tiled=True),
-        lax.psum_scatter(grad_gain_two, ("lon", "head"), scatter_dimension=0, tiled=True),
-        lax.psum_scatter(grad_shift_two, ("lon", "head"), scatter_dimension=0, tiled=True),
+        lax.psum_scatter(grad_patch, (LON, HEAD), scatter_dimension=2, tiled=True),
+        lax.psum_scatter(grad_variable, (LON, HEAD), scatter_dimension=1, tiled=True),
+        lax.psum_scatter(grad_lead, (LON, HEAD), scatter_dimension=1, tiled=True),
+        lax.psum_scatter(grad_gain_one, (LON, HEAD), scatter_dimension=0, tiled=True),
+        lax.psum_scatter(grad_shift_one, (LON, HEAD), scatter_dimension=0, tiled=True),
+        lax.psum_scatter(grad_gain_two, (LON, HEAD), scatter_dimension=0, tiled=True),
+        lax.psum_scatter(grad_shift_two, (LON, HEAD), scatter_dimension=0, tiled=True),
     )
     return (
         predicted,
@@ -573,57 +576,1567 @@
     )
 
 
+MESH = pl.DeviceIdType.MESH
+BOTH = (LON, HEAD)
+LON_SIZE = 16
+HEAD_SIZE = 2
+CHUNK = 256
+low = jnp.bfloat16
+wide = jnp.float32
+
+
+def planned(mesh):
+    return mesh.shape[LON] == LON_SIZE and mesh.shape[HEAD] == HEAD_SIZE
+
+
+def dot(left, right, left_dim=1, right_dim=0):
+    return lax.dot_general(
+        left, right, (((left_dim,), (right_dim,)), ((), ())), preferred_element_type=wide
+    )
+
+
+def position():
+    lon = lax.axis_index(LON)
+    x = lax.axis_index(HEAD)
+    z = lax.div(lon, 4)
+    y = lax.rem(lax.div(lon, 2), 2)
+    c = lax.rem(lon, 2)
+    return x, z, y, c
+
+
+def partners(x, z, y, c):
+    here = z * 4 + y * 2 + c
+    across = {
+        "x": (here, 1 - x),
+        "y": (z * 4 + (1 - y) * 2 + c, x),
+        "c": (z * 4 + y * 2 + 1 - c, x),
+    }
+    line = [(lax.rem(z + step, 4) * 4 + y * 2 + c, x) for step in (1, 2, 3)]
+    return across, line
+
+
+def sector_of(z, y, c, x, part, side):
+    return (y * 2 + c) * 4 + x * 2 + part, side
+
+
+def block_of(z, y, row):
+    return row * 4 + z, y
+
+
+def meet(peers, others=(), own=None):
+    barrier = pltpu.get_barrier_semaphore()
+    for device in peers:
+        pl.semaphore_signal(barrier, inc=1, device_id=device, device_id_type=MESH)
+    for device in others:
+
+        @pl.when(jnp.logical_not(same(device, own)))
+        def _():
+            pl.semaphore_signal(barrier, inc=1, device_id=device, device_id_type=MESH)
+
+    expected = len(peers)
+    for device in others:
+        expected = expected + 1 - same(device, own).astype(jnp.int32)
+    pl.semaphore_wait(barrier, expected)
+
+
+def same(device, own):
+    return jnp.logical_and(device[0] == own[0], device[1] == own[1])
+
+
+def post(source, target, send_sem, recv_sem, device, own):
+    here = same(device, own)
+
+    @pl.when(here)
+    def _():
+        pltpu.make_async_copy(source, target, recv_sem).start()
+
+    @pl.when(jnp.logical_not(here))
+    def _():
+        remote(source, target, send_sem, recv_sem, device).start()
+
+
+def settle(source, target, send_sem, recv_sem, device, own):
+    @pl.when(jnp.logical_not(same(device, own)))
+    def _():
+        remote(source, target, send_sem, recv_sem, device).wait_send()
+
+
+def remote(source, target, send_sem, recv_sem, device):
+    return pltpu.make_async_remote_copy(
+        src_ref=source,
+        dst_ref=target,
+        send_sem=send_sem,
+        recv_sem=recv_sem,
+        device_id=device,
+        device_id_type=MESH,
+    )
+
+
+def gather_kernel(items, count, *refs):
+    ins, outs = refs[:count], refs[count + 2 : 2 * count + 2]
+    patch_in, grad_in = refs[count : count + 2]
+    patch_out, grad_out = refs[2 * count + 2 : 2 * count + 4]
+    own_sem, line_send, line_recv, hop_send, hop_recv, post_send, post_recv = refs[
+        2 * count + 4 :
+    ]
+    x, z, y, c = position()
+    across, line = partners(x, z, y, c)
+    own = (z * 4 + y * 2 + c, x)
+    sources = [sector_of(z, y, c, x, part, side) for part in range(2) for side in range(2)]
+    meet(list(across.values()) + line, sources, own)
+    letters = []
+    for part in range(2):
+        row = 2 * x + part
+        letters.append(
+            (patch_in.at[part], patch_out.at[c], post_send.at[part], post_recv.at[c])
+            + (block_of(z, y, row), own)
+        )
+    for row in range(4):
+        letters.append(
+            (grad_in.at[row], grad_out.at[x, c], post_send.at[2 + row])
+            + (post_recv.at[2 + 2 * x + c], block_of(z, y, row), own)
+        )
+    for letter in letters:
+        post(*letter)
+
+    def views(item):
+        index, lead, first, rows, _ = item
+        source, target = ins[index], outs[index]
+        if lead is not None:
+            source, target = source.at[lead], target.at[lead]
+        return source.at[pl.ds(first, rows)], target, pl.ds(first, rows)
+
+    def copies(number):
+        item = items[number]
+        source, target, span = views(item)
+        own = target.at[x, z, y, c, span]
+        keep = pltpu.make_async_copy(source, own, own_sem.at[number])
+        along = [
+            remote(source, own, line_send.at[number, d], line_recv.at[number, d], line[d])
+            for d in range(3)
+        ]
+        quarter = target.at[x, :, y, c, span]
+        if item[4] == 0:
+            half, order = target.at[x, :, :, c, span], ("y", "x")
+        else:
+            half, order = target.at[:, :, y, c, span], ("x", "y")
+        full = target.at[:, :, :, c, span]
+        hops = [
+            remote(part, part, hop_send.at[number, k], hop_recv.at[number, k], across[axis])
+            for k, (part, axis) in enumerate(
+                ((quarter, order[0]), (half, order[1]), (full, "c"))
+            )
+        ]
+        return keep, along, hops
+
+    plan = [copies(number) for number in range(len(items))]
+    total = len(items)
+    for step in range(total + 8):
+        if step < total:
+            keep, along, _ = plan[step]
+            keep.start()
+            for one in along:
+                one.start()
+        if 0 <= step - 2 < total:
+            keep, along, hops = plan[step - 2]
+            keep.wait()
+            for one in along:
+                one.wait_recv()
+            hops[0].start()
+        if 0 <= step - 4 < total:
+            hops = plan[step - 4][2]
+            hops[0].wait_recv()
+            hops[1].start()
+        if 0 <= step - 6 < total:
+            hops = plan[step - 6][2]
+            hops[1].wait_recv()
+            hops[2].start()
+        if 0 <= step - 8 < total:
+            plan[step - 8][2][2].wait_recv()
+    for _, along, hops in plan:
+        for one in along + hops:
+            one.wait_send()
+    for letter in letters:
+        settle(*letter)
+    for part in range(2):
+        pltpu.make_async_copy(patch_in.at[part], patch_out.at[part], post_recv.at[part]).wait()
+    for side in range(2):
+        for part in range(2):
+            pltpu.make_async_copy(
+                grad_in.at[0], grad_out.at[side, part], post_recv.at[2 + 2 * side + part]
+            ).wait()
+
+
+def gather_all(arrays, patches, grads, number):
+    items = []
+    for index, array in enumerate(arrays):
+        leads = range(array.shape[0]) if array.ndim == 3 else (None,)
+        rows = array.shape[-2]
+        for lead in leads:
+            if rows >= 64:
+                half = rows // 2
+                items.append((index, lead, 0, half, 0))
+                items.append((index, lead, half, half, 1))
+            else:
+                items.append((index, lead, 0, rows, 0))
+    count = len(arrays)
+    shapes = [
+        jax.ShapeDtypeStruct(a.shape[:-2] + (2, 4, 2, 2) + a.shape[-2:], a.dtype) for a in arrays
+    ] + [
+        jax.ShapeDtypeStruct(patches.shape, low),
+        jax.ShapeDtypeStruct((2, 2) + grads.shape[1:], low),
+    ]
+    sem = pltpu.SemaphoreType.DMA
+    gathered = pl.pallas_call(
+        partial(gather_kernel, items, count),
+        out_shape=shapes,
+        in_specs=[pl.BlockSpec(memory_space=pl.ANY)] * (count + 2),
+        out_specs=[pl.BlockSpec(memory_space=pl.ANY)] * (count + 2),
+        scratch_shapes=[
+            sem((len(items),)),
+            sem((len(items), 3)),
+            sem((len(items), 3)),
+            sem((len(items), 3)),
+            sem((len(items), 3)),
+            sem((6,)),
+            sem((6,)),
+        ],
+        compiler_params=pltpu.CompilerParams(collective_id=number, has_side_effects=True),
+    )(*arrays, patches, grads)
+    return [
+        g.reshape(a.shape[:-2] + (2, 16 * a.shape[-2], a.shape[-1]))
+        for g, a in zip(gathered, arrays)
+    ] + list(gathered[count:])
+
+
+def plane_kernel(source, target, own_sem, send_sem, recv_sem):
+    x, z, y, c = position()
+    here = y * 4 + c * 2 + x
+    copies = []
+    for flip in range(1, 8):
+        there_y = 1 - y if flip & 4 else y
+        there_c = 1 - c if flip & 2 else c
+        there_x = 1 - x if flip & 1 else x
+        there = there_y * 4 + there_c * 2 + there_x
+        copies.append(
+            remote(
+                source.at[there],
+                target.at[here],
+                send_sem.at[flip],
+                recv_sem.at[flip],
+                (z * 4 + there_y * 2 + there_c, there_x),
+            )
+        )
+    keep = pltpu.make_async_copy(source.at[here], target.at[here], own_sem)
+    keep.start()
+    barrier = pltpu.get_barrier_semaphore()
+    for flip in range(1, 8):
+        there_y = 1 - y if flip & 4 else y
+        there_c = 1 - c if flip & 2 else c
+        there_x = 1 - x if flip & 1 else x
+        pl.semaphore_signal(
+            barrier,
+            inc=1,
+            device_id=(z * 4 + there_y * 2 + there_c, there_x),
+            device_id_type=MESH,
+        )
+    pl.semaphore_wait(barrier, 7)
+    for copy in copies:
+        copy.start()
+    keep.wait()
+    for copy in copies:
+        copy.wait()
+
+
+def exchange(values, number):
+    sem = pltpu.SemaphoreType.DMA
+    return pl.pallas_call(
+        plane_kernel,
+        out_shape=jax.ShapeDtypeStruct(values.shape, values.dtype),
+        in_specs=[pl.BlockSpec(memory_space=pl.ANY)],
+        out_specs=pl.BlockSpec(memory_space=pl.ANY),
+        scratch_shapes=[sem, sem((8,)), sem((8,))],
+        compiler_params=pltpu.CompilerParams(collective_id=number, has_side_effects=True),
+    )(values)
+
+
+def reduce_kernel(chunks, count, *refs):
+    ins, value_in, grad_in = refs[:count], refs[count], refs[count + 1]
+    out, value_out, grad_out = refs[count + 2 : count + 5]
+    mine, other, first_a, first_b, second, third = refs[count + 5 : count + 11]
+    own_sem, core_send, core_recv, hop_send, hop_recv, line_send, line_recv = refs[
+        count + 11 : count + 18
+    ]
+    value_send, value_recv, grad_send, grad_recv = refs[count + 18 :]
+    x, z, y, c = position()
+    across, line = partners(x, z, y, c)
+    own = (z * 4 + y * 2 + c, x)
+    sources = [block_of(z, y, row) for row in range(4)]
+    meet(list(across.values()) + line, sources, own)
+    letters = []
+    for part in range(2):
+        for side in range(2):
+            device = sector_of(z, y, c, x, part, side)
+            at = 2 * part + side
+            letters.append(
+                (value_in.at[side, part], value_out.at[z], value_send.at[at], value_recv.at[z])
+                + (device, own)
+            )
+            letters.append(
+                (grad_in.at[part], grad_out.at[z], grad_send.at[at], grad_recv.at[z])
+                + (device, own)
+            )
+    for letter in letters:
+        post(*letter)
+    total = len(chunks)
+
+    def plan(k):
+        keep, core = [], []
+        for side in range(2):
+            index, lead, offset = chunks[k][side]
+            source = ins[index] if lead is None else ins[index].at[lead]
+            span = pl.ds(offset, CHUNK)
+            keep.append(
+                pltpu.make_async_copy(
+                    source.at[:, :, c, :, span], mine.at[2 * k + side], own_sem.at[k, side]
+                )
+            )
+            core.append(
+                remote(
+                    source.at[:, :, 1 - c, :, span],
+                    other.at[2 * k + side],
+                    core_send.at[k, side],
+                    core_recv.at[k, side],
+                    across["c"],
+                )
+            )
+        if k % 2 == 0:
+            one, axis_one = (mine.at[2 * k + 1 - x], first_a.at[k // 2]), "x"
+            two, axis_two = mine.at[2 * k + x, :, 1 - y], "y"
+        else:
+            one, axis_one = (mine.at[pl.ds(2 * k, 2), :, 1 - y], first_b.at[k // 2]), "y"
+            two, axis_two = mine.at[2 * k + 1 - x, :, y], "x"
+        hops = [
+            remote(one[0], one[1], hop_send.at[k, 0], hop_recv.at[k, 0], across[axis_one]),
+            remote(two, second.at[k], hop_send.at[k, 1], hop_recv.at[k, 1], across[axis_two]),
+        ]
+        along = [
+            remote(
+                mine.at[2 * k + x, lax.rem(z + d + 1, 4), y],
+                third.at[k, d],
+                line_send.at[k, d],
+                line_recv.at[k, d],
+                line[d],
+            )
+            for d in range(3)
+        ]
+        return keep, core, hops, along
+
+    plans = [plan(k) for k in range(total)]
+
+    def joined(left, right):
+        return (left.astype(wide) + right.astype(wide)).astype(low)
+
+    def add_core(k):
+        def body(step, carry):
+            side, row = lax.div(step, 4), lax.rem(step, 4)
+            for line_y in range(2):
+                mine[2 * k + side, row, line_y] = joined(
+                    mine[2 * k + side, row, line_y], other[2 * k + side, row, line_y]
+                )
+            return carry
+
+        lax.fori_loop(0, 8, body, 0)
+
+    def add_first(k):
+        def body(row, carry):
+            for part in range(2):
+                if k % 2 == 0:
+                    mine[2 * k + x, row, part] = joined(
+                        mine[2 * k + x, row, part], first_a[k // 2, row, part]
+                    )
+                else:
+                    mine[2 * k + part, row, y] = joined(
+                        mine[2 * k + part, row, y], first_b[k // 2, part, row]
+                    )
+            return carry
+
+        lax.fori_loop(0, 4, body, 0)
+
+    def add_second(k):
+        def body(row, carry):
+            mine[2 * k + x, row, y] = joined(mine[2 * k + x, row, y], second[k, row])
+            return carry
+
+        lax.fori_loop(0, 4, body, 0)
+
+    def add_third(k):
+        result = mine[2 * k + x, z, y].astype(wide)
+        for d in range(3):
+            result = result + third[k, d].astype(wide)
+        out[:, pl.ds(k * CHUNK, CHUNK)] = result
+
+    for step in range(total + 8):
+        if step < total:
+            keep, core, _, _ = plans[step]
+            for copy in core + keep:
+                copy.start()
+        if 0 <= step - 2 < total:
+            k = step - 2
+            keep, core, hops, _ = plans[k]
+            for copy in keep:
+                copy.wait()
+            for copy in core:
+                copy.wait_recv()
+            add_core(k)
+            hops[0].start()
+        if 0 <= step - 4 < total:
+            k = step - 4
+            hops = plans[k][2]
+            hops[0].wait_recv()
+            add_first(k)
+            hops[1].start()
+        if 0 <= step - 6 < total:
+            k = step - 6
+            plans[k][2][1].wait_recv()
+            add_second(k)
+            for copy in plans[k][3]:
+                copy.start()
+        if 0 <= step - 8 < total:
+            k = step - 8
+            for copy in plans[k][3]:
+                copy.wait_recv()
+            add_third(k)
+    for _, core, hops, along in plans:
+        for copy in core + hops + along:
+            copy.wait_send()
+    for letter in letters:
+        settle(*letter)
+    for row in range(4):
+        pltpu.make_async_copy(value_in.at[0, 0], value_out.at[row], value_recv.at[row]).wait()
+        pltpu.make_async_copy(grad_in.at[0], grad_out.at[row], grad_recv.at[row]).wait()
+
+
+def reduce_all(items, values, grads, number):
+    chunks, views = [], []
+    for index, item in enumerate(items):
+        rows, columns = item.shape[-2:]
+        lead = item.shape[:-2]
+        item = item.reshape((-1, 4, 2, 2, rows // 16, columns))
+        if not lead:
+            views.append(item[0])
+            for offset in range(0, columns // 2, CHUNK):
+                chunks.append(((index, None, offset), (index, None, columns // 2 + offset)))
+            continue
+        views.append(item)
+        for first in range(0, item.shape[0], 2):
+            for offset in range(0, columns, CHUNK):
+                chunks.append(((index, first, offset), (index, first + 1, offset)))
+    rows = views[0].shape[-2]
+    count, total = len(views), len(chunks)
+    sem = pltpu.SemaphoreType.DMA
+    return pl.pallas_call(
+        partial(reduce_kernel, chunks, count),
+        out_shape=[
+            jax.ShapeDtypeStruct((rows, total * CHUNK), wide),
+            jax.ShapeDtypeStruct((4,) + values.shape[2:], values.dtype),
+            jax.ShapeDtypeStruct((4,) + grads.shape[1:], grads.dtype),
+        ],
+        in_specs=[pl.BlockSpec(memory_space=pl.ANY)] * (count + 2),
+        out_specs=[pl.BlockSpec(memory_space=pltpu.VMEM)]
+        + [pl.BlockSpec(memory_space=pl.ANY)] * 2,
+        scratch_shapes=[
+            pltpu.VMEM((2 * total, 4, 2, rows, CHUNK), low),
+            pltpu.VMEM((2 * total, 4, 2, rows, CHUNK), low),
+            pltpu.VMEM(((total + 1) // 2, 4, 2, rows, CHUNK), low),
+            pltpu.VMEM(((total + 1) // 2, 2, 4, rows, CHUNK), low),
+            pltpu.VMEM((total, 4, rows, CHUNK), low),
+            pltpu.VMEM((total, 3, rows, CHUNK), low),
+            sem((total, 2)),
+            sem((total, 2)),
+            sem((total, 2)),
+            sem((total, 2)),
+            sem((total, 2)),
+            sem((total, 3)),
+            sem((total, 3)),
+            sem((4,)),
+            sem((4,)),
+            sem((4,)),
+            sem((4,)),
+        ],
+        compiler_params=pltpu.CompilerParams(
+            collective_id=number, has_side_effects=True, vmem_limit_bytes=60 * 2**20
+        ),
+    )(*views, values, grads)
+
+
+def diagonal(var_count, columns):
+    column = lax.broadcasted_iota(jnp.int32, (var_count, columns), 1)
+    row = lax.broadcasted_iota(jnp.int32, (var_count, columns), 0)
+    return (lax.rem(column, var_count) == row) & (column < 5 * var_count)
+
+
+def patch_kernel(field_ref, lat_ref, shift_ref, patch_ref):
+    lat_count, var_count, _ = field_ref.shape
+    row_count, lanes = lat_ref.shape
+    slots = lanes // 2
+    for r in range(row_count):
+        lat = lat_ref[r : r + 1, :]
+        west = shift_ref[r : r + 1, :] < 0
+
+        def body(b, carry):
+            top, bottom = carry
+            wide_row = field_ref[b].astype(wide)
+            chosen = jnp.where(west, wide_row[:, :lanes], wide_row[:, lanes:])
+            return (jnp.where(lat == b, chosen, top), jnp.where(lat == b - 1, chosen, bottom))
+
+        zero = jnp.zeros((var_count, lanes), wide)
+        rows = lax.fori_loop(0, lat_count, body, (zero, zero), unroll=4)
+        for py in range(2):
+            for px in range(2):
+                k = 2 * py + px
+                patch_ref[r, k * var_count : (k + 1) * var_count, :] = rows[py][
+                    :, px * slots : (px + 1) * slots
+                ].astype(low)
+
+
+def cut_patches(field, lat_lanes, shift_lanes):
+    row_count, lanes = lat_lanes.shape
+    return pl.pallas_call(
+        patch_kernel,
+        out_shape=jax.ShapeDtypeStruct((row_count, 4 * field.shape[1], lanes // 2), low),
+    )(field, lat_lanes, shift_lanes)
+
+
+def paste_kernel(grad_ref, lat_ref, shift_ref, field_ref):
+    lat_count, var_count, _ = field_ref.shape
+    row_count, lanes = lat_ref.shape
+    field_ref[...] = jnp.zeros_like(field_ref)
+    for r in range(row_count):
+        lat = lat_ref[r : r + 1, :]
+        west = shift_ref[r : r + 1, :] < 0
+        lat_both = jnp.concatenate([lat, lat], axis=1)
+        both = []
+        for py in range(2):
+            k = 2 * py
+            grads = jnp.concatenate(
+                [
+                    grad_ref[r, k * var_count : (k + 1) * var_count, :],
+                    grad_ref[r, (k + 1) * var_count : (k + 2) * var_count, :],
+                ],
+                axis=1,
+            )
+            left = jnp.where(west, grads, 0.0)
+            both.append(jnp.concatenate([left, grads - left], axis=1))
+
+        def body(b, carry):
+            field_ref[b] += jnp.where(lat_both == b, both[0], 0.0) + jnp.where(
+                lat_both == b - 1, both[1], 0.0
+            )
+            return carry
+
+        lax.fori_loop(0, lat_count, body, 0)
+
+
+def paste_patches(grads, lat_lanes, shift_lanes, lat_count):
+    return pl.pallas_call(
+        paste_kernel,
+        out_shape=jax.ShapeDtypeStruct(
+            (lat_count, grads.shape[1] // 4, 2 * lat_lanes.shape[1]), wide
+        ),
+    )(grads, lat_lanes, shift_lanes)
+
+
+def mixer_forward_kernel(cut_ref, score_ref, value_ref, patch_ref, prob_ref, mixed_ref):
+    head_count, var_count, tokens = prob_ref.shape
+    parts, taps, width = cut_ref.shape
+    for part in range(parts):
+        patch_ref[:taps, part * width : (part + 1) * width] = cut_ref[part]
+    patch_ref[taps : taps + var_count, :] = jnp.ones((var_count, tokens), low)
+    rest = patch_ref.shape[0] - 5 * var_count
+    patch_ref[5 * var_count :, :] = jnp.zeros((rest, tokens), low)
+    mask = diagonal(var_count, patch_ref.shape[0])
+
+    def head_step(h, carry):
+        spread = jnp.where(mask, score_ref[pl.ds(h, 1), :], 0.0)
+        upper = spread.astype(low)
+        lower = (spread - upper.astype(wide)).astype(low)
+        patch = patch_ref[...]
+        scores = dot(upper, patch) + dot(lower, patch)
+        raised = jnp.exp(scores - jnp.max(scores, axis=0, keepdims=True))
+        prob = raised / jnp.sum(raised, axis=0, keepdims=True)
+        prob_ref[h] = prob
+        pooled = jnp.concatenate(
+            [
+                (prob * patch_ref[k * var_count : (k + 1) * var_count, :].astype(wide)).astype(low)
+                for k in range(5)
+            ]
+            + [jnp.zeros((rest, tokens), low)],
+            axis=0,
+        )
+        start = pl.multiple_of(h * HEAD_DIM, HEAD_DIM)
+        mixed_ref[pl.ds(start, HEAD_DIM), :] = dot(
+            value_ref[pl.ds(start, HEAD_DIM), :], pooled
+        ).astype(low)
+        return carry
+
+    lax.fori_loop(0, head_count, head_step, 0)
+
+
+def mixer_forward(cut, score_table, value_table):
+    head_count, padded = score_table.shape
+    var_count = cut.shape[1] // 4
+    tokens = cut.shape[0] * cut.shape[2]
+    return pl.pallas_call(
+        mixer_forward_kernel,
+        out_shape=[
+            jax.ShapeDtypeStruct((padded, tokens), low),
+            jax.ShapeDtypeStruct((head_count, var_count, tokens), wide),
+            jax.ShapeDtypeStruct((head_count * HEAD_DIM, tokens), low),
+        ],
+        compiler_params=pltpu.CompilerParams(vmem_limit_bytes=40 * 2**20),
+    )(cut, score_table, value_table)
+
+
+def mixer_backward_kernel(
+    patch_ref,
+    prob_ref,
+    score_ref,
+    value_ref,
+    grad_ref,
+    pooled_ref,
+    count_ref,
+    cut_ref,
+    patch_grad_ref,
+):
+    head_count, var_count, _ = prob_ref.shape
+    padded, tokens = patch_ref.shape
+    rest = padded - 5 * var_count
+    mask = diagonal(var_count, padded)
+    patch_grad_ref[...] = jnp.zeros_like(patch_grad_ref)
+
+    def head_step(h, carry):
+        start = pl.multiple_of(h * HEAD_DIM, HEAD_DIM)
+        grads = grad_ref[pl.ds(start, HEAD_DIM), :]
+        prob = prob_ref[h]
+        back = dot(value_ref[pl.ds(start, HEAD_DIM), :], grads, 0, 0)
+        pieces = [patch_ref[k * var_count : (k + 1) * var_count, :].astype(wide) for k in range(5)]
+        backs = [back[k * var_count : (k + 1) * var_count, :] for k in range(5)]
+        prob_grad = pieces[0] * backs[0]
+        for k in range(1, 5):
+            prob_grad = prob_grad + pieces[k] * backs[k]
+        mean = jnp.sum(prob * prob_grad, axis=0, keepdims=True)
+        delta = prob * (prob_grad - mean)
+        upper = delta.astype(low)
+        lower = (delta - upper.astype(wide)).astype(low)
+        spread = jnp.where(mask, score_ref[pl.ds(h, 1), :], 0.0).astype(low)
+        patch_grad_ref[...] += dot(spread, upper, 0, 0)
+        for k in range(4):
+            patch_grad_ref[k * var_count : (k + 1) * var_count, :] += prob * backs[k]
+        patch = patch_ref[...]
+        counts = dot(upper, patch, 1, 1) + dot(lower, patch, 1, 1)
+        count_ref[pl.ds(h, 1), :] = jnp.sum(jnp.where(mask, counts, 0.0), axis=0, keepdims=True)
+        pooled = jnp.concatenate(
+            [(prob * piece).astype(low) for piece in pieces] + [jnp.zeros((rest, tokens), low)],
+            axis=0,
+        )
+        pooled_ref[pl.ds(start, HEAD_DIM), :] = dot(grads, pooled, 1, 1)
+        return carry
+
+    lax.fori_loop(0, head_count, head_step, 0)
+    parts, taps, width = cut_ref.shape
+    for part in range(parts):
+        cut_ref[part] = patch_grad_ref[:taps, part * width : (part + 1) * width]
+
+
+def mixer_backward(patches, probs, score_table, value_table, mixed_grads):
+    head_count, padded = score_table.shape
+    var_count = probs.shape[1]
+    tokens = patches.shape[1]
+    return pl.pallas_call(
+        mixer_backward_kernel,
+        out_shape=[
+            jax.ShapeDtypeStruct((head_count * HEAD_DIM, padded), wide),
+            jax.ShapeDtypeStruct((head_count, padded), wide),
+            jax.ShapeDtypeStruct((2, 4 * var_count, tokens // 2), wide),
+        ],
+        scratch_shapes=[pltpu.VMEM((padded, tokens), wide)],
+        compiler_params=pltpu.CompilerParams(vmem_limit_bytes=40 * 2**20),
+    )(patches, probs, score_table, value_table, mixed_grads)
+
+
+def head_lanes(values, h):
+    lane = lax.broadcasted_iota(jnp.int32, values.shape, values.ndim - 1)
+    inside = lane < HEAD_DIM if h == 0 else lane >= HEAD_DIM
+    return jnp.where(inside, values, jnp.zeros_like(values))
+
+
+def attention_forward_kernel(joint_ref, tag_ref, crop_ref, low_ref, wide_ref, total_ref):
+    blocks, _, share, lanes = joint_ref.shape
+    count = low_ref.shape[0]
+    step = pl.program_id(0)
+    queries = joint_ref[pl.ds(step * count, count), 0].reshape(count * share, lanes)
+    keys = joint_ref[:, 1].reshape(blocks * share, lanes)
+    values = joint_ref[:, 2].reshape(blocks * share, lanes)
+    allowed = crop_ref[...] == tag_ref[...]
+    result = None
+    for h in range(2):
+        scores = dot(head_lanes(queries, h), keys, 1, 1)
+        scores = jnp.where(allowed, scores, masked_score)
+        largest = jnp.max(scores, axis=1, keepdims=True)
+        weights = jnp.exp(scores - largest)
+        total = jnp.sum(weights, axis=1, keepdims=True)
+        weights = (weights * (1.0 / total)).astype(low)
+        part = head_lanes(dot(weights, values), h)
+        result = part if result is None else result + part
+        total_ref[h] = largest + jnp.log(total)
+    wide_ref[...] = result
+    low_ref[...] = result.astype(low).reshape(low_ref.shape)
+
+
+def attention_forward(joint, tags, crops, steps):
+    blocks, _, share, lanes = joint.shape
+    slots = blocks * share
+    width = slots // steps
+    return pl.pallas_call(
+        attention_forward_kernel,
+        grid=(steps,),
+        out_shape=[
+            jax.ShapeDtypeStruct((blocks, share, lanes), low),
+            jax.ShapeDtypeStruct((slots, lanes), wide),
+            jax.ShapeDtypeStruct((2, slots, 1), wide),
+        ],
+        in_specs=[
+            pl.BlockSpec(joint.shape, lambda i: (0, 0, 0, 0)),
+            pl.BlockSpec((1, slots), lambda i: (0, 0)),
+            pl.BlockSpec((width, 1), lambda i: (i, 0)),
+        ],
+        out_specs=[
+            pl.BlockSpec((blocks // steps, share, lanes), lambda i: (i, 0, 0)),
+            pl.BlockSpec((width, lanes), lambda i: (i, 0)),
+            pl.BlockSpec((2, width, 1), lambda i: (0, i, 0)),
+        ],
+        compiler_params=pltpu.CompilerParams(vmem_limit_bytes=50 * 2**20),
+    )(joint, tags, crops)
+
+
+def attention_backward_kernel(
+    joint_ref, tag_ref, crop_ref, grad_ref, out_ref, total_ref, result_ref, key_acc, value_acc
+):
+    blocks, _, share, lanes = joint_ref.shape
+    count = grad_ref.shape[0]
+    step = pl.program_id(0)
+    queries = joint_ref[pl.ds(step * count, count), 0].reshape(count * share, lanes)
+    keys = joint_ref[:, 1].reshape(blocks * share, lanes)
+    values = joint_ref[:, 2].reshape(blocks * share, lanes)
+    grads = grad_ref[...].reshape(count * share, lanes)
+    product = grads.astype(wide) * out_ref[...]
+    allowed = crop_ref[...] == tag_ref[...]
+    scale = HEAD_DIM ** (-0.5)
+
+    @pl.when(step == 0)
+    def _():
+        key_acc[...] = jnp.zeros_like(key_acc)
+        value_acc[...] = jnp.zeros_like(value_acc)
+
+    query_grad = None
+    for h in range(2):
+        query_part, grad_part = head_lanes(queries, h), head_lanes(grads, h)
+        scores = jnp.where(allowed, dot(query_part, keys, 1, 1), masked_score)
+        weights = jnp.exp(scores - total_ref[h])
+        weight_grads = dot(grad_part, values, 1, 1)
+        delta = jnp.sum(head_lanes(product, h), axis=1, keepdims=True)
+        score_grads = (weights * (weight_grads - delta)).astype(low)
+        weights = weights.astype(low)
+        value_acc[...] += dot(grad_part, weights, 0, 0)
+        key_acc[...] += dot(query_part, score_grads, 0, 0)
+        part = head_lanes(dot(score_grads, keys), h)
+        query_grad = part if query_grad is None else query_grad + part
+    result_ref[pl.ds(step * count, count), 0] = (
+        (query_grad * scale).astype(low).reshape(count, share, lanes)
+    )
+
+    @pl.when(step == pl.num_programs(0) - 1)
+    def _():
+        shape = (blocks, share, lanes)
+        result_ref[:, 1] = key_acc[...].T.astype(low).reshape(shape)
+        result_ref[:, 2] = value_acc[...].T.astype(low).reshape(shape)
+
+
+def attention_backward(joint, tags, crops, grads, outputs, totals, steps):
+    blocks, _, share, lanes = joint.shape
+    slots = blocks * share
+    width = slots // steps
+    return pl.pallas_call(
+        attention_backward_kernel,
+        grid=(steps,),
+        out_shape=jax.ShapeDtypeStruct(joint.shape, low),
+        in_specs=[
+            pl.BlockSpec(joint.shape, lambda i: (0, 0, 0, 0)),
+            pl.BlockSpec((1, slots), lambda i: (0, 0)),
+            pl.BlockSpec((width, 1), lambda i: (i, 0)),
+            pl.BlockSpec((blocks // steps, share, lanes), lambda i: (i, 0, 0)),
+            pl.BlockSpec((width, lanes), lambda i: (i, 0)),
+            pl.BlockSpec((2, width, 1), lambda i: (0, i, 0)),
+        ],
+        out_specs=pl.BlockSpec(joint.shape, lambda i: (0, 0, 0, 0)),
+        scratch_shapes=[pltpu.VMEM((lanes, slots), wide), pltpu.VMEM((lanes, slots), wide)],
+        compiler_params=pltpu.CompilerParams(vmem_limit_bytes=56 * 2**20),
+    )(joint, tags, crops, grads, outputs, totals)
+
+
+def whole(array):
+    rank = len(array.shape)
+    return pl.BlockSpec(array.shape, lambda *_: (0,) * rank)
+
+
+def norm_parts(values):
+    center = values - jnp.mean(values, axis=-1, keepdims=True)
+    inverse = lax.rsqrt(jnp.mean(center * center, axis=-1, keepdims=True) + epsilon)
+    return center * inverse, inverse
+
+
+def norm_back(values, gain, grads):
+    normed, inverse = norm_parts(values)
+    scaled = grads * gain
+    inner = (
+        scaled
+        - jnp.mean(scaled, axis=-1, keepdims=True)
+        - normed * jnp.mean(scaled * normed, axis=-1, keepdims=True)
+    )
+    return (
+        inner * inverse,
+        jnp.sum(grads * normed, axis=0, keepdims=True),
+        jnp.sum(grads, axis=0, keepdims=True),
+    )
+
+
+def project_kernel(mixed_ref, back_ref, lead_ref, vector_ref, weight_ref, start_ref, low_ref, out_ref):
+    step = pl.program_id(0)
+    halves, _, half_width = back_ref.shape
+    row_count, _, _, share, lanes = out_ref.shape
+
+    @pl.when(step == 0)
+    def _():
+        total = lead_ref[...] * vector_ref[0:1] + vector_ref[1:2]
+        mixed = mixed_ref[...].T
+        for side in range(halves):
+            total = total + dot(
+                mixed[:, side * half_width : (side + 1) * half_width], back_ref[side], 1, 1
+            )
+        start_ref[...] = total
+        normed, _ = norm_parts(total)
+        low_ref[...] = (normed * vector_ref[2:3] + vector_ref[3:4]).astype(low)
+
+    kind, side = lax.div(step, halves), lax.rem(step, halves)
+    result = dot(low_ref[...], weight_ref[...].reshape(weight_ref.shape[2:])).astype(low)
+    result = result * jnp.where(kind == 0, HEAD_DIM ** (-0.5), 1.0).astype(low)
+    pairs = half_width // lanes
+    for pair in range(pairs):
+        out_ref[:, side * pairs + pair, kind] = result[
+            :, pair * lanes : (pair + 1) * lanes
+        ].reshape(row_count, share, lanes)
+
+
+def project(mixed, back_weight, lead_column, vectors, weights, row_count):
+    model, tokens = mixed.shape
+    kinds, halves, _, half_width = weights.shape
+    return pl.pallas_call(
+        project_kernel,
+        grid=(kinds * halves,),
+        out_shape=[
+            jax.ShapeDtypeStruct((tokens, model), wide),
+            jax.ShapeDtypeStruct((tokens, model), low),
+            jax.ShapeDtypeStruct(
+                (row_count, halves * half_width // 128, kinds, tokens // row_count, 128), low
+            ),
+        ],
+        in_specs=[
+            whole(mixed),
+            whole(back_weight),
+            whole(lead_column),
+            whole(vectors),
+            pl.BlockSpec((1, 1, model, half_width), lambda i: (i // halves, i % halves, 0, 0)),
+        ],
+        out_specs=[
+            pl.BlockSpec((tokens, model), lambda i: (0, 0)),
+            pl.BlockSpec((tokens, model), lambda i: (0, 0)),
+            pl.BlockSpec(
+                (row_count, halves * half_width // 128, kinds, tokens // row_count, 128),
+                lambda i: (0, 0, 0, 0, 0),
+            ),
+        ],
+        compiler_params=pltpu.CompilerParams(vmem_limit_bytes=40 * 2**20),
+    )(mixed, back_weight, lead_column, vectors, weights)
+
+
+def feed_kernel(
+    attended_ref,
+    proj_ref,
+    start_ref,
+    vector_ref,
+    up_ref,
+    down_ref,
+    bias_ref,
+    final_ref,
+    masked_ref,
+    keep_ref,
+    predicted_ref,
+    middle_grad_ref,
+    unit_ref,
+    grad_up_ref,
+    grad_down_ref,
+    grad_proj_ref,
+    grad_final_ref,
+    grad_bias_ref,
+    grad_vector_ref,
+    flat,
+    middle,
+    second,
+    second_turned,
+    active,
+    slope,
+    total,
+    grad_low,
+    grad_turned,
+    grad_final,
+):
+    step = pl.program_id(0)
+    count = active.shape[0]
+    row_count, units, share, lanes = attended_ref.shape
+    halves, _, half_width = proj_ref.shape
+    tokens = row_count * share
+
+    @pl.when(step == 0)
+    def _():
+        for unit in range(units):
+            flat[:, unit * lanes : (unit + 1) * lanes] = attended_ref[:, unit].reshape(
+                tokens, lanes
+            )
+        result = start_ref[...]
+        for side in range(halves):
+            result = result + dot(
+                flat[:, side * half_width : (side + 1) * half_width], proj_ref[side], 1, 1
+            )
+        middle[...] = result
+        normed, _ = norm_parts(result)
+        normed = (normed * vector_ref[4:5] + vector_ref[5:6]).astype(low)
+        second[...] = normed
+        second_turned[...] = normed.T
+        total[...] = result
+
+    @pl.when(step < count)
+    def _():
+        hidden = dot(second[...], up_ref[0]) + bias_ref[...]
+        share_of = 0.5 * (1.0 + lax.erf(hidden * (0.5**0.5)))
+        fired = (hidden * share_of).astype(low)
+        active[step] = fired
+        slope[step] = share_of + hidden * jnp.exp(-0.5 * hidden * hidden) * (
+            0.5 / 1.2533141373155003
+        )
+        total[...] += dot(fired, down_ref[0], 1, 1)
+
+    @pl.when(step == count - 1)
+    def _():
+        final_low = total[...].astype(low)
+        final_turned = final_low.T
+        grads = None
+        for side in range(halves):
+            predicted_ref[side] = (dot(final_low, final_ref[side]) * keep_ref[...]).astype(low)
+            part = dot(masked_ref[side], final_ref[side], 1, 1)
+            grads = part if grads is None else grads + part
+            grad_final_ref[side] = dot(final_turned, masked_ref[side]).astype(low)
+        grad_final[...] = grads
+        grad_low[...] = grads.astype(low)
+        grad_turned[...] = grads.astype(low).T
+        total[...] = jnp.zeros_like(total)
+
+    @pl.when(step >= count)
+    def _():
+        block = step - count
+        hidden_grad = dot(grad_low[...], down_ref[0]) * slope[block]
+        hidden_low = hidden_grad.astype(low)
+        grad_bias_ref[...] = jnp.sum(hidden_low.astype(wide), axis=0, keepdims=True)
+        total[...] += dot(hidden_low, up_ref[0], 1, 1)
+        grad_down_ref[0] = dot(grad_turned[...], active[block]).astype(low)
+        grad_up_ref[0] = dot(second_turned[...], hidden_low).astype(low)
+
+    @pl.when(step == 2 * count - 1)
+    def _():
+        part, grad_gain, grad_shift = norm_back(middle[...], vector_ref[4:5], total[...])
+        result = grad_final[...] + part
+        middle_grad_ref[...] = result
+        grad_vector_ref[0:1] = grad_gain
+        grad_vector_ref[1:2] = grad_shift
+        result_low = result.astype(low)
+        result_turned = result_low.T
+        pairs = half_width // lanes
+        for side in range(halves):
+            span = slice(side * half_width, (side + 1) * half_width)
+            grad_proj_ref[side] = dot(result_turned, flat[:, span]).astype(low)
+            out = dot(result_low, proj_ref[side]).astype(low)
+            for pair in range(pairs):
+                unit_ref[:, side * pairs + pair] = out[
+                    :, pair * lanes : (pair + 1) * lanes
+                ].reshape(row_count, share, lanes)
+
+
+def feed(attended, proj, start, vectors, up_weight, down_weight, up_bias, final_weight, masked, keep):
+    halves, model, full = up_weight.shape
+    half_width = proj.shape[2]
+    tokens = start.shape[0]
+    block = 512
+    each = full // block
+    count = halves * each
+
+    def block_at(i):
+        j = lax.rem(i, count)
+        return (lax.div(j, each), 0, lax.rem(j, each))
+
+    def late_block(i):
+        j = lax.max(i - count, 0)
+        return (lax.div(j, each), 0, lax.rem(j, each))
+
+    def fixed(shape, dtype):
+        rank = len(shape)
+        return jax.ShapeDtypeStruct(shape, dtype), pl.BlockSpec(shape, lambda i: (0,) * rank)
+
+    outs = [
+        fixed((halves, tokens, 128), low),
+        fixed((tokens, model), wide),
+        fixed(attended.shape, low),
+        (
+            jax.ShapeDtypeStruct(up_weight.shape, low),
+            pl.BlockSpec((1, model, block), late_block),
+        ),
+        (
+            jax.ShapeDtypeStruct(up_weight.shape, low),
+            pl.BlockSpec((1, model, block), late_block),
+        ),
+        fixed((halves, model, half_width), low),
+        fixed((halves, model, 128), low),
+        (
+            jax.ShapeDtypeStruct((1, halves * full), wide),
+            pl.BlockSpec((1, block), lambda i: (0, lax.max(i - count, 0))),
+        ),
+        fixed((2, model), wide),
+    ]
+    return pl.pallas_call(
+        feed_kernel,
+        grid=(2 * count,),
+        out_shape=[shape for shape, _ in outs],
+        in_specs=[
+            whole(attended),
+            whole(proj),
+            whole(start),
+            whole(vectors),
+            pl.BlockSpec((1, model, block), block_at),
+            pl.BlockSpec((1, model, block), block_at),
+            pl.BlockSpec((1, block), lambda i: (0, lax.rem(i, count))),
+            whole(final_weight),
+            whole(masked),
+            whole(keep),
+        ],
+        out_specs=[spec for _, spec in outs],
+        scratch_shapes=[
+            pltpu.VMEM((tokens, model), low),
+            pltpu.VMEM((tokens, model), wide),
+            pltpu.VMEM((tokens, model), low),
+            pltpu.VMEM((model, tokens), low),
+            pltpu.VMEM((count, tokens, block), low),
+            pltpu.VMEM((count, tokens, block), wide),
+            pltpu.VMEM((tokens, model), wide),
+            pltpu.VMEM((tokens, model), low),
+            pltpu.VMEM((model, tokens), low),
+            pltpu.VMEM((tokens, model), wide),
+        ],
+        compiler_params=pltpu.CompilerParams(vmem_limit_bytes=56 * 2**20),
+    )(attended, proj, start, vectors, up_weight, down_weight, up_bias, final_weight, masked, keep)
+
+
+def return_kernel(
+    grads_ref,
+    weight_ref,
+    low_ref,
+    start_ref,
+    middle_grad_ref,
+    vector_ref,
+    lead_ref,
+    back_ref,
+    mixed_ref,
+    grad_input_ref,
+    grad_mixer_ref,
+    mixed_grad_ref,
+    grad_vector_ref,
+    turned,
+    total,
+):
+    step = pl.program_id(0)
+    halves, _, half_width = back_ref.shape
+    row_count, _, _, share, lanes = grads_ref.shape
+    tokens = row_count * share
+    pairs = half_width // lanes
+
+    @pl.when(step == 0)
+    def _():
+        turned[...] = low_ref[...].T
+        total[...] = jnp.zeros_like(total)
+
+    kind, side = lax.div(step, halves), lax.rem(step, halves)
+    piece = jnp.concatenate(
+        [grads_ref[:, side * pairs + pair, kind].reshape(tokens, lanes) for pair in range(pairs)],
+        axis=1,
+    )
+    total[...] += dot(piece, weight_ref[0, 0], 1, 1)
+    grad_input_ref[0, 0] = dot(turned[...], piece).astype(low)
+
+    @pl.when(step == pl.num_programs(0) - 1)
+    def _():
+        part, grad_gain, grad_shift = norm_back(start_ref[...], vector_ref[2:3], total[...])
+        result = middle_grad_ref[...] + part
+        grad_vector_ref[0:1] = jnp.sum(result * lead_ref[...], axis=0, keepdims=True)
+        grad_vector_ref[1:2] = jnp.sum(result, axis=0, keepdims=True)
+        grad_vector_ref[2:3] = grad_gain
+        grad_vector_ref[3:4] = grad_shift
+        result_low = result.astype(low)
+        result_turned = result_low.T
+        for half in range(halves):
+            span = slice(half * half_width, (half + 1) * half_width)
+            grad_mixer_ref[half] = dot(result_turned, mixed_ref[span, :], 1, 1).astype(low)
+            mixed_grad_ref[span, :] = dot(result_low, back_ref[half]).astype(low).T
+
+
+def go_back(grads, weights, first_low, start, middle_grad, vectors, lead_column, back_weight, mixed):
+    kinds, halves, model, half_width = weights.shape
+    tokens = start.shape[0]
+    block = pl.BlockSpec((1, 1, model, half_width), lambda i: (i // halves, i % halves, 0, 0))
+    return pl.pallas_call(
+        return_kernel,
+        grid=(kinds * halves,),
+        out_shape=[
+            jax.ShapeDtypeStruct(weights.shape, low),
+            jax.ShapeDtypeStruct((halves, model, half_width), low),
+            jax.ShapeDtypeStruct((model, tokens), low),
+            jax.ShapeDtypeStruct((4, model), wide),
+        ],
+        in_specs=[
+            whole(grads),
+            block,
+            whole(first_low),
+            whole(start),
+            whole(middle_grad),
+            whole(vectors),
+            whole(lead_column),
+            whole(back_weight),
+            whole(mixed),
+        ],
+        out_specs=[
+            block,
+            pl.BlockSpec((halves, model, half_width), lambda i: (0, 0, 0)),
+            pl.BlockSpec((model, tokens), lambda i: (0, 0)),
+            pl.BlockSpec((4, model), lambda i: (0, 0)),
+        ],
+        scratch_shapes=[pltpu.VMEM((model, tokens), low), pltpu.VMEM((tokens, model), wide)],
+        compiler_params=pltpu.CompilerParams(vmem_limit_bytes=50 * 2**20),
+    )(grads, weights, first_low, start, middle_grad, vectors, lead_column, back_weight, mixed)
+
+
+def einsum(spec, left, right):
+    return jnp.einsum(spec, left, right, preferred_element_type=wide)
+
+
+def fast_local(
+    pixels,
+    crop_starts,
+    crop_shifts,
+    slot_crops,
+    occupied,
+    lead_hours,
+    patch_weight,
+    variable_embed,
+    mixer_query,
+    mixer_keys,
+    mixer_values,
+    mixer_output,
+    lead_embed,
+    first_gain,
+    first_bias,
+    attention_in,
+    attention_out,
+    second_gain,
+    second_bias,
+    expand_weight,
+    expand_bias,
+    reduce_weight,
+    output_weight,
+    cotangent,
+):
+    lon, head = lax.axis_index(LON), lax.axis_index(HEAD)
+    row_count, slot_width = slot_crops.shape
+    share = slot_width // HEAD_SIZE
+    tokens = row_count * share
+    var_count, lat_count, column_count = pixels.shape
+    head_half, query_width = mixer_query.shape
+    head_count = HEAD_SIZE * head_half
+    half_width = head_half * HEAD_DIM
+    out_half = output_weight.shape[1]
+    slice_width = patch_weight.shape[2]
+    model = slice_width * LON_SIZE * HEAD_SIZE
+    block_rows = model // LON_SIZE
+    taps = 4 * var_count
+    pairs = half_width // 128
+    scale = HEAD_DIM ** (-0.5)
+
+    last = lax.slice_in_dim(pixels, column_count - 1, column_count, axis=2)
+    up = [(i, (i + 1) % LON_SIZE) for i in range(LON_SIZE)]
+    down = [(j, i) for i, j in up]
+    before = lax.ppermute(last, LON, up)
+    after = lax.ppermute(pixels[:, :, :1], LON, down)
+    lat_slot = crop_lookup(crop_starts, slot_crops)
+    shift_slot = crop_lookup(crop_shifts, slot_crops)
+    lat_lanes = jnp.tile(lat_slot, (1, 2))
+    shift_lanes = jnp.tile(shift_slot, (1, 2))
+    wanted = jnp.arange(2 * 2 * slot_width)
+    side, wanted = wanted // (2 * slot_width), wanted % (2 * slot_width)
+    wanted = 2 * (wanted % slot_width) + 2 * side + wanted // slot_width - 1
+    select = (jnp.arange(column_count)[:, None] == wanted[None, :]).astype(low)
+    field = einsum("vac,cn->avn", pixels, select)
+    field = field + jnp.where(wanted == -1, jnp.transpose(before, (1, 0, 2)).astype(wide), 0.0)
+    field = field + jnp.where(
+        wanted == column_count, jnp.transpose(after, (1, 0, 2)).astype(wide), 0.0
+    )
+    field = field.astype(low)
+    pair_rows = row_count // HEAD_SIZE
+    cut = cut_patches(
+        field,
+        block_slice(lat_lanes, head, pair_rows, 0),
+        block_slice(shift_lanes, head, pair_rows, 0),
+    )
+    masked = cotangent * occupied[:, :, None].astype(low)
+    masked = jnp.pad(masked, ((0, 0), (0, 0), (0, 128 - out_half)))
+    my_crops = block_slice(slot_crops, head, share, 1)
+    my_occupied = block_slice(occupied, head, share, 1)
+
+    around = (HEAD, LON)
+    up_weight = lax.all_gather(expand_weight, around, axis=0, tiled=True)
+    up_weight = up_weight.reshape(HEAD_SIZE, model, -1)
+    down_weight = lax.all_gather(reduce_weight.T, around, axis=0, tiled=True)
+    down_weight = down_weight.reshape(HEAD_SIZE, model, -1)
+    padded = 256
+    small = jnp.concatenate(
+        [
+            jnp.transpose(patch_weight, (1, 0, 2)).reshape(taps, slice_width),
+            variable_embed,
+            lead_embed,
+            first_gain[None],
+            first_bias[None],
+            second_gain[None],
+            second_bias[None],
+            jnp.zeros((padded - taps - var_count - 6, slice_width), low),
+        ]
+    ).T
+    small = jnp.concatenate([small[:, :128], small[:, 128:]])
+    pieces = [
+        jnp.where(my_occupied == 1, my_crops, -1).astype(low).reshape(-1),
+        my_crops.astype(low).reshape(-1),
+        jnp.pad(mixer_query.reshape(-1), (0, 128 - head_half * query_width)),
+        expand_bias.reshape(-1),
+    ]
+    used = sum(piece.shape[0] for piece in pieces)
+    misc = jnp.concatenate(pieces + [jnp.zeros((2048 - used,), low)]).reshape(16, 128)
+    out_block = jnp.pad(output_weight, ((0, 0), (0, 128 - out_half)))
+    (
+        misc_all,
+        small_all,
+        key_weight,
+        value_weight,
+        mixer_weight,
+        input_weight,
+        output_proj,
+        final_weight,
+        cut,
+        masked,
+    ) = gather_all(
+        [
+            misc,
+            small,
+            mixer_keys,
+            mixer_values,
+            mixer_output.T,
+            attention_in,
+            attention_out.T,
+            out_block,
+        ],
+        cut,
+        masked,
+        1,
+    )
+    masked = masked.reshape(HEAD_SIZE, tokens, 128)
+    misc_all = misc_all.reshape(HEAD_SIZE, LON_SIZE, 2048)
+    slots_all = jnp.transpose(
+        misc_all[:, :, : 2 * row_count * share].reshape(
+            HEAD_SIZE, LON_SIZE, 2, row_count, share
+        ),
+        (2, 3, 1, 0, 4),
+    ).reshape(2, row_count, -1)
+    my_row = lax.div(lon, LON_SIZE // row_count)
+    my_block = lax.rem(lon, LON_SIZE // row_count) * HEAD_SIZE + head
+    slots_row = lax.dynamic_index_in_dim(slots_all, my_row, 1, keepdims=False).astype(wide)
+    tag_row, crop_column = slots_row[0:1], slots_row[1][:, None]
+    my_slots = block_slice(slots_row, my_block, tokens, 1)
+    keep_mask = jnp.where(my_slots[0] >= 0.0, 1.0, 0.0)[:, None]
+    my_hours = lax.dynamic_index_in_dim(lead_hours, my_row, 0)
+    lead_column = crop_lookup(my_hours, my_slots[1:2].astype(jnp.int32)).astype(wide)
+    lead_column = lead_column.reshape(tokens, 1) / 100.0
+    at = 2 * row_count * share
+    query = jnp.transpose(
+        misc_all[:, :, at : at + head_half * query_width].reshape(
+            HEAD_SIZE, LON_SIZE, head_half, query_width
+        ),
+        (0, 2, 1, 3),
+    ).reshape(head_count, HEAD_DIM)
+    query = query.astype(wide)
+    at += 128
+    bias_rows = expand_bias.shape[0]
+    up_bias = jnp.transpose(
+        misc_all[:, :, at : at + expand_bias.size].reshape(HEAD_SIZE, LON_SIZE, bias_rows, -1),
+        (0, 2, 1, 3),
+    ).reshape(HEAD_SIZE, -1)
+    up_bias = up_bias.astype(wide)
+    patch_full = jnp.transpose(
+        small_all.reshape(HEAD_SIZE, LON_SIZE, 2, slice_width, 128), (1, 0, 3, 2, 4)
+    ).reshape(model, padded)
+    vectors = patch_full[:, taps + var_count : taps + var_count + 6].T.astype(wide)
+    patch_full = jnp.where(jnp.arange(padded)[None, :] < taps + var_count, patch_full, 0)
+
+    key_table = einsum("xde,dm->xem", key_weight, patch_full).reshape(model, padded)
+    value_table = einsum("xde,dm->xem", value_weight, patch_full).astype(low).reshape(model, padded)
+    score_table = (
+        jnp.sum(key_table.reshape(head_count, HEAD_DIM, padded) * query[:, :, None], axis=1) * scale
+    )
+
+    patches, probs, mixed = mixer_forward(cut, score_table, value_table)
+    start_sum, first_low, projected = project(
+        mixed, mixer_weight, lead_column, vectors, input_weight, 1
+    )
+    units = HEAD_SIZE * pairs
+    joint = exchange(projected.reshape(units, 3, tokens, 128), 3)
+    steps = 8
+    attended_unit, attended_wide, totals = attention_forward(joint, tag_row, crop_column, steps)
+    attended = exchange(attended_unit, 4)[None]
+    (
+        predicted,
+        middle_grad,
+        out_grads,
+        grad_up,
+        grad_down,
+        grad_proj,
+        grad_out,
+        grad_up_bias,
+        second_vectors,
+    ) = feed(
+        attended,
+        output_proj,
+        start_sum,
+        vectors,
+        up_weight,
+        down_weight,
+        up_bias.reshape(1, -1),
+        final_weight,
+        masked,
+        keep_mask,
+    )
+    unit_grads = exchange(out_grads.reshape(units, tokens, 128), 5)
+    joint_grads = attention_backward(
+        joint, tag_row, crop_column, unit_grads, attended_wide, totals, steps
+    )
+    stacked = exchange(joint_grads, 6)[None]
+    grad_input, grad_mixer, mixed_grads, first_vectors = go_back(
+        stacked,
+        input_weight,
+        first_low,
+        start_sum,
+        middle_grad,
+        vectors,
+        lead_column,
+        mixer_weight,
+        mixed,
+    )
+    pooled_grads, counts, cut_grads = mixer_backward(
+        patches, probs, score_table, value_table, mixed_grads
+    )
+    counts = counts * scale
+    pooled_low = pooled_grads.astype(low)
+    grad_values = dot(patch_full, pooled_low, 1, 1).astype(low)
+    key_low = (query[:, :, None] * counts[:, None, :]).astype(low).reshape(model, padded)
+    grad_small = einsum(
+        "xde,xem->dm", key_weight, key_low.reshape(HEAD_SIZE, half_width, padded)
+    ) + einsum("xde,xem->dm", value_weight, pooled_low.reshape(HEAD_SIZE, half_width, padded))
+    head_sums = einsum("dm,hm->dh", patch_full.astype(wide), counts)
+    grad_query = jnp.sum(
+        key_table.reshape(head_count, HEAD_DIM, padded) * counts[:, None, :], axis=2
+    )
+
+    vector_grads = jnp.concatenate([first_vectors, second_vectors]).T
+    spot = taps + var_count
+    grad_small = jnp.concatenate(
+        [grad_small[:, :spot], vector_grads, jnp.zeros((model, padded - spot - 6), wide)], axis=1
+    )
+    grad_small = jnp.transpose(
+        grad_small.reshape(LON_SIZE, HEAD_SIZE, slice_width, 2, 128), (0, 3, 2, 1, 4)
+    ).reshape(model, HEAD_SIZE, 128)
+    head_block = head_sums.reshape(model, HEAD_SIZE, head_half)
+    bias_cols = expand_bias.shape[1]
+    bias_block = jnp.transpose(
+        grad_up_bias.reshape(HEAD_SIZE, bias_rows, LON_SIZE, bias_cols), (2, 1, 0, 3)
+    )
+    bias_block = jnp.pad(
+        bias_block, ((0, 0), (0, block_rows - bias_rows), (0, 0), (0, 0))
+    ).reshape(model, HEAD_SIZE, bias_cols)
+    query_block = jnp.transpose(
+        grad_query.reshape(HEAD_SIZE, head_half, LON_SIZE, query_width), (2, 1, 0, 3)
+    )
+    query_block = jnp.pad(
+        query_block, ((0, 0), (0, block_rows - head_half), (0, 0), (0, 0))
+    ).reshape(model, HEAD_SIZE, query_width)
+    extra = head_half + bias_cols + query_width
+    filler = jnp.zeros((model, 128 - out_half - extra), wide)
+    tail = jnp.stack(
+        [
+            jnp.concatenate(
+                [
+                    grad_small[:, side],
+                    grad_out[side, :, :out_half].astype(wide),
+                    head_block[:, side],
+                    bias_block[:, side],
+                    query_block[:, side],
+                    filler,
+                ],
+                axis=1,
+            )
+            for side in range(2)
+        ]
+    ).astype(low)
+    sums, predicted, cut_grads = reduce_all(
+        [grad_up, grad_down, grad_proj, grad_input, grad_mixer, grad_values, tail],
+        predicted.reshape(HEAD_SIZE, 2, slot_width, 128),
+        cut_grads,
+        2,
+    )
+    predicted = predicted[:, :, :out_half]
+    full_half = up_weight.shape[2]
+    place = [0]
+
+    def take(width):
+        begin = place[0]
+        place[0] = begin + width
+        return sums[:, begin : begin + width]
+
+    out_up = take(full_half)
+    out_down = take(full_half).T
+    out_proj = take(half_width).T
+    out_input = jnp.stack([take(half_width) for _ in range(3)])
+    out_mixer = take(half_width).T
+    out_values = take(half_width)
+    tail_small = take(128)
+    tail_rest = take(128)
+    tail_small = jnp.concatenate([tail_small[:slice_width], tail_small[slice_width:]], axis=1).T
+    out_patch = jnp.transpose(tail_small[:taps].reshape(4, var_count, slice_width), (1, 0, 2))
+    out_variable = tail_small[taps:spot]
+    out_lead = tail_small[spot : spot + 2]
+    out_final = tail_rest[:, :out_half]
+    at = out_half
+    my_heads = tail_rest[:, at : at + head_half]
+    at += head_half
+    out_bias = tail_rest[:bias_rows, at : at + bias_cols]
+    at += bias_cols
+    out_query = tail_rest[:head_half, at : at + query_width]
+    my_query = block_slice(query, head, head_half, 0)
+    out_keys = (my_heads[:, :, None] * my_query[None]).reshape(block_rows, half_width)
+
+    field_grads = paste_patches(cut_grads, lat_lanes, shift_lanes, lat_count)
+    choose = (jnp.arange(column_count + 2)[:, None] - 1 == wanted[None, :]).astype(wide)
+    columns = jnp.einsum("avn,cn->vac", field_grads, choose, precision=highest)
+    from_west = lax.ppermute(columns[:, :, -1:], LON, up)
+    from_east = lax.ppermute(columns[:, :, :1], LON, down)
+    spot_at = jnp.arange(column_count)
+    pixel_grad = columns[:, :, 1:-1] + jnp.where(spot_at == 0, from_west, 0.0)
+    pixel_grad = pixel_grad + jnp.where(spot_at == column_count - 1, from_east, 0.0)
+    return (
+        predicted,
+        pixel_grad,
+        out_patch,
+        out_variable,
+        out_query,
+        out_keys,
+        out_values,
+        out_mixer,
+        out_lead,
+        tail_small[spot + 2],
+        tail_small[spot + 3],
+        out_input,
+        out_proj,
+        tail_small[spot + 4],
+        tail_small[spot + 5],
+        out_up,
+        out_bias,
+        out_down,
+        out_final,
+    )
+
+
 def solution(mesh):
+    body = fast_local if planned(mesh) else local
     placed = (
-        P(None, None, "lon"),
+        P(None, None, LON),
         P(),
         P(),
-        P(None, "lon"),
-        P(None, "lon"),
+        P(None, LON),
+        P(None, LON),
         P(),
-        P(None, None, ("lon", "head")),
-        P(None, ("lon", "head")),
-        P("head", "lon"),
-        P("lon", "head"),
-        P("lon", "head"),
-        P("head", "lon"),
-        P(None, ("lon", "head")),
-        P(("lon", "head")),
-        P(("lon", "head")),
-        P(None, "lon", "head"),
-        P("head", "lon"),
-        P(("lon", "head")),
-        P(("lon", "head")),
-        P("lon", "head"),
-        P("head", "lon"),
-        P("head", "lon"),
-        P("lon", "head"),
-        P(None, "lon", "head"),
+        P(None, None, (LON, HEAD)),
+        P(None, (LON, HEAD)),
+        P(HEAD, LON),
+        P(LON, HEAD),
+        P(LON, HEAD),
+        P(HEAD, LON),
+        P(None, (LON, HEAD)),
+        P((LON, HEAD)),
+        P((LON, HEAD)),
+        P(None, LON, HEAD),
+        P(HEAD, LON),
+        P((LON, HEAD)),
+        P((LON, HEAD)),
+        P(LON, HEAD),
+        P(HEAD, LON),
+        P(HEAD, LON),
+        P(LON, HEAD),
+        P(None, LON, HEAD),
     )
     return jax.shard_map(
-        local,
+        body,
         mesh=mesh,
         in_specs=placed,
         out_specs=(
-            P(None, "lon", "head"),
-            P(None, None, "lon"),
-            P(None, None, ("lon", "head")),
-            P(None, ("lon", "head")),
-            P("head", "lon"),
-            P("lon", "head"),
-            P("lon", "head"),
-            P("head", "lon"),
-            P(None, ("lon", "head")),
-            P(("lon", "head")),
-            P(("lon", "head")),
-            P(None, "lon", "head"),
-            P("head", "lon"),
-            P(("lon", "head")),
-            P(("lon", "head")),
-            P("lon", "head"),
-            P("head", "lon"),
-            P("head", "lon"),
-            P("lon", "head"),
+            P(None, LON, HEAD),
+            P(None, None, LON),
+            P(None, None, (LON, HEAD)),
+            P(None, (LON, HEAD)),
+            P(HEAD, LON),
+            P(LON, HEAD),
+            P(LON, HEAD),
+            P(HEAD, LON),
+            P(None, (LON, HEAD)),
+            P((LON, HEAD)),
+            P((LON, HEAD)),
+            P(None, LON, HEAD),
+            P(HEAD, LON),
+            P((LON, HEAD)),
+            P((LON, HEAD)),
+            P(LON, HEAD),
+            P(HEAD, LON),
+            P(HEAD, LON),
+            P(LON, HEAD),
         ),
         check_vma=False,
     )

time: 3510 us -> 590 us (0.17)
  waiting for transfers between devices: 910 us -> 1.39 us
  local copies, waits for them, and re-layouts: 903 us -> 56.1 us
  matrix products: 846 us -> 17.5 us
  Pallas kernels: 0 us -> 472 us
  blocking collectives: 420 us -> 0 us
  other arithmetic: 345 us -> 13.1 us
    dot_general x88 -> x8, matrix products: 846 us -> 17.5 us  [the longest x6 10.9 us: einsum(): return jnp.einsum(spec, left, right, preferred_element_type=wide)]
    pallas_call x0 -> x15, Pallas kernels: none -> 472 us  [the longest x1 153 us: reduce_all(): pl.pallas_call(partial(reduce_kernel, chunks, count), out_shape=[jax.Shap...]
    reshape x28 -> x13, local copies, waits for them, and re-layouts: 404 us -> 4.88 us  [the longest x1 2.5 us: gather_all(): g.reshape(a.shape[:-2] + (2, 16 * a.shape[-2], a.shape[-1]))]
    reduce_scatter x15 -> x0, waiting for transfers between devices: 375 us -> none  [the longest x1 137 us: local(): lax.psum_scatter(grad_patch, ('lon', 'head'), scatter_dimension=2, tiled=...]
    all_gather x15 -> x2, waiting for transfers between devices: 369 us -> 0.01 us  [the longest x1 0.01 us: fast_local(): up_weight = lax.all_gather(expand_weight, around, axis=0, tiled=True)]
    all_gather x7 -> x0, blocking collectives: 281 us -> none  [the longest x1 72.4 us: local(): lax.all_gather(patch_weight, ('lon', 'head'), axis=2, tiled=True)]
    convert_element_type x16 -> x7, local copies, waits for them, and re-layouts: 186 us -> 2.62 us  [the longest x2 1.39 us: fast_local(): up_bias = up_bias.astype(wide)]
    unnamed x39 -> x2, waiting for transfers between devices: 165 us -> 1.38 us
  transfers between devices with their start and end apart: 39 -> 6, of which waited for: 20 -> 0; matrix products, arithmetic and copies ran while one was open for 54% -> 8% of each run, Pallas kernels for 0% -> 33%
where the time goes in v1:
time: 590 us; the launch traced here: 585 us
  Pallas kernels  472 us (80%)
  local copies, waits for them, and re-layouts  56.1 us (10%)
  matrix products  17.5 us (3%)
  between operations  15.4 us (3%)
  other arithmetic  13.1 us (2%)
  starting transfers between devices  10 us (2%)
    pallas_call x1, Pallas kernels, reduce_all(): pl.pallas_call(partial(reduce_kernel, chunks, count), out_shape=[jax.Shap...  153 us
    pallas_call x1, Pallas kernels, gather_all(): pl.pallas_call(partial(gather_kernel, items, count), out_shape=shapes, in...  115 us
    pallas_call x4, Pallas kernels, exchange(): pl.pallas_call(plane_kernel, out_shape=jax.ShapeDtypeStruct(values.shape,...  75.7 us
    pallas_call x1, Pallas kernels, feed(): pl.pallas_call(feed_kernel, grid=(2 * count,), out_shape=[shape for shape...  34.9 us
    pallas_call x1, Pallas kernels, attention_backward(): pl.pallas_call(attention_backward_kernel, grid=(steps,), out_shape=jax.Sh...  30.8 us
    pallas_call x1, Pallas kernels, attention_forward(): pl.pallas_call(attention_forward_kernel, grid=(steps,), out_shape=[jax.Sh...  22.2 us
    unnamed x140, local copies, waits for them, and re-layouts  16.1 us
    pallas_call x1, Pallas kernels, go_back(): pl.pallas_call(return_kernel, grid=(kinds * halves,), out_shape=[jax.Shap...  13.3 us
  transfers between devices with their start and end apart: 6, of which 0 were waited for; matrix products, arithmetic and copies ran while one was open for 8% of the time, Pallas kernels for 33%

profile of v1, /device:TPU:0, one launch (start us, length us, event | category | flops | bytes accessed | tf_op | source)
XLA Modules:
  0.0 585.3 jit_solution(10195700199776212712)
XLA Ops:
  10.7 5.5 collective-permute-start.1
  24.7 2.0 fusion.1.field_ref
  26.7 2.8 shard_map.375.refs_8_
  29.5 114.9 %shard_map.376 = (bf16[2,4,2,2,16,128]{5,4,3,2,1,0:T(8,128)(2,1)}, bf16[2,4,2,2,64,128]{5,4,3,2,1,0:T(8,128)(2,1)}, bf16[2,4,2,2,64,512]{5,4,3,2,1,0:T(8,128)(2,...) custom-call(bf16[16,128]{1,0:T(8,128)(2,1)} %bitcast.245, ...), custom_call_target="tpu_custom_call" | custom-call | tf_op jit(solution)/shard_map/pallas_call | solution.py:790
  148.9 2.6 broadcast_select_fusion
  152.9 2.5 copy.269
  156.4 3.4 multiply_reduce_fusion.1
  159.8 1.9 convolution_convert_fusion.1
  161.8 6.4 %shard_map.377 = (bf16[256,256]{1,0:T(8,128)(2,1)S(1)}, f32[16,48,256]{2,1,0:T(8,128)S(1)}, bf16[1024,256]{1,0:T(8,128)(2,1)S(1)}) custom-call(bf16[2,192,128]{2,1,0:T(8,128)(2,1)S(1)} %copy-done.17, f32[16,256]{1,0:T(8,128)S(1)} %broadcast_multiply_fusion.3.score_ref, bf16[1024,256]{1,0:T(8,128)(2,1)S(1)} %bitcast.184), custom_call_target="tpu_custom_call" | custom-call | tf_op jit(solution)/shard_map/pallas_call | solution.py:1190
  168.3 3.8 shard_map.378
  175.1 35.7 %shard_map.379.joint_ref = bf16[8,3,256,128]{3,2,1,0:T(8,128)(2,1)} custom-call(bf16[8,3,256,128]{3,2,1,0:T(8,128)(2,1)} %bitcast.186), custom_call_target="tpu_custom_call" | custom-call | tf_op jit(solution)/shard_map/pallas_call | solution.py:853
  211.2 22.2 %shard_map.380 = (bf16[8,256,128]{2,1,0:T(8,128)(2,1)S(1)}, f32[2048,128]{1,0:T(8,128)S(1)}, f32[2,2048,1]{2,1,0:T(8,128)}) custom-call(bf16[8,3,256,128]{3,2,1,0:T(8,128)(2,1)} %shard_map.379.joint_ref, f32[1,2048]{1,0:T(1,128)S(1)} %get-tuple-element.242.tag_ref, f32[2048,1]{1,0:T(8,128)S(1)} %copy.278.crop_ref), custom_call_target="tpu_custom_call" | custom-call | tf_op jit(solution)/shard_map/pallas_call | solution.py:1301
  235.2 9.5 %shard_map.381 = bf16[8,256,128]{2,1,0:T(8,128)(2,1)} custom-call(bf16[8,256,128]{2,1,0:T(8,128)(2,1)} %copy-done.15), custom_call_target="tpu_custom_call" | custom-call | tf_op jit(solution)/shard_map/pallas_call | solution.py:853
  248.1 34.9 %shard_map.382 = (bf16[2,256,128]{2,1,0:T(8,128)(2,1)}, f32[256,1024]{1,0:T(8,128)}, bf16[1,8,256,128]{3,2,1,0:T(8,128)(2,1)}, bf16[2,1024,2048]{2,1,0:T(8,128)(...) custom-call(bf16[1,8,256,128]{3,2,1,0:T(8,128)(2,1)} %bitcast.201, ...), custom_call_target="tpu_custom_call" | custom-call | tf_op jit(solution)/shard_map/pallas_call | solution.py:1624
  283.0 9.6 %shard_map.383.grad_ref = bf16[8,256,128]{2,1,0:T(8,128)(2,1)} custom-call(bf16[8,256,128]{2,1,0:T(8,128)(2,1)} %bitcast.225), custom_call_target="tpu_custom_call" | custom-call | tf_op jit(solution)/shard_map/pallas_call | solution.py:853
  292.6 30.8 %shard_map.384.source = bf16[8,3,256,128]{3,2,1,0:T(8,128)(2,1)} custom-call(bf16[8,3,256,128]{3,2,1,0:T(8,128)(2,1)} %shard_map.379.joint_ref, f32[1,2048]{1,0:T(1,128)} %copy-done.18, f32[2048,1]{1,0:T(8,128)} %copy-done.2, bf16[8,256,128]{2,1,0:T(8,128)(2,1)} %shard_map.383.grad_ref, f32[2048,128]{1,0:T(8,128)} %copy-done.7, ...), custom_call_target="tpu_custom_call" | custom-call | tf_op jit(solution)/shard_map/pallas_call | solution.py:1370
  323.4 20.8 %shard_map.385 = bf16[8,3,256,128]{3,2,1,0:T(8,128)(2,1)} custom-call(bf16[8,3,256,128]{3,2,1,0:T(8,128)(2,1)} %shard_map.384.source), custom_call_target="tpu_custom_call" | custom-call | tf_op jit(solution)/shard_map/pallas_call | solution.py:853
  345.4 13.3 %shard_map.386 = (bf16[3,2,1024,512]{3,2,1,0:T(8,128)(2,1)}, bf16[2,1024,512]{2,1,0:T(8,128)(2,1)}, bf16[1024,256]{1,0:T(8,128)(2,1)S(1)}, f32[4,1024]{1,0:T(4,128)S(1)}) custom-call(bf16[1,8,3,256,128]{4,3,2,1,0:T(8,128)(2,1)} %bitcast.192, bf16[3,2,1024,512]{3,2,1,0:T(8,128)(2,1)} %bitcast.178, bf16[256,1024]{1,0:T(8,128)(2,1)S(1)} %copy-done.14, ...), custom_call_target="tpu_custom_call" | custom-call | tf_op jit(solution)/shard_map/pallas_call | solution.py:1713
  358.7 8.5 %shard_map.387 = (f32[1024,256]{1,0:T(8,128)S(1)}, f32[16,256]{1,0:T(8,128)S(1)}, f32[2,192,128]{2,1,0:T(8,128)S(1)}) custom-call(bf16[256,256]{1,0:T(8,128)(2,1)S(1)} %get-tuple-element.81.patch_ref, f32[16,48,256]{2,1,0:T(8,128)S(1)} %copy-done.10, f32[16,256]{1,0:T(8,128)S(1)} %broadcast_multiply_fusion.3.score_ref, bf16[1024,256]{1,0:T(8,128)(2,1)S(1)} %bitcast.185, ...), custom_call_target="tpu_custom_call" | custom-call | tf_op jit(solution)/shard_map/pallas_call | solution.py:1256
  370.5 2.5 convolution_bitcast_fusion.1
  379.1 2.1 convolution_convert_fusion
  384.4 152.7 %shard_map.388 = (f32[64,7424]{1,0:T(8,128)}, bf16[4,128,128]{2,1,0:T(8,128)(2,1)}, f32[4,192,128]{2,1,0:T(8,128)}) custom-call(bf16[2,4,2,2,64,2048]{5,4,3,2,1,0:T(8,128)(2,1)} %bitcast.189, bf16[2,4,2,2,64,2048]{5,4,3,2,1,0:T(8,128)(2,1)} %bitcast.190, bf16[2,4,2,2,64,512]{5,4,3,2,1,0:T(8,128)(2,1)} %bitcast.209, ...), custom_call_target="tpu_custom_call" | custom-call | tf_op jit(solution)/shard_map/pallas_call | solution.py:1038
  537.1 2.0 slice_bitcast_fusion.1
  541.3 2.3 slice_bitcast_fusion
  543.9 5.7 shard_map.389
  549.6 4.6 convolution_bitcast_fusion
  555.4 2.0 copy.298
  558.3 4.4 collective-permute-start.3
  564.2 1.7 pad_maximum_fusion.1
  571.6 1.6 copy.302
  574.6 1.6 fusion.2
  576.2 2.1 copy.303
  (274 shorter events, 53.3 us)
Async XLA Ops:
  7.2 14.4 %copy-start = (s32[4,8]{1,0:T(4,128)S(1)}, s32[4,8]{1,0:T(4,128)}, u32[]{:S(2)}) copy-start(s32[4,8]{1,0:T(4,128)} %param.29) | copy-start | bytes 388
  7.2 17.4 %copy-start.29 = (bf16[48,32,256]{2,1,0:T(8,128)(2,1)S(1)}, bf16[48,32,256]{2,1,0:T(8,128)(2,1)}, u32[]{:S(2)}) copy-start(bf16[48,32,256]{2,1,0:T(8,128)(2,1)} %param.24) | copy-start | bytes 2359300
  7.3 9.8 %copy-start.52 = (bf16[32]{0:T(256)(128)(2,1)S(1)}, bf16[32]{0:T(256)(128)(2,1)}, u32[]{:S(2)}) copy-start(bf16[32]{0:T(256)(128)(2,1)} %param.37) | copy-start | bytes 196
  7.3 9.9 %copy-start.53 = (bf16[32]{0:T(256)(128)(2,1)S(1)}, bf16[32]{0:T(256)(128)(2,1)}, u32[]{:S(2)}) copy-start(bf16[32]{0:T(256)(128)(2,1)} %param.38) | copy-start | bytes 196
  7.3 10.0 %copy-start.54 = (bf16[32]{0:T(256)(128)(2,1)S(1)}, bf16[32]{0:T(256)(128)(2,1)}, u32[]{:S(2)}) copy-start(bf16[32]{0:T(256)(128)(2,1)} %param.41) | copy-start | bytes 196
  7.3 10.1 %copy-start.55 = (bf16[32]{0:T(256)(128)(2,1)S(1)}, bf16[32]{0:T(256)(128)(2,1)}, u32[]{:S(2)}) copy-start(bf16[32]{0:T(256)(128)(2,1)} %param.42) | copy-start | bytes 196
  7.3 10.2 %copy-start.33 = (bf16[4,128,96]{1,2,0:T(8,128)(2,1)S(1)}, bf16[4,128,96]{1,2,0:T(8,128)(2,1)}, u32[]{:S(2)}) copy-start(bf16[4,128,96]{1,2,0:T(8,128)(2,1)} %param.47) | copy-start | bytes 294916
  7.3 10.4 %copy-start.42 = (s32[4,128]{1,0:T(4,128)S(1)}, s32[4,128]{1,0:T(4,128)}, u32[]{:S(2)}) copy-start(s32[4,128]{1,0:T(4,128)} %param.28) | copy-start | bytes 6148
  7.3 10.4 %copy-start.43 = (bf16[48,32]{0,1:T(8,128)(2,1)S(1)}, bf16[48,32]{0,1:T(8,128)(2,1)}, u32[]{:S(2)}) copy-start(bf16[48,32]{0,1:T(8,128)(2,1)} %param.31) | copy-start | bytes 9220
  7.3 14.4 %copy-start.47 = (bf16[8,4]{0,1:T(4,128)(2,1)S(1)}, bf16[8,4]{0,1:T(4,128)(2,1)}, u32[]{:S(2)}) copy-start(bf16[8,4]{0,1:T(4,128)(2,1)} %param.32) | copy-start | bytes 196
  7.4 14.6 %copy-start.48 = (bf16[32,4]{0,1:T(4,128)(2,1)S(1)}, bf16[32,4]{0,1:T(4,128)(2,1)}, u32[]{:S(2)}) copy-start(bf16[32,4]{0,1:T(4,128)(2,1)} %param.44) | copy-start | bytes 772
  7.4 15.5 %copy-start.37 = (bf16[64,96]{1,0:T(8,128)(2,1)S(1)}, bf16[64,96]{1,0:T(8,128)(2,1)}, u32[]{:S(2)}) copy-start(bf16[64,96]{1,0:T(8,128)(2,1)} %param.46) | copy-start | bytes 36868
  7.4 240.7 %all-gather.3.cloned.1.call-start = ((), (), s32[]{:S(2)}) async-start(), calls=%async_computation | async-start | bytes 8650752 | tf_op jit(solution)/shard_map/all_gather | solution.py:1821
  8.1 240.0 %all-gather.5.cloned.1.call-start = ((), (), s32[]{:S(2)}) async-start(), calls=%async_computation.1 | async-start | bytes 8650752 | tf_op jit(solution)/shard_map/all_gather | solution.py:1823
  10.7 14.0 %collective-permute-start.1 = (bf16[48,32,1]{0,1,2:T(8,128)(2,1)S(1)}, bf16[48,32,1]{0,1,2:T(8,128)(2,1)S(1)}, u32[]{:S(2)}, u32[]{:S(2)}) collective-permute-start(bf16[48,32,1]{0,1,2:T(8,128)(2,1)S(1)} %copy.310), channel_id=1, source_target_pairs={{2,0},{4,2},{6,4},{8,6},{10,8},{12,10},{14,12},{16,14},{18,16},{20... | collective-permute-start | bytes 9224 | tf_op jit(solution)/shard_map/ppermute | solution.py:1794
  16.7 8.0 %collective-permute-start = (bf16[48,32,1]{0,1,2:T(8,128)(2,1)S(1)}, bf16[48,32,1]{0,1,2:T(8,128)(2,1)S(1)}, u32[]{:S(2)}, u32[]{:S(2)}) collective-permute-start(bf16[48,32,1]{0,1,2:T(8,128)(2,1)S(1)} %copy.309), channel_id=1, source_target_pairs={{0,2},{2,4},{4,6},{6,8},{8,10},{10,12},{12,14},{14,16},{16,18},{18... | collective-permute-start | bytes 9224 | tf_op jit(solution)/shard_map/ppermute | solution.py:1793
  16.9 9.9 %copy-start.35 = (s32[1,4,2,128]{3,1,2,0:T(4,128)}, s32[1,4,2,128]{3,1,2,0:T(4,128)S(1)}, u32[]{:S(2)}) copy-start(s32[1,4,2,128]{3,1,2,0:T(4,128)S(1)} %copy.333) | copy-start | bytes 12292
  16.9 9.8 %copy-start.36 = (s32[1,4,2,128]{3,1,2,0:T(4,128)}, s32[1,4,2,128]{3,1,2,0:T(4,128)S(1)}, u32[]{:S(2)}) copy-start(s32[1,4,2,128]{3,1,2,0:T(4,128)S(1)} %copy.334) | copy-start | bytes 12292
  155.6 12.7 %slice-start = ((s8[6291456]{0:T(1024)(128)(4,1)}), s8[2097152]{0:T(1024)(128)(4,1)S(1)}, s32[]{:S(2)}) async-start(s8[6291456]{0:T(1024)(128)(4,1)} %bitcast.179), calls=%async_computation.2 | async-start | bytes 4194304
  156.4 11.9 %slice-start.1 = ((s8[6291456]{0:T(1024)(128)(4,1)}), s8[4194304]{0:T(1024)(128)(4,1)S(1)}, s32[]{:S(2)}) async-start(s8[6291456]{0:T(1024)(128)(4,1)} %bitcast.179), calls=%async_computation.3 | async-start | bytes 8388608
  210.8 33.9 %copy-start.18 = (f32[1,2048]{1,0:T(1,128)}, f32[1,2048]{1,0:T(1,128)S(1)}, u32[]{:S(2)}) copy-start(f32[1,2048]{1,0:T(1,128)S(1)} %get-tuple-element.242.tag_ref) | copy-start | bytes 24580
  211.2 35.6 %copy-start.2 = (f32[2048,1]{1,0:T(8,128)}, f32[2048,1]{1,0:T(8,128)S(1)}, u32[]{:S(2)}) copy-start(f32[2048,1]{1,0:T(8,128)S(1)} %copy.278.crop_ref) | copy-start | bytes 24580
  211.2 36.6 %copy-start.30 = (f32[2,8,16,4]{3,2,1,0:T(8,128)S(1)}, f32[2,8,16,4]{3,2,1,0:T(8,128)}, u32[]{:S(2)}) copy-start(f32[2,8,16,4]{3,2,1,0:T(8,128)} %copy.284) | copy-start | bytes 12292
  323.4 20.9 %copy-start.5 = (f32[256,1024]{1,0:T(8,128)S(1)}, f32[256,1024]{1,0:T(8,128)}, u32[]{:S(2)}) copy-start(f32[256,1024]{1,0:T(8,128)} %copy-done.4) | copy-start | bytes 3145732
  323.4 20.9 %copy-start.8 = (f32[256,1024]{1,0:T(8,128)S(1)}, f32[256,1024]{1,0:T(8,128)}, u32[]{:S(2)}) copy-start(f32[256,1024]{1,0:T(8,128)} %get-tuple-element.78.middle_grad_ref) | copy-start | bytes 3145732
  323.4 20.9 %copy-start.12 = (f32[6,1024]{1,0:T(8,128)S(1)}, f32[6,1024]{1,0:T(8,128)}, u32[]{:S(2)}) copy-start(f32[6,1024]{1,0:T(8,128)} %copy-done.11) | copy-start | bytes 73732
  345.4 13.3 %copy-start.10 = (f32[16,48,256]{2,1,0:T(8,128)S(1)}, f32[16,48,256]{2,1,0:T(8,128)}, u32[]{:S(2)}) copy-start(f32[16,48,256]{2,1,0:T(8,128)} %copy-done.9) | copy-start | bytes 2359300
  345.4 22.5 %copy-start.25 = (bf16[1024,256,1]{1,0,2:T(8,128)(2,1)S(1)}, bf16[1024,256,1]{1,0,2:T(8,128)(2,1)}, u32[]{:S(2)}) copy-start(bf16[1024,256,1]{1,0,2:T(8,128)(2,1)} %copy-done.24) | copy-start | bytes 1572868
  555.4 19.2 %copy-start.49 = (pred[256]{0:T(512)(128)(4,1)S(1)}, pred[256]{0:T(512)(128)(4,1)}, u32[]{:S(2)}) copy-start(pred[256]{0:T(512)(128)(4,1)} %get-tuple-element.253) | copy-start | bytes 772
  555.4 19.2 %copy-start.50 = (pred[256]{0:T(512)(128)(4,1)S(1)}, pred[256]{0:T(512)(128)(4,1)}, u32[]{:S(2)}) copy-start(pred[256]{0:T(512)(128)(4,1)} %get-tuple-element.254) | copy-start | bytes 772
  557.4 17.2 %collective-permute-start.2 = (f32[48,32,1]{0,1,2:T(8,128)}, f32[48,32,1]{0,1,2:T(8,128)}, u32[]{:S(2)}, u32[]{:S(2)}) collective-permute-start(f32[48,32,1]{0,1,2:T(8,128)} %copy.298), channel_id=1, source_target_pairs={{0,2},{2,4},{4,6},{6,8},{8,10},{10,12},{12,14},{14,16},{16,18},{18... | collective-permute-start | bytes 18440 | tf_op jit(solution)/shard_map/ppermute | solution.py:2060
  558.3 16.2 %collective-permute-start.3 = (f32[48,32,1]{0,1,2:T(8,128)}, f32[48,32,1]{0,1,2:T(8,128)S(1)}, u32[]{:S(2)}, u32[]{:S(2)}) collective-permute-start(f32[48,32,1]{0,1,2:T(8,128)} %copy.299), channel_id=1, source_target_pairs={{2,0},{4,2},{6,4},{8,6},{10,8},{12,10},{14,12},{16,14},{18,16},{20... | collective-permute-start | bytes 18440 | tf_op jit(solution)/shard_map/ppermute | solution.py:2061
  (33 other events, 135.9 us)
Sparse Core Ops, SparseCore 0:
  11.1 116.0 all-gather.2
  130.1 92.1 all-gather.4

commit v2 on v1

--- a/solution.py
+++ b/solution.py
@@ -809,64 +809,10 @@
     ] + list(gathered[count:])
 
 
-def plane_kernel(source, target, own_sem, send_sem, recv_sem):
-    x, z, y, c = position()
-    here = y * 4 + c * 2 + x
-    copies = []
-    for flip in range(1, 8):
-        there_y = 1 - y if flip & 4 else y
-        there_c = 1 - c if flip & 2 else c
-        there_x = 1 - x if flip & 1 else x
-        there = there_y * 4 + there_c * 2 + there_x
-        copies.append(
-            remote(
-                source.at[there],
-                target.at[here],
-                send_sem.at[flip],
-                recv_sem.at[flip],
-                (z * 4 + there_y * 2 + there_c, there_x),
-            )
-        )
-    keep = pltpu.make_async_copy(source.at[here], target.at[here], own_sem)
-    keep.start()
-    barrier = pltpu.get_barrier_semaphore()
-    for flip in range(1, 8):
-        there_y = 1 - y if flip & 4 else y
-        there_c = 1 - c if flip & 2 else c
-        there_x = 1 - x if flip & 1 else x
-        pl.semaphore_signal(
-            barrier,
-            inc=1,
-            device_id=(z * 4 + there_y * 2 + there_c, there_x),
-            device_id_type=MESH,
-        )
-    pl.semaphore_wait(barrier, 7)
-    for copy in copies:
-        copy.start()
-    keep.wait()
-    for copy in copies:
-        copy.wait()
-
-
-def exchange(values, number):
-    sem = pltpu.SemaphoreType.DMA
-    return pl.pallas_call(
-        plane_kernel,
-        out_shape=jax.ShapeDtypeStruct(values.shape, values.dtype),
-        in_specs=[pl.BlockSpec(memory_space=pl.ANY)],
-        out_specs=pl.BlockSpec(memory_space=pl.ANY),
-        scratch_shapes=[sem, sem((8,)), sem((8,))],
-        compiler_params=pltpu.CompilerParams(collective_id=number, has_side_effects=True),
-    )(values)
-
-
 def reduce_kernel(chunks, count, *refs):
     ins, value_in, grad_in = refs[:count], refs[count], refs[count + 1]
     out, value_out, grad_out = refs[count + 2 : count + 5]
-    mine, other, first_a, first_b, second, third = refs[count + 5 : count + 11]
-    own_sem, core_send, core_recv, hop_send, hop_recv, line_send, line_recv = refs[
-        count + 11 : count + 18
-    ]
+    buffers, sems = refs[count + 5 : count + 11], refs[count + 11 : count + 18]
     value_send, value_recv, grad_send, grad_recv = refs[count + 18 :]
     x, z, y, c = position()
     across, line = partners(x, z, y, c)
@@ -890,126 +836,21 @@
         post(*letter)
     total = len(chunks)
 
-    def plan(k):
-        keep, core = [], []
-        for side in range(2):
-            index, lead, offset = chunks[k][side]
-            source = ins[index] if lead is None else ins[index].at[lead]
-            span = pl.ds(offset, CHUNK)
-            keep.append(
-                pltpu.make_async_copy(
-                    source.at[:, :, c, :, span], mine.at[2 * k + side], own_sem.at[k, side]
-                )
-            )
-            core.append(
-                remote(
-                    source.at[:, :, 1 - c, :, span],
-                    other.at[2 * k + side],
-                    core_send.at[k, side],
-                    core_recv.at[k, side],
-                    across["c"],
-                )
-            )
-        if k % 2 == 0:
-            one, axis_one = (mine.at[2 * k + 1 - x], first_a.at[k // 2]), "x"
-            two, axis_two = mine.at[2 * k + x, :, 1 - y], "y"
-        else:
-            one, axis_one = (mine.at[pl.ds(2 * k, 2), :, 1 - y], first_b.at[k // 2]), "y"
-            two, axis_two = mine.at[2 * k + 1 - x, :, y], "x"
-        hops = [
-            remote(one[0], one[1], hop_send.at[k, 0], hop_recv.at[k, 0], across[axis_one]),
-            remote(two, second.at[k], hop_send.at[k, 1], hop_recv.at[k, 1], across[axis_two]),
-        ]
-        along = [
-            remote(
-                mine.at[2 * k + x, lax.rem(z + d + 1, 4), y],
-                third.at[k, d],
-                line_send.at[k, d],
-                line_recv.at[k, d],
-                line[d],
-            )
-            for d in range(3)
-        ]
-        return keep, core, hops, along
-
-    plans = [plan(k) for k in range(total)]
-
-    def joined(left, right):
-        return (left.astype(wide) + right.astype(wide)).astype(low)
-
-    def add_core(k):
-        def body(step, carry):
-            side, row = lax.div(step, 4), lax.rem(step, 4)
-            for line_y in range(2):
-                mine[2 * k + side, row, line_y] = joined(
-                    mine[2 * k + side, row, line_y], other[2 * k + side, row, line_y]
-                )
-            return carry
-
-        lax.fori_loop(0, 8, body, 0)
-
-    def add_first(k):
-        def body(row, carry):
-            for part in range(2):
-                if k % 2 == 0:
-                    mine[2 * k + x, row, part] = joined(
-                        mine[2 * k + x, row, part], first_a[k // 2, row, part]
-                    )
-                else:
-                    mine[2 * k + part, row, y] = joined(
-                        mine[2 * k + part, row, y], first_b[k // 2, part, row]
-                    )
-            return carry
-
-        lax.fori_loop(0, 4, body, 0)
-
-    def add_second(k):
-        def body(row, carry):
-            mine[2 * k + x, row, y] = joined(mine[2 * k + x, row, y], second[k, row])
-            return carry
-
-        lax.fori_loop(0, 4, body, 0)
-
-    def add_third(k):
-        result = mine[2 * k + x, z, y].astype(wide)
-        for d in range(3):
-            result = result + third[k, d].astype(wide)
-        out[:, pl.ds(k * CHUNK, CHUNK)] = result
-
+    def source_of(pair, color, side, core):
+        index, lead, offset = chunks[2 * pair + color][side]
+        source = ins[index] if lead is None else ins[index].at[lead]
+        return source.at[:, :, core, :, pl.ds(offset, CHUNK)]
+
+    begin, stage_core, stage_first, stage_second, stage_third, finish = reducer(
+        source_of, buffers, sems, out
+    )
+    plan = ((0, begin), (2, stage_core), (4, stage_first), (6, stage_second), (8, stage_third))
     for step in range(total + 8):
-        if step < total:
-            keep, core, _, _ = plans[step]
-            for copy in core + keep:
-                copy.start()
-        if 0 <= step - 2 < total:
-            k = step - 2
-            keep, core, hops, _ = plans[k]
-            for copy in keep:
-                copy.wait()
-            for copy in core:
-                copy.wait_recv()
-            add_core(k)
-            hops[0].start()
-        if 0 <= step - 4 < total:
-            k = step - 4
-            hops = plans[k][2]
-            hops[0].wait_recv()
-            add_first(k)
-            hops[1].start()
-        if 0 <= step - 6 < total:
-            k = step - 6
-            plans[k][2][1].wait_recv()
-            add_second(k)
-            for copy in plans[k][3]:
-                copy.start()
-        if 0 <= step - 8 < total:
-            k = step - 8
-            for copy in plans[k][3]:
-                copy.wait_recv()
-            add_third(k)
-    for _, core, hops, along in plans:
-        for copy in core + hops + along:
-            copy.wait_send()
+        for back, stage in plan:
+            if 0 <= step - back < total:
+                stage((step - back) // 2, (step - back) % 2)
+    for k in range(total):
+        finish(k // 2, k % 2)
     for letter in letters:
         settle(*letter)
     for row in range(4):
@@ -1045,20 +886,8 @@
         in_specs=[pl.BlockSpec(memory_space=pl.ANY)] * (count + 2),
         out_specs=[pl.BlockSpec(memory_space=pltpu.VMEM)]
         + [pl.BlockSpec(memory_space=pl.ANY)] * 2,
-        scratch_shapes=[
-            pltpu.VMEM((2 * total, 4, 2, rows, CHUNK), low),
-            pltpu.VMEM((2 * total, 4, 2, rows, CHUNK), low),
-            pltpu.VMEM(((total + 1) // 2, 4, 2, rows, CHUNK), low),
-            pltpu.VMEM(((total + 1) // 2, 2, 4, rows, CHUNK), low),
-            pltpu.VMEM((total, 4, rows, CHUNK), low),
-            pltpu.VMEM((total, 3, rows, CHUNK), low),
-            sem((total, 2)),
-            sem((total, 2)),
-            sem((total, 2)),
-            sem((total, 2)),
-            sem((total, 2)),
-            sem((total, 3)),
-            sem((total, 3)),
+        scratch_shapes=reducer_scratch(total, rows)
+        + [
             sem((4,)),
             sem((4,)),
             sem((4,)),
@@ -1271,118 +1100,499 @@
     return jnp.where(inside, values, jnp.zeros_like(values))
 
 
-def attention_forward_kernel(joint_ref, tag_ref, crop_ref, low_ref, wide_ref, total_ref):
-    blocks, _, share, lanes = joint_ref.shape
-    count = low_ref.shape[0]
-    step = pl.program_id(0)
-    queries = joint_ref[pl.ds(step * count, count), 0].reshape(count * share, lanes)
-    keys = joint_ref[:, 1].reshape(blocks * share, lanes)
-    values = joint_ref[:, 2].reshape(blocks * share, lanes)
-    allowed = crop_ref[...] == tag_ref[...]
-    result = None
-    for h in range(2):
-        scores = dot(head_lanes(queries, h), keys, 1, 1)
-        scores = jnp.where(allowed, scores, masked_score)
-        largest = jnp.max(scores, axis=1, keepdims=True)
-        weights = jnp.exp(scores - largest)
-        total = jnp.sum(weights, axis=1, keepdims=True)
-        weights = (weights * (1.0 / total)).astype(low)
-        part = head_lanes(dot(weights, values), h)
-        result = part if result is None else result + part
-        total_ref[h] = largest + jnp.log(total)
-    wide_ref[...] = result
-    low_ref[...] = result.astype(low).reshape(low_ref.shape)
-
-
-def attention_forward(joint, tags, crops, steps):
-    blocks, _, share, lanes = joint.shape
-    slots = blocks * share
-    width = slots // steps
+def plane_device(z, index):
+    return z * 4 + lax.div(index, 2), lax.rem(index, 2)
+
+
+def plane_meet(x, z, y, c):
+    barrier = pltpu.get_barrier_semaphore()
+    for flip in range(1, 8):
+        there_y = 1 - y if flip & 4 else y
+        there_c = 1 - c if flip & 2 else c
+        there_x = 1 - x if flip & 1 else x
+        device = (z * 4 + there_y * 2 + there_c, there_x)
+        pl.semaphore_signal(barrier, inc=1, device_id=device, device_id_type=MESH)
+    return barrier
+
+
+def attend_kernel(
+    source,
+    tag_ref,
+    crop_ref,
+    joint,
+    received,
+    wide_ref,
+    total_ref,
+    sending,
+    own_sem,
+    send_sem,
+    recv_sem,
+    out_own,
+    out_send,
+    out_recv,
+):
+    x, z, y, c = position()
+    me = y * 4 + c * 2 + x
+    peers, kinds, share, lanes = joint.shape
+    slots = peers * share
+    keep = pltpu.make_async_copy(source.at[me], joint.at[me], own_sem)
+    keep.start()
+    barrier = plane_meet(x, z, y, c)
+    pl.semaphore_wait(barrier, peers - 1)
+
+    def inward(step):
+        there = lax.rem(me + step, peers)
+        return remote(
+            source.at[there],
+            joint.at[me],
+            send_sem.at[there],
+            recv_sem.at[me],
+            plane_device(z, there),
+        )
+
+    def arrived(index):
+        return pltpu.make_async_copy(joint.at[index], joint.at[index], recv_sem.at[index])
+
+    for step in range(1, peers):
+        inward(step).start()
+    keep.wait()
+    for step in range(1, peers):
+        arrived(lax.rem(me + step, peers)).wait()
+
+    def block(step, carry):
+        index = lax.rem(me + 1 + step, peers)
+        span = pl.ds(pl.multiple_of(index * share, share), share)
+        queries = joint[index, 0]
+        keys = joint[:, 1].reshape(slots, lanes)
+        values = joint[:, 2].reshape(slots, lanes)
+        allowed = crop_ref[span, :] == tag_ref[...]
+        result = None
+        for h in range(2):
+            scores = dot(head_lanes(queries, h), keys, 1, 1)
+            scores = jnp.where(allowed, scores, masked_score)
+            largest = jnp.max(scores, axis=1, keepdims=True)
+            weights = jnp.exp(scores - largest)
+            total = jnp.sum(weights, axis=1, keepdims=True)
+            weights = (weights * (1.0 / total)).astype(low)
+            part = head_lanes(dot(weights, values), h)
+            result = part if result is None else result + part
+            total_ref[h, span, :] = largest + jnp.log(total)
+        wide_ref[span, :] = result
+        sending[index] = result.astype(low)
+
+        @pl.when(step < peers - 1)
+        def _():
+            outward(index).start()
+
+        return carry
+
+    def outward(index):
+        return remote(
+            sending.at[index],
+            received.at[me],
+            out_send.at[index],
+            out_recv.at[me],
+            plane_device(z, index),
+        )
+
+    lax.fori_loop(0, peers, block, 0)
+    last = pltpu.make_async_copy(sending.at[me], received.at[me], out_own)
+    last.start()
+    for step in range(1, peers):
+        inward(step).wait_send()
+        outward(lax.rem(me + step, peers)).wait_send()
+        there = lax.rem(me + step, peers)
+        pltpu.make_async_copy(
+            sending.at[there], received.at[there], out_recv.at[there]
+        ).wait()
+    last.wait()
+
+
+def attend_all(source, tags, crops, number):
+    peers, kinds, share, lanes = source.shape
+    slots = peers * share
+    sem = pltpu.SemaphoreType.DMA
+    vmem = pl.BlockSpec(memory_space=pltpu.VMEM)
+    hbm = pl.BlockSpec(memory_space=pl.ANY)
     return pl.pallas_call(
-        attention_forward_kernel,
-        grid=(steps,),
+        attend_kernel,
         out_shape=[
-            jax.ShapeDtypeStruct((blocks, share, lanes), low),
+            jax.ShapeDtypeStruct(source.shape, low),
+            jax.ShapeDtypeStruct((peers, share, lanes), low),
             jax.ShapeDtypeStruct((slots, lanes), wide),
             jax.ShapeDtypeStruct((2, slots, 1), wide),
         ],
-        in_specs=[
-            pl.BlockSpec(joint.shape, lambda i: (0, 0, 0, 0)),
-            pl.BlockSpec((1, slots), lambda i: (0, 0)),
-            pl.BlockSpec((width, 1), lambda i: (i, 0)),
+        in_specs=[hbm, vmem, vmem],
+        out_specs=[vmem, hbm, vmem, vmem],
+        scratch_shapes=[
+            pltpu.VMEM((peers, share, lanes), low),
+            sem,
+            sem((peers,)),
+            sem((peers,)),
+            sem,
+            sem((peers,)),
+            sem((peers,)),
         ],
-        out_specs=[
-            pl.BlockSpec((blocks // steps, share, lanes), lambda i: (i, 0, 0)),
-            pl.BlockSpec((width, lanes), lambda i: (i, 0)),
-            pl.BlockSpec((2, width, 1), lambda i: (0, i, 0)),
+        compiler_params=pltpu.CompilerParams(
+            collective_id=number, has_side_effects=True, vmem_limit_bytes=50 * 2**20
+        ),
+    )(source, tags, crops)
+
+
+def joined(left, right):
+    return (left.astype(wide) + right.astype(wide)).astype(low)
+
+
+def reducer(source_of, buffers, sems, out):
+    mine, other, first_a, first_b, second, third = buffers
+    own_sem, core_send, core_recv, hop_send, hop_recv, line_send, line_recv = sems
+    x, z, y, c = position()
+    across, line = partners(x, z, y, c)
+
+    def keeps(pair, color):
+        k = 2 * pair + color
+        return [
+            pltpu.make_async_copy(
+                source_of(pair, color, side, c), mine.at[2 * k + side], own_sem.at[k, side]
+            )
+            for side in range(2)
+        ]
+
+    def swaps(pair, color):
+        k = 2 * pair + color
+        return [
+            remote(
+                source_of(pair, color, side, 1 - c),
+                other.at[2 * k + side],
+                core_send.at[k, side],
+                core_recv.at[k, side],
+                across["c"],
+            )
+            for side in range(2)
+        ]
+
+    def hop_one(pair, color):
+        k = 2 * pair + color
+        if color == 0:
+            source, target, axis = mine.at[2 * k + 1 - x], first_a.at[pair], "x"
+        else:
+            source = mine.at[pl.ds(2 * k, 2), :, 1 - y]
+            target, axis = first_b.at[pair], "y"
+        return remote(source, target, hop_send.at[k, 0], hop_recv.at[k, 0], across[axis])
+
+    def hop_two(pair, color):
+        k = 2 * pair + color
+        if color == 0:
+            source, axis = mine.at[2 * k + x, :, 1 - y], "y"
+        else:
+            source, axis = mine.at[2 * k + 1 - x, :, y], "x"
+        return remote(source, second.at[k], hop_send.at[k, 1], hop_recv.at[k, 1], across[axis])
+
+    def along(pair, color):
+        k = 2 * pair + color
+        return [
+            remote(
+                mine.at[2 * k + x, lax.rem(z + d + 1, 4), y],
+                third.at[k, d],
+                line_send.at[k, d],
+                line_recv.at[k, d],
+                line[d],
+            )
+            for d in range(3)
+        ]
+
+    def begin(pair, color):
+        for copy in swaps(pair, color) + keeps(pair, color):
+            copy.start()
+
+    def stage_core(pair, color):
+        k = 2 * pair + color
+        for copy in keeps(pair, color):
+            copy.wait()
+        for copy in swaps(pair, color):
+            copy.wait_recv()
+
+        def body(step, carry):
+            side, row = lax.div(step, 4), lax.rem(step, 4)
+            for part in range(2):
+                mine[2 * k + side, row, part] = joined(
+                    mine[2 * k + side, row, part], other[2 * k + side, row, part]
+                )
+            return carry
+
+        lax.fori_loop(0, 8, body, 0)
+        hop_one(pair, color).start()
+
+    def stage_first(pair, color):
+        k = 2 * pair + color
+        hop_one(pair, color).wait_recv()
+
+        def body(row, carry):
+            for part in range(2):
+                if color == 0:
+                    mine[2 * k + x, row, part] = joined(
+                        mine[2 * k + x, row, part], first_a[pair, row, part]
+                    )
+                else:
+                    mine[2 * k + part, row, y] = joined(
+                        mine[2 * k + part, row, y], first_b[pair, part, row]
+                    )
+            return carry
+
+        lax.fori_loop(0, 4, body, 0)
+        hop_two(pair, color).start()
+
+    def stage_second(pair, color):
+        k = 2 * pair + color
+        hop_two(pair, color).wait_recv()
+
+        def body(row, carry):
+            mine[2 * k + x, row, y] = joined(mine[2 * k + x, row, y], second[k, row])
+            return carry
+
+        lax.fori_loop(0, 4, body, 0)
+        for copy in along(pair, color):
+            copy.start()
+
+    def stage_third(pair, color):
+        k = 2 * pair + color
+        for copy in along(pair, color):
+            copy.wait_recv()
+        result = mine[2 * k + x, z, y].astype(wide)
+        for d in range(3):
+            result = result + third[k, d].astype(wide)
+        start = k * CHUNK
+        if not isinstance(k, int):
+            start = pl.multiple_of(start, CHUNK)
+        out[:, pl.ds(start, CHUNK)] = result
+
+    def finish(pair, color):
+        hop_one(pair, color).wait_send()
+        hop_two(pair, color).wait_send()
+        for copy in swaps(pair, color) + along(pair, color):
+            copy.wait_send()
+
+    return begin, stage_core, stage_first, stage_second, stage_third, finish
+
+
+def reducer_scratch(total, rows):
+    sem = pltpu.SemaphoreType.DMA
+    pairs = (total + 1) // 2
+    return [
+        pltpu.VMEM((2 * total, 4, 2, rows, CHUNK), low),
+        pltpu.VMEM((2 * total, 4, 2, rows, CHUNK), low),
+        pltpu.VMEM((pairs, 4, 2, rows, CHUNK), low),
+        pltpu.VMEM((pairs, 2, 4, rows, CHUNK), low),
+        pltpu.VMEM((total, 4, rows, CHUNK), low),
+        pltpu.VMEM((total, 3, rows, CHUNK), low),
+    ] + [
+        sem((total, 2)),
+        sem((total, 2)),
+        sem((total, 2)),
+        sem((total, 2)),
+        sem((total, 2)),
+        sem((total, 3)),
+        sem((total, 3)),
+    ]
+
+
+def attend_back_kernel(
+    joint,
+    tag_ref,
+    crop_ref,
+    out_ref,
+    total_ref,
+    source,
+    feed_ref,
+    stacked,
+    sums,
+    grads,
+    result,
+    key_acc,
+    value_acc,
+    *rest
+):
+    buffers, sems = rest[:6], rest[6:13]
+    in_own, in_send, in_recv, back_own, back_send, back_recv = rest[13:]
+    x, z, y, c = position()
+    across, line = partners(x, z, y, c)
+    me = y * 4 + c * 2 + x
+    peers, kinds, share, lanes = joint.shape
+    slots = peers * share
+    scale = HEAD_DIM ** (-0.5)
+    each = feed_ref.shape[-1] // CHUNK
+
+    def source_of(pair, color, side, core):
+        k = 2 * pair + color
+        offset = pl.multiple_of(lax.rem(k, each) * CHUNK, CHUNK)
+        return feed_ref.at[lax.div(k, each), side, :, :, core, :, pl.ds(offset, CHUNK)]
+
+    begin, stage_core, stage_first, stage_second, stage_third, finish = reducer(
+        source_of, buffers, sems, sums
+    )
+    keep = pltpu.make_async_copy(source.at[me], grads.at[me], in_own)
+    keep.start()
+    barrier = plane_meet(x, z, y, c)
+    for device in line:
+        pl.semaphore_signal(barrier, inc=1, device_id=device, device_id_type=MESH)
+    pl.semaphore_wait(barrier, peers - 1 + len(line))
+
+    def inward(there):
+        return remote(
+            source.at[there],
+            grads.at[me],
+            in_send.at[there],
+            in_recv.at[me],
+            plane_device(z, there),
+        )
+
+    def outward(there, part):
+        span = pl.ds(0, 1) if part == 0 else pl.ds(1, 2)
+        return remote(
+            result.at[there, span],
+            stacked.at[me, span],
+            back_send.at[there, part],
+            back_recv.at[me, part],
+            plane_device(z, there),
+        )
+
+    for step in range(1, peers):
+        inward(lax.rem(me + step, peers)).start()
+    key_acc[...] = jnp.zeros_like(key_acc)
+    value_acc[...] = jnp.zeros_like(value_acc)
+    pairs = feed_ref.shape[0] * each // 2
+
+    def attention(index):
+        span = pl.ds(pl.multiple_of(index * share, share), share)
+        queries = joint[index, 0]
+        keys = joint[:, 1].reshape(slots, lanes)
+        values = joint[:, 2].reshape(slots, lanes)
+        grad = grads[index]
+        product = grad.astype(wide) * out_ref[span, :]
+        allowed = crop_ref[span, :] == tag_ref[...]
+        query_grad = None
+        for h in range(2):
+            query_part, grad_part = head_lanes(queries, h), head_lanes(grad, h)
+            scores = jnp.where(allowed, dot(query_part, keys, 1, 1), masked_score)
+            weights = jnp.exp(scores - total_ref[h, span, :])
+            weight_grads = dot(grad_part, values, 1, 1)
+            delta = jnp.sum(head_lanes(product, h), axis=1, keepdims=True)
+            score_grads = (weights * (weight_grads - delta)).astype(low)
+            weights = weights.astype(low)
+            value_acc[...] += dot(grad_part, weights, 0, 0)
+            key_acc[...] += dot(query_part, score_grads, 0, 0)
+            part = head_lanes(dot(score_grads, keys), h)
+            query_grad = part if query_grad is None else query_grad + part
+        result[index, 0] = (query_grad * scale).astype(low)
+
+    def step_body(step, carry):
+        @pl.when(step < pairs)
+        def _():
+            begin(step, 0)
+            begin(step, 1)
+
+        for back, stage in ((1, stage_core), (2, stage_first), (3, stage_second), (4, stage_third)):
+
+            @pl.when(jnp.logical_and(step >= back, step < pairs + back))
+            def _():
+                stage(step - back, 0)
+                stage(step - back, 1)
+
+        @pl.when(step < peers)
+        def _():
+            index = lax.rem(me + step, peers)
+
+            @pl.when(step == 0)
+            def _():
+                keep.wait()
+
+            @pl.when(step > 0)
+            def _():
+                pltpu.make_async_copy(
+                    grads.at[index], grads.at[index], in_recv.at[index]
+                ).wait()
+
+            attention(index)
+
+            @pl.when(step > 0)
+            def _():
+                outward(index, 0).start()
+
+        @pl.when(step == peers - 1)
+        def _():
+            for index in range(peers):
+                span = slice(index * share, (index + 1) * share)
+                result[index, 1] = key_acc[:, span].T.astype(low)
+                result[index, 2] = value_acc[:, span].T.astype(low)
+            for other in range(1, peers):
+                outward(lax.rem(me + other, peers), 1).start()
+            pltpu.make_async_copy(result.at[me], stacked.at[me], back_own).start()
+
+        return carry
+
+    lax.fori_loop(0, pairs + 4, step_body, 0)
+
+    def finish_body(pair, carry):
+        finish(pair, 0)
+        finish(pair, 1)
+        return carry
+
+    lax.fori_loop(0, pairs, finish_body, 0)
+    for step in range(1, peers):
+        there = lax.rem(me + step, peers)
+        inward(there).wait_send()
+        for part in range(2):
+            outward(there, part).wait_send()
+            span = pl.ds(0, 1) if part == 0 else pl.ds(1, 2)
+            pltpu.make_async_copy(
+                result.at[there, span], stacked.at[there, span], back_recv.at[there, part]
+            ).wait()
+    pltpu.make_async_copy(result.at[me], stacked.at[me], back_own).wait()
+
+
+def attend_back(joint, tags, crops, outputs, totals, source, feed_grads, number):
+    peers, kinds, share, lanes = joint.shape
+    slots = peers * share
+    sides, halves, rows, columns = feed_grads.shape
+    total = sides * columns // CHUNK
+    sem = pltpu.SemaphoreType.DMA
+    vmem = pl.BlockSpec(memory_space=pltpu.VMEM)
+    hbm = pl.BlockSpec(memory_space=pl.ANY)
+    return pl.pallas_call(
+        attend_back_kernel,
+        out_shape=[
+            jax.ShapeDtypeStruct(joint.shape, low),
+            jax.ShapeDtypeStruct((rows // 16, total * CHUNK), wide),
         ],
-        compiler_params=pltpu.CompilerParams(vmem_limit_bytes=50 * 2**20),
-    )(joint, tags, crops)
-
-
-def attention_backward_kernel(
-    joint_ref, tag_ref, crop_ref, grad_ref, out_ref, total_ref, result_ref, key_acc, value_acc
-):
-    blocks, _, share, lanes = joint_ref.shape
-    count = grad_ref.shape[0]
-    step = pl.program_id(0)
-    queries = joint_ref[pl.ds(step * count, count), 0].reshape(count * share, lanes)
-    keys = joint_ref[:, 1].reshape(blocks * share, lanes)
-    values = joint_ref[:, 2].reshape(blocks * share, lanes)
-    grads = grad_ref[...].reshape(count * share, lanes)
-    product = grads.astype(wide) * out_ref[...]
-    allowed = crop_ref[...] == tag_ref[...]
-    scale = HEAD_DIM ** (-0.5)
-
-    @pl.when(step == 0)
-    def _():
-        key_acc[...] = jnp.zeros_like(key_acc)
-        value_acc[...] = jnp.zeros_like(value_acc)
-
-    query_grad = None
-    for h in range(2):
-        query_part, grad_part = head_lanes(queries, h), head_lanes(grads, h)
-        scores = jnp.where(allowed, dot(query_part, keys, 1, 1), masked_score)
-        weights = jnp.exp(scores - total_ref[h])
-        weight_grads = dot(grad_part, values, 1, 1)
-        delta = jnp.sum(head_lanes(product, h), axis=1, keepdims=True)
-        score_grads = (weights * (weight_grads - delta)).astype(low)
-        weights = weights.astype(low)
-        value_acc[...] += dot(grad_part, weights, 0, 0)
-        key_acc[...] += dot(query_part, score_grads, 0, 0)
-        part = head_lanes(dot(score_grads, keys), h)
-        query_grad = part if query_grad is None else query_grad + part
-    result_ref[pl.ds(step * count, count), 0] = (
-        (query_grad * scale).astype(low).reshape(count, share, lanes)
-    )
-
-    @pl.when(step == pl.num_programs(0) - 1)
-    def _():
-        shape = (blocks, share, lanes)
-        result_ref[:, 1] = key_acc[...].T.astype(low).reshape(shape)
-        result_ref[:, 2] = value_acc[...].T.astype(low).reshape(shape)
-
-
-def attention_backward(joint, tags, crops, grads, outputs, totals, steps):
-    blocks, _, share, lanes = joint.shape
-    slots = blocks * share
-    width = slots // steps
-    return pl.pallas_call(
-        attention_backward_kernel,
-        grid=(steps,),
-        out_shape=jax.ShapeDtypeStruct(joint.shape, low),
-        in_specs=[
-            pl.BlockSpec(joint.shape, lambda i: (0, 0, 0, 0)),
-            pl.BlockSpec((1, slots), lambda i: (0, 0)),
-            pl.BlockSpec((width, 1), lambda i: (i, 0)),
-            pl.BlockSpec((blocks // steps, share, lanes), lambda i: (i, 0, 0)),
-            pl.BlockSpec((width, lanes), lambda i: (i, 0)),
-            pl.BlockSpec((2, width, 1), lambda i: (0, i, 0)),
+        in_specs=[vmem] * 5 + [hbm] * 2,
+        out_specs=[hbm, vmem],
+        scratch_shapes=[
+            pltpu.VMEM((peers, share, lanes), low),
+            pltpu.VMEM(joint.shape, low),
+            pltpu.VMEM((lanes, slots), wide),
+            pltpu.VMEM((lanes, slots), wide),
+        ]
+        + reducer_scratch(total, rows // 16)
+        + [
+            sem,
+            sem((peers,)),
+            sem((peers,)),
+            sem,
+            sem((peers, 2)),
+            sem((peers, 2)),
         ],
-        out_specs=pl.BlockSpec(joint.shape, lambda i: (0, 0, 0, 0)),
-        scratch_shapes=[pltpu.VMEM((lanes, slots), wide), pltpu.VMEM((lanes, slots), wide)],
-        compiler_params=pltpu.CompilerParams(vmem_limit_bytes=56 * 2**20),
-    )(joint, tags, crops, grads, outputs, totals)
+        compiler_params=pltpu.CompilerParams(
+            collective_id=number, has_side_effects=True, vmem_limit_bytes=60 * 2**20
+        ),
+    )(
+        joint,
+        tags,
+        crops,
+        outputs,
+        totals,
+        source,
+        feed_grads.reshape(sides, halves, 4, 2, 2, rows // 16, columns),
+    )
 
 
 def whole(array):
@@ -1484,8 +1694,7 @@
     predicted_ref,
     middle_grad_ref,
     unit_ref,
-    grad_up_ref,
-    grad_down_ref,
+    grad_feed_ref,
     grad_proj_ref,
     grad_final_ref,
     grad_bias_ref,
@@ -1558,8 +1767,8 @@
         hidden_low = hidden_grad.astype(low)
         grad_bias_ref[...] = jnp.sum(hidden_low.astype(wide), axis=0, keepdims=True)
         total[...] += dot(hidden_low, up_ref[0], 1, 1)
-        grad_down_ref[0] = dot(grad_turned[...], active[block]).astype(low)
-        grad_up_ref[0] = dot(second_turned[...], hidden_low).astype(low)
+        grad_feed_ref[0, 0] = dot(second_turned[...], hidden_low).astype(low)
+        grad_feed_ref[1, 0] = dot(grad_turned[...], active[block]).astype(low)
 
     @pl.when(step == 2 * count - 1)
     def _():
@@ -1595,7 +1804,7 @@
 
     def late_block(i):
         j = lax.max(i - count, 0)
-        return (lax.div(j, each), 0, lax.rem(j, each))
+        return (0, lax.div(j, each), 0, lax.rem(j, each))
 
     def fixed(shape, dtype):
         rank = len(shape)
@@ -1606,12 +1815,8 @@
         fixed((tokens, model), wide),
         fixed(attended.shape, low),
         (
-            jax.ShapeDtypeStruct(up_weight.shape, low),
-            pl.BlockSpec((1, model, block), late_block),
-        ),
-        (
-            jax.ShapeDtypeStruct(up_weight.shape, low),
-            pl.BlockSpec((1, model, block), late_block),
+            jax.ShapeDtypeStruct((2,) + up_weight.shape, low),
+            pl.BlockSpec((2, 1, model, block), late_block),
         ),
         fixed((halves, model, half_width), low),
         fixed((halves, model, 128), low),
@@ -1920,16 +2125,15 @@
         mixed, mixer_weight, lead_column, vectors, input_weight, 1
     )
     units = HEAD_SIZE * pairs
-    joint = exchange(projected.reshape(units, 3, tokens, 128), 3)
-    steps = 8
-    attended_unit, attended_wide, totals = attention_forward(joint, tag_row, crop_column, steps)
-    attended = exchange(attended_unit, 4)[None]
+    joint, attended, attended_wide, totals = attend_all(
+        projected.reshape(units, 3, tokens, 128), tag_row, crop_column, 3
+    )
+    attended = attended[None]
     (
         predicted,
         middle_grad,
         out_grads,
-        grad_up,
-        grad_down,
+        grad_feed,
         grad_proj,
         grad_out,
         grad_up_bias,
@@ -1946,11 +2150,17 @@
         masked,
         keep_mask,
     )
-    unit_grads = exchange(out_grads.reshape(units, tokens, 128), 5)
-    joint_grads = attention_backward(
-        joint, tag_row, crop_column, unit_grads, attended_wide, totals, steps
-    )
-    stacked = exchange(joint_grads, 6)[None]
+    stacked, feed_sums = attend_back(
+        joint,
+        tag_row,
+        crop_column,
+        attended_wide,
+        totals,
+        out_grads.reshape(units, tokens, 128),
+        grad_feed,
+        4,
+    )
+    stacked = stacked[None]
     grad_input, grad_mixer, mixed_grads, first_vectors = go_back(
         stacked,
         input_weight,
@@ -2018,7 +2228,7 @@
         ]
     ).astype(low)
     sums, predicted, cut_grads = reduce_all(
-        [grad_up, grad_down, grad_proj, grad_input, grad_mixer, grad_values, tail],
+        [grad_proj, grad_input, grad_mixer, grad_values, tail],
         predicted.reshape(HEAD_SIZE, 2, slot_width, 128),
         cut_grads,
         2,
@@ -2032,8 +2242,8 @@
         place[0] = begin + width
         return sums[:, begin : begin + width]
 
-    out_up = take(full_half)
-    out_down = take(full_half).T
+    out_up = feed_sums[:, :full_half]
+    out_down = feed_sums[:, full_half:].T
     out_proj = take(half_width).T
     out_input = jnp.stack([take(half_width) for _ in range(3)])
     out_mixer = take(half_width).T

time: 590 us -> 555 us (0.941)
  Pallas kernels: 472 us -> 439 us
    pallas_call x1, Pallas kernels: 153 us -> 81.7 us  [reduce_all(): pl.pallas_call(partial(reduce_kernel, chunks, count), out_shape=[jax.Shap...]
    pallas_call x6 -> x2, Pallas kernels: 129 us -> 166 us  [the longest x1 112 us: attend_back(): pl.pallas_call(attend_back_kernel, out_shape=[jax.ShapeDtypeStruct(joint....]
    unnamed x140 -> x146, local copies, waits for them, and re-layouts: 16.1 us -> 13.6 us
where the time goes in v2:
time: 555 us; the launch traced here: 550 us
  Pallas kernels  439 us (79%)
  local copies, waits for them, and re-layouts  56.6 us (10%)
  matrix products  17.6 us (3%)
  between operations  15.5 us (3%)
  other arithmetic  10.2 us (2%)
  starting transfers between devices  10.1 us (2%)
    pallas_call x1, Pallas kernels, gather_all(): pl.pallas_call(partial(gather_kernel, items, count), out_shape=shapes, in...  116 us
    pallas_call x1, Pallas kernels, attend_back(): pl.pallas_call(attend_back_kernel, out_shape=[jax.ShapeDtypeStruct(joint....  112 us
    pallas_call x1, Pallas kernels, reduce_all(): pl.pallas_call(partial(reduce_kernel, chunks, count), out_shape=[jax.Shap...  81.7 us
    pallas_call x1, Pallas kernels, attend_all(): pl.pallas_call(attend_kernel, out_shape=[jax.ShapeDtypeStruct(source.shap...  53.1 us
    pallas_call x1, Pallas kernels, feed(): pl.pallas_call(feed_kernel, grid=(2 * count,), out_shape=[shape for shape...  34.9 us
    unnamed x146, local copies, waits for them, and re-layouts  13.6 us
    pallas_call x1, Pallas kernels, go_back(): pl.pallas_call(return_kernel, grid=(kinds * halves,), out_shape=[jax.Shap...  13.3 us
  transfers between devices with their start and end apart: 6, of which 0 were waited for; matrix products, arithmetic and copies ran while one was open for 8% of the time, Pallas kernels for 33%

profile of v2, /device:TPU:0, one launch (start us, length us, event | category | flops | bytes accessed | tf_op | source)
XLA Modules:
  0.0 550.0 jit_solution(7564751437352782879)
XLA Ops:
  10.7 5.5 collective-permute-start.1
  24.1 2.0 fusion.1.field_ref
  26.2 2.8 shard_map.375.refs_8_
  29.0 115.8 %shard_map.376 = (bf16[2,4,2,2,16,128]{5,4,3,2,1,0:T(8,128)(2,1)}, bf16[2,4,2,2,64,128]{5,4,3,2,1,0:T(8,128)(2,1)}, bf16[2,4,2,2,64,512]{5,4,3,2,1,0:T(8,128)(2,...) custom-call(bf16[16,128]{1,0:T(8,128)(2,1)} %bitcast.243, ...), custom_call_target="tpu_custom_call" | custom-call | tf_op jit(solution)/shard_map/pallas_call | solution.py:790
  147.1 1.6 copy.270
  148.7 1.8 broadcast_select_fusion
  151.6 2.5 copy.269
  157.6 2.0 reshape.486.bias_ref
  160.8 3.5 multiply_reduce_fusion.1
  164.3 1.9 convolution_convert_fusion.1
  166.3 6.4 %shard_map.377 = (bf16[256,256]{1,0:T(8,128)(2,1)S(1)}, f32[16,48,256]{2,1,0:T(8,128)S(1)}, bf16[1024,256]{1,0:T(8,128)(2,1)S(1)}) custom-call(bf16[2,192,128]{2,1,0:T(8,128)(2,1)S(1)} %copy-done.21, f32[16,256]{1,0:T(8,128)S(1)} %broadcast_multiply_fusion.3.score_ref, bf16[1024,256]{1,0:T(8,128)(2,1)S(1)} %bitcast.183), custom_call_target="tpu_custom_call" | custom-call | tf_op jit(solution)/shard_map/pallas_call | solution.py:1019
  172.8 3.8 shard_map.378
  179.6 53.1 %shard_map.379 = (bf16[8,3,256,128]{3,2,1,0:T(8,128)(2,1)}, bf16[8,256,128]{2,1,0:T(8,128)(2,1)S(1)}, f32[2048,128]{1,0:T(8,128)S(1)}, f32[2,2048,1]{2,1,0:T(8,128)}) custom-call(bf16[8,3,256,128]{3,2,1,0:T(8,128)(2,1)} %bitcast.185, f32[1,2048]{1,0:T(1,128)S(1)} %get-tuple-element.246.tag_ref, f32[2048,1]{1,0:T(8,128)S(1)} %copy.278.crop_ref), custom_call_target="tpu_custom_call" | custom-call | tf_op jit(solution)/shard_map/pallas_call | solution.py:1217
  234.6 34.9 %shard_map.380 = (bf16[2,256,128]{2,1,0:T(8,128)(2,1)}, f32[256,1024]{1,0:T(8,128)}, bf16[1,8,256,128]{3,2,1,0:T(8,128)(2,1)}, bf16[2,2,1024,2048]{3,2,1,0:T(8,1...) custom-call(bf16[1,8,256,128]{3,2,1,0:T(8,128)(2,1)} %bitcast.186, ...), custom_call_target="tpu_custom_call" | custom-call | tf_op jit(solution)/shard_map/pallas_call | solution.py:1829
  269.5 112.5 %shard_map.381 = (bf16[8,3,256,128]{3,2,1,0:T(8,128)(2,1)}, f32[64,4096]{1,0:T(8,128)}) custom-call(bf16[8,3,256,128]{3,2,1,0:T(8,128)(2,1)} %get-tuple-element.74.joint, f32[1,2048]{1,0:T(1,128)} %copy-done.22, f32[2048,1]{1,0:T(8,128)} %copy-done.2, f32[2048,128]{1,0:T(8,128)} %copy-done.12, f32[2,2048,1]{2,1,0:T(8,128)} %get-tuple-element.76.total_ref, ...), custom_call_target="tpu_custom_call" | custom-call | tf_op jit(solution)/shard_map/pallas_call | solution.py:1561
  382.1 13.3 %shard_map.382 = (bf16[3,2,1024,512]{3,2,1,0:T(8,128)(2,1)}, bf16[2,1024,512]{2,1,0:T(8,128)(2,1)}, bf16[1024,256]{1,0:T(8,128)(2,1)S(1)}, f32[4,1024]{1,0:T(4,128)S(1)}) custom-call(bf16[1,8,3,256,128]{4,3,2,1,0:T(8,128)(2,1)} %bitcast.208, bf16[3,2,1024,512]{3,2,1,0:T(8,128)(2,1)} %bitcast.177, bf16[256,1024]{1,0:T(8,128)(2,1)S(1)} %copy-done.18, ...), custom_call_target="tpu_custom_call" | custom-call | tf_op jit(solution)/shard_map/pallas_call | solution.py:1918
  395.4 8.5 %shard_map.383 = (f32[1024,256]{1,0:T(8,128)S(1)}, f32[16,256]{1,0:T(8,128)S(1)}, f32[2,192,128]{2,1,0:T(8,128)S(1)}) custom-call(bf16[256,256]{1,0:T(8,128)(2,1)S(1)} %get-tuple-element.84.patch_ref, f32[16,48,256]{2,1,0:T(8,128)S(1)} %copy-done.14, f32[16,256]{1,0:T(8,128)S(1)} %broadcast_multiply_fusion.3.score_ref, bf16[1024,256]{1,0:T(8,128)(2,1)S(1)} %bitcast.184, ...), custom_call_target="tpu_custom_call" | custom-call | tf_op jit(solution)/shard_map/pallas_call | solution.py:1085
  406.5 1.3 copy.285
  407.9 2.5 convolution_bitcast_fusion.1
  416.5 2.1 convolution_convert_fusion
  418.6 1.4 concatenate.55
  421.8 81.7 %shard_map.384 = (f32[64,3328]{1,0:T(8,128)}, bf16[4,128,128]{2,1,0:T(8,128)(2,1)}, f32[4,192,128]{2,1,0:T(8,128)}) custom-call(bf16[2,4,2,2,64,512]{5,4,3,2,1,0:T(8,128)(2,1)} %bitcast.206, bf16[6,4,2,2,64,512]{5,4,3,2,1,0:T(8,128)(2,1)} %bitcast.191, bf16[2,4,2,2,64,512]{5,4,3,2,1,0:T(8,128)(2,1)} %bitcast.207, bf16[4,2,2,64,1024]{4,3,2,1,0:T(8,128)(2,1)} %bitcast.190, ...), custom_call_target="tpu_custom_call" | custom-call | tf_op jit(solution)/shard_map/pallas_call | solution.py:879
  503.5 2.0 slice_bitcast_fusion.1
  506.3 1.4 fusion.39
  507.9 5.8 %shard_map.385 = f32[32,48,512]{2,1,0:T(8,128)} custom-call(f32[4,192,128]{2,1,0:T(8,128)} %get-tuple-element.96.grad_ref, s32[4,256]{1,0:T(4,128)} %bitcast.241, s32[4,256]{1,0:T(4,128)} %bitcast.239), custom_call_target="tpu_custom_call" | custom-call | tf_op jit(solution)/shard_map/pallas_call | solution.py:971
  513.7 4.6 convolution_bitcast_fusion
  519.4 2.0 copy.298
  522.4 4.5 collective-permute-start.3
  526.9 2.3 slice_bitcast_fusion
  532.8 1.4 slice.214
  539.2 1.6 fusion.2
  540.8 2.1 copy.303
  (276 shorter events, 46.0 us)
Async XLA Ops:
  7.2 13.8 %copy-start = (s32[4,8]{1,0:T(4,128)S(1)}, s32[4,8]{1,0:T(4,128)}, u32[]{:S(2)}) copy-start(s32[4,8]{1,0:T(4,128)} %param.29) | copy-start | bytes 388
  7.2 16.9 %copy-start.33 = (bf16[48,32,256]{2,1,0:T(8,128)(2,1)S(1)}, bf16[48,32,256]{2,1,0:T(8,128)(2,1)}, u32[]{:S(2)}) copy-start(bf16[48,32,256]{2,1,0:T(8,128)(2,1)} %param.24) | copy-start | bytes 2359300
  7.3 10.0 %copy-start.58 = (bf16[32]{0:T(256)(128)(2,1)S(1)}, bf16[32]{0:T(256)(128)(2,1)}, u32[]{:S(2)}) copy-start(bf16[32]{0:T(256)(128)(2,1)} %param.41) | copy-start | bytes 196
  7.3 10.1 %copy-start.59 = (bf16[32]{0:T(256)(128)(2,1)S(1)}, bf16[32]{0:T(256)(128)(2,1)}, u32[]{:S(2)}) copy-start(bf16[32]{0:T(256)(128)(2,1)} %param.42) | copy-start | bytes 196
  7.3 10.2 %copy-start.37 = (bf16[4,128,96]{1,2,0:T(8,128)(2,1)S(1)}, bf16[4,128,96]{1,2,0:T(8,128)(2,1)}, u32[]{:S(2)}) copy-start(bf16[4,128,96]{1,2,0:T(8,128)(2,1)} %param.47) | copy-start | bytes 294916
  7.3 10.4 %copy-start.46 = (s32[4,128]{1,0:T(4,128)S(1)}, s32[4,128]{1,0:T(4,128)}, u32[]{:S(2)}) copy-start(s32[4,128]{1,0:T(4,128)} %param.28) | copy-start | bytes 6148
  7.3 10.4 %copy-start.47 = (bf16[48,32]{0,1:T(8,128)(2,1)S(1)}, bf16[48,32]{0,1:T(8,128)(2,1)}, u32[]{:S(2)}) copy-start(bf16[48,32]{0,1:T(8,128)(2,1)} %param.31) | copy-start | bytes 9220
  7.3 13.9 %copy-start.51 = (bf16[8,4]{0,1:T(4,128)(2,1)S(1)}, bf16[8,4]{0,1:T(4,128)(2,1)}, u32[]{:S(2)}) copy-start(bf16[8,4]{0,1:T(4,128)(2,1)} %param.32) | copy-start | bytes 196
  7.4 14.1 %copy-start.52 = (bf16[32,4]{0,1:T(4,128)(2,1)S(1)}, bf16[32,4]{0,1:T(4,128)(2,1)}, u32[]{:S(2)}) copy-start(bf16[32,4]{0,1:T(4,128)(2,1)} %param.44) | copy-start | bytes 772
  7.4 15.0 %copy-start.41 = (bf16[64,96]{1,0:T(8,128)(2,1)S(1)}, bf16[64,96]{1,0:T(8,128)(2,1)}, u32[]{:S(2)}) copy-start(bf16[64,96]{1,0:T(8,128)(2,1)} %param.46) | copy-start | bytes 36868
  7.4 227.2 %all-gather.3.cloned.1.call-start = ((), (), s32[]{:S(2)}) async-start(), calls=%async_computation | async-start | bytes 8650752 | tf_op jit(solution)/shard_map/all_gather | solution.py:2026
  8.1 226.4 %all-gather.5.cloned.1.call-start = ((), (), s32[]{:S(2)}) async-start(), calls=%async_computation.1 | async-start | bytes 8650752 | tf_op jit(solution)/shard_map/all_gather | solution.py:2028
  10.7 13.4 %collective-permute-start.1 = (bf16[48,32,1]{0,1,2:T(8,128)(2,1)S(1)}, bf16[48,32,1]{0,1,2:T(8,128)(2,1)S(1)}, u32[]{:S(2)}, u32[]{:S(2)}) collective-permute-start(bf16[48,32,1]{0,1,2:T(8,128)(2,1)S(1)} %copy.310), channel_id=1, source_target_pairs={{2,0},{4,2},{6,4},{8,6},{10,8},{12,10},{14,12},{16,14},{18,16},{20... | collective-permute-start | bytes 9224 | tf_op jit(solution)/shard_map/ppermute | solution.py:1999
  16.7 7.4 %collective-permute-start = (bf16[48,32,1]{0,1,2:T(8,128)(2,1)S(1)}, bf16[48,32,1]{0,1,2:T(8,128)(2,1)S(1)}, u32[]{:S(2)}, u32[]{:S(2)}) collective-permute-start(bf16[48,32,1]{0,1,2:T(8,128)(2,1)S(1)} %copy.309), channel_id=1, source_target_pairs={{0,2},{2,4},{4,6},{6,8},{8,10},{10,12},{12,14},{14,16},{16,18},{18... | collective-permute-start | bytes 9224 | tf_op jit(solution)/shard_map/ppermute | solution.py:1998
  155.0 24.6 %copy-start.22 = (f32[1,2048]{1,0:T(1,128)}, f32[1,2048]{1,0:T(1,128)S(1)}, u32[]{:S(2)}) copy-start(f32[1,2048]{1,0:T(1,128)S(1)} %get-tuple-element.246.tag_ref) | copy-start | bytes 24580
  155.0 17.8 %slice-start = ((s8[6291456]{0:T(1024)(128)(4,1)}), s8[2097152]{0:T(1024)(128)(4,1)S(1)}, s32[]{:S(2)}) async-start(s8[6291456]{0:T(1024)(128)(4,1)} %bitcast.178), calls=%async_computation.2 | async-start | bytes 4194304
  155.4 24.2 %copy-start.2 = (f32[2048,1]{1,0:T(8,128)}, f32[2048,1]{1,0:T(8,128)S(1)}, u32[]{:S(2)}) copy-start(f32[2048,1]{1,0:T(8,128)S(1)} %copy.278.crop_ref) | copy-start | bytes 24580
  160.8 12.0 %slice-start.1 = ((s8[6291456]{0:T(1024)(128)(4,1)}), s8[4194304]{0:T(1024)(128)(4,1)S(1)}, s32[]{:S(2)}) async-start(s8[6291456]{0:T(1024)(128)(4,1)} %bitcast.178), calls=%async_computation.3 | async-start | bytes 8388608
  166.3 10.4 %copy-start.8 = (bf16[2,512,256]{2,1,0:T(8,128)(2,1)}, bf16[2,512,256]{2,1,0:T(8,128)(2,1)S(1)}, u32[]{:S(2)}) copy-start(bf16[2,512,256]{2,1,0:T(8,128)(2,1)S(1)} %convolution_convert_fusion.1) | copy-start | bytes 1572868
  269.5 112.5 %copy-start.5 = (f32[256,1024]{1,0:T(8,128)S(1)}, f32[256,1024]{1,0:T(8,128)}, u32[]{:S(2)}) copy-start(f32[256,1024]{1,0:T(8,128)} %copy-done.4) | copy-start | bytes 3145732
  269.5 112.5 %copy-start.7 = (bf16[1024,256]{1,0:T(8,128)(2,1)S(1)}, bf16[1024,256]{1,0:T(8,128)(2,1)}, u32[]{:S(2)}) copy-start(bf16[1024,256]{1,0:T(8,128)(2,1)} %copy-done.6) | copy-start | bytes 1572868
  269.5 112.5 %copy-start.11 = (f32[256,1024]{1,0:T(8,128)S(1)}, f32[256,1024]{1,0:T(8,128)}, u32[]{:S(2)}) copy-start(f32[256,1024]{1,0:T(8,128)} %get-tuple-element.81.middle_grad_ref) | copy-start | bytes 3145732
  269.5 112.5 %copy-start.16 = (f32[6,1024]{1,0:T(8,128)S(1)}, f32[6,1024]{1,0:T(8,128)}, u32[]{:S(2)}) copy-start(f32[6,1024]{1,0:T(8,128)} %copy-done.15) | copy-start | bytes 73732
  269.5 112.5 %copy-start.18 = (bf16[256,1024]{1,0:T(8,128)(2,1)S(1)}, bf16[256,1024]{1,0:T(8,128)(2,1)}, u32[]{:S(2)}) copy-start(bf16[256,1024]{1,0:T(8,128)(2,1)} %copy-done.17) | copy-start | bytes 1572868
  382.1 13.3 %copy-start.9 = (bf16[2,512,256]{2,1,0:T(8,128)(2,1)S(1)}, bf16[2,512,256]{2,1,0:T(8,128)(2,1)}, u32[]{:S(2)}) copy-start(bf16[2,512,256]{2,1,0:T(8,128)(2,1)} %copy-done.8) | copy-start | bytes 1572868
  382.1 13.3 %copy-start.14 = (f32[16,48,256]{2,1,0:T(8,128)S(1)}, f32[16,48,256]{2,1,0:T(8,128)}, u32[]{:S(2)}) copy-start(f32[16,48,256]{2,1,0:T(8,128)} %copy-done.13) | copy-start | bytes 2359300
  382.1 22.4 %copy-start.28 = (bf16[1024,256,1]{1,0,2:T(8,128)(2,1)S(1)}, bf16[1024,256,1]{1,0,2:T(8,128)(2,1)}, u32[]{:S(2)}) copy-start(bf16[1024,256,1]{1,0,2:T(8,128)(2,1)} %reshape.496) | copy-start | bytes 1572868
  521.5 17.7 %collective-permute-start.2 = (f32[48,32,1]{0,1,2:T(8,128)}, f32[48,32,1]{0,1,2:T(8,128)}, u32[]{:S(2)}, u32[]{:S(2)}) collective-permute-start(f32[48,32,1]{0,1,2:T(8,128)} %copy.298), channel_id=1, source_target_pairs={{0,2},{2,4},{4,6},{6,8},{8,10},{10,12},{12,14},{14,16},{16,18},{18... | collective-permute-start | bytes 18440 | tf_op jit(solution)/shard_map/ppermute | solution.py:2270
  522.4 14.7 %copy-start.36 = (bf16[4,128,128]{2,1,0:T(8,128)(2,1)S(1)}, bf16[4,128,128]{2,1,0:T(8,128)(2,1)}, u32[]{:S(2)}) copy-start(bf16[4,128,128]{2,1,0:T(8,128)(2,1)} %get-tuple-element.95) | copy-start | bytes 393220
  522.4 16.8 %copy-start.53 = (pred[256]{0:T(512)(128)(4,1)S(1)}, pred[256]{0:T(512)(128)(4,1)}, u32[]{:S(2)}) copy-start(pred[256]{0:T(512)(128)(4,1)} %get-tuple-element.257) | copy-start | bytes 772
  522.4 16.8 %copy-start.54 = (pred[256]{0:T(512)(128)(4,1)S(1)}, pred[256]{0:T(512)(128)(4,1)}, u32[]{:S(2)}) copy-start(pred[256]{0:T(512)(128)(4,1)} %get-tuple-element.258) | copy-start | bytes 772
  522.4 16.8 %collective-permute-start.3 = (f32[48,32,1]{0,1,2:T(8,128)}, f32[48,32,1]{0,1,2:T(8,128)S(1)}, u32[]{:S(2)}, u32[]{:S(2)}) collective-permute-start(f32[48,32,1]{0,1,2:T(8,128)} %copy.299), channel_id=1, source_target_pairs={{2,0},{4,2},{6,4},{8,6},{10,8},{12,10},{14,12},{16,14},{18,16},{20... | collective-permute-start | bytes 18440 | tf_op jit(solution)/shard_map/ppermute | solution.py:2271
  (36 other events, 177.2 us)
Sparse Core Ops, SparseCore 0:
  11.1 115.9 all-gather.2
  130.0 92.4 all-gather.4

commit v3 on v2

--- a/solution.py
+++ b/solution.py
@@ -810,15 +810,19 @@
 
 
 def reduce_kernel(chunks, count, *refs):
-    ins, value_in, grad_in = refs[:count], refs[count], refs[count + 1]
-    out, value_out, grad_out = refs[count + 2 : count + 5]
-    buffers, sems = refs[count + 5 : count + 11], refs[count + 11 : count + 18]
-    value_send, value_recv, grad_send, grad_recv = refs[count + 18 :]
+    ins = refs[:count]
+    value_in, grad_in, lat_ref, shift_ref = refs[count : count + 4]
+    out, value_out, pixel_out = refs[count + 4 : count + 7]
+    buffers, sems = refs[count + 7 : count + 13], refs[count + 13 : count + 20]
+    grad_out, field, edge, west_edge, east_edge = refs[count + 20 : count + 25]
+    value_send, value_recv, grad_send, grad_recv, edge_send, edge_recv = refs[count + 25 :]
     x, z, y, c = position()
     across, line = partners(x, z, y, c)
-    own = (z * 4 + y * 2 + c, x)
+    lon = z * 4 + y * 2 + c
+    own = (lon, x)
+    east, west = (lax.rem(lon + 1, 16), x), (lax.rem(lon + 15, 16), x)
     sources = [block_of(z, y, row) for row in range(4)]
-    meet(list(across.values()) + line, sources, own)
+    meet(list(across.values()) + line + [east, west], sources, own)
     letters = []
     for part in range(2):
         for side in range(2):
@@ -836,6 +840,100 @@
         post(*letter)
     total = len(chunks)
 
+    lat_count, var_count, lanes = field.shape
+    half = lanes // 2
+    column_count = pixel_out.shape[2]
+
+    def paste(row):
+        pltpu.make_async_copy(grad_in.at[0], grad_out.at[row], grad_recv.at[row]).wait()
+        lat = lat_ref[row : row + 1, :]
+        going_west = shift_ref[row : row + 1, :] < 0
+        lat_both = jnp.concatenate([lat, lat], axis=1)
+        both = []
+        for py in range(2):
+            k = 2 * py
+            grads = jnp.concatenate(
+                [
+                    grad_out[row, k * var_count : (k + 1) * var_count, :],
+                    grad_out[row, (k + 1) * var_count : (k + 2) * var_count, :],
+                ],
+                axis=1,
+            )
+            left = jnp.where(going_west, grads, 0.0)
+            both.append(jnp.concatenate([left, grads - left], axis=1))
+
+        def body(b, carry):
+            piece = jnp.where(lat_both == b, both[0], 0.0) + jnp.where(
+                lat_both == b - 1, both[1], 0.0
+            )
+            if row == 0:
+                field[b] = piece
+            else:
+                field[b] += piece
+            return carry
+
+        lax.fori_loop(0, lat_count, body, 0)
+
+    def thirds(values):
+        one = values.astype(low)
+        rest = values - one.astype(wide)
+        two = rest.astype(low)
+        return one, two, (rest - two.astype(wide)).astype(low)
+
+    def columns_of(shape, axis):
+        spot = lax.broadcasted_iota(jnp.int32, shape, axis)
+        side, spot = lax.div(spot, half), lax.rem(spot, half)
+        slots = half // 2
+        return 2 * lax.rem(spot, slots) + 2 * side + lax.div(spot, slots) - 1
+
+    def edges():
+        kind = lax.broadcasted_iota(jnp.int32, (8, lanes), 0)
+        wanted = columns_of((8, lanes), 1)
+        pick = jnp.where(
+            jnp.logical_or(
+                jnp.logical_and(kind == 0, wanted == -1),
+                jnp.logical_and(kind == 1, wanted == column_count),
+            ),
+            1.0,
+            0.0,
+        ).astype(low)
+        flat = field[...].reshape(lat_count * var_count, lanes)
+        one, two, three = thirds(flat)
+        edge[...] = dot(pick, one, 1, 1) + dot(pick, two, 1, 1) + dot(pick, three, 1, 1)
+        remote(edge, west_edge, edge_send.at[0], edge_recv.at[0], east).start()
+        remote(edge, east_edge, edge_send.at[1], edge_recv.at[1], west).start()
+
+    def pixels():
+        remote(edge, west_edge, edge_send.at[0], edge_recv.at[0], east).wait()
+        remote(edge, east_edge, edge_send.at[1], edge_recv.at[1], west).wait()
+        wanted = columns_of((lanes, column_count), 0)
+        column = lax.broadcasted_iota(jnp.int32, (lanes, column_count), 1)
+        place = jnp.where(wanted == column, 1.0, 0.0).astype(low)
+        kind = lax.broadcasted_iota(jnp.int32, (8, column_count), 0)
+        column = lax.broadcasted_iota(jnp.int32, (8, column_count), 1)
+        from_west = jnp.logical_and(kind == 1, column == 0)
+        from_east = jnp.logical_and(kind == 0, column == column_count - 1)
+        west_place = jnp.where(from_west, 1.0, 0.0).astype(low)
+        east_place = jnp.where(from_east, 1.0, 0.0).astype(low)
+        borders = None
+        for values, target in ((west_edge[...], west_place), (east_edge[...], east_place)):
+            for part in thirds(values):
+                piece = dot(part, target, 0, 0)
+                borders = piece if borders is None else borders + piece
+        pixel_out[...] = borders.reshape(pixel_out.shape)
+
+        def body(b, carry):
+            result = pixel_out[b]
+            for part in thirds(field[b]):
+                result = result + dot(part, place)
+            pixel_out[b] = result
+            return carry
+
+        lax.fori_loop(0, lat_count, body, 0)
+
+    extra = {3: lambda: paste(0), 4: lambda: paste(1), 5: lambda: paste(2), 6: lambda: paste(3)}
+    extra.update({7: edges, 10: pixels})
+
     def source_of(pair, color, side, core):
         index, lead, offset = chunks[2 * pair + color][side]
         source = ins[index] if lead is None else ins[index].at[lead]
@@ -849,16 +947,17 @@
         for back, stage in plan:
             if 0 <= step - back < total:
                 stage((step - back) // 2, (step - back) % 2)
+        if step in extra:
+            extra[step]()
     for k in range(total):
         finish(k // 2, k % 2)
     for letter in letters:
         settle(*letter)
     for row in range(4):
         pltpu.make_async_copy(value_in.at[0, 0], value_out.at[row], value_recv.at[row]).wait()
-        pltpu.make_async_copy(grad_in.at[0], grad_out.at[row], grad_recv.at[row]).wait()
-
-
-def reduce_all(items, values, grads, number):
+
+
+def reduce_all(items, values, grads, lat_lanes, shift_lanes, lat_count, number):
     chunks, views = [], []
     for index, item in enumerate(items):
         rows, columns = item.shape[-2:]
@@ -874,6 +973,11 @@
             for offset in range(0, columns, CHUNK):
                 chunks.append(((index, first, offset), (index, first + 1, offset)))
     rows = views[0].shape[-2]
+    var_count = grads.shape[1] // 4
+    lanes = 2 * lat_lanes.shape[1]
+    columns = lat_lanes.shape[1]
+    vmem = pl.BlockSpec(memory_space=pltpu.VMEM)
+    hbm = pl.BlockSpec(memory_space=pl.ANY)
     count, total = len(views), len(chunks)
     sem = pltpu.SemaphoreType.DMA
     return pl.pallas_call(
@@ -881,22 +985,28 @@
         out_shape=[
             jax.ShapeDtypeStruct((rows, total * CHUNK), wide),
             jax.ShapeDtypeStruct((4,) + values.shape[2:], values.dtype),
-            jax.ShapeDtypeStruct((4,) + grads.shape[1:], grads.dtype),
+            jax.ShapeDtypeStruct((lat_count, var_count, columns), wide),
         ],
-        in_specs=[pl.BlockSpec(memory_space=pl.ANY)] * (count + 2),
-        out_specs=[pl.BlockSpec(memory_space=pltpu.VMEM)]
-        + [pl.BlockSpec(memory_space=pl.ANY)] * 2,
+        in_specs=[hbm] * (count + 2) + [vmem] * 2,
+        out_specs=[vmem, hbm, vmem],
         scratch_shapes=reducer_scratch(total, rows)
         + [
+            pltpu.VMEM((4,) + grads.shape[1:], wide),
+            pltpu.VMEM((lat_count, var_count, lanes), wide),
+            pltpu.VMEM((8, lat_count * var_count), wide),
+            pltpu.VMEM((8, lat_count * var_count), wide),
+            pltpu.VMEM((8, lat_count * var_count), wide),
             sem((4,)),
             sem((4,)),
             sem((4,)),
             sem((4,)),
+            sem((2,)),
+            sem((2,)),
         ],
         compiler_params=pltpu.CompilerParams(
             collective_id=number, has_side_effects=True, vmem_limit_bytes=60 * 2**20
         ),
-    )(*views, values, grads)
+    )(*views, values, grads, lat_lanes, shift_lanes)
 
 
 def diagonal(var_count, columns):
@@ -935,45 +1045,6 @@
         patch_kernel,
         out_shape=jax.ShapeDtypeStruct((row_count, 4 * field.shape[1], lanes // 2), low),
     )(field, lat_lanes, shift_lanes)
-
-
-def paste_kernel(grad_ref, lat_ref, shift_ref, field_ref):
-    lat_count, var_count, _ = field_ref.shape
-    row_count, lanes = lat_ref.shape
-    field_ref[...] = jnp.zeros_like(field_ref)
-    for r in range(row_count):
-        lat = lat_ref[r : r + 1, :]
-        west = shift_ref[r : r + 1, :] < 0
-        lat_both = jnp.concatenate([lat, lat], axis=1)
-        both = []
-        for py in range(2):
-            k = 2 * py
-            grads = jnp.concatenate(
-                [
-                    grad_ref[r, k * var_count : (k + 1) * var_count, :],
-                    grad_ref[r, (k + 1) * var_count : (k + 2) * var_count, :],
-                ],
-                axis=1,
-            )
-            left = jnp.where(west, grads, 0.0)
-            both.append(jnp.concatenate([left, grads - left], axis=1))
-
-        def body(b, carry):
-            field_ref[b] += jnp.where(lat_both == b, both[0], 0.0) + jnp.where(
-                lat_both == b - 1, both[1], 0.0
-            )
-            return carry
-
-        lax.fori_loop(0, lat_count, body, 0)
-
-
-def paste_patches(grads, lat_lanes, shift_lanes, lat_count):
-    return pl.pallas_call(
-        paste_kernel,
-        out_shape=jax.ShapeDtypeStruct(
-            (lat_count, grads.shape[1] // 4, 2 * lat_lanes.shape[1]), wide
-        ),
-    )(grads, lat_lanes, shift_lanes)
 
 
 def mixer_forward_kernel(cut_ref, score_ref, value_ref, patch_ref, prob_ref, mixed_ref):
@@ -2227,10 +2298,13 @@
             for side in range(2)
         ]
     ).astype(low)
-    sums, predicted, cut_grads = reduce_all(
+    sums, predicted, pixel_grad = reduce_all(
         [grad_proj, grad_input, grad_mixer, grad_values, tail],
         predicted.reshape(HEAD_SIZE, 2, slot_width, 128),
         cut_grads,
+        lat_lanes,
+        shift_lanes,
+        lat_count,
         2,
     )
     predicted = predicted[:, :, :out_half]
@@ -2264,14 +2338,7 @@
     my_query = block_slice(query, head, head_half, 0)
     out_keys = (my_heads[:, :, None] * my_query[None]).reshape(block_rows, half_width)
 
-    field_grads = paste_patches(cut_grads, lat_lanes, shift_lanes, lat_count)
-    choose = (jnp.arange(column_count + 2)[:, None] - 1 == wanted[None, :]).astype(wide)
-    columns = jnp.einsum("avn,cn->vac", field_grads, choose, precision=highest)
-    from_west = lax.ppermute(columns[:, :, -1:], LON, up)
-    from_east = lax.ppermute(columns[:, :, :1], LON, down)
-    spot_at = jnp.arange(column_count)
-    pixel_grad = columns[:, :, 1:-1] + jnp.where(spot_at == 0, from_west, 0.0)
-    pixel_grad = pixel_grad + jnp.where(spot_at == column_count - 1, from_east, 0.0)
+    pixel_grad = jnp.transpose(pixel_grad, (1, 0, 2))
     return (
         predicted,
         pixel_grad,

time: 555 us -> 537 us (0.968)
  local copies, waits for them, and re-layouts: 56.6 us -> 50.8 us
    pallas_call x1 -> x0, Pallas kernels: 5.77 us -> none  [paste_patches(): pl.pallas_call(paste_kernel, out_shape=jax.ShapeDtypeStruct((lat_count, g...]
    unnamed x146 -> x142, local copies, waits for them, and re-layouts: 13.6 us -> 13.6 us
  transfers between devices with their start and end apart: 6 -> 4, of which waited for: 0 -> 0; matrix products, arithmetic and copies ran while one was open for 8% -> 6% of each run, Pallas kernels for 33% -> 35%
where the time goes in v3:
time: 537 us; the launch traced here: 529 us
  Pallas kernels  436 us (81%)
  local copies, waits for them, and re-layouts  50.8 us (9%)
  between operations  15.5 us (3%)
  matrix products  13.1 us (2%)
  other arithmetic  6.67 us (1%)
  starting transfers between devices  5.58 us (1%)
    pallas_call x1, Pallas kernels, gather_all(): pl.pallas_call(partial(gather_kernel, items, count), out_shape=shapes, in...  117 us
    pallas_call x1, Pallas kernels, attend_back(): pl.pallas_call(attend_back_kernel, out_shape=[jax.ShapeDtypeStruct(joint....  112 us
    pallas_call x1, Pallas kernels, reduce_all(): pl.pallas_call(partial(reduce_kernel, chunks, count), out_shape=[jax.Shap...  84.2 us
    pallas_call x1, Pallas kernels, attend_all(): pl.pallas_call(attend_kernel, out_shape=[jax.ShapeDtypeStruct(source.shap...  53.3 us
    pallas_call x1, Pallas kernels, feed(): pl.pallas_call(feed_kernel, grid=(2 * count,), out_shape=[shape for shape...  34.9 us
    unnamed x142, local copies, waits for them, and re-layouts  13.6 us
    pallas_call x1, Pallas kernels, go_back(): pl.pallas_call(return_kernel, grid=(kinds * halves,), out_shape=[jax.Shap...  13.3 us
    dot_general x6, matrix products, einsum(): return jnp.einsum(spec, left, right, preferred_element_type=wide)  11 us
  transfers between devices with their start and end apart: 4, of which 0 were waited for; matrix products, arithmetic and copies ran while one was open for 6% of the time, Pallas kernels for 35%

profile of v3, /device:TPU:0, one launch (start us, length us, event | category | flops | bytes accessed | tf_op | source)
XLA Modules:
  0.0 529.1 jit_solution(12346845864689187914)
XLA Ops:
  8.9 1.3 fusion.34
  10.7 5.5 %collective-permute-start.1 = (bf16[48,32,1]{0,1,2:T(8,128)(2,1)S(1)}, bf16[48,32,1]{0,1,2:T(8,128)(2,1)S(1)}, u32[]{:S(2)}, u32[]{:S(2)}) collective-permute-start(bf16[48,32,1]{0,1,2:T(8,128)(2,1)S(1)} %copy.304), channel_id=1, source_target_pairs={{2,0},{4,2},{6,4},{8,6},{10,8},{12,10},{14,12},{16,14},{18,16},{20... | collective-permute-start | bytes 9224 | tf_op jit(solution)/shard_map/ppermute | solution.py:2070
  23.0 2.0 fusion.1.field_ref
  25.0 2.8 shard_map.375.refs_8_
  27.8 116.5 %shard_map.376 = (bf16[2,4,2,2,16,128]{5,4,3,2,1,0:T(8,128)(2,1)}, bf16[2,4,2,2,64,128]{5,4,3,2,1,0:T(8,128)(2,1)}, bf16[2,4,2,2,64,512]{5,4,3,2,1,0:T(8,128)(2,...) custom-call(bf16[16,128]{1,0:T(8,128)(2,1)} %bitcast.236, ...), custom_call_target="tpu_custom_call" | custom-call | tf_op jit(solution)/shard_map/pallas_call | solution.py:790
  144.4 1.1 reshape_reshape.10
  146.7 1.6 copy.266
  148.3 1.8 broadcast_select_fusion
  150.1 1.1 reshape.491
  151.2 2.5 copy.265
  156.0 1.2 copy.276
  157.2 2.0 reshape.481.bias_ref
  160.4 3.5 multiply_reduce_fusion.1
  164.0 1.9 convolution_convert_fusion.1
  166.0 6.4 %shard_map.377 = (bf16[256,256]{1,0:T(8,128)(2,1)S(1)}, f32[16,48,256]{2,1,0:T(8,128)S(1)}, bf16[1024,256]{1,0:T(8,128)(2,1)S(1)}) custom-call(bf16[2,192,128]{2,1,0:T(8,128)(2,1)S(1)} %copy-done.21, f32[16,256]{1,0:T(8,128)S(1)} %broadcast_multiply_fusion.3.score_ref, bf16[1024,256]{1,0:T(8,128)(2,1)S(1)} %bitcast.176), custom_call_target="tpu_custom_call" | custom-call | tf_op jit(solution)/shard_map/pallas_call | solution.py:1090
  172.5 3.8 shard_map.378
  177.3 1.1 copy-done.10
  179.3 53.3 %shard_map.379 = (bf16[8,3,256,128]{3,2,1,0:T(8,128)(2,1)}, bf16[8,256,128]{2,1,0:T(8,128)(2,1)S(1)}, f32[2048,128]{1,0:T(8,128)S(1)}, f32[2,2048,1]{2,1,0:T(8,128)}) custom-call(bf16[8,3,256,128]{3,2,1,0:T(8,128)(2,1)} %bitcast.178, f32[1,2048]{1,0:T(1,128)S(1)} %get-tuple-element.244.tag_ref, f32[2048,1]{1,0:T(8,128)S(1)} %copy.274.crop_ref), custom_call_target="tpu_custom_call" | custom-call | tf_op jit(solution)/shard_map/pallas_call | solution.py:1288
  234.4 34.9 %shard_map.380 = (bf16[2,256,128]{2,1,0:T(8,128)(2,1)}, f32[256,1024]{1,0:T(8,128)}, bf16[1,8,256,128]{3,2,1,0:T(8,128)(2,1)}, bf16[2,2,1024,2048]{3,2,1,0:T(8,1...) custom-call(bf16[1,8,256,128]{3,2,1,0:T(8,128)(2,1)} %bitcast.179, ...), custom_call_target="tpu_custom_call" | custom-call | tf_op jit(solution)/shard_map/pallas_call | solution.py:1900
  269.3 112.4 %shard_map.381 = (bf16[8,3,256,128]{3,2,1,0:T(8,128)(2,1)}, f32[64,4096]{1,0:T(8,128)}) custom-call(bf16[8,3,256,128]{3,2,1,0:T(8,128)(2,1)} %get-tuple-element.74.joint, f32[1,2048]{1,0:T(1,128)} %copy-done.22, f32[2048,1]{1,0:T(8,128)} %copy-done.2, f32[2048,128]{1,0:T(8,128)} %copy-done.12, f32[2,2048,1]{2,1,0:T(8,128)} %get-tuple-element.76.total_ref, ...), custom_call_target="tpu_custom_call" | custom-call | tf_op jit(solution)/shard_map/pallas_call | solution.py:1632
  381.8 13.3 %shard_map.382 = (bf16[3,2,1024,512]{3,2,1,0:T(8,128)(2,1)}, bf16[2,1024,512]{2,1,0:T(8,128)(2,1)}, bf16[1024,256]{1,0:T(8,128)(2,1)S(1)}, f32[4,1024]{1,0:T(4,128)S(1)}) custom-call(bf16[1,8,3,256,128]{4,3,2,1,0:T(8,128)(2,1)} %bitcast.201, bf16[3,2,1024,512]{3,2,1,0:T(8,128)(2,1)} %bitcast.170, bf16[256,1024]{1,0:T(8,128)(2,1)S(1)} %copy-done.18, ...), custom_call_target="tpu_custom_call" | custom-call | tf_op jit(solution)/shard_map/pallas_call | solution.py:1989
  395.1 8.5 %shard_map.383 = (f32[1024,256]{1,0:T(8,128)S(1)}, f32[16,256]{1,0:T(8,128)S(1)}, f32[2,192,128]{2,1,0:T(8,128)S(1)}) custom-call(bf16[256,256]{1,0:T(8,128)(2,1)S(1)} %get-tuple-element.84.patch_ref, f32[16,48,256]{2,1,0:T(8,128)S(1)} %copy-done.14, f32[16,256]{1,0:T(8,128)S(1)} %broadcast_multiply_fusion.3.score_ref, bf16[1024,256]{1,0:T(8,128)(2,1)S(1)} %bitcast.177, ...), custom_call_target="tpu_custom_call" | custom-call | tf_op jit(solution)/shard_map/pallas_call | solution.py:1156
  406.3 1.3 copy.281
  407.6 2.5 convolution_bitcast_fusion
  416.2 2.1 convolution_convert_fusion
  418.3 1.4 concatenate.55
  420.4 1.1 pad_maximum_fusion.refs_4_
  421.5 84.2 %shard_map.384 = (f32[64,3328]{1,0:T(8,128)}, bf16[4,128,128]{2,1,0:T(8,128)(2,1)}, f32[32,48,256]{2,1,0:T(8,128)}) custom-call(bf16[2,4,2,2,64,512]{5,4,3,2,1,0:T(8,128)(2,1)} %bitcast.199, bf16[6,4,2,2,64,512]{5,4,3,2,1,0:T(8,128)(2,1)} %bitcast.184, bf16[2,4,2,2,64,512]{5,4,3,2,1,0:T(8,128)(2,1)} %bitcast.200, bf16[4,2,2,64,1024]{4,3,2,1,0:T(8,128)(2,1)} %bitcast.183, ...), custom_call_target="tpu_custom_call" | custom-call | tf_op jit(solution)/shard_map/pallas_call | solution.py:983
  505.7 2.1 slice_bitcast_fusion.1
  510.9 1.4 slice.202
  515.4 2.1 copy.297
  519.5 1.0 slice_bitcast_fusion
  (260 shorter events, 35.9 us)
Async XLA Ops:
  7.2 12.7 %copy-start = (s32[4,8]{1,0:T(4,128)S(1)}, s32[4,8]{1,0:T(4,128)}, u32[]{:S(2)}) copy-start(s32[4,8]{1,0:T(4,128)} %param.29) | copy-start | bytes 388
  7.2 15.8 %copy-start.35 = (bf16[48,32,256]{2,1,0:T(8,128)(2,1)S(1)}, bf16[48,32,256]{2,1,0:T(8,128)(2,1)}, u32[]{:S(2)}) copy-start(bf16[48,32,256]{2,1,0:T(8,128)(2,1)} %param.24) | copy-start | bytes 2359300
  7.3 9.6 %copy-start.39 = (bf16[48,4,32]{0,2,1:T(8,128)(2,1)S(1)}, bf16[48,4,32]{0,2,1:T(8,128)(2,1)}, u32[]{:S(2)}) copy-start(bf16[48,4,32]{0,2,1:T(8,128)(2,1)} %param.30) | copy-start | bytes 36868
  7.3 9.8 %copy-start.53 = (bf16[2,32]{1,0:T(2,128)(2,1)S(1)}, bf16[2,32]{1,0:T(2,128)(2,1)}, u32[]{:S(2)}) copy-start(bf16[2,32]{1,0:T(2,128)(2,1)} %param.36) | copy-start | bytes 388
  7.3 9.9 %copy-start.54 = (bf16[32]{0:T(256)(128)(2,1)S(1)}, bf16[32]{0:T(256)(128)(2,1)}, u32[]{:S(2)}) copy-start(bf16[32]{0:T(256)(128)(2,1)} %param.37) | copy-start | bytes 196
  7.3 9.9 %copy-start.55 = (bf16[32]{0:T(256)(128)(2,1)S(1)}, bf16[32]{0:T(256)(128)(2,1)}, u32[]{:S(2)}) copy-start(bf16[32]{0:T(256)(128)(2,1)} %param.38) | copy-start | bytes 196
  7.3 10.0 %copy-start.56 = (bf16[32]{0:T(256)(128)(2,1)S(1)}, bf16[32]{0:T(256)(128)(2,1)}, u32[]{:S(2)}) copy-start(bf16[32]{0:T(256)(128)(2,1)} %param.41) | copy-start | bytes 196
  7.3 10.1 %copy-start.57 = (bf16[32]{0:T(256)(128)(2,1)S(1)}, bf16[32]{0:T(256)(128)(2,1)}, u32[]{:S(2)}) copy-start(bf16[32]{0:T(256)(128)(2,1)} %param.42) | copy-start | bytes 196
  7.3 10.2 %copy-start.38 = (bf16[4,128,96]{1,2,0:T(8,128)(2,1)S(1)}, bf16[4,128,96]{1,2,0:T(8,128)(2,1)}, u32[]{:S(2)}) copy-start(bf16[4,128,96]{1,2,0:T(8,128)(2,1)} %param.47) | copy-start | bytes 294916
  7.3 10.4 %copy-start.46 = (s32[4,128]{1,0:T(4,128)S(1)}, s32[4,128]{1,0:T(4,128)}, u32[]{:S(2)}) copy-start(s32[4,128]{1,0:T(4,128)} %param.28) | copy-start | bytes 6148
  7.3 10.4 %copy-start.47 = (bf16[48,32]{0,1:T(8,128)(2,1)S(1)}, bf16[48,32]{0,1:T(8,128)(2,1)}, u32[]{:S(2)}) copy-start(bf16[48,32]{0,1:T(8,128)(2,1)} %param.31) | copy-start | bytes 9220
  7.3 12.8 %copy-start.51 = (bf16[8,4]{0,1:T(4,128)(2,1)S(1)}, bf16[8,4]{0,1:T(4,128)(2,1)}, u32[]{:S(2)}) copy-start(bf16[8,4]{0,1:T(4,128)(2,1)} %param.32) | copy-start | bytes 196
  7.4 12.9 %copy-start.52 = (bf16[32,4]{0,1:T(4,128)(2,1)S(1)}, bf16[32,4]{0,1:T(4,128)(2,1)}, u32[]{:S(2)}) copy-start(bf16[32,4]{0,1:T(4,128)(2,1)} %param.44) | copy-start | bytes 772
  7.4 13.8 %copy-start.42 = (bf16[64,96]{1,0:T(8,128)(2,1)S(1)}, bf16[64,96]{1,0:T(8,128)(2,1)}, u32[]{:S(2)}) copy-start(bf16[64,96]{1,0:T(8,128)(2,1)} %param.46) | copy-start | bytes 36868
  7.4 227.0 %all-gather.3.cloned.1.call-start = ((), (), s32[]{:S(2)}) async-start(), calls=%async_computation | async-start | bytes 8650752 | tf_op jit(solution)/shard_map/all_gather | solution.py:2097
  8.1 226.3 %all-gather.5.cloned.1.call-start = ((), (), s32[]{:S(2)}) async-start(), calls=%async_computation.1 | async-start | bytes 8650752 | tf_op jit(solution)/shard_map/all_gather | solution.py:2099
  10.7 12.3 %collective-permute-start.1 = (bf16[48,32,1]{0,1,2:T(8,128)(2,1)S(1)}, bf16[48,32,1]{0,1,2:T(8,128)(2,1)S(1)}, u32[]{:S(2)}, u32[]{:S(2)}) collective-permute-start(bf16[48,32,1]{0,1,2:T(8,128)(2,1)S(1)} %copy.304), channel_id=1, source_target_pairs={{2,0},{4,2},{6,4},{8,6},{10,8},{12,10},{14,12},{16,14},{18,16},{20... | collective-permute-start | bytes 9224 | tf_op jit(solution)/shard_map/ppermute | solution.py:2070
  16.7 6.3 %collective-permute-start = (bf16[48,32,1]{0,1,2:T(8,128)(2,1)S(1)}, bf16[48,32,1]{0,1,2:T(8,128)(2,1)S(1)}, u32[]{:S(2)}, u32[]{:S(2)}) collective-permute-start(bf16[48,32,1]{0,1,2:T(8,128)(2,1)S(1)} %copy.303), channel_id=1, source_target_pairs={{0,2},{2,4},{4,6},{6,8},{8,10},{10,12},{12,14},{14,16},{16,18},{18... | collective-permute-start | bytes 9224 | tf_op jit(solution)/shard_map/ppermute | solution.py:2069
  154.7 24.6 %copy-start.22 = (f32[1,2048]{1,0:T(1,128)}, f32[1,2048]{1,0:T(1,128)S(1)}, u32[]{:S(2)}) copy-start(f32[1,2048]{1,0:T(1,128)S(1)} %get-tuple-element.244.tag_ref) | copy-start | bytes 24580
  154.7 17.8 %slice-start = ((s8[6291456]{0:T(1024)(128)(4,1)}), s8[2097152]{0:T(1024)(128)(4,1)S(1)}, s32[]{:S(2)}) async-start(s8[6291456]{0:T(1024)(128)(4,1)} %bitcast.171), calls=%async_computation.2 | async-start | bytes 4194304
  155.1 24.2 %copy-start.2 = (f32[2048,1]{1,0:T(8,128)}, f32[2048,1]{1,0:T(8,128)S(1)}, u32[]{:S(2)}) copy-start(f32[2048,1]{1,0:T(8,128)S(1)} %copy.274.crop_ref) | copy-start | bytes 24580
  160.4 12.1 %slice-start.1 = ((s8[6291456]{0:T(1024)(128)(4,1)}), s8[4194304]{0:T(1024)(128)(4,1)S(1)}, s32[]{:S(2)}) async-start(s8[6291456]{0:T(1024)(128)(4,1)} %bitcast.171), calls=%async_computation.3 | async-start | bytes 8388608
  166.0 10.4 %copy-start.8 = (bf16[2,512,256]{2,1,0:T(8,128)(2,1)}, bf16[2,512,256]{2,1,0:T(8,128)(2,1)S(1)}, u32[]{:S(2)}) copy-start(bf16[2,512,256]{2,1,0:T(8,128)(2,1)S(1)} %convolution_convert_fusion.1) | copy-start | bytes 1572868
  269.3 112.5 %copy-start.5 = (f32[256,1024]{1,0:T(8,128)S(1)}, f32[256,1024]{1,0:T(8,128)}, u32[]{:S(2)}) copy-start(f32[256,1024]{1,0:T(8,128)} %copy-done.4) | copy-start | bytes 3145732
  269.3 112.5 %copy-start.7 = (bf16[1024,256]{1,0:T(8,128)(2,1)S(1)}, bf16[1024,256]{1,0:T(8,128)(2,1)}, u32[]{:S(2)}) copy-start(bf16[1024,256]{1,0:T(8,128)(2,1)} %copy-done.6) | copy-start | bytes 1572868
  269.3 112.5 %copy-start.11 = (f32[256,1024]{1,0:T(8,128)S(1)}, f32[256,1024]{1,0:T(8,128)}, u32[]{:S(2)}) copy-start(f32[256,1024]{1,0:T(8,128)} %get-tuple-element.81.middle_grad_ref) | copy-start | bytes 3145732
  269.3 112.5 %copy-start.16 = (f32[6,1024]{1,0:T(8,128)S(1)}, f32[6,1024]{1,0:T(8,128)}, u32[]{:S(2)}) copy-start(f32[6,1024]{1,0:T(8,128)} %copy-done.15) | copy-start | bytes 73732
  269.3 112.5 %copy-start.18 = (bf16[256,1024]{1,0:T(8,128)(2,1)S(1)}, bf16[256,1024]{1,0:T(8,128)(2,1)}, u32[]{:S(2)}) copy-start(bf16[256,1024]{1,0:T(8,128)(2,1)} %copy-done.17) | copy-start | bytes 1572868
  381.8 13.3 %copy-start.9 = (bf16[2,512,256]{2,1,0:T(8,128)(2,1)S(1)}, bf16[2,512,256]{2,1,0:T(8,128)(2,1)}, u32[]{:S(2)}) copy-start(bf16[2,512,256]{2,1,0:T(8,128)(2,1)} %copy-done.8) | copy-start | bytes 1572868
  381.8 13.3 %copy-start.14 = (f32[16,48,256]{2,1,0:T(8,128)S(1)}, f32[16,48,256]{2,1,0:T(8,128)}, u32[]{:S(2)}) copy-start(f32[16,48,256]{2,1,0:T(8,128)} %copy-done.13) | copy-start | bytes 2359300
  381.8 22.5 %copy-start.28 = (bf16[1024,256,1]{1,0,2:T(8,128)(2,1)S(1)}, bf16[1024,256,1]{1,0,2:T(8,128)(2,1)}, u32[]{:S(2)}) copy-start(bf16[1024,256,1]{1,0,2:T(8,128)(2,1)} %reshape.491) | copy-start | bytes 1572868
  505.7 9.7 %copy-start.29 = (f32[32,48,256]{2,1,0:T(8,128)S(1)}, f32[32,48,256]{2,1,0:T(8,128)}, u32[]{:S(2)}) copy-start(f32[32,48,256]{2,1,0:T(8,128)} %get-tuple-element.96) | copy-start | bytes 4718596
  (32 other events, 133.7 us)
Sparse Core Ops, SparseCore 0:
  11.1 116.4 all-gather.2
  130.4 91.6 all-gather.4

commit v4 on v3

--- a/solution.py
+++ b/solution.py
@@ -672,141 +672,67 @@
     )
 
 
-def gather_kernel(items, count, *refs):
-    ins, outs = refs[:count], refs[count + 2 : 2 * count + 2]
-    patch_in, grad_in = refs[count : count + 2]
-    patch_out, grad_out = refs[2 * count + 2 : 2 * count + 4]
-    own_sem, line_send, line_recv, hop_send, hop_recv, post_send, post_recv = refs[
-        2 * count + 4 :
-    ]
+def gatherer(views, sems):
+    own_sem, line_send, line_recv, hop_send, hop_recv = sems
     x, z, y, c = position()
     across, line = partners(x, z, y, c)
-    own = (z * 4 + y * 2 + c, x)
-    sources = [sector_of(z, y, c, x, part, side) for part in range(2) for side in range(2)]
-    meet(list(across.values()) + line, sources, own)
-    letters = []
-    for part in range(2):
-        row = 2 * x + part
-        letters.append(
-            (patch_in.at[part], patch_out.at[c], post_send.at[part], post_recv.at[c])
-            + (block_of(z, y, row), own)
+
+    def keep(number):
+        source, target, span, _ = views(number)
+        return pltpu.make_async_copy(source, target.at[x, z, y, c, span], own_sem.at[number])
+
+    def along(number, d):
+        source, target, span, _ = views(number)
+        return remote(
+            source,
+            target.at[x, z, y, c, span],
+            line_send.at[number, d],
+            line_recv.at[number, d],
+            line[d],
         )
-    for row in range(4):
-        letters.append(
-            (grad_in.at[row], grad_out.at[x, c], post_send.at[2 + row])
-            + (post_recv.at[2 + 2 * x + c], block_of(z, y, row), own)
+
+    def hop(number, k):
+        _, target, span, color = views(number)
+        if k == 0:
+            part, axis = target.at[x, :, y, c, span], "yx"[color]
+        elif k == 1 and color == 0:
+            part, axis = target.at[x, :, :, c, span], "x"
+        elif k == 1:
+            part, axis = target.at[:, :, y, c, span], "y"
+        else:
+            part, axis = target.at[:, :, :, c, span], "c"
+        return remote(
+            part, part, hop_send.at[number, k], hop_recv.at[number, k], across[axis]
         )
-    for letter in letters:
-        post(*letter)
-
-    def views(item):
-        index, lead, first, rows, _ = item
-        source, target = ins[index], outs[index]
-        if lead is not None:
-            source, target = source.at[lead], target.at[lead]
-        return source.at[pl.ds(first, rows)], target, pl.ds(first, rows)
-
-    def copies(number):
-        item = items[number]
-        source, target, span = views(item)
-        own = target.at[x, z, y, c, span]
-        keep = pltpu.make_async_copy(source, own, own_sem.at[number])
-        along = [
-            remote(source, own, line_send.at[number, d], line_recv.at[number, d], line[d])
-            for d in range(3)
-        ]
-        quarter = target.at[x, :, y, c, span]
-        if item[4] == 0:
-            half, order = target.at[x, :, :, c, span], ("y", "x")
-        else:
-            half, order = target.at[:, :, y, c, span], ("x", "y")
-        full = target.at[:, :, :, c, span]
-        hops = [
-            remote(part, part, hop_send.at[number, k], hop_recv.at[number, k], across[axis])
-            for k, (part, axis) in enumerate(
-                ((quarter, order[0]), (half, order[1]), (full, "c"))
-            )
-        ]
-        return keep, along, hops
-
-    plan = [copies(number) for number in range(len(items))]
-    total = len(items)
-    for step in range(total + 8):
-        if step < total:
-            keep, along, _ = plan[step]
-            keep.start()
-            for one in along:
-                one.start()
-        if 0 <= step - 2 < total:
-            keep, along, hops = plan[step - 2]
-            keep.wait()
-            for one in along:
-                one.wait_recv()
-            hops[0].start()
-        if 0 <= step - 4 < total:
-            hops = plan[step - 4][2]
-            hops[0].wait_recv()
-            hops[1].start()
-        if 0 <= step - 6 < total:
-            hops = plan[step - 6][2]
-            hops[1].wait_recv()
-            hops[2].start()
-        if 0 <= step - 8 < total:
-            plan[step - 8][2][2].wait_recv()
-    for _, along, hops in plan:
-        for one in along + hops:
-            one.wait_send()
-    for letter in letters:
-        settle(*letter)
-    for part in range(2):
-        pltpu.make_async_copy(patch_in.at[part], patch_out.at[part], post_recv.at[part]).wait()
-    for side in range(2):
-        for part in range(2):
-            pltpu.make_async_copy(
-                grad_in.at[0], grad_out.at[side, part], post_recv.at[2 + 2 * side + part]
-            ).wait()
-
-
-def gather_all(arrays, patches, grads, number):
-    items = []
-    for index, array in enumerate(arrays):
-        leads = range(array.shape[0]) if array.ndim == 3 else (None,)
-        rows = array.shape[-2]
-        for lead in leads:
-            if rows >= 64:
-                half = rows // 2
-                items.append((index, lead, 0, half, 0))
-                items.append((index, lead, half, half, 1))
-            else:
-                items.append((index, lead, 0, rows, 0))
-    count = len(arrays)
-    shapes = [
-        jax.ShapeDtypeStruct(a.shape[:-2] + (2, 4, 2, 2) + a.shape[-2:], a.dtype) for a in arrays
-    ] + [
-        jax.ShapeDtypeStruct(patches.shape, low),
-        jax.ShapeDtypeStruct((2, 2) + grads.shape[1:], low),
-    ]
-    sem = pltpu.SemaphoreType.DMA
-    gathered = pl.pallas_call(
-        partial(gather_kernel, items, count),
-        out_shape=shapes,
-        in_specs=[pl.BlockSpec(memory_space=pl.ANY)] * (count + 2),
-        out_specs=[pl.BlockSpec(memory_space=pl.ANY)] * (count + 2),
-        scratch_shapes=[
-            sem((len(items),)),
-            sem((len(items), 3)),
-            sem((len(items), 3)),
-            sem((len(items), 3)),
-            sem((len(items), 3)),
-            sem((6,)),
-            sem((6,)),
-        ],
-        compiler_params=pltpu.CompilerParams(collective_id=number, has_side_effects=True),
-    )(*arrays, patches, grads)
-    return [
-        g.reshape(a.shape[:-2] + (2, 16 * a.shape[-2], a.shape[-1]))
-        for g, a in zip(gathered, arrays)
-    ] + list(gathered[count:])
+
+    def begin(number):
+        keep(number).start()
+        for d in range(3):
+            along(number, d).start()
+
+    def spread(number):
+        keep(number).wait()
+        for d in range(3):
+            along(number, d).wait_recv()
+        hop(number, 0).start()
+
+    def widen(number):
+        hop(number, 0).wait_recv()
+        hop(number, 1).start()
+
+    def pair_up(number):
+        hop(number, 1).wait_recv()
+        hop(number, 2).start()
+
+    def close(number):
+        hop(number, 2).wait_recv()
+
+    def finish(number):
+        for k in range(3):
+            along(number, k).wait_send()
+            hop(number, k).wait_send()
+
+    return (begin, spread, widen, pair_up, close), finish
 
 
 def reduce_kernel(chunks, count, *refs):
@@ -1047,57 +973,6 @@
     )(field, lat_lanes, shift_lanes)
 
 
-def mixer_forward_kernel(cut_ref, score_ref, value_ref, patch_ref, prob_ref, mixed_ref):
-    head_count, var_count, tokens = prob_ref.shape
-    parts, taps, width = cut_ref.shape
-    for part in range(parts):
-        patch_ref[:taps, part * width : (part + 1) * width] = cut_ref[part]
-    patch_ref[taps : taps + var_count, :] = jnp.ones((var_count, tokens), low)
-    rest = patch_ref.shape[0] - 5 * var_count
-    patch_ref[5 * var_count :, :] = jnp.zeros((rest, tokens), low)
-    mask = diagonal(var_count, patch_ref.shape[0])
-
-    def head_step(h, carry):
-        spread = jnp.where(mask, score_ref[pl.ds(h, 1), :], 0.0)
-        upper = spread.astype(low)
-        lower = (spread - upper.astype(wide)).astype(low)
-        patch = patch_ref[...]
-        scores = dot(upper, patch) + dot(lower, patch)
-        raised = jnp.exp(scores - jnp.max(scores, axis=0, keepdims=True))
-        prob = raised / jnp.sum(raised, axis=0, keepdims=True)
-        prob_ref[h] = prob
-        pooled = jnp.concatenate(
-            [
-                (prob * patch_ref[k * var_count : (k + 1) * var_count, :].astype(wide)).astype(low)
-                for k in range(5)
-            ]
-            + [jnp.zeros((rest, tokens), low)],
-            axis=0,
-        )
-        start = pl.multiple_of(h * HEAD_DIM, HEAD_DIM)
-        mixed_ref[pl.ds(start, HEAD_DIM), :] = dot(
-            value_ref[pl.ds(start, HEAD_DIM), :], pooled
-        ).astype(low)
-        return carry
-
-    lax.fori_loop(0, head_count, head_step, 0)
-
-
-def mixer_forward(cut, score_table, value_table):
-    head_count, padded = score_table.shape
-    var_count = cut.shape[1] // 4
-    tokens = cut.shape[0] * cut.shape[2]
-    return pl.pallas_call(
-        mixer_forward_kernel,
-        out_shape=[
-            jax.ShapeDtypeStruct((padded, tokens), low),
-            jax.ShapeDtypeStruct((head_count, var_count, tokens), wide),
-            jax.ShapeDtypeStruct((head_count * HEAD_DIM, tokens), low),
-        ],
-        compiler_params=pltpu.CompilerParams(vmem_limit_bytes=40 * 2**20),
-    )(cut, score_table, value_table)
-
-
 def mixer_backward_kernel(
     patch_ref,
     prob_ref,
@@ -1186,130 +1061,6 @@
     return barrier
 
 
-def attend_kernel(
-    source,
-    tag_ref,
-    crop_ref,
-    joint,
-    received,
-    wide_ref,
-    total_ref,
-    sending,
-    own_sem,
-    send_sem,
-    recv_sem,
-    out_own,
-    out_send,
-    out_recv,
-):
-    x, z, y, c = position()
-    me = y * 4 + c * 2 + x
-    peers, kinds, share, lanes = joint.shape
-    slots = peers * share
-    keep = pltpu.make_async_copy(source.at[me], joint.at[me], own_sem)
-    keep.start()
-    barrier = plane_meet(x, z, y, c)
-    pl.semaphore_wait(barrier, peers - 1)
-
-    def inward(step):
-        there = lax.rem(me + step, peers)
-        return remote(
-            source.at[there],
-            joint.at[me],
-            send_sem.at[there],
-            recv_sem.at[me],
-            plane_device(z, there),
-        )
-
-    def arrived(index):
-        return pltpu.make_async_copy(joint.at[index], joint.at[index], recv_sem.at[index])
-
-    for step in range(1, peers):
-        inward(step).start()
-    keep.wait()
-    for step in range(1, peers):
-        arrived(lax.rem(me + step, peers)).wait()
-
-    def block(step, carry):
-        index = lax.rem(me + 1 + step, peers)
-        span = pl.ds(pl.multiple_of(index * share, share), share)
-        queries = joint[index, 0]
-        keys = joint[:, 1].reshape(slots, lanes)
-        values = joint[:, 2].reshape(slots, lanes)
-        allowed = crop_ref[span, :] == tag_ref[...]
-        result = None
-        for h in range(2):
-            scores = dot(head_lanes(queries, h), keys, 1, 1)
-            scores = jnp.where(allowed, scores, masked_score)
-            largest = jnp.max(scores, axis=1, keepdims=True)
-            weights = jnp.exp(scores - largest)
-            total = jnp.sum(weights, axis=1, keepdims=True)
-            weights = (weights * (1.0 / total)).astype(low)
-            part = head_lanes(dot(weights, values), h)
-            result = part if result is None else result + part
-            total_ref[h, span, :] = largest + jnp.log(total)
-        wide_ref[span, :] = result
-        sending[index] = result.astype(low)
-
-        @pl.when(step < peers - 1)
-        def _():
-            outward(index).start()
-
-        return carry
-
-    def outward(index):
-        return remote(
-            sending.at[index],
-            received.at[me],
-            out_send.at[index],
-            out_recv.at[me],
-            plane_device(z, index),
-        )
-
-    lax.fori_loop(0, peers, block, 0)
-    last = pltpu.make_async_copy(sending.at[me], received.at[me], out_own)
-    last.start()
-    for step in range(1, peers):
-        inward(step).wait_send()
-        outward(lax.rem(me + step, peers)).wait_send()
-        there = lax.rem(me + step, peers)
-        pltpu.make_async_copy(
-            sending.at[there], received.at[there], out_recv.at[there]
-        ).wait()
-    last.wait()
-
-
-def attend_all(source, tags, crops, number):
-    peers, kinds, share, lanes = source.shape
-    slots = peers * share
-    sem = pltpu.SemaphoreType.DMA
-    vmem = pl.BlockSpec(memory_space=pltpu.VMEM)
-    hbm = pl.BlockSpec(memory_space=pl.ANY)
-    return pl.pallas_call(
-        attend_kernel,
-        out_shape=[
-            jax.ShapeDtypeStruct(source.shape, low),
-            jax.ShapeDtypeStruct((peers, share, lanes), low),
-            jax.ShapeDtypeStruct((slots, lanes), wide),
-            jax.ShapeDtypeStruct((2, slots, 1), wide),
-        ],
-        in_specs=[hbm, vmem, vmem],
-        out_specs=[vmem, hbm, vmem, vmem],
-        scratch_shapes=[
-            pltpu.VMEM((peers, share, lanes), low),
-            sem,
-            sem((peers,)),
-            sem((peers,)),
-            sem,
-            sem((peers,)),
-            sem((peers,)),
-        ],
-        compiler_params=pltpu.CompilerParams(
-            collective_id=number, has_side_effects=True, vmem_limit_bytes=50 * 2**20
-        ),
-    )(source, tags, crops)
-
-
 def joined(left, right):
     return (left.astype(wide) + right.astype(wide)).astype(low)
 
@@ -1540,7 +1291,7 @@
         values = joint[:, 2].reshape(slots, lanes)
         grad = grads[index]
         product = grad.astype(wide) * out_ref[span, :]
-        allowed = crop_ref[span, :] == tag_ref[...]
+        allowed = crop_ref[span, :] == tag_ref[0:1, :]
         query_grad = None
         for h in range(2):
             query_part, grad_part = head_lanes(queries, h), head_lanes(grad, h)
@@ -1692,63 +1443,386 @@
     )
 
 
-def project_kernel(mixed_ref, back_ref, lead_ref, vector_ref, weight_ref, start_ref, low_ref, out_ref):
-    step = pl.program_id(0)
-    halves, _, half_width = back_ref.shape
-    row_count, _, _, share, lanes = out_ref.shape
-
-    @pl.when(step == 0)
-    def _():
+def front_kernel(items, *refs):
+    arrays, refs = refs[:8], refs[8:]
+    cut_in, grad_in, hour_ref, refs = refs[0], refs[1], refs[2], refs[3:]
+    outs, grad_out, received, refs = refs[:8], refs[8], refs[9], refs[10:]
+    joint, wide_ref, total_ref, tag_ref, crop_ref, refs = refs[:5] + (refs[5:],)
+    patch_ref, prob_ref, mixed_ref, value_table, key_table, score_table, refs = refs[:6] + (
+        refs[6:],
+    )
+    full_ref, vector_ref, query_ref, start_ref, low_ref, lead_ref, keep_ref, refs = refs[:7] + (
+        refs[7:],
+    )
+    cut_ref, misc_ref, small_ref, weight_a, weight_b, projected, sending, turned, refs = refs[
+        :8
+    ] + (refs[8:],)
+    gather_sems, refs = refs[:5], refs[5:]
+    post_send, post_recv, load_sem, own_sem, send_sem, recv_sem, out_own, out_send, out_recv = refs
+    x, z, y, c = position()
+    across, line = partners(x, z, y, c)
+    own = (z * 4 + y * 2 + c, x)
+    me = y * 4 + c * 2 + x
+    peers, kinds, share, lanes = joint.shape
+    slots = peers * share
+    head_count, var_count, tokens = prob_ref.shape
+    padded = patch_ref.shape[0]
+    taps = 4 * var_count
+    halves = 2
+    half_width = weight_a.shape[-1]
+
+    everyone = [across["x"], across["y"], across["c"]] + line
+    for flip in (3, 5, 6, 7):
+        there_y = 1 - y if flip & 4 else y
+        there_c = 1 - c if flip & 2 else c
+        there_x = 1 - x if flip & 1 else x
+        everyone.append((z * 4 + there_y * 2 + there_c, there_x))
+    sources = [sector_of(z, y, c, x, part, side) for part in range(2) for side in range(2)]
+    meet(everyone, sources, own)
+    letters = []
+    for part in range(2):
+        row = 2 * x + part
+        letters.append(
+            (cut_in.at[part], cut_ref.at[c], post_send.at[part], post_recv.at[c])
+            + (block_of(z, y, row), own)
+        )
+    for row in range(4):
+        letters.append(
+            (grad_in.at[row], grad_out.at[x, c], post_send.at[2 + row])
+            + (post_recv.at[2 + 2 * x + c], block_of(z, y, row), own)
+        )
+    for letter in letters:
+        post(*letter)
+
+    def views(number):
+        index, lead, first, rows, color = items[number]
+        source, target = arrays[index], outs[index]
+        if lead is not None:
+            source, target = source.at[lead], target.at[lead]
+        return source.at[pl.ds(first, rows)], target, pl.ds(first, rows), color
+
+    stages, finish = gatherer(views, gather_sems)
+
+    def load(source, target, spot):
+        return pltpu.make_async_copy(source, target, load_sem.at[spot])
+
+    def ask_small():
+        load(outs[0], misc_ref, 0).start()
+        load(outs[1], small_ref, 1).start()
+        load(outs[2], weight_a, 2).start()
+        load(outs[3], weight_b, 3).start()
+
+    def read_small():
+        load(outs[0], misc_ref, 0).wait()
+        load(outs[1], small_ref, 1).wait()
+        sector = small_ref.shape[4] // 2
+        for lon in range(16):
+            at = (lon // 4, lon // 2 % 2, lon % 2)
+            for side in range(2):
+                rows = slice((2 * lon + side) * sector, (2 * lon + side + 1) * sector)
+                for half in range(2):
+                    full_ref[rows, half * 128 : (half + 1) * 128] = small_ref[
+                        (side,) + at + (slice(half * sector, (half + 1) * sector),)
+                    ]
+        upper = full_ref[:, 128:]
+        vector_ref[...] = upper.astype(wide).T[taps + var_count - 128 : taps + var_count - 120]
+        lane = lax.broadcasted_iota(jnp.int32, upper.shape, 1)
+        full_ref[:, 128:] = jnp.where(lane < taps + var_count - 128, upper.astype(wide), 0.0).astype(
+            low
+        )
+        kind = lax.broadcasted_iota(jnp.int32, (16, 128), 0)
+        across_rows = lax.broadcasted_iota(jnp.int32, (128, 128), 0)
+        across_lanes = lax.broadcasted_iota(jnp.int32, (128, 128), 1)
+        queries = [None, None]
+        for lon in range(16):
+            at = (lon // 4, lon // 2 % 2, lon % 2)
+            span = slice(lon * 128, (lon + 1) * 128)
+            block = misc_ref[(0,) + at + (slice(0, 16),)].astype(wide)
+            tag = jnp.sum(jnp.where(kind == z, block, 0.0), axis=0, keepdims=True)
+            crop = jnp.sum(jnp.where(kind == 4 + z, block, 0.0), axis=0, keepdims=True)
+            tag_ref[0:1, span] = tag
+            for row, target in ((crop, crop_ref), (tag, turned)):
+                target[span, :] = jnp.sum(
+                    jnp.where(across_rows == across_lanes, row, 0.0), axis=1, keepdims=True
+                )
+            for side in range(2):
+                block = misc_ref[(side,) + at + (slice(0, 16),)].astype(wide)[8:16]
+                queries[side] = block if lon == 0 else queries[side] + block
+        query_ref[...] = jnp.concatenate(queries, axis=0)
+        mine = pl.ds(pl.multiple_of(me * share, share), share)
+        keep_ref[...] = jnp.where(turned[mine, :] >= 0.0, 1.0, 0.0)
+        crops = crop_ref[mine, :]
+        hours = jnp.zeros((tokens, 1), wide)
+        for k in range(8):
+            hours = hours + jnp.where(crops == float(k), hour_ref[0:1, k : k + 1], 0.0)
+        lead_ref[...] = hours
+        for part in range(2):
+            pltpu.make_async_copy(cut_in.at[part], cut_ref.at[part], post_recv.at[part]).wait()
+            patch_ref[:taps, part * 128 : (part + 1) * 128] = cut_ref[part]
+        patch_ref[taps : taps + var_count, :] = jnp.ones((var_count, tokens), low)
+        patch_ref[taps + var_count :, :] = jnp.zeros((padded - taps - var_count, tokens), low)
+
+    def tables(weight, spot, table):
+        load(outs[spot], weight, spot).wait()
+        for side in range(halves):
+            product = dot(weight[side].reshape(-1, half_width), full_ref[...], 0, 0)
+            table[side * half_width : (side + 1) * half_width, :] = product.astype(table.dtype)
+
+    def score():
+        tables(weight_a, 2, key_table)
+        wide_query = jnp.concatenate([query_ref[...]] * (head_count * HEAD_DIM // 128), axis=1)
+        head = lax.div(lax.broadcasted_iota(jnp.int32, wide_query.shape, 1), HEAD_DIM)
+        row = lax.broadcasted_iota(jnp.int32, wide_query.shape, 0)
+        wide_query = jnp.where(head == row, wide_query, 0.0).astype(low)
+        rest, result = key_table[...], None
+        for _ in range(3):
+            part = rest.astype(low)
+            rest = rest - part.astype(wide)
+            piece = dot(wide_query, part)
+            result = piece if result is None else result + piece
+        score_table[...] = result * HEAD_DIM ** (-0.5)
+
+    def ask_back():
+        load(outs[4], weight_a, 2).start()
+
+    def heads(first):
+        mask = diagonal(var_count, padded)
+
+        def head_step(h, carry):
+            spread = jnp.where(mask, score_table[pl.ds(h, 1), :], 0.0)
+            upper = spread.astype(low)
+            lower = (spread - upper.astype(wide)).astype(low)
+            patch = patch_ref[...]
+            scores = dot(upper, patch) + dot(lower, patch)
+            raised = jnp.exp(scores - jnp.max(scores, axis=0, keepdims=True))
+            prob = raised / jnp.sum(raised, axis=0, keepdims=True)
+            prob_ref[h] = prob
+            pooled = jnp.concatenate(
+                [
+                    (prob * patch_ref[k * var_count : (k + 1) * var_count, :].astype(wide)).astype(
+                        low
+                    )
+                    for k in range(5)
+                ]
+                + [jnp.zeros((padded - 5 * var_count, tokens), low)],
+                axis=0,
+            )
+            start = pl.multiple_of(h * HEAD_DIM, HEAD_DIM)
+            mixed_ref[pl.ds(start, HEAD_DIM), :] = dot(
+                value_table[pl.ds(start, HEAD_DIM), :], pooled
+            ).astype(low)
+            return carry
+
+        lax.fori_loop(first, first + 4, head_step, 0)
+
+    def begin_block():
+        load(outs[4], weight_a, 2).wait()
         total = lead_ref[...] * vector_ref[0:1] + vector_ref[1:2]
         mixed = mixed_ref[...].T
         for side in range(halves):
             total = total + dot(
-                mixed[:, side * half_width : (side + 1) * half_width], back_ref[side], 1, 1
+                mixed[:, side * half_width : (side + 1) * half_width],
+                weight_a[side].reshape(-1, half_width),
+                1,
+                1,
             )
         start_ref[...] = total
         normed, _ = norm_parts(total)
         low_ref[...] = (normed * vector_ref[2:3] + vector_ref[3:4]).astype(low)
 
-    kind, side = lax.div(step, halves), lax.rem(step, halves)
-    result = dot(low_ref[...], weight_ref[...].reshape(weight_ref.shape[2:])).astype(low)
-    result = result * jnp.where(kind == 0, HEAD_DIM ** (-0.5), 1.0).astype(low)
-    pairs = half_width // lanes
-    for pair in range(pairs):
-        out_ref[:, side * pairs + pair, kind] = result[
-            :, pair * lanes : (pair + 1) * lanes
-        ].reshape(row_count, share, lanes)
-
-
-def project(mixed, back_weight, lead_column, vectors, weights, row_count):
-    model, tokens = mixed.shape
-    kinds, halves, _, half_width = weights.shape
-    return pl.pallas_call(
-        project_kernel,
-        grid=(kinds * halves,),
-        out_shape=[
-            jax.ShapeDtypeStruct((tokens, model), wide),
-            jax.ShapeDtypeStruct((tokens, model), low),
-            jax.ShapeDtypeStruct(
-                (row_count, halves * half_width // 128, kinds, tokens // row_count, 128), low
-            ),
-        ],
-        in_specs=[
-            whole(mixed),
-            whole(back_weight),
-            whole(lead_column),
-            whole(vectors),
-            pl.BlockSpec((1, 1, model, half_width), lambda i: (i // halves, i % halves, 0, 0)),
-        ],
-        out_specs=[
-            pl.BlockSpec((tokens, model), lambda i: (0, 0)),
-            pl.BlockSpec((tokens, model), lambda i: (0, 0)),
-            pl.BlockSpec(
-                (row_count, halves * half_width // 128, kinds, tokens // row_count, 128),
-                lambda i: (0, 0, 0, 0, 0),
-            ),
-        ],
-        compiler_params=pltpu.CompilerParams(vmem_limit_bytes=40 * 2**20),
-    )(mixed, back_weight, lead_column, vectors, weights)
+    def ask_input(kind):
+        target = weight_b if kind % 2 == 0 else weight_a
+        load(outs[5].at[kind], target, 3 - kind % 2).start()
+
+    def project(kind):
+        target = weight_b if kind % 2 == 0 else weight_a
+        load(outs[5].at[kind], target, 3 - kind % 2).wait()
+        pairs = half_width // lanes
+        for side in range(halves):
+            result = dot(low_ref[...], target[side].reshape(-1, half_width)).astype(low)
+            if kind == 0:
+                result = result * low(HEAD_DIM ** (-0.5))
+            for pair in range(pairs):
+                projected[side * pairs + pair, kind] = result[
+                    :, pair * lanes : (pair + 1) * lanes
+                ]
+
+    def inward(step):
+        there = lax.rem(me + step, peers)
+        return remote(
+            projected.at[there],
+            joint.at[me],
+            send_sem.at[there],
+            recv_sem.at[me],
+            plane_device(z, there),
+        )
+
+    def outward(index):
+        return remote(
+            sending.at[index],
+            received.at[me],
+            out_send.at[index],
+            out_recv.at[me],
+            plane_device(z, index),
+        )
+
+    def send_heads():
+        pltpu.make_async_copy(projected.at[me], joint.at[me], own_sem).start()
+        for step in range(1, peers):
+            inward(step).start()
+
+    def take_heads():
+        pltpu.make_async_copy(projected.at[me], joint.at[me], own_sem).wait()
+        for step in range(1, peers):
+            there = lax.rem(me + step, peers)
+            pltpu.make_async_copy(joint.at[there], joint.at[there], recv_sem.at[there]).wait()
+
+    def attention(first, count):
+        def block(step, carry):
+            index = lax.rem(me + 1 + step, peers)
+            span = pl.ds(pl.multiple_of(index * share, share), share)
+            queries = joint[index, 0]
+            keys = joint[:, 1].reshape(slots, lanes)
+            values = joint[:, 2].reshape(slots, lanes)
+            allowed = crop_ref[span, :] == tag_ref[0:1, :]
+            result = None
+            for h in range(2):
+                scores = dot(head_lanes(queries, h), keys, 1, 1)
+                scores = jnp.where(allowed, scores, masked_score)
+                largest = jnp.max(scores, axis=1, keepdims=True)
+                weights = jnp.exp(scores - largest)
+                total = jnp.sum(weights, axis=1, keepdims=True)
+                weights = (weights * (1.0 / total)).astype(low)
+                part = head_lanes(dot(weights, values), h)
+                result = part if result is None else result + part
+                total_ref[h, span, :] = largest + jnp.log(total)
+            wide_ref[span, :] = result
+            sending[index] = result.astype(low)
+
+            @pl.when(step < peers - 1)
+            def _():
+                outward(index).start()
+
+            return carry
+
+        lax.fori_loop(first, first + count, block, 0)
+
+    ready = {}
+    for number, item in enumerate(items):
+        ready[item[:2]] = number + 8
+    at = ready[(3, None)]
+    extra = {at: [ask_small, read_small], at + 1: [score]}
+    extra[at + 2] = [lambda: tables(weight_b, 3, value_table), ask_back]
+    for quarter in range(4):
+        extra.setdefault(at + 3 + quarter // 2, []).append(partial(heads, 4 * quarter))
+    at = max(at + 5, ready[(5, 2)])
+    extra.setdefault(at, []).extend([partial(ask_input, 0), begin_block, partial(ask_input, 1)])
+    extra[at + 1] = [partial(project, 0), partial(ask_input, 2), partial(project, 1)]
+    extra[at + 2] = [partial(project, 2), send_heads]
+    at += 5
+    extra[at] = [take_heads]
+    for step in range(4):
+        extra.setdefault(at + step, []).append(partial(attention, 2 * step, 2))
+    total = len(items)
+    for step in range(max(total + 8, max(extra) + 1)):
+        for back, stage in enumerate(stages):
+            if 0 <= step - 2 * back < total:
+                stage(step - 2 * back)
+        for work in extra.get(step, []):
+            work()
+    last = pltpu.make_async_copy(sending.at[me], received.at[me], out_own)
+    last.start()
+    for number in range(total):
+        finish(number)
+    for letter in letters:
+        settle(*letter)
+    for side in range(2):
+        for part in range(2):
+            pltpu.make_async_copy(
+                grad_in.at[0], grad_out.at[side, part], post_recv.at[2 + 2 * side + part]
+            ).wait()
+    for step in range(1, peers):
+        there = lax.rem(me + step, peers)
+        inward(step).wait_send()
+        outward(there).wait_send()
+        pltpu.make_async_copy(sending.at[there], received.at[there], out_recv.at[there]).wait()
+    last.wait()
+
+
+def front(arrays, cut, grads, hours, head_count, number):
+    items = []
+    for index, array in enumerate(arrays):
+        for lead in range(array.shape[0]) if array.ndim == 3 else (None,):
+            rows = array.shape[-2]
+            if rows % 64:
+                items.append((index, lead, 0, rows, 0))
+                continue
+            for color in range(2):
+                items.append((index, lead, color * rows // 2, rows // 2, color))
+    width = arrays[2].shape[1]
+    model = 2 * width
+    var_count = cut.shape[1] // 4
+    tokens = 2 * cut.shape[2]
+    padded = 2 * arrays[1].shape[1]
+    slots = 8 * tokens
+    sem = pltpu.SemaphoreType.DMA
+    vmem = pl.BlockSpec(memory_space=pltpu.VMEM)
+    hbm = pl.BlockSpec(memory_space=pl.ANY)
+    block = (2, 4, 2, 2)
+
+    def all_of(array):
+        return array.shape[:-2] + block + array.shape[-2:]
+
+    low_outs = [all_of(a) for a in arrays] + [(2, 2) + grads.shape[1:], (8, tokens, 128)]
+    vmem_outs = [
+        ((8, 3, tokens, 128), low),
+        ((slots, 128), wide),
+        ((2, slots, 1), wide),
+        ((8, slots), wide),
+        ((slots, 1), wide),
+        ((padded, tokens), low),
+        ((head_count, var_count, tokens), wide),
+        ((model, tokens), low),
+        ((model, padded), low),
+        ((model, padded), wide),
+        ((head_count, padded), wide),
+        ((model, padded), low),
+        ((8, model), wide),
+        ((head_count, 128), wide),
+        ((tokens, model), wide),
+        ((tokens, model), low),
+        ((tokens, 1), wide),
+        ((tokens, 1), wide),
+    ]
+    result = pl.pallas_call(
+        partial(front_kernel, items),
+        out_shape=[jax.ShapeDtypeStruct(shape, low) for shape in low_outs]
+        + [jax.ShapeDtypeStruct(shape, dtype) for shape, dtype in vmem_outs],
+        in_specs=[hbm] * (len(arrays) + 2) + [vmem],
+        out_specs=[hbm] * len(low_outs) + [vmem] * len(vmem_outs),
+        scratch_shapes=[
+            pltpu.VMEM(cut.shape, low),
+            pltpu.VMEM(all_of(arrays[0]), low),
+            pltpu.VMEM(all_of(arrays[1]), low),
+            pltpu.VMEM(all_of(arrays[2]), low),
+            pltpu.VMEM(all_of(arrays[2]), low),
+            pltpu.VMEM((8, 3, tokens, 128), low),
+            pltpu.VMEM((8, tokens, 128), low),
+            pltpu.VMEM((slots, 1), wide),
+            sem((len(items),)),
+        ]
+        + [sem((len(items), 3))] * 4
+        + [sem((6,)), sem((6,)), sem((4,)), sem, sem((8,)), sem((8,)), sem, sem((8,)), sem((8,))],
+        compiler_params=pltpu.CompilerParams(
+            collective_id=number, has_side_effects=True, vmem_limit_bytes=58 * 2**20
+        ),
+    )(*arrays, cut, grads, hours)
+    count = len(arrays)
+    gathered = [
+        g.reshape(a.shape[:-2] + (2, 16 * a.shape[-2], a.shape[-1]))
+        for g, a in zip(result, arrays)
+    ]
+    return gathered, result[count:]
 
 
 def feed_kernel(
@@ -1784,7 +1858,7 @@
     step = pl.program_id(0)
     count = active.shape[0]
     row_count, units, share, lanes = attended_ref.shape
-    halves, _, half_width = proj_ref.shape
+    _, halves, _, half_width = proj_ref.shape
     tokens = row_count * share
 
     @pl.when(step == 0)
@@ -1796,7 +1870,7 @@
         result = start_ref[...]
         for side in range(halves):
             result = result + dot(
-                flat[:, side * half_width : (side + 1) * half_width], proj_ref[side], 1, 1
+                flat[:, side * half_width : (side + 1) * half_width], proj_ref[0, side], 1, 1
             )
         middle[...] = result
         normed, _ = norm_parts(result)
@@ -1807,14 +1881,14 @@
 
     @pl.when(step < count)
     def _():
-        hidden = dot(second[...], up_ref[0]) + bias_ref[...]
+        hidden = dot(second[...], up_ref[0, 0]) + bias_ref[...]
         share_of = 0.5 * (1.0 + lax.erf(hidden * (0.5**0.5)))
         fired = (hidden * share_of).astype(low)
         active[step] = fired
         slope[step] = share_of + hidden * jnp.exp(-0.5 * hidden * hidden) * (
             0.5 / 1.2533141373155003
         )
-        total[...] += dot(fired, down_ref[0], 1, 1)
+        total[...] += dot(fired, down_ref[0, 0], 1, 1)
 
     @pl.when(step == count - 1)
     def _():
@@ -1834,10 +1908,10 @@
     @pl.when(step >= count)
     def _():
         block = step - count
-        hidden_grad = dot(grad_low[...], down_ref[0]) * slope[block]
+        hidden_grad = dot(grad_low[...], down_ref[0, 0]) * slope[block]
         hidden_low = hidden_grad.astype(low)
         grad_bias_ref[...] = jnp.sum(hidden_low.astype(wide), axis=0, keepdims=True)
-        total[...] += dot(hidden_low, up_ref[0], 1, 1)
+        total[...] += dot(hidden_low, up_ref[0, 0], 1, 1)
         grad_feed_ref[0, 0] = dot(second_turned[...], hidden_low).astype(low)
         grad_feed_ref[1, 0] = dot(grad_turned[...], active[block]).astype(low)
 
@@ -1854,24 +1928,27 @@
         for side in range(halves):
             span = slice(side * half_width, (side + 1) * half_width)
             grad_proj_ref[side] = dot(result_turned, flat[:, span]).astype(low)
-            out = dot(result_low, proj_ref[side]).astype(low)
+            out = dot(result_low, proj_ref[0, side]).astype(low)
             for pair in range(pairs):
                 unit_ref[:, side * pairs + pair] = out[
                     :, pair * lanes : (pair + 1) * lanes
                 ].reshape(row_count, share, lanes)
 
 
-def feed(attended, proj, start, vectors, up_weight, down_weight, up_bias, final_weight, masked, keep):
-    halves, model, full = up_weight.shape
-    half_width = proj.shape[2]
+def feed(attended, start, vectors, late, up_bias, final_weight, masked, keep):
+    blocks, halves, model, block = late.shape
+    half_width = block
+    each = blocks // 2
+    full = each * block
     tokens = start.shape[0]
-    block = 512
-    each = full // block
     count = halves * each
 
-    def block_at(i):
-        j = lax.rem(i, count)
-        return (lax.div(j, each), 0, lax.rem(j, each))
+    def block_of_kind(kind):
+        def block_at(i):
+            j = lax.rem(i, count)
+            return (kind * each + lax.rem(j, each), lax.div(j, each), 0, 0)
+
+        return pl.BlockSpec((1, 1, model, block), block_at)
 
     def late_block(i):
         j = lax.max(i - count, 0)
@@ -1886,7 +1963,7 @@
         fixed((tokens, model), wide),
         fixed(attended.shape, low),
         (
-            jax.ShapeDtypeStruct((2,) + up_weight.shape, low),
+            jax.ShapeDtypeStruct((2, halves, model, full), low),
             pl.BlockSpec((2, 1, model, block), late_block),
         ),
         fixed((halves, model, half_width), low),
@@ -1903,11 +1980,11 @@
         out_shape=[shape for shape, _ in outs],
         in_specs=[
             whole(attended),
-            whole(proj),
+            pl.BlockSpec((1, halves, model, block), lambda i: (blocks - 1, 0, 0, 0)),
             whole(start),
             whole(vectors),
-            pl.BlockSpec((1, model, block), block_at),
-            pl.BlockSpec((1, model, block), block_at),
+            block_of_kind(0),
+            block_of_kind(1),
             pl.BlockSpec((1, block), lambda i: (0, lax.rem(i, count))),
             whole(final_weight),
             whole(masked),
@@ -1927,7 +2004,7 @@
             pltpu.VMEM((tokens, model), wide),
         ],
         compiler_params=pltpu.CompilerParams(vmem_limit_bytes=56 * 2**20),
-    )(attended, proj, start, vectors, up_weight, down_weight, up_bias, final_weight, masked, keep)
+    )(attended, late, start, vectors, late, late, up_bias, final_weight, masked, keep)
 
 
 def return_kernel(
@@ -2090,14 +2167,12 @@
     )
     masked = cotangent * occupied[:, :, None].astype(low)
     masked = jnp.pad(masked, ((0, 0), (0, 0), (0, 128 - out_half)))
-    my_crops = block_slice(slot_crops, head, share, 1)
-    my_occupied = block_slice(occupied, head, share, 1)
-
-    around = (HEAD, LON)
-    up_weight = lax.all_gather(expand_weight, around, axis=0, tiled=True)
-    up_weight = up_weight.reshape(HEAD_SIZE, model, -1)
-    down_weight = lax.all_gather(reduce_weight.T, around, axis=0, tiled=True)
-    down_weight = down_weight.reshape(HEAD_SIZE, model, -1)
+    late = jnp.concatenate(
+        [
+            jnp.transpose(part.reshape(block_rows, -1, half_width), (1, 0, 2))
+            for part in (expand_weight, reduce_weight.T, attention_out.T)
+        ]
+    )
     padded = 256
     small = jnp.concatenate(
         [
@@ -2112,27 +2187,16 @@
         ]
     ).T
     small = jnp.concatenate([small[:, :128], small[:, 128:]])
-    pieces = [
-        jnp.where(my_occupied == 1, my_crops, -1).astype(low).reshape(-1),
-        my_crops.astype(low).reshape(-1),
-        jnp.pad(mixer_query.reshape(-1), (0, 128 - head_half * query_width)),
-        expand_bias.reshape(-1),
-    ]
-    used = sum(piece.shape[0] for piece in pieces)
-    misc = jnp.concatenate(pieces + [jnp.zeros((2048 - used,), low)]).reshape(16, 128)
+    tags = jnp.where(occupied == 1, slot_crops, -1).astype(low)
+    lane = jnp.arange(128) % (LON_SIZE * query_width) // query_width
+    spread = jnp.tile(jnp.concatenate([mixer_query, expand_bias]), (1, 128 // query_width))
+    spread = jnp.where(lane == lon, spread, 0)
+    misc = jnp.concatenate([tags, slot_crops.astype(low), spread])
     out_block = jnp.pad(output_weight, ((0, 0), (0, 128 - out_half)))
-    (
-        misc_all,
-        small_all,
-        key_weight,
-        value_weight,
-        mixer_weight,
-        input_weight,
-        output_proj,
-        final_weight,
-        cut,
-        masked,
-    ) = gather_all(
+    my_row = lax.div(lon, LON_SIZE // row_count)
+    hours = lax.dynamic_index_in_dim(lead_hours, my_row, 0).astype(wide) / 100.0
+    hours = jnp.pad(hours, ((0, 0), (0, 128 - hours.shape[1])))
+    gathered, made = front(
         [
             misc,
             small,
@@ -2140,66 +2204,26 @@
             mixer_values,
             mixer_output.T,
             attention_in,
-            attention_out.T,
             out_block,
+            late,
         ],
         cut,
         masked,
+        hours,
+        head_count,
         1,
     )
+    misc_all, _, key_weight, value_weight, mixer_weight, input_weight, final_weight, late = gathered
+    masked, attended, joint, attended_wide, totals, tag_row, crop_column = made[:7]
+    patches, probs, mixed, value_table, key_table, score_table = made[7:13]
+    patch_full, vectors, query, start_sum, first_low, lead_column, keep_mask = made[13:]
     masked = masked.reshape(HEAD_SIZE, tokens, 128)
-    misc_all = misc_all.reshape(HEAD_SIZE, LON_SIZE, 2048)
-    slots_all = jnp.transpose(
-        misc_all[:, :, : 2 * row_count * share].reshape(
-            HEAD_SIZE, LON_SIZE, 2, row_count, share
-        ),
-        (2, 3, 1, 0, 4),
-    ).reshape(2, row_count, -1)
-    my_row = lax.div(lon, LON_SIZE // row_count)
-    my_block = lax.rem(lon, LON_SIZE // row_count) * HEAD_SIZE + head
-    slots_row = lax.dynamic_index_in_dim(slots_all, my_row, 1, keepdims=False).astype(wide)
-    tag_row, crop_column = slots_row[0:1], slots_row[1][:, None]
-    my_slots = block_slice(slots_row, my_block, tokens, 1)
-    keep_mask = jnp.where(my_slots[0] >= 0.0, 1.0, 0.0)[:, None]
-    my_hours = lax.dynamic_index_in_dim(lead_hours, my_row, 0)
-    lead_column = crop_lookup(my_hours, my_slots[1:2].astype(jnp.int32)).astype(wide)
-    lead_column = lead_column.reshape(tokens, 1) / 100.0
-    at = 2 * row_count * share
-    query = jnp.transpose(
-        misc_all[:, :, at : at + head_half * query_width].reshape(
-            HEAD_SIZE, LON_SIZE, head_half, query_width
-        ),
-        (0, 2, 1, 3),
-    ).reshape(head_count, HEAD_DIM)
-    query = query.astype(wide)
-    at += 128
+    attended = attended[None]
+    query = query[:, :HEAD_DIM]
     bias_rows = expand_bias.shape[0]
-    up_bias = jnp.transpose(
-        misc_all[:, :, at : at + expand_bias.size].reshape(HEAD_SIZE, LON_SIZE, bias_rows, -1),
-        (0, 2, 1, 3),
-    ).reshape(HEAD_SIZE, -1)
-    up_bias = up_bias.astype(wide)
-    patch_full = jnp.transpose(
-        small_all.reshape(HEAD_SIZE, LON_SIZE, 2, slice_width, 128), (1, 0, 3, 2, 4)
-    ).reshape(model, padded)
-    vectors = patch_full[:, taps + var_count : taps + var_count + 6].T.astype(wide)
-    patch_full = jnp.where(jnp.arange(padded)[None, :] < taps + var_count, patch_full, 0)
-
-    key_table = einsum("xde,dm->xem", key_weight, patch_full).reshape(model, padded)
-    value_table = einsum("xde,dm->xem", value_weight, patch_full).astype(low).reshape(model, padded)
-    score_table = (
-        jnp.sum(key_table.reshape(head_count, HEAD_DIM, padded) * query[:, :, None], axis=1) * scale
-    )
-
-    patches, probs, mixed = mixer_forward(cut, score_table, value_table)
-    start_sum, first_low, projected = project(
-        mixed, mixer_weight, lead_column, vectors, input_weight, 1
-    )
+    up_bias = misc_all.reshape(HEAD_SIZE, LON_SIZE, -1, 128)[:, :, 2 * row_count + head_half :]
+    up_bias = jnp.sum(up_bias[..., : LON_SIZE * query_width].astype(wide), axis=1)
     units = HEAD_SIZE * pairs
-    joint, attended, attended_wide, totals = attend_all(
-        projected.reshape(units, 3, tokens, 128), tag_row, crop_column, 3
-    )
-    attended = attended[None]
     (
         predicted,
         middle_grad,
@@ -2211,11 +2235,9 @@
         second_vectors,
     ) = feed(
         attended,
-        output_proj,
         start_sum,
         vectors,
-        up_weight,
-        down_weight,
+        late,
         up_bias.reshape(1, -1),
         final_weight,
         masked,
@@ -2308,7 +2330,7 @@
         2,
     )
     predicted = predicted[:, :, :out_half]
-    full_half = up_weight.shape[2]
+    full_half = expand_weight.shape[1]
     place = [0]
 
     def take(width):

time: 537 us -> 506 us (0.942)
  local copies, waits for them, and re-layouts: 50.8 us -> 30 us
  between operations: 15.5 us -> 1.8 us
  Pallas kernels: 436 us -> 446 us
  matrix products: 13.1 us -> 5.87 us
    pallas_call x4 -> x1, Pallas kernels: 180 us -> 191 us  [front(): pl.pallas_call(partial(front_kernel, items), out_shape=[jax.ShapeDtypeStr...]
    dot_general x6 -> x4, matrix products: 11 us -> 3.75 us  [einsum(): return jnp.einsum(spec, left, right, preferred_element_type=wide)]
    unnamed x142 -> x100, local copies, waits for them, and re-layouts: 13.6 us -> 9.02 us
  transfers between devices with their start and end apart: 4 -> 2, of which waited for: 0 -> 0; matrix products, arithmetic and copies ran while one was open for 6% -> 2% of each run, Pallas kernels for 35% -> 0%
where the time goes in v4:
time: 506 us; the launch traced here: 497 us
  Pallas kernels  446 us (88%)
  local copies, waits for them, and re-layouts  30 us (6%)
  other arithmetic  8.19 us (2%)
  matrix products  5.87 us (1%)
  starting transfers between devices  5.52 us (1%)
    pallas_call x1, Pallas kernels, front(): pl.pallas_call(partial(front_kernel, items), out_shape=[jax.ShapeDtypeStr...  191 us
    pallas_call x1, Pallas kernels, attend_back(): pl.pallas_call(attend_back_kernel, out_shape=[jax.ShapeDtypeStruct(joint....  111 us
    pallas_call x1, Pallas kernels, reduce_all(): pl.pallas_call(partial(reduce_kernel, chunks, count), out_shape=[jax.Shap...  84.5 us
    pallas_call x1, Pallas kernels, feed(): pl.pallas_call(feed_kernel, grid=(2 * count,), out_shape=[shape for shape...  34.7 us
    pallas_call x1, Pallas kernels, go_back(): pl.pallas_call(return_kernel, grid=(kinds * halves,), out_shape=[jax.Shap...  13 us
  transfers between devices with their start and end apart: 2, of which 0 were waited for; matrix products, arithmetic and copies ran while one was open for 2% of the time, Pallas kernels for 0%

profile of v4, /device:TPU:0, one launch (start us, length us, event | category | flops | bytes accessed | tf_op | source)
XLA Modules:
  0.0 497.4 jit_solution(6846078867660373082)
XLA Ops:
  0.8 1.4 fusion.29
  2.8 5.5 %collective-permute-start.1 = (bf16[48,32,1]{0,1,2:T(8,128)(2,1)S(1)}, bf16[48,32,1]{0,1,2:T(8,128)(2,1)S(1)}, u32[]{:S(2)}, u32[]{:S(2)}) collective-permute-start(bf16[48,32,1]{0,1,2:T(8,128)(2,1)S(1)} %copy.185), channel_id=1, source_target_pairs={{2,0},{4,2},{6,4},{8,6},{10,8},{12,10},{14,12},{16,14},{18,16},{20... | collective-permute-start | bytes 9224 | tf_op jit(solution)/shard_map/ppermute | solution.py:2147
  12.8 0.9 pad_maximum_fusion.1.refs_7_
  13.7 0.7 fusion.26
  14.4 0.7 pad.21.refs_9_
  16.3 2.0 fusion.1.field_ref
  18.3 2.8 shard_map.375.refs_8_
  21.1 190.9 %shard_map.376 = (bf16[2,4,2,2,48,128]{5,4,3,2,1,0:T(8,128)(2,1)}, bf16[2,4,2,2,64,128]{5,4,3,2,1,0:T(8,128)(2,1)}, bf16[2,4,2,2,64,512]{5,4,3,2,1,0:T(8,128)(2,...) custom-call(bf16[48,128]{1,0:T(8,128)(2,1)} %pad_maximum_fusion.4.re, ...), custom_call_target="tpu_custom_call" | custom-call | tf_op jit(solution)/shard_map/pallas_call | solution.py:1797
  212.1 1.0 convert_reduce_fusion
  213.1 0.7 reshape.253.bias_ref
  213.8 34.7 %shard_map.377 = (bf16[2,256,128]{2,1,0:T(8,128)(2,1)}, f32[256,1024]{1,0:T(8,128)}, bf16[1,8,256,128]{3,2,1,0:T(8,128)(2,1)}, bf16[2,2,1024,2048]{3,2,1,0:T(8,1...) custom-call(bf16[1,8,256,128]{3,2,1,0:T(8,128)(2,1)} %bitcast.168, ...), custom_call_target="tpu_custom_call" | custom-call | tf_op jit(solution)/shard_map/pallas_call | solution.py:1977
  248.5 111.4 %shard_map.378 = (bf16[8,3,256,128]{3,2,1,0:T(8,128)(2,1)}, f32[64,4096]{1,0:T(8,128)}) custom-call(bf16[8,3,256,128]{3,2,1,0:T(8,128)(2,1)} %get-tuple-element.75.joint, f32[8,2048]{1,0:T(8,128)} %get-tuple-element.76.tag_ref, f32[2048,1]{1,0:T(8,128)} %get-tuple-element.77.crop_ref, f32[2048,128]{1,0:T(8,128)} %get-tuple-element.78.out_ref, ...), custom_call_target="tpu_custom_call" | custom-call | tf_op jit(solution)/shard_map/pallas_call | solution.py:1383
  360.1 13.0 %shard_map.379 = (bf16[3,2,1024,512]{3,2,1,0:T(8,128)(2,1)}, bf16[2,1024,512]{2,1,0:T(8,128)(2,1)}, bf16[1024,256]{1,0:T(8,128)(2,1)S(1)}, f32[4,1024]{1,0:T(4,128)S(1)}) custom-call(bf16[1,8,3,256,128]{4,3,2,1,0:T(8,128)(2,1)} %bitcast.154, bf16[3,2,1024,512]{3,2,1,0:T(8,128)(2,1)} %bitcast.144, bf16[256,1024]{1,0:T(8,128)(2,1)S(1)} %copy-done.4, ...), custom_call_target="tpu_custom_call" | custom-call | tf_op jit(solution)/shard_map/pallas_call | solution.py:2066
  373.1 8.7 %shard_map.380 = (f32[1024,256]{1,0:T(8,128)S(1)}, f32[16,256]{1,0:T(8,128)S(1)}, f32[2,192,128]{2,1,0:T(8,128)S(1)}) custom-call(bf16[256,256]{1,0:T(8,128)(2,1)S(1)} %copy-done.9, f32[16,48,256]{2,1,0:T(8,128)S(1)} %copy-done.2, f32[16,256]{1,0:T(8,128)S(1)} %copy-done.10, bf16[1024,256]{1,0:T(8,128)(2,1)S(1)} %copy-done.5, ...), custom_call_target="tpu_custom_call" | custom-call | tf_op jit(solution)/shard_map/pallas_call | solution.py:1031
  384.1 2.1 convolution_convert_fusion
  386.5 1.3 copy-done.12
  387.8 0.8 convolution_bitcast_fusion.1
  388.6 0.8 convolution_bitcast_fusion
  391.2 0.7 reduce.12
  395.2 1.1 pad_maximum_fusion.refs_4_
  396.3 84.5 %shard_map.381 = (f32[64,3328]{1,0:T(8,128)}, bf16[4,128,128]{2,1,0:T(8,128)(2,1)}, f32[32,48,256]{2,1,0:T(8,128)}) custom-call(bf16[2,4,2,2,64,512]{5,4,3,2,1,0:T(8,128)(2,1)} %bitcast.152, bf16[6,4,2,2,64,512]{5,4,3,2,1,0:T(8,128)(2,1)} %bitcast.143, bf16[2,4,2,2,64,512]{5,4,3,2,1,0:T(8,128)(2,1)} %bitcast.153, bf16[4,2,2,64,1024]{4,3,2,1,0:T(8,128)(2,1)} %bitcast.142, ...), custom_call_target="tpu_custom_call" | custom-call | tf_op jit(solution)/shard_map/pallas_call | solution.py:909
  480.7 2.1 slice_bitcast_fusion.1
  482.8 0.8 slice.158
  483.7 0.7 fusion.28
  485.2 0.7 slice_reduce_fusion
  485.9 1.4 slice.173
  487.3 0.8 slice.171
  488.1 0.8 slice.157
  490.5 2.1 copy.178
  492.6 0.7 copy.177
  494.7 1.0 slice_bitcast_fusion
  496.4 0.8 pad_maximum_fusion.2
  (174 shorter events, 18.1 us)
Async XLA Ops:
  0.7 9.5 %copy-start.37 = (bf16[8,4]{0,1:T(4,128)(2,1)S(1)}, bf16[8,4]{0,1:T(4,128)(2,1)}, u32[]{:S(2)}) copy-start(bf16[8,4]{0,1:T(4,128)(2,1)} %param.32) | copy-start | bytes 196
  0.7 9.5 %copy-start.36 = (bf16[32,4]{0,1:T(4,128)(2,1)S(1)}, bf16[32,4]{0,1:T(4,128)(2,1)}, u32[]{:S(2)}) copy-start(bf16[32,4]{0,1:T(4,128)(2,1)} %param.44) | copy-start | bytes 772
  0.7 9.7 %copy-start.35 = (s32[4,128]{1,0:T(4,128)S(1)}, s32[4,128]{1,0:T(4,128)}, u32[]{:S(2)}) copy-start(s32[4,128]{1,0:T(4,128)} %param.28) | copy-start | bytes 6148
  0.7 9.7 %copy-start.22 = (bf16[4,128,96]{1,2,0:T(8,128)(2,1)S(1)}, bf16[4,128,96]{1,2,0:T(8,128)(2,1)}, u32[]{:S(2)}) copy-start(bf16[4,128,96]{1,2,0:T(8,128)(2,1)} %param.47) | copy-start | bytes 294916
  0.7 9.8 %copy-start.24 = (bf16[48,4,32]{0,2,1:T(8,128)(2,1)S(1)}, bf16[48,4,32]{0,2,1:T(8,128)(2,1)}, u32[]{:S(2)}) copy-start(bf16[48,4,32]{0,2,1:T(8,128)(2,1)} %param.30) | copy-start | bytes 36868
  0.7 10.0 %copy-start.38 = (bf16[2,32]{1,0:T(2,128)(2,1)S(1)}, bf16[2,32]{1,0:T(2,128)(2,1)}, u32[]{:S(2)}) copy-start(bf16[2,32]{1,0:T(2,128)(2,1)} %param.36) | copy-start | bytes 388
  0.8 10.1 %copy-start.39 = (bf16[32]{0:T(256)(128)(2,1)S(1)}, bf16[32]{0:T(256)(128)(2,1)}, u32[]{:S(2)}) copy-start(bf16[32]{0:T(256)(128)(2,1)} %param.37) | copy-start | bytes 196
  0.8 10.2 %copy-start.40 = (bf16[32]{0:T(256)(128)(2,1)S(1)}, bf16[32]{0:T(256)(128)(2,1)}, u32[]{:S(2)}) copy-start(bf16[32]{0:T(256)(128)(2,1)} %param.38) | copy-start | bytes 196
  0.8 10.3 %copy-start.41 = (bf16[32]{0:T(256)(128)(2,1)S(1)}, bf16[32]{0:T(256)(128)(2,1)}, u32[]{:S(2)}) copy-start(bf16[32]{0:T(256)(128)(2,1)} %param.41) | copy-start | bytes 196
  0.8 10.3 %copy-start.42 = (bf16[32]{0:T(256)(128)(2,1)S(1)}, bf16[32]{0:T(256)(128)(2,1)}, u32[]{:S(2)}) copy-start(bf16[32]{0:T(256)(128)(2,1)} %param.42) | copy-start | bytes 196
  0.8 10.4 %copy-start.32 = (bf16[48,32]{0,1:T(8,128)(2,1)S(1)}, bf16[48,32]{0,1:T(8,128)(2,1)}, u32[]{:S(2)}) copy-start(bf16[48,32]{0,1:T(8,128)(2,1)} %param.31) | copy-start | bytes 9220
  0.8 10.6 %copy-start.20 = (bf16[64,2048]{1,0:T(8,128)(2,1)S(1)}, bf16[64,2048]{1,0:T(8,128)(2,1)}, u32[]{:S(2)}) copy-start(bf16[64,2048]{1,0:T(8,128)(2,1)} %param.43) | copy-start | bytes 786436
  0.8 10.6 %copy-start.19 = (bf16[2048,64]{0,1:T(8,128)(2,1)S(1)}, bf16[2048,64]{0,1:T(8,128)(2,1)}, u32[]{:S(2)}) copy-start(bf16[2048,64]{0,1:T(8,128)(2,1)} %param.45) | copy-start | bytes 786436
  0.8 12.0 %copy-start.23 = (bf16[512,64]{0,1:T(8,128)(2,1)S(1)}, bf16[512,64]{0,1:T(8,128)(2,1)}, u32[]{:S(2)}) copy-start(bf16[512,64]{0,1:T(8,128)(2,1)} %param.40) | copy-start | bytes 196612
  2.3 12.8 %copy-start.28 = (bf16[64,96]{1,0:T(8,128)(2,1)S(1)}, bf16[64,96]{1,0:T(8,128)(2,1)}, u32[]{:S(2)}) copy-start(bf16[64,96]{1,0:T(8,128)(2,1)} %param.46) | copy-start | bytes 36868
  2.8 13.5 %copy-start.17 = (bf16[48,32,256]{2,1,0:T(8,128)(2,1)S(1)}, bf16[48,32,256]{2,1,0:T(8,128)(2,1)}, u32[]{:S(2)}) copy-start(bf16[48,32,256]{2,1,0:T(8,128)(2,1)} %param.24) | copy-start | bytes 2359300
  2.8 13.5 %collective-permute-start.1 = (bf16[48,32,1]{0,1,2:T(8,128)(2,1)S(1)}, bf16[48,32,1]{0,1,2:T(8,128)(2,1)S(1)}, u32[]{:S(2)}, u32[]{:S(2)}) collective-permute-start(bf16[48,32,1]{0,1,2:T(8,128)(2,1)S(1)} %copy.185), channel_id=1, source_target_pairs={{2,0},{4,2},{6,4},{8,6},{10,8},{12,10},{14,12},{16,14},{18,16},{20... | collective-permute-start | bytes 9224 | tf_op jit(solution)/shard_map/ppermute | solution.py:2147
  8.8 7.5 %collective-permute-start = (bf16[48,32,1]{0,1,2:T(8,128)(2,1)S(1)}, bf16[48,32,1]{0,1,2:T(8,128)(2,1)S(1)}, u32[]{:S(2)}, u32[]{:S(2)}) collective-permute-start(bf16[48,32,1]{0,1,2:T(8,128)(2,1)S(1)} %copy.184), channel_id=1, source_target_pairs={{0,2},{2,4},{4,6},{6,8},{8,10},{10,12},{12,14},{14,16},{16,18},{18... | collective-permute-start | bytes 9224 | tf_op jit(solution)/shard_map/ppermute | solution.py:2146
  248.5 111.5 %copy-start = (f32[256,1024]{1,0:T(8,128)S(1)}, f32[256,1024]{1,0:T(8,128)}, u32[]{:S(2)}) copy-start(f32[256,1024]{1,0:T(8,128)} %get-tuple-element.68.start_ref) | copy-start | bytes 3145732
  248.5 111.5 %copy-start.1 = (f32[256,1024]{1,0:T(8,128)S(1)}, f32[256,1024]{1,0:T(8,128)}, u32[]{:S(2)}) copy-start(f32[256,1024]{1,0:T(8,128)} %get-tuple-element.85.middle_grad_ref) | copy-start | bytes 3145732
  248.5 111.5 %copy-start.3 = (bf16[1024,256]{1,0:T(8,128)(2,1)S(1)}, bf16[1024,256]{1,0:T(8,128)(2,1)}, u32[]{:S(2)}) copy-start(bf16[1024,256]{1,0:T(8,128)(2,1)} %get-tuple-element.88.mixed_ref) | copy-start | bytes 1572868
  248.5 111.5 %copy-start.4 = (bf16[256,1024]{1,0:T(8,128)(2,1)S(1)}, bf16[256,1024]{1,0:T(8,128)(2,1)}, u32[]{:S(2)}) copy-start(bf16[256,1024]{1,0:T(8,128)(2,1)} %get-tuple-element.84.low_ref) | copy-start | bytes 1572868
  248.5 111.5 %copy-start.7 = (f32[256,1]{1,0:T(8,128)S(1)}, f32[256,1]{1,0:T(8,128)}, u32[]{:S(2)}) copy-start(f32[256,1]{1,0:T(8,128)} %get-tuple-element.86.lead_ref) | copy-start | bytes 3076
  248.5 111.5 %copy-start.8 = (f32[8,1024]{1,0:T(8,128)S(1)}, f32[8,1024]{1,0:T(8,128)}, u32[]{:S(2)}) copy-start(f32[8,1024]{1,0:T(8,128)} %get-tuple-element.69.vector_ref) | copy-start | bytes 98308
  360.0 13.1 %copy-start.2 = (f32[16,48,256]{2,1,0:T(8,128)S(1)}, f32[16,48,256]{2,1,0:T(8,128)}, u32[]{:S(2)}) copy-start(f32[16,48,256]{2,1,0:T(8,128)} %get-tuple-element.93.prob_ref) | copy-start | bytes 2359300
  360.0 13.1 %copy-start.5 = (bf16[1024,256]{1,0:T(8,128)(2,1)S(1)}, bf16[1024,256]{1,0:T(8,128)(2,1)}, u32[]{:S(2)}) copy-start(bf16[1024,256]{1,0:T(8,128)(2,1)} %get-tuple-element.95.value_ref) | copy-start | bytes 1572868
  360.0 13.1 %copy-start.9 = (bf16[256,256]{1,0:T(8,128)(2,1)S(1)}, bf16[256,256]{1,0:T(8,128)(2,1)}, u32[]{:S(2)}) copy-start(bf16[256,256]{1,0:T(8,128)(2,1)} %get-tuple-element.92.patch_ref) | copy-start | bytes 393220
  360.0 13.1 %copy-start.10 = (f32[16,256]{1,0:T(8,128)S(1)}, f32[16,256]{1,0:T(8,128)}, u32[]{:S(2)}) copy-start(f32[16,256]{1,0:T(8,128)} %get-tuple-element.94.score_ref) | copy-start | bytes 49156
  373.1 9.4 %copy-start.16 = (f32[1024,256]{1,0:T(8,128)S(1)}, f32[1024,256]{1,0:T(8,128)}, u32[]{:S(2)}) copy-start(f32[1024,256]{1,0:T(8,128)} %get-tuple-element.106) | copy-start | bytes 3145732
  373.1 10.4 %copy-start.13 = (bf16[1024,256]{1,0:T(8,128)(2,1)S(1)}, bf16[1024,256]{1,0:T(8,128)(2,1)}, u32[]{:S(2)}) copy-start(bf16[1024,256]{1,0:T(8,128)(2,1)} %get-tuple-element.91) | copy-start | bytes 1572868
  373.1 10.8 %copy-start.27 = (f32[16,128]{1,0:T(8,128)S(1)}, f32[16,128]{1,0:T(8,128)}, u32[]{:S(2)}) copy-start(f32[16,128]{1,0:T(8,128)} %get-tuple-element.99) | copy-start | bytes 24580
  480.7 9.8 %copy-start.14 = (f32[32,48,256]{2,1,0:T(8,128)S(1)}, f32[32,48,256]{2,1,0:T(8,128)}, u32[]{:S(2)}) copy-start(f32[32,48,256]{2,1,0:T(8,128)} %get-tuple-element.110) | copy-start | bytes 4718596
  (13 other events, 61.3 us)

commit v5 on v4

--- a/solution.py
+++ b/solution.py
@@ -736,12 +736,21 @@
 
 
 def reduce_kernel(chunks, count, *refs):
-    ins = refs[:count]
-    value_in, grad_in, lat_ref, shift_ref = refs[count : count + 4]
-    out, value_out, pixel_out = refs[count + 4 : count + 7]
-    buffers, sems = refs[count + 7 : count + 13], refs[count + 13 : count + 20]
-    grad_out, field, edge, west_edge, east_edge = refs[count + 20 : count + 25]
-    value_send, value_recv, grad_send, grad_recv, edge_send, edge_recv = refs[count + 25 :]
+    ins, refs = refs[:count], refs[count:]
+    value_in, key_weight, value_weight, lat_ref, shift_ref, refs = refs[:5] + (refs[5:],)
+    patch_ref, prob_ref, score_table, value_table, key_table, mixed_grad, refs = refs[:6] + (
+        refs[6:],
+    )
+    full_ref, query_ref, first_ref, second_ref, rest_ref, refs = refs[:5] + (refs[5:],)
+    out, value_out, pixel_out, refs = refs[:3] + (refs[3:],)
+    buffers, sems, refs = refs[:6], refs[6:13], refs[13:]
+    grad_out, field, edge, west_edge, east_edge, refs = refs[:5] + (refs[5:],)
+    value_send, value_recv, grad_send, grad_recv, edge_send, edge_recv, refs = refs[:6] + (
+        refs[6:],
+    )
+    grad_in, pooled_ref, count_ref, patch_grad, weight_a, weight_b, key_low, query_grad = refs[:8]
+    values_ref, tail_ref, load_sem = refs[8:]
+    ins = ins + (values_ref, tail_ref)
     x, z, y, c = position()
     across, line = partners(x, z, y, c)
     lon = z * 4 + y * 2 + c
@@ -755,16 +764,146 @@
             device = sector_of(z, y, c, x, part, side)
             at = 2 * part + side
             letters.append(
+                (grad_in.at[part], grad_out.at[z], grad_send.at[at], grad_recv.at[z])
+                + (device, own)
+            )
+            letters.append(
                 (value_in.at[side, part], value_out.at[z], value_send.at[at], value_recv.at[z])
                 + (device, own)
             )
-            letters.append(
-                (grad_in.at[part], grad_out.at[z], grad_send.at[at], grad_recv.at[z])
-                + (device, own)
-            )
-    for letter in letters:
+    for letter in letters[1::2]:
         post(*letter)
     total = len(chunks)
+    loads = [
+        pltpu.make_async_copy(key_weight, weight_a, load_sem.at[0]),
+        pltpu.make_async_copy(value_weight, weight_b, load_sem.at[1]),
+    ]
+    for copy in loads:
+        copy.start()
+    head_total, var_total, tokens = prob_ref.shape
+    padded = patch_ref.shape[0]
+    scale = HEAD_DIM ** (-0.5)
+
+    def halves_of(values):
+        upper = values.astype(low)
+        return upper, (values - upper.astype(wide)).astype(low)
+
+    def heads(first):
+        mask = diagonal(var_total, padded)
+        if first == 0:
+            patch_grad[...] = jnp.zeros_like(patch_grad)
+            query_grad[...] = jnp.zeros_like(query_grad)
+
+        def head_step(h, carry):
+            span = pl.ds(pl.multiple_of(h * HEAD_DIM, HEAD_DIM), HEAD_DIM)
+            grads = mixed_grad[span, :]
+            prob = prob_ref[h]
+            back = dot(value_table[span, :], grads, 0, 0)
+            pieces = [
+                patch_ref[k * var_total : (k + 1) * var_total, :].astype(wide) for k in range(5)
+            ]
+            backs = [back[k * var_total : (k + 1) * var_total, :] for k in range(5)]
+            prob_grad = pieces[0] * backs[0]
+            for k in range(1, 5):
+                prob_grad = prob_grad + pieces[k] * backs[k]
+            mean = jnp.sum(prob * prob_grad, axis=0, keepdims=True)
+            upper, lower = halves_of(prob * (prob_grad - mean))
+            spread = jnp.where(mask, score_table[pl.ds(h, 1), :], 0.0).astype(low)
+            patch_grad[...] += dot(spread, upper, 0, 0)
+            for k in range(4):
+                patch_grad[k * var_total : (k + 1) * var_total, :] += prob * backs[k]
+            patch = patch_ref[...]
+            counts = dot(upper, patch, 1, 1) + dot(lower, patch, 1, 1)
+            counts = jnp.sum(jnp.where(mask, counts, 0.0), axis=0, keepdims=True) * scale
+            count_ref[pl.ds(h, 1), :] = counts
+            table = key_table[span, :].astype(low)
+            upper, lower = halves_of(counts)
+            query_grad[pl.ds(h, 1), :HEAD_DIM] = dot(upper, table, 1, 1) + dot(lower, table, 1, 1)
+            pooled = jnp.concatenate(
+                [(prob * piece).astype(low) for piece in pieces]
+                + [jnp.zeros((padded - 5 * var_total, tokens), low)],
+                axis=0,
+            )
+            pooled_ref[span, :] = dot(grads, pooled, 1, 1).astype(low)
+            return carry
+
+        lax.fori_loop(first, first + head_total // 4, head_step, 0)
+
+    def send_cut():
+        taps = 4 * var_total
+        for part in range(2):
+            grad_in[part] = patch_grad[:taps, part * 128 : (part + 1) * 128]
+        for letter in letters[0::2]:
+            post(*letter)
+
+    def value_grads():
+        rows = full_ref.shape[0] // 4
+        for part in range(4):
+            piece = dot(full_ref[part * rows : (part + 1) * rows, :], pooled_ref[...], 1, 1)
+            values_ref[part] = piece.astype(low).reshape(values_ref.shape[1:])
+
+    def tail_grads():
+        for copy in loads:
+            copy.wait()
+        half_width = weight_a.shape[-1]
+        wide_query = jnp.concatenate([query_ref[...]] * (head_total * HEAD_DIM // 128), axis=1)
+        head = lax.div(lax.broadcasted_iota(jnp.int32, wide_query.shape, 1), HEAD_DIM)
+        row = lax.broadcasted_iota(jnp.int32, wide_query.shape, 0)
+        wide_query = jnp.where(head == row, wide_query, 0.0).astype(low)
+        count_parts = halves_of(count_ref[...])
+        key_low[...] = sum(dot(wide_query, part, 0, 0) for part in count_parts).astype(low)
+        spots = lax.broadcasted_iota(jnp.int32, (8, padded), 1) - 5 * var_total
+        kinds = lax.broadcasted_iota(jnp.int32, (8, padded), 0)
+        vectors = jnp.concatenate(
+            [first_ref[...], second_ref[...], jnp.zeros((2, first_ref.shape[1]), wide)], axis=0
+        )
+        result = dot(vectors.astype(low), jnp.where(spots == kinds, 1.0, 0.0).astype(low), 0, 0)
+        for side in range(2):
+            span = slice(side * half_width, (side + 1) * half_width)
+            result = result + dot(weight_a[side], key_low[span, :])
+            result = result + dot(weight_b[side], pooled_ref[span, :])
+        result = result.astype(low)
+        sector = tail_ref.shape[-2] // 2
+        for place in range(16):
+            at = (place // 4, place // 2 % 2, place % 2)
+            for side in range(2):
+                first = (2 * place + side) * sector
+                for half in range(2):
+                    tail_ref[
+                        (side,) + at + (slice(half * sector, (half + 1) * sector), slice(0, 128))
+                    ] = result[first : first + sector, half * 128 : (half + 1) * 128]
+
+    def rest_grads():
+        used = rest_ref.shape[2] - 32
+        head_half = head_total // 2
+        model = full_ref.shape[0]
+        count_parts = halves_of(count_ref[...])
+        head = lax.broadcasted_iota(jnp.int32, (head_total, 128), 0)
+        lane = lax.broadcasted_iota(jnp.int32, (head_total, 128), 1)
+        rows = lax.broadcasted_iota(jnp.int32, (model, head_total), 0)
+        columns = lax.broadcasted_iota(jnp.int32, (model, head_total), 1)
+        inner = lax.rem(rows, model // 16)
+        sectors = lax.div(lax.broadcasted_iota(jnp.int32, (model, 128), 0), model // 16)
+        lanes_at = lax.broadcasted_iota(jnp.int32, (model, 128), 1)
+        source_lane = lax.broadcasted_iota(jnp.int32, (128, 128), 0)
+        target_lane = lax.broadcasted_iota(jnp.int32, (128, 128), 1)
+        query_at = used + head_half + 4
+        move = jnp.where(target_lane == query_at + lax.rem(source_lane, 4), 1.0, 0.0).astype(low)
+        for side in range(2):
+            spot = used + head - head_half * side
+            inside = lax.div(head, head_half) == side
+            target = jnp.where(jnp.logical_and(inside, lane == spot), 1.0, 0.0).astype(low)
+            sums = sum(dot(part, target, 0, 0) for part in count_parts)
+            result = rest_ref[side].astype(wide)
+            for part in halves_of(sums):
+                result = result + dot(full_ref[...], part)
+            chosen = jnp.logical_and(inner < head_half, columns == inner + head_half * side)
+            spread = dot(jnp.where(chosen, 1.0, 0.0).astype(low), query_grad[...].astype(low))
+            spread = jnp.where(lax.div(lanes_at, 4) == sectors, spread, 0.0).astype(low)
+            result = result + dot(spread, move)
+            tail_ref[side, :, :, :, :, 128:] = result.astype(low).reshape(
+                tail_ref.shape[1:-1] + (128,)
+            )
 
     lat_count, var_count, lanes = field.shape
     half = lanes // 2
@@ -806,15 +945,9 @@
         two = rest.astype(low)
         return one, two, (rest - two.astype(wide)).astype(low)
 
-    def columns_of(shape, axis):
-        spot = lax.broadcasted_iota(jnp.int32, shape, axis)
-        side, spot = lax.div(spot, half), lax.rem(spot, half)
-        slots = half // 2
-        return 2 * lax.rem(spot, slots) + 2 * side + lax.div(spot, slots) - 1
-
     def edges():
         kind = lax.broadcasted_iota(jnp.int32, (8, lanes), 0)
-        wanted = columns_of((8, lanes), 1)
+        wanted = columns_of((8, lanes), 1, half)
         pick = jnp.where(
             jnp.logical_or(
                 jnp.logical_and(kind == 0, wanted == -1),
@@ -832,7 +965,7 @@
     def pixels():
         remote(edge, west_edge, edge_send.at[0], edge_recv.at[0], east).wait()
         remote(edge, east_edge, edge_send.at[1], edge_recv.at[1], west).wait()
-        wanted = columns_of((lanes, column_count), 0)
+        wanted = columns_of((lanes, column_count), 0, half)
         column = lax.broadcasted_iota(jnp.int32, (lanes, column_count), 1)
         place = jnp.where(wanted == column, 1.0, 0.0).astype(low)
         kind = lax.broadcasted_iota(jnp.int32, (8, column_count), 0)
@@ -857,8 +990,11 @@
 
         lax.fori_loop(0, lat_count, body, 0)
 
-    extra = {3: lambda: paste(0), 4: lambda: paste(1), 5: lambda: paste(2), 6: lambda: paste(3)}
-    extra.update({7: edges, 10: pixels})
+    quarter = head_total // 4
+    extra = {step: partial(heads, step * quarter) for step in range(4)}
+    extra.update({4: send_cut, 5: value_grads, 6: tail_grads, 7: rest_grads})
+    extra.update({8 + row: partial(paste, row) for row in range(4)})
+    extra.update({12: edges, 15: pixels})
 
     def source_of(pair, color, side, core):
         index, lead, offset = chunks[2 * pair + color][side]
@@ -883,28 +1019,30 @@
         pltpu.make_async_copy(value_in.at[0, 0], value_out.at[row], value_recv.at[row]).wait()
 
 
-def reduce_all(items, values, grads, lat_lanes, shift_lanes, lat_count, number):
+def reduce_all(items, values, weights, lat_lanes, shift_lanes, mixer, rest, lat_count, number):
     chunks, views = [], []
     for index, item in enumerate(items):
         rows, columns = item.shape[-2:]
-        lead = item.shape[:-2]
-        item = item.reshape((-1, 4, 2, 2, rows // 16, columns))
-        if not lead:
-            views.append(item[0])
-            for offset in range(0, columns // 2, CHUNK):
-                chunks.append(((index, None, offset), (index, None, columns // 2 + offset)))
-            continue
-        views.append(item)
-        for first in range(0, item.shape[0], 2):
+        views.append(item.reshape((-1, 4, 2, 2, rows // 16, columns)))
+        for first in range(0, views[index].shape[0], 2):
             for offset in range(0, columns, CHUNK):
                 chunks.append(((index, first, offset), (index, first + 1, offset)))
+    count = len(views)
+    half = weights[0].shape[-1]
+    for offset in range(0, half, CHUNK):
+        chunks.append(((count, None, offset), (count, None, half + offset)))
+    chunks.append(((count + 1, 0, 0), (count + 1, 1, 0)))
+    total = len(chunks)
     rows = views[0].shape[-2]
-    var_count = grads.shape[1] // 4
+    probs = mixer[1]
+    head_count, var_count, tokens = probs.shape
+    padded = mixer[0].shape[0]
+    model = head_count * HEAD_DIM
     lanes = 2 * lat_lanes.shape[1]
     columns = lat_lanes.shape[1]
+    cut = (4, 4 * var_count, 128)
     vmem = pl.BlockSpec(memory_space=pltpu.VMEM)
     hbm = pl.BlockSpec(memory_space=pl.ANY)
-    count, total = len(views), len(chunks)
     sem = pltpu.SemaphoreType.DMA
     return pl.pallas_call(
         partial(reduce_kernel, chunks, count),
@@ -913,11 +1051,11 @@
             jax.ShapeDtypeStruct((4,) + values.shape[2:], values.dtype),
             jax.ShapeDtypeStruct((lat_count, var_count, columns), wide),
         ],
-        in_specs=[hbm] * (count + 2) + [vmem] * 2,
+        in_specs=[hbm] * (count + 3) + [vmem] * (2 + len(mixer) + len(rest)),
         out_specs=[vmem, hbm, vmem],
         scratch_shapes=reducer_scratch(total, rows)
         + [
-            pltpu.VMEM((4,) + grads.shape[1:], wide),
+            pltpu.VMEM(cut, wide),
             pltpu.VMEM((lat_count, var_count, lanes), wide),
             pltpu.VMEM((8, lat_count * var_count), wide),
             pltpu.VMEM((8, lat_count * var_count), wide),
@@ -928,116 +1066,28 @@
             sem((4,)),
             sem((2,)),
             sem((2,)),
+            pltpu.VMEM((2,) + cut[1:], wide),
+            pltpu.VMEM((model, padded), low),
+            pltpu.VMEM((head_count, padded), wide),
+            pltpu.VMEM((padded, tokens), wide),
+            pltpu.VMEM(weights[0].shape, low),
+            pltpu.VMEM(weights[0].shape, low),
+            pltpu.VMEM((model, padded), low),
+            pltpu.VMEM((head_count, 128), wide),
+            pltpu.VMEM((4, 2, 2, rows, 2 * half), low),
+            pltpu.VMEM((2, 4, 2, 2, rows, CHUNK), low),
+            sem((2,)),
         ],
         compiler_params=pltpu.CompilerParams(
             collective_id=number, has_side_effects=True, vmem_limit_bytes=60 * 2**20
         ),
-    )(*views, values, grads, lat_lanes, shift_lanes)
+    )(*views, values, *weights, lat_lanes, shift_lanes, *mixer, *rest)
 
 
 def diagonal(var_count, columns):
     column = lax.broadcasted_iota(jnp.int32, (var_count, columns), 1)
     row = lax.broadcasted_iota(jnp.int32, (var_count, columns), 0)
     return (lax.rem(column, var_count) == row) & (column < 5 * var_count)
-
-
-def patch_kernel(field_ref, lat_ref, shift_ref, patch_ref):
-    lat_count, var_count, _ = field_ref.shape
-    row_count, lanes = lat_ref.shape
-    slots = lanes // 2
-    for r in range(row_count):
-        lat = lat_ref[r : r + 1, :]
-        west = shift_ref[r : r + 1, :] < 0
-
-        def body(b, carry):
-            top, bottom = carry
-            wide_row = field_ref[b].astype(wide)
-            chosen = jnp.where(west, wide_row[:, :lanes], wide_row[:, lanes:])
-            return (jnp.where(lat == b, chosen, top), jnp.where(lat == b - 1, chosen, bottom))
-
-        zero = jnp.zeros((var_count, lanes), wide)
-        rows = lax.fori_loop(0, lat_count, body, (zero, zero), unroll=4)
-        for py in range(2):
-            for px in range(2):
-                k = 2 * py + px
-                patch_ref[r, k * var_count : (k + 1) * var_count, :] = rows[py][
-                    :, px * slots : (px + 1) * slots
-                ].astype(low)
-
-
-def cut_patches(field, lat_lanes, shift_lanes):
-    row_count, lanes = lat_lanes.shape
-    return pl.pallas_call(
-        patch_kernel,
-        out_shape=jax.ShapeDtypeStruct((row_count, 4 * field.shape[1], lanes // 2), low),
-    )(field, lat_lanes, shift_lanes)
-
-
-def mixer_backward_kernel(
-    patch_ref,
-    prob_ref,
-    score_ref,
-    value_ref,
-    grad_ref,
-    pooled_ref,
-    count_ref,
-    cut_ref,
-    patch_grad_ref,
-):
-    head_count, var_count, _ = prob_ref.shape
-    padded, tokens = patch_ref.shape
-    rest = padded - 5 * var_count
-    mask = diagonal(var_count, padded)
-    patch_grad_ref[...] = jnp.zeros_like(patch_grad_ref)
-
-    def head_step(h, carry):
-        start = pl.multiple_of(h * HEAD_DIM, HEAD_DIM)
-        grads = grad_ref[pl.ds(start, HEAD_DIM), :]
-        prob = prob_ref[h]
-        back = dot(value_ref[pl.ds(start, HEAD_DIM), :], grads, 0, 0)
-        pieces = [patch_ref[k * var_count : (k + 1) * var_count, :].astype(wide) for k in range(5)]
-        backs = [back[k * var_count : (k + 1) * var_count, :] for k in range(5)]
-        prob_grad = pieces[0] * backs[0]
-        for k in range(1, 5):
-            prob_grad = prob_grad + pieces[k] * backs[k]
-        mean = jnp.sum(prob * prob_grad, axis=0, keepdims=True)
-        delta = prob * (prob_grad - mean)
-        upper = delta.astype(low)
-        lower = (delta - upper.astype(wide)).astype(low)
-        spread = jnp.where(mask, score_ref[pl.ds(h, 1), :], 0.0).astype(low)
-        patch_grad_ref[...] += dot(spread, upper, 0, 0)
-        for k in range(4):
-            patch_grad_ref[k * var_count : (k + 1) * var_count, :] += prob * backs[k]
-        patch = patch_ref[...]
-        counts = dot(upper, patch, 1, 1) + dot(lower, patch, 1, 1)
-        count_ref[pl.ds(h, 1), :] = jnp.sum(jnp.where(mask, counts, 0.0), axis=0, keepdims=True)
-        pooled = jnp.concatenate(
-            [(prob * piece).astype(low) for piece in pieces] + [jnp.zeros((rest, tokens), low)],
-            axis=0,
-        )
-        pooled_ref[pl.ds(start, HEAD_DIM), :] = dot(grads, pooled, 1, 1)
-        return carry
-
-    lax.fori_loop(0, head_count, head_step, 0)
-    parts, taps, width = cut_ref.shape
-    for part in range(parts):
-        cut_ref[part] = patch_grad_ref[:taps, part * width : (part + 1) * width]
-
-
-def mixer_backward(patches, probs, score_table, value_table, mixed_grads):
-    head_count, padded = score_table.shape
-    var_count = probs.shape[1]
-    tokens = patches.shape[1]
-    return pl.pallas_call(
-        mixer_backward_kernel,
-        out_shape=[
-            jax.ShapeDtypeStruct((head_count * HEAD_DIM, padded), wide),
-            jax.ShapeDtypeStruct((head_count, padded), wide),
-            jax.ShapeDtypeStruct((2, 4 * var_count, tokens // 2), wide),
-        ],
-        scratch_shapes=[pltpu.VMEM((padded, tokens), wide)],
-        compiler_params=pltpu.CompilerParams(vmem_limit_bytes=40 * 2**20),
-    )(patches, probs, score_table, value_table, mixed_grads)
 
 
 def head_lanes(values, h):
@@ -1443,9 +1493,16 @@
     )
 
 
+def columns_of(shape, axis, half):
+    spot = lax.broadcasted_iota(jnp.int32, shape, axis)
+    side, spot = lax.div(spot, half), lax.rem(spot, half)
+    slots = half // 2
+    return 2 * lax.rem(spot, slots) + 2 * side + lax.div(spot, slots) - 1
+
+
 def front_kernel(items, *refs):
     arrays, refs = refs[:8], refs[8:]
-    cut_in, grad_in, hour_ref, refs = refs[0], refs[1], refs[2], refs[3:]
+    grad_in, hour_ref, pixel_ref, lat_ref, shift_ref, refs = refs[:5] + (refs[5:],)
     outs, grad_out, received, refs = refs[:8], refs[8], refs[9], refs[10:]
     joint, wide_ref, total_ref, tag_ref, crop_ref, refs = refs[:5] + (refs[5:],)
     patch_ref, prob_ref, mixed_ref, value_table, key_table, score_table, refs = refs[:6] + (
@@ -1458,10 +1515,15 @@
         :8
     ] + (refs[8:],)
     gather_sems, refs = refs[:5], refs[5:]
-    post_send, post_recv, load_sem, own_sem, send_sem, recv_sem, out_own, out_send, out_recv = refs
+    post_send, post_recv, load_sem, own_sem, send_sem, recv_sem, out_own, refs = refs[:7] + (
+        refs[7:],
+    )
+    out_send, out_recv, cut_in, cut_rows, field, edge, west_edge, east_edge, edge_send, edge_recv = refs
     x, z, y, c = position()
     across, line = partners(x, z, y, c)
-    own = (z * 4 + y * 2 + c, x)
+    lon = z * 4 + y * 2 + c
+    own = (lon, x)
+    east, west = (lax.rem(lon + 1, 16), x), (lax.rem(lon + 15, 16), x)
     me = y * 4 + c * 2 + x
     peers, kinds, share, lanes = joint.shape
     slots = peers * share
@@ -1478,7 +1540,7 @@
         there_x = 1 - x if flip & 1 else x
         everyone.append((z * 4 + there_y * 2 + there_c, there_x))
     sources = [sector_of(z, y, c, x, part, side) for part in range(2) for side in range(2)]
-    meet(everyone, sources, own)
+    meet(everyone + [east, west], sources, own)
     letters = []
     for part in range(2):
         row = 2 * x + part
@@ -1491,8 +1553,64 @@
             (grad_in.at[row], grad_out.at[x, c], post_send.at[2 + row])
             + (post_recv.at[2 + 2 * x + c], block_of(z, y, row), own)
         )
-    for letter in letters:
+    for letter in letters[2:]:
         post(*letter)
+    var_total, lat_count, column_count = pixel_ref.shape
+    half = lat_ref.shape[1]
+
+    def edge_copies():
+        return [
+            remote(edge, west_edge, edge_send.at[0], edge_recv.at[0], east),
+            remote(edge, east_edge, edge_send.at[1], edge_recv.at[1], west),
+        ]
+
+    def send_edges():
+        kind = lax.broadcasted_iota(jnp.int32, (16, column_count), 0)
+        column = lax.broadcasted_iota(jnp.int32, (16, column_count), 1)
+        pick = jnp.where(column == kind * (column_count - 1), 1.0, 0.0).astype(low)
+        flat = pixel_ref[...].reshape(var_total * lat_count, column_count)
+        edge[...] = dot(pick, flat, 1, 1).astype(low)
+        for copy in edge_copies():
+            copy.start()
+
+    def make_field():
+        for copy in edge_copies():
+            copy.wait()
+        wanted = columns_of((column_count, 2 * half), 1, half)
+        column = lax.broadcasted_iota(jnp.int32, (column_count, 2 * half), 0)
+        select = jnp.where(wanted == column, 1.0, 0.0).astype(low)
+        kind = lax.broadcasted_iota(jnp.int32, (16, 2 * half), 0)
+        wanted = columns_of((16, 2 * half), 1, half)
+        from_west = jnp.logical_and(kind == 1, wanted == -1)
+        from_east = jnp.logical_and(kind == 0, wanted == column_count)
+        flat = pixel_ref[...].reshape(var_total * lat_count, column_count)
+        result = dot(flat, select)
+        for values, place in ((west_edge, from_west), (east_edge, from_east)):
+            result = result + dot(values[...], jnp.where(place, 1.0, 0.0).astype(low), 0, 0)
+        field[...] = result.astype(low).reshape(field.shape)
+
+    def cut_row(part):
+        lat = jnp.where(x == 0, lat_ref[part : part + 1, :], lat_ref[part + 2 : part + 3, :])
+        shift = jnp.where(x == 0, shift_ref[part : part + 1, :], shift_ref[part + 2 : part + 3, :])
+        row = lax.broadcasted_iota(jnp.int32, (lat_count, half), 0)
+        slots = half // 2
+
+        def body(v, carry):
+            values = field[v].astype(wide)
+            chosen = jnp.where(shift < 0, values[:, :half], values[:, half:])
+            for py in range(2):
+                taken = jnp.sum(jnp.where(row == lat + py, chosen, 0.0), axis=0, keepdims=True)
+                for px in range(2):
+                    spot = pl.ds((2 * py + px) * var_total + v, 1)
+                    cut_rows[part, spot, :] = taken[:, px * slots : (px + 1) * slots]
+            return carry
+
+        lax.fori_loop(0, var_total, body, 0)
+
+    def send_cut():
+        cut_in[...] = cut_rows[...].astype(low)
+        for letter in letters[:2]:
+            post(*letter)
 
     def views(number):
         index, lead, first, rows, color = items[number]
@@ -1711,7 +1829,8 @@
     for number, item in enumerate(items):
         ready[item[:2]] = number + 8
     at = ready[(3, None)]
-    extra = {at: [ask_small, read_small], at + 1: [score]}
+    extra = {0: [send_edges], 3: [make_field], 4: [partial(cut_row, 0)], 5: [partial(cut_row, 1)]}
+    extra.update({6: [send_cut], at: [ask_small, read_small], at + 1: [score]})
     extra[at + 2] = [lambda: tables(weight_b, 3, value_table), ask_back]
     for quarter in range(4):
         extra.setdefault(at + 3 + quarter // 2, []).append(partial(heads, 4 * quarter))
@@ -1749,7 +1868,7 @@
     last.wait()
 
 
-def front(arrays, cut, grads, hours, head_count, number):
+def front(arrays, grads, hours, pixels, lat_lanes, shift_lanes, head_count, number):
     items = []
     for index, array in enumerate(arrays):
         for lead in range(array.shape[0]) if array.ndim == 3 else (None,):
@@ -1761,8 +1880,9 @@
                 items.append((index, lead, color * rows // 2, rows // 2, color))
     width = arrays[2].shape[1]
     model = 2 * width
-    var_count = cut.shape[1] // 4
-    tokens = 2 * cut.shape[2]
+    var_count, lat_count = pixels.shape[:2]
+    tokens = lat_lanes.shape[1]
+    cut_shape = (2, 4 * var_count, tokens // 2)
     padded = 2 * arrays[1].shape[1]
     slots = 8 * tokens
     sem = pltpu.SemaphoreType.DMA
@@ -1798,10 +1918,10 @@
         partial(front_kernel, items),
         out_shape=[jax.ShapeDtypeStruct(shape, low) for shape in low_outs]
         + [jax.ShapeDtypeStruct(shape, dtype) for shape, dtype in vmem_outs],
-        in_specs=[hbm] * (len(arrays) + 2) + [vmem],
+        in_specs=[hbm] * (len(arrays) + 1) + [vmem] * 4,
         out_specs=[hbm] * len(low_outs) + [vmem] * len(vmem_outs),
         scratch_shapes=[
-            pltpu.VMEM(cut.shape, low),
+            pltpu.VMEM(cut_shape, low),
             pltpu.VMEM(all_of(arrays[0]), low),
             pltpu.VMEM(all_of(arrays[1]), low),
             pltpu.VMEM(all_of(arrays[2]), low),
@@ -1812,11 +1932,21 @@
             sem((len(items),)),
         ]
         + [sem((len(items), 3))] * 4
-        + [sem((6,)), sem((6,)), sem((4,)), sem, sem((8,)), sem((8,)), sem, sem((8,)), sem((8,))],
+        + [sem((6,)), sem((6,)), sem((4,)), sem, sem((8,)), sem((8,)), sem, sem((8,)), sem((8,))]
+        + [
+            pltpu.VMEM(cut_shape, low),
+            pltpu.VMEM(cut_shape, wide),
+            pltpu.VMEM((var_count, lat_count, 2 * tokens), low),
+            pltpu.VMEM((16, var_count * lat_count), low),
+            pltpu.VMEM((16, var_count * lat_count), low),
+            pltpu.VMEM((16, var_count * lat_count), low),
+            sem((2,)),
+            sem((2,)),
+        ],
         compiler_params=pltpu.CompilerParams(
             collective_id=number, has_side_effects=True, vmem_limit_bytes=58 * 2**20
         ),
-    )(*arrays, cut, grads, hours)
+    )(*arrays, grads, hours, pixels, lat_lanes, shift_lanes)
     count = len(arrays)
     gathered = [
         g.reshape(a.shape[:-2] + (2, 16 * a.shape[-2], a.shape[-1]))
@@ -2140,31 +2270,8 @@
     pairs = half_width // 128
     scale = HEAD_DIM ** (-0.5)
 
-    last = lax.slice_in_dim(pixels, column_count - 1, column_count, axis=2)
-    up = [(i, (i + 1) % LON_SIZE) for i in range(LON_SIZE)]
-    down = [(j, i) for i, j in up]
-    before = lax.ppermute(last, LON, up)
-    after = lax.ppermute(pixels[:, :, :1], LON, down)
-    lat_slot = crop_lookup(crop_starts, slot_crops)
-    shift_slot = crop_lookup(crop_shifts, slot_crops)
-    lat_lanes = jnp.tile(lat_slot, (1, 2))
-    shift_lanes = jnp.tile(shift_slot, (1, 2))
-    wanted = jnp.arange(2 * 2 * slot_width)
-    side, wanted = wanted // (2 * slot_width), wanted % (2 * slot_width)
-    wanted = 2 * (wanted % slot_width) + 2 * side + wanted // slot_width - 1
-    select = (jnp.arange(column_count)[:, None] == wanted[None, :]).astype(low)
-    field = einsum("vac,cn->avn", pixels, select)
-    field = field + jnp.where(wanted == -1, jnp.transpose(before, (1, 0, 2)).astype(wide), 0.0)
-    field = field + jnp.where(
-        wanted == column_count, jnp.transpose(after, (1, 0, 2)).astype(wide), 0.0
-    )
-    field = field.astype(low)
-    pair_rows = row_count // HEAD_SIZE
-    cut = cut_patches(
-        field,
-        block_slice(lat_lanes, head, pair_rows, 0),
-        block_slice(shift_lanes, head, pair_rows, 0),
-    )
+    lat_lanes = jnp.tile(crop_lookup(crop_starts, slot_crops), (1, 2))
+    shift_lanes = jnp.tile(crop_lookup(crop_shifts, slot_crops), (1, 2))
     masked = cotangent * occupied[:, :, None].astype(low)
     masked = jnp.pad(masked, ((0, 0), (0, 0), (0, 128 - out_half)))
     late = jnp.concatenate(
@@ -2178,12 +2285,16 @@
         [
             jnp.transpose(patch_weight, (1, 0, 2)).reshape(taps, slice_width),
             variable_embed,
-            lead_embed,
-            first_gain[None],
-            first_bias[None],
-            second_gain[None],
-            second_bias[None],
-            jnp.zeros((padded - taps - var_count - 6, slice_width), low),
+            jnp.concatenate(
+                [
+                    lead_embed.reshape(-1),
+                    first_gain,
+                    first_bias,
+                    second_gain,
+                    second_bias,
+                    jnp.zeros(((padded - taps - var_count - 6) * slice_width,), low),
+                ]
+            ).reshape(-1, slice_width),
         ]
     ).T
     small = jnp.concatenate([small[:, :128], small[:, 128:]])
@@ -2207,9 +2318,11 @@
             out_block,
             late,
         ],
-        cut,
         masked,
         hours,
+        pixels,
+        lat_lanes,
+        shift_lanes,
         head_count,
         1,
     )
@@ -2219,7 +2332,7 @@
     patch_full, vectors, query, start_sum, first_low, lead_column, keep_mask = made[13:]
     masked = masked.reshape(HEAD_SIZE, tokens, 128)
     attended = attended[None]
-    query = query[:, :HEAD_DIM]
+    query_wide, query = query, query[:, :HEAD_DIM]
     bias_rows = expand_bias.shape[0]
     up_bias = misc_all.reshape(HEAD_SIZE, LON_SIZE, -1, 128)[:, :, 2 * row_count + head_half :]
     up_bias = jnp.sum(up_bias[..., : LON_SIZE * query_width].astype(wide), axis=1)
@@ -2265,67 +2378,30 @@
         mixer_weight,
         mixed,
     )
-    pooled_grads, counts, cut_grads = mixer_backward(
-        patches, probs, score_table, value_table, mixed_grads
-    )
-    counts = counts * scale
-    pooled_low = pooled_grads.astype(low)
-    grad_values = dot(patch_full, pooled_low, 1, 1).astype(low)
-    key_low = (query[:, :, None] * counts[:, None, :]).astype(low).reshape(model, padded)
-    grad_small = einsum(
-        "xde,xem->dm", key_weight, key_low.reshape(HEAD_SIZE, half_width, padded)
-    ) + einsum("xde,xem->dm", value_weight, pooled_low.reshape(HEAD_SIZE, half_width, padded))
-    head_sums = einsum("dm,hm->dh", patch_full.astype(wide), counts)
-    grad_query = jnp.sum(
-        key_table.reshape(head_count, HEAD_DIM, padded) * counts[:, None, :], axis=2
-    )
-
-    vector_grads = jnp.concatenate([first_vectors, second_vectors]).T
-    spot = taps + var_count
-    grad_small = jnp.concatenate(
-        [grad_small[:, :spot], vector_grads, jnp.zeros((model, padded - spot - 6), wide)], axis=1
-    )
-    grad_small = jnp.transpose(
-        grad_small.reshape(LON_SIZE, HEAD_SIZE, slice_width, 2, 128), (0, 3, 2, 1, 4)
-    ).reshape(model, HEAD_SIZE, 128)
-    head_block = head_sums.reshape(model, HEAD_SIZE, head_half)
     bias_cols = expand_bias.shape[1]
     bias_block = jnp.transpose(
-        grad_up_bias.reshape(HEAD_SIZE, bias_rows, LON_SIZE, bias_cols), (2, 1, 0, 3)
-    )
+        grad_up_bias.reshape(HEAD_SIZE, bias_rows, LON_SIZE, bias_cols), (0, 2, 1, 3)
+    )
+    bias_at = out_half + head_half
     bias_block = jnp.pad(
-        bias_block, ((0, 0), (0, block_rows - bias_rows), (0, 0), (0, 0))
-    ).reshape(model, HEAD_SIZE, bias_cols)
-    query_block = jnp.transpose(
-        grad_query.reshape(HEAD_SIZE, head_half, LON_SIZE, query_width), (2, 1, 0, 3)
-    )
-    query_block = jnp.pad(
-        query_block, ((0, 0), (0, block_rows - head_half), (0, 0), (0, 0))
-    ).reshape(model, HEAD_SIZE, query_width)
-    extra = head_half + bias_cols + query_width
-    filler = jnp.zeros((model, 128 - out_half - extra), wide)
-    tail = jnp.stack(
-        [
-            jnp.concatenate(
-                [
-                    grad_small[:, side],
-                    grad_out[side, :, :out_half].astype(wide),
-                    head_block[:, side],
-                    bias_block[:, side],
-                    query_block[:, side],
-                    filler,
-                ],
-                axis=1,
-            )
-            for side in range(2)
-        ]
-    ).astype(low)
+        bias_block,
+        (
+            (0, 0),
+            (0, 0),
+            (0, block_rows - bias_rows),
+            (bias_at, 128 - bias_at - bias_cols),
+        ),
+    ).reshape(HEAD_SIZE, model, 128)
+    rest = grad_out + bias_block.astype(low)
+    spot = taps + var_count
     sums, predicted, pixel_grad = reduce_all(
-        [grad_proj, grad_input, grad_mixer, grad_values, tail],
+        [grad_proj, grad_input, grad_mixer],
         predicted.reshape(HEAD_SIZE, 2, slot_width, 128),
-        cut_grads,
+        (key_weight, value_weight),
         lat_lanes,
         shift_lanes,
+        (patches, probs, score_table, value_table, key_table, mixed_grads),
+        (patch_full, query_wide, first_vectors, second_vectors, rest),
         lat_count,
         2,
     )

time: 506 us -> 489 us (0.966)
  local copies, waits for them, and re-layouts: 30 us -> 22.6 us
  matrix products: 5.87 us -> 0 us
  starting transfers between devices: 5.52 us -> 0 us
    pallas_call x1, Pallas kernels: 84.5 us -> 96.3 us  [reduce_all(): pl.pallas_call(partial(reduce_kernel, chunks, count), out_shape=[jax.Shap...]
    pallas_call x2 -> x0, Pallas kernels: 11.5 us -> none  [the longest x1 8.65 us: mixer_backward(): pl.pallas_call(mixer_backward_kernel, out_shape=[jax.ShapeDtypeStruct((he...]
    dot_general x5 -> x0, matrix products: 5.87 us -> none  [the longest x4 3.75 us: einsum(): return jnp.einsum(spec, left, right, preferred_element_type=wide)]
    ppermute x2 -> x0, starting transfers between devices: 5.52 us -> none  [the longest x1 5.48 us: fast_local(): after = lax.ppermute(pixels[:, :, :1], LON, down)]
  transfers between devices with their start and end apart: 2 -> 0, of which waited for: 0 -> 0; matrix products, arithmetic and copies ran while one was open for 2% -> 0% of each run, Pallas kernels for 0% -> 0%
where the time goes in v5:
time: 489 us; the launch traced here: 484 us
  Pallas kernels  448 us (92%)
  local copies, waits for them, and re-layouts  22.6 us (5%)
  other arithmetic  11.4 us (2%)
    pallas_call x1, Pallas kernels, front(): pl.pallas_call(partial(front_kernel, items), out_shape=[jax.ShapeDtypeStr...  191 us
    pallas_call x1, Pallas kernels, attend_back(): pl.pallas_call(attend_back_kernel, out_shape=[jax.ShapeDtypeStruct(joint....  113 us
    pallas_call x1, Pallas kernels, reduce_all(): pl.pallas_call(partial(reduce_kernel, chunks, count), out_shape=[jax.Shap...  96.3 us
    pallas_call x1, Pallas kernels, feed(): pl.pallas_call(feed_kernel, grid=(2 * count,), out_shape=[shape for shape...  34.7 us
    pallas_call x1, Pallas kernels, go_back(): pl.pallas_call(return_kernel, grid=(kinds * halves,), out_shape=[jax.Shap...  12.9 us

profile of v5, /device:TPU:0, one launch (start us, length us, event | category | flops | bytes accessed | tf_op | source)
XLA Modules:
  0.0 483.8 jit_solution(5239291428065176495)
XLA Ops:
  0.8 0.8 convert_multiply_fusion
  2.1 0.8 pad_maximum_fusion.4
  2.9 0.8 fusion.3
  4.3 0.8 select_reduce_fusion
  6.3 1.1 bitcast_bitcast_fusion
  7.4 1.7 pad_maximum_fusion.refs_7_
  9.4 0.7 pad.18.refs_8_
  11.9 191.3 %shard_map.375 = (bf16[2,4,2,2,48,128]{5,4,3,2,1,0:T(8,128)(2,1)}, bf16[2,4,2,2,64,128]{5,4,3,2,1,0:T(8,128)(2,1)}, bf16[2,4,2,2,64,512]{5,4,3,2,1,0:T(8,128)(2,...) custom-call(bf16[48,128]{1,0:T(8,128)(2,1)} %pad_maximum_fusion.3.re, ...), custom_call_target="tpu_custom_call" | custom-call | tf_op jit(solution)/shard_map/pallas_call | solution.py:1917
  203.2 1.0 convert_reduce_fusion
  204.3 0.7 reshape.133.bias_ref
  204.9 34.7 %shard_map.376 = (bf16[2,256,128]{2,1,0:T(8,128)(2,1)}, f32[256,1024]{1,0:T(8,128)}, bf16[1,8,256,128]{3,2,1,0:T(8,128)(2,1)}, bf16[2,2,1024,2048]{3,2,1,0:T(8,1...) custom-call(bf16[1,8,256,128]{3,2,1,0:T(8,128)(2,1)} %bitcast.89, ...), custom_call_target="tpu_custom_call" | custom-call | tf_op jit(solution)/shard_map/pallas_call | solution.py:2107
  239.6 0.8 convert_reduce_fusion.1
  241.2 1.9 bitcast_add_fusion.refs_18_
  243.2 113.1 %shard_map.377 = (bf16[8,3,256,128]{3,2,1,0:T(8,128)(2,1)}, f32[64,4096]{1,0:T(8,128)}) custom-call(bf16[8,3,256,128]{3,2,1,0:T(8,128)(2,1)} %get-tuple-element.72.joint, f32[8,2048]{1,0:T(8,128)} %get-tuple-element.73.tag_ref, f32[2048,1]{1,0:T(8,128)} %get-tuple-element.74.crop_ref, f32[2048,128]{1,0:T(8,128)} %get-tuple-element.75.out_ref, ...), custom_call_target="tpu_custom_call" | custom-call | tf_op jit(solution)/shard_map/pallas_call | solution.py:1433
  356.4 12.9 %shard_map.378 = (bf16[3,2,1024,512]{3,2,1,0:T(8,128)(2,1)}, bf16[2,1024,512]{2,1,0:T(8,128)(2,1)}, bf16[1024,256]{1,0:T(8,128)(2,1)S(1)}, f32[4,1024]{1,0:T(4,128)S(1)}) custom-call(bf16[1,8,3,256,128]{4,3,2,1,0:T(8,128)(2,1)} %bitcast.84, bf16[3,2,1024,512]{3,2,1,0:T(8,128)(2,1)} %bitcast.78, bf16[256,1024]{1,0:T(8,128)(2,1)S(1)} %copy-done.3, ...), custom_call_target="tpu_custom_call" | custom-call | tf_op jit(solution)/shard_map/pallas_call | solution.py:2196
  369.3 0.8 copy-done.4
  370.7 96.3 %shard_map.379 = (f32[64,3328]{1,0:T(8,128)}, bf16[4,128,128]{2,1,0:T(8,128)(2,1)}, f32[32,48,256]{2,1,0:T(8,128)}) custom-call(bf16[2,4,2,2,64,512]{5,4,3,2,1,0:T(8,128)(2,1)} %bitcast.82, bf16[6,4,2,2,64,512]{5,4,3,2,1,0:T(8,128)(2,1)} %bitcast.77, bf16[2,4,2,2,64,512]{5,4,3,2,1,0:T(8,128)(2,1)} %bitcast.83, bf16[2,2,128,128]{3,2,1,0:T(8,128)(2,1)} %bitcast.94, ...), custom_call_target="tpu_custom_call" | custom-call | tf_op jit(solution)/shard_map/pallas_call | solution.py:1047
  467.0 2.1 slice_bitcast_fusion.1
  469.0 0.8 pad_maximum_fusion.1
  469.8 0.8 slice.97
  471.0 0.7 broadcast_multiply_fusion
  471.7 0.7 fusion.1
  473.9 0.7 slice.118
  474.5 0.7 slice_reduce_fusion
  475.3 2.1 copy.75
  477.3 0.7 copy.74
  478.1 1.4 slice.113
  479.5 0.8 slice.111
  480.3 0.7 copy.78
  480.9 0.7 slice.96
  481.7 0.7 copy.76
  482.3 1.0 slice_bitcast_fusion
  (75 shorter events, 7.8 us)
Async XLA Ops:
  0.7 8.5 %copy-start.11 = (bf16[4,128,96]{1,2,0:T(8,128)(2,1)S(1)}, bf16[4,128,96]{1,2,0:T(8,128)(2,1)}, u32[]{:S(2)}) copy-start(bf16[4,128,96]{1,2,0:T(8,128)(2,1)} %param.47) | copy-start | bytes 294916
  0.7 9.4 %copy-start.12 = (bf16[48,4,32]{0,2,1:T(8,128)(2,1)S(1)}, bf16[48,4,32]{0,2,1:T(8,128)(2,1)}, u32[]{:S(2)}) copy-start(bf16[48,4,32]{0,2,1:T(8,128)(2,1)} %param.30) | copy-start | bytes 36868
  0.7 9.5 %copy-start.20 = (bf16[2,32]{1,0:T(2,128)(2,1)S(1)}, bf16[2,32]{1,0:T(2,128)(2,1)}, u32[]{:S(2)}) copy-start(bf16[2,32]{1,0:T(2,128)(2,1)} %param.36) | copy-start | bytes 388
  0.7 9.6 %copy-start.16 = (bf16[32]{0:T(256)(128)(2,1)S(1)}, bf16[32]{0:T(256)(128)(2,1)}, u32[]{:S(2)}) copy-start(bf16[32]{0:T(256)(128)(2,1)} %param.37) | copy-start | bytes 196
  0.7 9.6 %copy-start.17 = (bf16[32]{0:T(256)(128)(2,1)S(1)}, bf16[32]{0:T(256)(128)(2,1)}, u32[]{:S(2)}) copy-start(bf16[32]{0:T(256)(128)(2,1)} %param.38) | copy-start | bytes 196
  0.7 9.6 %copy-start.18 = (bf16[32]{0:T(256)(128)(2,1)S(1)}, bf16[32]{0:T(256)(128)(2,1)}, u32[]{:S(2)}) copy-start(bf16[32]{0:T(256)(128)(2,1)} %param.41) | copy-start | bytes 196
  0.7 9.6 %copy-start.19 = (bf16[32]{0:T(256)(128)(2,1)S(1)}, bf16[32]{0:T(256)(128)(2,1)}, u32[]{:S(2)}) copy-start(bf16[32]{0:T(256)(128)(2,1)} %param.42) | copy-start | bytes 196
  0.7 9.9 %copy-start.15 = (bf16[48,32]{0,1:T(8,128)(2,1)S(1)}, bf16[48,32]{0,1:T(8,128)(2,1)}, u32[]{:S(2)}) copy-start(bf16[48,32]{0,1:T(8,128)(2,1)} %param.31) | copy-start | bytes 9220
  0.7 10.6 %copy-start.14 = (bf16[64,96]{1,0:T(8,128)(2,1)S(1)}, bf16[64,96]{1,0:T(8,128)(2,1)}, u32[]{:S(2)}) copy-start(bf16[64,96]{1,0:T(8,128)(2,1)} %param.46) | copy-start | bytes 36868
  243.1 113.2 %copy-start = (f32[256,1024]{1,0:T(8,128)S(1)}, f32[256,1024]{1,0:T(8,128)}, u32[]{:S(2)}) copy-start(f32[256,1024]{1,0:T(8,128)} %get-tuple-element.65.start_ref) | copy-start | bytes 3145732
  243.1 113.2 %copy-start.1 = (f32[256,1024]{1,0:T(8,128)S(1)}, f32[256,1024]{1,0:T(8,128)}, u32[]{:S(2)}) copy-start(f32[256,1024]{1,0:T(8,128)} %get-tuple-element.82.middle_grad_ref) | copy-start | bytes 3145732
  243.1 113.2 %copy-start.2 = (bf16[1024,256]{1,0:T(8,128)(2,1)S(1)}, bf16[1024,256]{1,0:T(8,128)(2,1)}, u32[]{:S(2)}) copy-start(bf16[1024,256]{1,0:T(8,128)(2,1)} %get-tuple-element.85.mixed_ref) | copy-start | bytes 1572868
  243.1 113.2 %copy-start.3 = (bf16[256,1024]{1,0:T(8,128)(2,1)S(1)}, bf16[256,1024]{1,0:T(8,128)(2,1)}, u32[]{:S(2)}) copy-start(bf16[256,1024]{1,0:T(8,128)(2,1)} %get-tuple-element.81.low_ref) | copy-start | bytes 1572868
  243.1 113.2 %copy-start.5 = (f32[256,1]{1,0:T(8,128)S(1)}, f32[256,1]{1,0:T(8,128)}, u32[]{:S(2)}) copy-start(f32[256,1]{1,0:T(8,128)} %get-tuple-element.83.lead_ref) | copy-start | bytes 3076
  243.2 113.2 %copy-start.6 = (f32[8,1024]{1,0:T(8,128)S(1)}, f32[8,1024]{1,0:T(8,128)}, u32[]{:S(2)}) copy-start(f32[8,1024]{1,0:T(8,128)} %get-tuple-element.66.vector_ref) | copy-start | bytes 98308
  369.3 0.8 copy-start.4
  370.1 0.6 copy-start.7
  466.9 4.0 copy-start.13
  466.9 8.3 %copy-start.8 = (f32[32,48,256]{2,1,0:T(8,128)S(1)}, f32[32,48,256]{2,1,0:T(8,128)}, u32[]{:S(2)}) copy-start(f32[32,48,256]{2,1,0:T(8,128)} %get-tuple-element.104) | copy-start | bytes 4718596
  470.8 6.6 %copy-start.10 = (bf16[4,128,128]{2,1,0:T(8,128)(2,1)S(1)}, bf16[4,128,128]{2,1,0:T(8,128)(2,1)}, u32[]{:S(2)}) copy-start(bf16[4,128,128]{2,1,0:T(8,128)(2,1)} %get-tuple-element.103) | copy-start | bytes 393220
  471.0 11.3 %copy-start.9 = (f32[64,4096]{1,0:T(8,128)S(1)}, f32[64,4096]{1,0:T(8,128)}, u32[]{:S(2)}) copy-start(f32[64,4096]{1,0:T(8,128)} %get-tuple-element.106) | copy-start | bytes 3145732

commit v6 on v5

--- a/solution.py
+++ b/solution.py
@@ -737,11 +737,13 @@
 
 def reduce_kernel(chunks, count, *refs):
     ins, refs = refs[:count], refs[count:]
-    value_in, key_weight, value_weight, lat_ref, shift_ref, refs = refs[:5] + (refs[5:],)
-    patch_ref, prob_ref, score_table, value_table, key_table, mixed_grad, refs = refs[:6] + (
+    value_in, key_weight, value_weight, input_weight, back_weight, refs = refs[:5] + (refs[5:],)
+    lat_ref, shift_ref, refs = refs[:2] + (refs[2:],)
+    patch_ref, prob_ref, score_table, value_table, key_table, mixed_ref, refs = refs[:6] + (
         refs[6:],
     )
-    full_ref, query_ref, first_ref, second_ref, rest_ref, refs = refs[:5] + (refs[5:],)
+    full_ref, query_ref, second_ref, rest_ref, bias_ref, refs = refs[:5] + (refs[5:],)
+    stacked_ref, low_ref, start_ref, middle_ref, vector_ref, lead_ref, refs = refs[:6] + (refs[6:],)
     out, value_out, pixel_out, refs = refs[:3] + (refs[3:],)
     buffers, sems, refs = refs[:6], refs[6:13], refs[13:]
     grad_out, field, edge, west_edge, east_edge, refs = refs[:5] + (refs[5:],)
@@ -749,8 +751,10 @@
         refs[6:],
     )
     grad_in, pooled_ref, count_ref, patch_grad, weight_a, weight_b, key_low, query_grad = refs[:8]
-    values_ref, tail_ref, load_sem = refs[8:]
-    ins = ins + (values_ref, tail_ref)
+    input_ref, mixer_ref, values_ref, tail_ref, load_sem, first_ref, mixed_grad, turned, total_ref = (
+        refs[8:]
+    )
+    ins = ins + (input_ref, mixer_ref, values_ref, tail_ref)
     x, z, y, c = position()
     across, line = partners(x, z, y, c)
     lon = z * 4 + y * 2 + c
@@ -774,12 +778,48 @@
     for letter in letters[1::2]:
         post(*letter)
     total = len(chunks)
-    loads = [
-        pltpu.make_async_copy(key_weight, weight_a, load_sem.at[0]),
-        pltpu.make_async_copy(value_weight, weight_b, load_sem.at[1]),
-    ]
-    for copy in loads:
-        copy.start()
+    weights = (weight_a, weight_b)
+    queue = [input_weight.at[0], input_weight.at[1], input_weight.at[2], back_weight]
+    queue += [key_weight, value_weight]
+
+    def load(number):
+        return pltpu.make_async_copy(queue[number], weights[number % 2], load_sem.at[number % 2])
+
+    load(0).start()
+    load(1).start()
+    half_width = weight_a.shape[-1]
+
+    def input_grads(kind):
+        if kind == 0:
+            turned[...] = low_ref[...].T
+            total_ref[...] = jnp.zeros_like(total_ref)
+        load(kind).wait()
+        pairs = half_width // stacked_ref.shape[-1]
+        for side in range(2):
+            piece = jnp.concatenate(
+                [stacked_ref[side * pairs + pair, kind] for pair in range(pairs)], axis=1
+            )
+            total_ref[...] += dot(piece, weights[kind % 2][side], 1, 1)
+            grads = dot(turned[...], piece).astype(low)
+            input_ref[2 * kind + side] = grads.reshape(input_ref.shape[1:])
+        load(kind + 2).start()
+
+    def start_grads():
+        part, grad_gain, grad_shift = norm_back(start_ref[...], vector_ref[2:3], total_ref[...])
+        result = middle_ref[...] + part
+        first_ref[0:1] = jnp.sum(result * lead_ref[...], axis=0, keepdims=True)
+        first_ref[1:2] = jnp.sum(result, axis=0, keepdims=True)
+        first_ref[2:3] = grad_gain
+        first_ref[3:4] = grad_shift
+        result_low = result.astype(low)
+        turned[...] = result_low.T
+        load(3).wait()
+        for side in range(2):
+            span = slice(side * half_width, (side + 1) * half_width)
+            grads = dot(turned[...], mixed_ref[span, :], 1, 1).astype(low)
+            mixer_ref[side] = grads.reshape(mixer_ref.shape[1:])
+            mixed_grad[span, :] = dot(result_low, weight_b[side]).astype(low).T
+        load(5).start()
     head_total, var_total, tokens = prob_ref.shape
     padded = patch_ref.shape[0]
     scale = HEAD_DIM ** (-0.5)
@@ -843,9 +883,8 @@
             values_ref[part] = piece.astype(low).reshape(values_ref.shape[1:])
 
     def tail_grads():
-        for copy in loads:
-            copy.wait()
-        half_width = weight_a.shape[-1]
+        load(4).wait()
+        load(5).wait()
         wide_query = jnp.concatenate([query_ref[...]] * (head_total * HEAD_DIM // 128), axis=1)
         head = lax.div(lax.broadcasted_iota(jnp.int32, wide_query.shape, 1), HEAD_DIM)
         row = lax.broadcasted_iota(jnp.int32, wide_query.shape, 0)
@@ -894,7 +933,7 @@
             inside = lax.div(head, head_half) == side
             target = jnp.where(jnp.logical_and(inside, lane == spot), 1.0, 0.0).astype(low)
             sums = sum(dot(part, target, 0, 0) for part in count_parts)
-            result = rest_ref[side].astype(wide)
+            result = rest_ref[side].astype(wide) + bias_ref[side]
             for part in halves_of(sums):
                 result = result + dot(full_ref[...], part)
             chosen = jnp.logical_and(inner < head_half, columns == inner + head_half * side)
@@ -991,10 +1030,12 @@
         lax.fori_loop(0, lat_count, body, 0)
 
     quarter = head_total // 4
-    extra = {step: partial(heads, step * quarter) for step in range(4)}
-    extra.update({4: send_cut, 5: value_grads, 6: tail_grads, 7: rest_grads})
-    extra.update({8 + row: partial(paste, row) for row in range(4)})
-    extra.update({12: edges, 15: pixels})
+    extra = {kind: partial(input_grads, kind) for kind in range(3)}
+    extra[3] = start_grads
+    extra.update({4 + step: partial(heads, step * quarter) for step in range(4)})
+    extra.update({8: lambda: (send_cut(), value_grads()), 9: tail_grads, 10: rest_grads})
+    extra.update({12 + row: partial(paste, row) for row in range(3)})
+    extra.update({15: lambda: (paste(3), edges()), 18: pixels})
 
     def source_of(pair, color, side, core):
         index, lead, offset = chunks[2 * pair + color][side]
@@ -1019,25 +1060,24 @@
         pltpu.make_async_copy(value_in.at[0, 0], value_out.at[row], value_recv.at[row]).wait()
 
 
-def reduce_all(items, values, weights, lat_lanes, shift_lanes, mixer, rest, lat_count, number):
-    chunks, views = [], []
-    for index, item in enumerate(items):
-        rows, columns = item.shape[-2:]
-        views.append(item.reshape((-1, 4, 2, 2, rows // 16, columns)))
-        for first in range(0, views[index].shape[0], 2):
-            for offset in range(0, columns, CHUNK):
+def reduce_all(item, values, weights, lat_lanes, shift_lanes, mixer, rest, block, lat_count, number):
+    chunks = []
+    model, half = item.shape[-2:]
+    views = [item.reshape((-1, 4, 2, 2, model // 16, half))]
+    kinds = weights[2].shape[0]
+    for index, leads in ((0, 1), (1, kinds), (2, 1)):
+        for first in range(0, 2 * leads, 2):
+            for offset in range(0, half, CHUNK):
                 chunks.append(((index, first, offset), (index, first + 1, offset)))
     count = len(views)
-    half = weights[0].shape[-1]
     for offset in range(0, half, CHUNK):
-        chunks.append(((count, None, offset), (count, None, half + offset)))
-    chunks.append(((count + 1, 0, 0), (count + 1, 1, 0)))
+        chunks.append(((3, None, offset), (3, None, half + offset)))
+    chunks.append(((4, 0, 0), (4, 1, 0)))
     total = len(chunks)
     rows = views[0].shape[-2]
     probs = mixer[1]
     head_count, var_count, tokens = probs.shape
     padded = mixer[0].shape[0]
-    model = head_count * HEAD_DIM
     lanes = 2 * lat_lanes.shape[1]
     columns = lat_lanes.shape[1]
     cut = (4, 4 * var_count, 128)
@@ -1051,7 +1091,7 @@
             jax.ShapeDtypeStruct((4,) + values.shape[2:], values.dtype),
             jax.ShapeDtypeStruct((lat_count, var_count, columns), wide),
         ],
-        in_specs=[hbm] * (count + 3) + [vmem] * (2 + len(mixer) + len(rest)),
+        in_specs=[hbm] * (count + 5) + [vmem] * (2 + len(mixer) + len(rest) + len(block)),
         out_specs=[vmem, hbm, vmem],
         scratch_shapes=reducer_scratch(total, rows)
         + [
@@ -1074,14 +1114,20 @@
             pltpu.VMEM(weights[0].shape, low),
             pltpu.VMEM((model, padded), low),
             pltpu.VMEM((head_count, 128), wide),
+            pltpu.VMEM((2 * kinds, 4, 2, 2, rows, half), low),
+            pltpu.VMEM((2, 4, 2, 2, rows, half), low),
             pltpu.VMEM((4, 2, 2, rows, 2 * half), low),
             pltpu.VMEM((2, 4, 2, 2, rows, CHUNK), low),
             sem((2,)),
+            pltpu.VMEM((4, model), wide),
+            pltpu.VMEM((model, tokens), low),
+            pltpu.VMEM((model, tokens), low),
+            pltpu.VMEM((tokens, model), wide),
         ],
         compiler_params=pltpu.CompilerParams(
             collective_id=number, has_side_effects=True, vmem_limit_bytes=60 * 2**20
         ),
-    )(*views, values, *weights, lat_lanes, shift_lanes, *mixer, *rest)
+    )(*views, values, *weights, lat_lanes, shift_lanes, *mixer, *rest, *block)
 
 
 def diagonal(var_count, columns):
@@ -2137,93 +2183,6 @@
     )(attended, late, start, vectors, late, late, up_bias, final_weight, masked, keep)
 
 
-def return_kernel(
-    grads_ref,
-    weight_ref,
-    low_ref,
-    start_ref,
-    middle_grad_ref,
-    vector_ref,
-    lead_ref,
-    back_ref,
-    mixed_ref,
-    grad_input_ref,
-    grad_mixer_ref,
-    mixed_grad_ref,
-    grad_vector_ref,
-    turned,
-    total,
-):
-    step = pl.program_id(0)
-    halves, _, half_width = back_ref.shape
-    row_count, _, _, share, lanes = grads_ref.shape
-    tokens = row_count * share
-    pairs = half_width // lanes
-
-    @pl.when(step == 0)
-    def _():
-        turned[...] = low_ref[...].T
-        total[...] = jnp.zeros_like(total)
-
-    kind, side = lax.div(step, halves), lax.rem(step, halves)
-    piece = jnp.concatenate(
-        [grads_ref[:, side * pairs + pair, kind].reshape(tokens, lanes) for pair in range(pairs)],
-        axis=1,
-    )
-    total[...] += dot(piece, weight_ref[0, 0], 1, 1)
-    grad_input_ref[0, 0] = dot(turned[...], piece).astype(low)
-
-    @pl.when(step == pl.num_programs(0) - 1)
-    def _():
-        part, grad_gain, grad_shift = norm_back(start_ref[...], vector_ref[2:3], total[...])
-        result = middle_grad_ref[...] + part
-        grad_vector_ref[0:1] = jnp.sum(result * lead_ref[...], axis=0, keepdims=True)
-        grad_vector_ref[1:2] = jnp.sum(result, axis=0, keepdims=True)
-        grad_vector_ref[2:3] = grad_gain
-        grad_vector_ref[3:4] = grad_shift
-        result_low = result.astype(low)
-        result_turned = result_low.T
-        for half in range(halves):
-            span = slice(half * half_width, (half + 1) * half_width)
-            grad_mixer_ref[half] = dot(result_turned, mixed_ref[span, :], 1, 1).astype(low)
-            mixed_grad_ref[span, :] = dot(result_low, back_ref[half]).astype(low).T
-
-
-def go_back(grads, weights, first_low, start, middle_grad, vectors, lead_column, back_weight, mixed):
-    kinds, halves, model, half_width = weights.shape
-    tokens = start.shape[0]
-    block = pl.BlockSpec((1, 1, model, half_width), lambda i: (i // halves, i % halves, 0, 0))
-    return pl.pallas_call(
-        return_kernel,
-        grid=(kinds * halves,),
-        out_shape=[
-            jax.ShapeDtypeStruct(weights.shape, low),
-            jax.ShapeDtypeStruct((halves, model, half_width), low),
-            jax.ShapeDtypeStruct((model, tokens), low),
-            jax.ShapeDtypeStruct((4, model), wide),
-        ],
-        in_specs=[
-            whole(grads),
-            block,
-            whole(first_low),
-            whole(start),
-            whole(middle_grad),
-            whole(vectors),
-            whole(lead_column),
-            whole(back_weight),
-            whole(mixed),
-        ],
-        out_specs=[
-            block,
-            pl.BlockSpec((halves, model, half_width), lambda i: (0, 0, 0)),
-            pl.BlockSpec((model, tokens), lambda i: (0, 0)),
-            pl.BlockSpec((4, model), lambda i: (0, 0)),
-        ],
-        scratch_shapes=[pltpu.VMEM((model, tokens), low), pltpu.VMEM((tokens, model), wide)],
-        compiler_params=pltpu.CompilerParams(vmem_limit_bytes=50 * 2**20),
-    )(grads, weights, first_low, start, middle_grad, vectors, lead_column, back_weight, mixed)
-
-
 def einsum(spec, left, right):
     return jnp.einsum(spec, left, right, preferred_element_type=wide)
 
@@ -2366,18 +2325,6 @@
         grad_feed,
         4,
     )
-    stacked = stacked[None]
-    grad_input, grad_mixer, mixed_grads, first_vectors = go_back(
-        stacked,
-        input_weight,
-        first_low,
-        start_sum,
-        middle_grad,
-        vectors,
-        lead_column,
-        mixer_weight,
-        mixed,
-    )
     bias_cols = expand_bias.shape[1]
     bias_block = jnp.transpose(
         grad_up_bias.reshape(HEAD_SIZE, bias_rows, LON_SIZE, bias_cols), (0, 2, 1, 3)
@@ -2392,16 +2339,16 @@
             (bias_at, 128 - bias_at - bias_cols),
         ),
     ).reshape(HEAD_SIZE, model, 128)
-    rest = grad_out + bias_block.astype(low)
     spot = taps + var_count
     sums, predicted, pixel_grad = reduce_all(
-        [grad_proj, grad_input, grad_mixer],
+        grad_proj,
         predicted.reshape(HEAD_SIZE, 2, slot_width, 128),
-        (key_weight, value_weight),
+        (key_weight, value_weight, input_weight, mixer_weight),
         lat_lanes,
         shift_lanes,
-        (patches, probs, score_table, value_table, key_table, mixed_grads),
-        (patch_full, query_wide, first_vectors, second_vectors, rest),
+        (patches, probs, score_table, value_table, key_table, mixed),
+        (patch_full, query_wide, second_vectors, grad_out, bias_block),
+        (stacked, first_low, start_sum, middle_grad, vectors, lead_column),
         lat_count,
         2,
     )

time: 489 us -> 475 us (0.971)
  Pallas kernels: 448 us -> 436 us
    pallas_call x1 -> x0, Pallas kernels: 12.9 us -> none  [go_back(): pl.pallas_call(return_kernel, grid=(kinds * halves,), out_shape=[jax.Shap...]
where the time goes in v6:
time: 475 us; the launch traced here: 470 us
  Pallas kernels  436 us (92%)
  local copies, waits for them, and re-layouts  22.8 us (5%)
  other arithmetic  9.45 us (2%)
    pallas_call x1, Pallas kernels, front(): pl.pallas_call(partial(front_kernel, items), out_shape=[jax.ShapeDtypeStr...  191 us
    pallas_call x1, Pallas kernels, attend_back(): pl.pallas_call(attend_back_kernel, out_shape=[jax.ShapeDtypeStruct(joint....  113 us
    pallas_call x1, Pallas kernels, reduce_all(): pl.pallas_call(partial(reduce_kernel, chunks, count), out_shape=[jax.Shap...  97.3 us
    pallas_call x1, Pallas kernels, feed(): pl.pallas_call(feed_kernel, grid=(2 * count,), out_shape=[shape for shape...  34.7 us

profile of v6, /device:TPU:0, one launch (start us, length us, event | category | flops | bytes accessed | tf_op | source)
XLA Modules:
  0.0 470.0 jit_solution(12460139591397468018)
XLA Ops:
  0.8 0.8 convert_multiply_fusion
  2.1 0.8 pad_maximum_fusion.4
  2.9 0.8 fusion.3
  4.3 0.8 select_reduce_fusion
  6.3 1.1 bitcast_bitcast_fusion
  7.4 1.7 pad_maximum_fusion.refs_7_
  9.4 0.7 pad.17.refs_8_
  11.9 191.3 %shard_map.375 = (bf16[2,4,2,2,48,128]{5,4,3,2,1,0:T(8,128)(2,1)}, bf16[2,4,2,2,64,128]{5,4,3,2,1,0:T(8,128)(2,1)}, bf16[2,4,2,2,64,512]{5,4,3,2,1,0:T(8,128)(2,...) custom-call(bf16[48,128]{1,0:T(8,128)(2,1)} %pad_maximum_fusion.3.re, ...), custom_call_target="tpu_custom_call" | custom-call | tf_op jit(solution)/shard_map/pallas_call | solution.py:1963
  203.3 1.0 convert_reduce_fusion
  204.3 0.7 reshape.127.bias_ref
  205.0 34.7 %shard_map.376 = (bf16[2,256,128]{2,1,0:T(8,128)(2,1)}, f32[256,1024]{1,0:T(8,128)}, bf16[1,8,256,128]{3,2,1,0:T(8,128)(2,1)}, bf16[2,2,1024,2048]{3,2,1,0:T(8,1...) custom-call(bf16[1,8,256,128]{3,2,1,0:T(8,128)(2,1)} %bitcast.83, ...), custom_call_target="tpu_custom_call" | custom-call | tf_op jit(solution)/shard_map/pallas_call | solution.py:2153
  239.7 113.0 %shard_map.377 = (bf16[8,3,256,128]{3,2,1,0:T(8,128)(2,1)}, f32[64,4096]{1,0:T(8,128)}) custom-call(bf16[8,3,256,128]{3,2,1,0:T(8,128)(2,1)} %get-tuple-element.84.joint, f32[8,2048]{1,0:T(8,128)} %get-tuple-element.85.tag_ref, f32[2048,1]{1,0:T(8,128)} %get-tuple-element.86.crop_ref, f32[2048,128]{1,0:T(8,128)} %get-tuple-element.87.out_ref, ...), custom_call_target="tpu_custom_call" | custom-call | tf_op jit(solution)/shard_map/pallas_call | solution.py:1479
  353.2 0.7 reduce.11
  354.6 1.2 pad.19.clone
  355.8 97.3 %shard_map.378 = (f32[64,3328]{1,0:T(8,128)}, bf16[4,128,128]{2,1,0:T(8,128)(2,1)}, f32[32,48,256]{2,1,0:T(8,128)}) custom-call(bf16[2,4,2,2,64,512]{5,4,3,2,1,0:T(8,128)(2,1)} %bitcast.79, bf16[2,2,128,128]{3,2,1,0:T(8,128)(2,1)} %bitcast.88, bf16[2,1024,512]{2,1,0:T(8,128)(2,1)} %bitcast.76, bf16[2,1024,512]{2,1,0:T(8,128)(2,1)} %bitcast.77, ...), custom_call_target="tpu_custom_call" | custom-call | tf_op jit(solution)/shard_map/pallas_call | solution.py:1087
  453.2 2.1 slice_bitcast_fusion.1
  455.2 0.8 pad_maximum_fusion.1
  456.0 0.8 slice.97
  457.2 0.7 broadcast_multiply_fusion
  457.9 0.7 fusion.1
  458.7 0.6 copy.89
  459.4 0.6 copy.77
  460.1 0.7 slice.118
  460.8 0.7 slice_reduce_fusion
  461.5 2.1 copy.75
  463.5 0.7 copy.74
  464.3 1.4 slice.113
  465.7 0.8 slice.111
  466.5 0.7 copy.78
  467.1 0.7 slice.96
  467.9 0.7 copy.76
  468.5 1.0 slice_bitcast_fusion
  (60 shorter events, 6.3 us)
Async XLA Ops:
  0.7 8.5 %copy-start.3 = (bf16[4,128,96]{1,2,0:T(8,128)(2,1)S(1)}, bf16[4,128,96]{1,2,0:T(8,128)(2,1)}, u32[]{:S(2)}) copy-start(bf16[4,128,96]{1,2,0:T(8,128)(2,1)} %param.47) | copy-start | bytes 294916
  0.7 9.4 %copy-start.4 = (bf16[48,4,32]{0,2,1:T(8,128)(2,1)S(1)}, bf16[48,4,32]{0,2,1:T(8,128)(2,1)}, u32[]{:S(2)}) copy-start(bf16[48,4,32]{0,2,1:T(8,128)(2,1)} %param.30) | copy-start | bytes 36868
  0.7 9.5 %copy-start.13 = (bf16[2,32]{1,0:T(2,128)(2,1)S(1)}, bf16[2,32]{1,0:T(2,128)(2,1)}, u32[]{:S(2)}) copy-start(bf16[2,32]{1,0:T(2,128)(2,1)} %param.36) | copy-start | bytes 388
  0.7 9.6 %copy-start.9 = (bf16[32]{0:T(256)(128)(2,1)S(1)}, bf16[32]{0:T(256)(128)(2,1)}, u32[]{:S(2)}) copy-start(bf16[32]{0:T(256)(128)(2,1)} %param.37) | copy-start | bytes 196
  0.7 9.6 %copy-start.10 = (bf16[32]{0:T(256)(128)(2,1)S(1)}, bf16[32]{0:T(256)(128)(2,1)}, u32[]{:S(2)}) copy-start(bf16[32]{0:T(256)(128)(2,1)} %param.38) | copy-start | bytes 196
  0.7 9.6 %copy-start.11 = (bf16[32]{0:T(256)(128)(2,1)S(1)}, bf16[32]{0:T(256)(128)(2,1)}, u32[]{:S(2)}) copy-start(bf16[32]{0:T(256)(128)(2,1)} %param.41) | copy-start | bytes 196
  0.7 9.6 %copy-start.12 = (bf16[32]{0:T(256)(128)(2,1)S(1)}, bf16[32]{0:T(256)(128)(2,1)}, u32[]{:S(2)}) copy-start(bf16[32]{0:T(256)(128)(2,1)} %param.42) | copy-start | bytes 196
  0.7 9.9 %copy-start.8 = (bf16[48,32]{0,1:T(8,128)(2,1)S(1)}, bf16[48,32]{0,1:T(8,128)(2,1)}, u32[]{:S(2)}) copy-start(bf16[48,32]{0,1:T(8,128)(2,1)} %param.31) | copy-start | bytes 9220
  0.7 10.6 %copy-start.6 = (bf16[64,96]{1,0:T(8,128)(2,1)S(1)}, bf16[64,96]{1,0:T(8,128)(2,1)}, u32[]{:S(2)}) copy-start(bf16[64,96]{1,0:T(8,128)(2,1)} %param.46) | copy-start | bytes 36868
  239.6 113.5 %copy-start.7 = (f32[1,4096]{1,0:T(1,128)S(1)}, f32[1,4096]{1,0:T(1,128)}, u32[]{:S(2)}) copy-start(f32[1,4096]{1,0:T(1,128)} %get-tuple-element.83) | copy-start | bytes 49156
  453.1 4.0 copy-start.5
  453.2 8.3 %copy-start = (f32[32,48,256]{2,1,0:T(8,128)S(1)}, f32[32,48,256]{2,1,0:T(8,128)}, u32[]{:S(2)}) copy-start(f32[32,48,256]{2,1,0:T(8,128)} %get-tuple-element.96) | copy-start | bytes 4718596
  457.0 6.6 %copy-start.2 = (bf16[4,128,128]{2,1,0:T(8,128)(2,1)S(1)}, bf16[4,128,128]{2,1,0:T(8,128)(2,1)}, u32[]{:S(2)}) copy-start(bf16[4,128,128]{2,1,0:T(8,128)(2,1)} %get-tuple-element.95) | copy-start | bytes 393220
  457.2 11.3 %copy-start.1 = (f32[64,4096]{1,0:T(8,128)S(1)}, f32[64,4096]{1,0:T(8,128)}, u32[]{:S(2)}) copy-start(f32[64,4096]{1,0:T(8,128)} %get-tuple-element.98) | copy-start | bytes 3145732

commit v7 on v6

--- a/solution.py
+++ b/solution.py
@@ -581,6 +581,7 @@
 LON_SIZE = 16
 HEAD_SIZE = 2
 CHUNK = 256
+LATE_PAIRS = 1
 low = jnp.bfloat16
 wide = jnp.float32
 
@@ -933,7 +934,7 @@
             inside = lax.div(head, head_half) == side
             target = jnp.where(jnp.logical_and(inside, lane == spot), 1.0, 0.0).astype(low)
             sums = sum(dot(part, target, 0, 0) for part in count_parts)
-            result = rest_ref[side].astype(wide) + bias_ref[side]
+            result = rest_ref[side].astype(wide) + bias_ref[side].astype(wide)
             for part in halves_of(sums):
                 result = result + dot(full_ref[...], part)
             chosen = jnp.logical_and(inner < head_half, columns == inner + head_half * side)
@@ -1060,19 +1061,24 @@
         pltpu.make_async_copy(value_in.at[0, 0], value_out.at[row], value_recv.at[row]).wait()
 
 
-def reduce_all(item, values, weights, lat_lanes, shift_lanes, mixer, rest, block, lat_count, number):
+def reduce_all(feed_grads, item, values, weights, lat_lanes, shift_lanes, mixer, rest, block, lat_count, number):
     chunks = []
     model, half = item.shape[-2:]
-    views = [item.reshape((-1, 4, 2, 2, model // 16, half))]
+    views = [
+        part.reshape((-1, 4, 2, 2, model // 16, part.shape[-1])) for part in (feed_grads, item)
+    ]
     kinds = weights[2].shape[0]
-    for index, leads in ((0, 1), (1, kinds), (2, 1)):
+    columns = feed_grads.shape[-1]
+    for offset in range(columns - 2 * LATE_PAIRS * CHUNK, columns, CHUNK):
+        chunks.append(((0, 2, offset), (0, 3, offset)))
+    for index, leads in ((1, 1), (2, kinds), (3, 1)):
         for first in range(0, 2 * leads, 2):
             for offset in range(0, half, CHUNK):
                 chunks.append(((index, first, offset), (index, first + 1, offset)))
     count = len(views)
     for offset in range(0, half, CHUNK):
-        chunks.append(((3, None, offset), (3, None, half + offset)))
-    chunks.append(((4, 0, 0), (4, 1, 0)))
+        chunks.append(((4, None, offset), (4, None, half + offset)))
+    chunks.append(((5, 0, 0), (5, 1, 0)))
     total = len(chunks)
     rows = views[0].shape[-2]
     probs = mixer[1]
@@ -1125,7 +1131,7 @@
             pltpu.VMEM((tokens, model), wide),
         ],
         compiler_params=pltpu.CompilerParams(
-            collective_id=number, has_side_effects=True, vmem_limit_bytes=60 * 2**20
+            collective_id=number, has_side_effects=True, vmem_limit_bytes=63 * 2**20
         ),
     )(*views, values, *weights, lat_lanes, shift_lanes, *mixer, *rest, *block)
 
@@ -1378,7 +1384,7 @@
         inward(lax.rem(me + step, peers)).start()
     key_acc[...] = jnp.zeros_like(key_acc)
     value_acc[...] = jnp.zeros_like(value_acc)
-    pairs = feed_ref.shape[0] * each // 2
+    pairs = feed_ref.shape[0] * each // 2 - LATE_PAIRS
 
     def attention(index):
         span = pl.ds(pl.multiple_of(index * share, share), share)
@@ -1472,7 +1478,7 @@
     peers, kinds, share, lanes = joint.shape
     slots = peers * share
     sides, halves, rows, columns = feed_grads.shape
-    total = sides * columns // CHUNK
+    total = sides * columns // CHUNK - 2 * LATE_PAIRS
     sem = pltpu.SemaphoreType.DMA
     vmem = pl.BlockSpec(memory_space=pltpu.VMEM)
     hbm = pl.BlockSpec(memory_space=pl.ANY)
@@ -2341,13 +2347,14 @@
     ).reshape(HEAD_SIZE, model, 128)
     spot = taps + var_count
     sums, predicted, pixel_grad = reduce_all(
+        grad_feed,
         grad_proj,
         predicted.reshape(HEAD_SIZE, 2, slot_width, 128),
         (key_weight, value_weight, input_weight, mixer_weight),
         lat_lanes,
         shift_lanes,
         (patches, probs, score_table, value_table, key_table, mixed),
-        (patch_full, query_wide, second_vectors, grad_out, bias_block),
+        (patch_full, query_wide, second_vectors, grad_out, bias_block.astype(low)),
         (stacked, first_low, start_sum, middle_grad, vectors, lead_column),
         lat_count,
         2,
@@ -2362,7 +2369,7 @@
         return sums[:, begin : begin + width]
 
     out_up = feed_sums[:, :full_half]
-    out_down = feed_sums[:, full_half:].T
+    out_down = jnp.concatenate([feed_sums[:, full_half:], take(2 * LATE_PAIRS * CHUNK)], axis=1).T
     out_proj = take(half_width).T
     out_input = jnp.stack([take(half_width) for _ in range(3)])
     out_mixer = take(half_width).T

time: 475 us -> 471 us (level)
    pallas_call x1, Pallas kernels: 113 us -> 101 us  [attend_back(): pl.pallas_call(attend_back_kernel, out_shape=[jax.ShapeDtypeStruct(joint....]
    pallas_call x1, Pallas kernels: 97.3 us -> 105 us  [reduce_all(): pl.pallas_call(partial(reduce_kernel, chunks, count), out_shape=[jax.Shap...]
where the time goes in v7:
time: 471 us; the launch traced here: 465 us
  Pallas kernels  432 us (92%)
  local copies, waits for them, and re-layouts  21.9 us (5%)
  other arithmetic  9.66 us (2%)
    pallas_call x1, Pallas kernels, front(): pl.pallas_call(partial(front_kernel, items), out_shape=[jax.ShapeDtypeStr...  191 us
    pallas_call x1, Pallas kernels, reduce_all(): pl.pallas_call(partial(reduce_kernel, chunks, count), out_shape=[jax.Shap...  105 us
    pallas_call x1, Pallas kernels, attend_back(): pl.pallas_call(attend_back_kernel, out_shape=[jax.ShapeDtypeStruct(joint....  101 us
    pallas_call x1, Pallas kernels, feed(): pl.pallas_call(feed_kernel, grid=(2 * count,), out_shape=[shape for shape...  34.7 us

profile of v7, /device:TPU:0, one launch (start us, length us, event | category | flops | bytes accessed | tf_op | source)
XLA Modules:
  0.0 465.0 jit_solution(164156451996477514)
XLA Ops:
  0.8 0.8 convert_multiply_fusion
  2.1 0.8 pad_maximum_fusion.4
  2.9 0.8 fusion.4
  4.3 0.8 select_reduce_fusion
  6.3 1.1 bitcast_bitcast_fusion
  7.4 1.7 pad_maximum_fusion.refs_7_
  9.4 0.7 pad.18.refs_8_
  11.9 191.4 %shard_map.375 = (bf16[2,4,2,2,48,128]{5,4,3,2,1,0:T(8,128)(2,1)}, bf16[2,4,2,2,64,128]{5,4,3,2,1,0:T(8,128)(2,1)}, bf16[2,4,2,2,64,512]{5,4,3,2,1,0:T(8,128)(2,...) custom-call(bf16[48,128]{1,0:T(8,128)(2,1)} %pad_maximum_fusion.3.re, ...), custom_call_target="tpu_custom_call" | custom-call | tf_op jit(solution)/shard_map/pallas_call | solution.py:1969
  203.3 1.0 convert_reduce_fusion
  204.4 0.7 reshape.130.bias_ref
  205.0 34.7 %shard_map.376 = (bf16[2,256,128]{2,1,0:T(8,128)(2,1)}, f32[256,1024]{1,0:T(8,128)}, bf16[1,8,256,128]{3,2,1,0:T(8,128)(2,1)}, bf16[2,2,1024,2048]{3,2,1,0:T(8,1...) custom-call(bf16[1,8,256,128]{3,2,1,0:T(8,128)(2,1)} %bitcast.85, ...), custom_call_target="tpu_custom_call" | custom-call | tf_op jit(solution)/shard_map/pallas_call | solution.py:2159
  239.7 101.4 %shard_map.377 = (bf16[8,3,256,128]{3,2,1,0:T(8,128)(2,1)}, f32[64,3584]{1,0:T(8,128)}) custom-call(bf16[8,3,256,128]{3,2,1,0:T(8,128)(2,1)} %get-tuple-element.85.joint, f32[8,2048]{1,0:T(8,128)} %get-tuple-element.86.tag_ref, f32[2048,1]{1,0:T(8,128)} %get-tuple-element.87.crop_ref, f32[2048,128]{1,0:T(8,128)} %get-tuple-element.88.out_ref, ...), custom_call_target="tpu_custom_call" | custom-call | tf_op jit(solution)/shard_map/pallas_call | solution.py:1485
  341.9 1.0 pad.20.clone
  342.9 104.5 %shard_map.378 = (f32[64,3840]{1,0:T(8,128)}, bf16[4,128,128]{2,1,0:T(8,128)(2,1)}, f32[32,48,256]{2,1,0:T(8,128)}) custom-call(bf16[4,4,2,2,64,2048]{5,4,3,2,1,0:T(8,128)(2,1)} %bitcast.74, bf16[2,4,2,2,64,512]{5,4,3,2,1,0:T(8,128)(2,1)} %bitcast.80, bf16[2,2,128,128]{3,2,1,0:T(8,128)(2,1)} %bitcast.90, bf16[2,1024,512]{2,1,0:T(8,128)(2,1)} %bitcast.77, ...), custom_call_target="tpu_custom_call" | custom-call | tf_op jit(solution)/shard_map/pallas_call | solution.py:1093
  447.4 2.1 fusion.1
  449.6 0.8 maximum_bitcast_fusion
  450.4 0.8 pad_maximum_fusion.1
  451.2 0.8 slice.100
  452.4 0.7 broadcast_multiply_fusion
  453.0 0.7 fusion.2
  453.9 0.6 copy.89
  454.6 0.6 copy.77
  455.2 0.7 slice.122
  455.9 0.7 slice_reduce_fusion
  456.7 2.1 copy.75
  458.7 0.7 copy.74
  459.5 1.4 slice.117
  460.8 0.8 slice.114
  461.6 0.7 copy.78
  462.3 0.8 slice.99
  463.0 0.7 copy.76
  463.7 0.8 slice.113
  (61 shorter events, 5.8 us)
Async XLA Ops:
  0.7 8.5 %copy-start.3 = (bf16[4,128,96]{1,2,0:T(8,128)(2,1)S(1)}, bf16[4,128,96]{1,2,0:T(8,128)(2,1)}, u32[]{:S(2)}) copy-start(bf16[4,128,96]{1,2,0:T(8,128)(2,1)} %param.47) | copy-start | bytes 294916
  0.7 9.4 %copy-start.4 = (bf16[48,4,32]{0,2,1:T(8,128)(2,1)S(1)}, bf16[48,4,32]{0,2,1:T(8,128)(2,1)}, u32[]{:S(2)}) copy-start(bf16[48,4,32]{0,2,1:T(8,128)(2,1)} %param.30) | copy-start | bytes 36868
  0.7 9.5 %copy-start.13 = (bf16[2,32]{1,0:T(2,128)(2,1)S(1)}, bf16[2,32]{1,0:T(2,128)(2,1)}, u32[]{:S(2)}) copy-start(bf16[2,32]{1,0:T(2,128)(2,1)} %param.36) | copy-start | bytes 388
  0.7 9.6 %copy-start.9 = (bf16[32]{0:T(256)(128)(2,1)S(1)}, bf16[32]{0:T(256)(128)(2,1)}, u32[]{:S(2)}) copy-start(bf16[32]{0:T(256)(128)(2,1)} %param.37) | copy-start | bytes 196
  0.7 9.6 %copy-start.10 = (bf16[32]{0:T(256)(128)(2,1)S(1)}, bf16[32]{0:T(256)(128)(2,1)}, u32[]{:S(2)}) copy-start(bf16[32]{0:T(256)(128)(2,1)} %param.38) | copy-start | bytes 196
  0.7 9.6 %copy-start.11 = (bf16[32]{0:T(256)(128)(2,1)S(1)}, bf16[32]{0:T(256)(128)(2,1)}, u32[]{:S(2)}) copy-start(bf16[32]{0:T(256)(128)(2,1)} %param.41) | copy-start | bytes 196
  0.7 9.6 %copy-start.12 = (bf16[32]{0:T(256)(128)(2,1)S(1)}, bf16[32]{0:T(256)(128)(2,1)}, u32[]{:S(2)}) copy-start(bf16[32]{0:T(256)(128)(2,1)} %param.42) | copy-start | bytes 196
  0.7 9.9 %copy-start.8 = (bf16[48,32]{0,1:T(8,128)(2,1)S(1)}, bf16[48,32]{0,1:T(8,128)(2,1)}, u32[]{:S(2)}) copy-start(bf16[48,32]{0,1:T(8,128)(2,1)} %param.31) | copy-start | bytes 9220
  0.7 10.6 %copy-start.7 = (bf16[64,96]{1,0:T(8,128)(2,1)S(1)}, bf16[64,96]{1,0:T(8,128)(2,1)}, u32[]{:S(2)}) copy-start(bf16[64,96]{1,0:T(8,128)(2,1)} %param.46) | copy-start | bytes 36868
  239.7 101.5 %copy-start.6 = (f32[1,4096]{1,0:T(1,128)S(1)}, f32[1,4096]{1,0:T(1,128)}, u32[]{:S(2)}) copy-start(f32[1,4096]{1,0:T(1,128)} %get-tuple-element.84) | copy-start | bytes 49156
  447.4 2.1 copy-start.1
  449.5 2.7 copy-start.5
  449.5 7.1 %copy-start = (f32[32,48,256]{2,1,0:T(8,128)S(1)}, f32[32,48,256]{2,1,0:T(8,128)}, u32[]{:S(2)}) copy-start(f32[32,48,256]{2,1,0:T(8,128)} %get-tuple-element.96) | copy-start | bytes 4718596
  452.1 6.6 %copy-start.2 = (bf16[4,128,128]{2,1,0:T(8,128)(2,1)S(1)}, bf16[4,128,128]{2,1,0:T(8,128)(2,1)}, u32[]{:S(2)}) copy-start(bf16[4,128,128]{2,1,0:T(8,128)(2,1)} %get-tuple-element.95) | copy-start | bytes 393220

commit v8 on v7

--- a/solution.py
+++ b/solution.py
@@ -873,7 +873,7 @@
     def send_cut():
         taps = 4 * var_total
         for part in range(2):
-            grad_in[part] = patch_grad[:taps, part * 128 : (part + 1) * 128]
+            grad_in[part] = patch_grad[:taps, part * 128 : (part + 1) * 128].astype(low)
         for letter in letters[0::2]:
             post(*letter)
 
@@ -959,8 +959,8 @@
             k = 2 * py
             grads = jnp.concatenate(
                 [
-                    grad_out[row, k * var_count : (k + 1) * var_count, :],
-                    grad_out[row, (k + 1) * var_count : (k + 2) * var_count, :],
+                    grad_out[row, k * var_count : (k + 1) * var_count, :].astype(wide),
+                    grad_out[row, (k + 1) * var_count : (k + 2) * var_count, :].astype(wide),
                 ],
                 axis=1,
             )
@@ -1101,7 +1101,7 @@
         out_specs=[vmem, hbm, vmem],
         scratch_shapes=reducer_scratch(total, rows)
         + [
-            pltpu.VMEM(cut, wide),
+            pltpu.VMEM(cut, low),
             pltpu.VMEM((lat_count, var_count, lanes), wide),
             pltpu.VMEM((8, lat_count * var_count), wide),
             pltpu.VMEM((8, lat_count * var_count), wide),
@@ -1112,7 +1112,7 @@
             sem((4,)),
             sem((2,)),
             sem((2,)),
-            pltpu.VMEM((2,) + cut[1:], wide),
+            pltpu.VMEM((2,) + cut[1:], low),
             pltpu.VMEM((model, padded), low),
             pltpu.VMEM((head_count, padded), wide),
             pltpu.VMEM((padded, tokens), wide),

time: 471 us -> 466 us (0.989)
  no operation moved by 1% of the time
where the time goes in v8:
time: 466 us; the launch traced here: 461 us
  Pallas kernels  428 us (92%)
  local copies, waits for them, and re-layouts  21.9 us (5%)
  other arithmetic  9.66 us (2%)
    pallas_call x1, Pallas kernels, front(): pl.pallas_call(partial(front_kernel, items), out_shape=[jax.ShapeDtypeStr...  191 us
    pallas_call x1, Pallas kernels, attend_back(): pl.pallas_call(attend_back_kernel, out_shape=[jax.ShapeDtypeStruct(joint....  101 us
    pallas_call x1, Pallas kernels, reduce_all(): pl.pallas_call(partial(reduce_kernel, chunks, count), out_shape=[jax.Shap...  100 us
    pallas_call x1, Pallas kernels, feed(): pl.pallas_call(feed_kernel, grid=(2 * count,), out_shape=[shape for shape...  34.7 us

profile of v8, /device:TPU:0, one launch (start us, length us, event | category | flops | bytes accessed | tf_op | source)
XLA Modules:
  0.0 460.9 jit_solution(14819993762278711764)
XLA Ops:
  0.8 0.8 convert_multiply_fusion
  2.1 0.8 pad_maximum_fusion.4
  2.9 0.8 fusion.4
  4.3 0.8 select_reduce_fusion
  6.3 1.1 bitcast_bitcast_fusion
  7.4 1.7 pad_maximum_fusion.refs_7_
  9.4 0.7 pad.18.refs_8_
  11.9 191.4 %shard_map.375 = (bf16[2,4,2,2,48,128]{5,4,3,2,1,0:T(8,128)(2,1)}, bf16[2,4,2,2,64,128]{5,4,3,2,1,0:T(8,128)(2,1)}, bf16[2,4,2,2,64,512]{5,4,3,2,1,0:T(8,128)(2,...) custom-call(bf16[48,128]{1,0:T(8,128)(2,1)} %pad_maximum_fusion.3.re, ...), custom_call_target="tpu_custom_call" | custom-call | tf_op jit(solution)/shard_map/pallas_call | solution.py:1969
  203.3 1.0 convert_reduce_fusion
  204.4 0.7 reshape.130.bias_ref
  205.0 34.7 %shard_map.376 = (bf16[2,256,128]{2,1,0:T(8,128)(2,1)}, f32[256,1024]{1,0:T(8,128)}, bf16[1,8,256,128]{3,2,1,0:T(8,128)(2,1)}, bf16[2,2,1024,2048]{3,2,1,0:T(8,1...) custom-call(bf16[1,8,256,128]{3,2,1,0:T(8,128)(2,1)} %bitcast.85, ...), custom_call_target="tpu_custom_call" | custom-call | tf_op jit(solution)/shard_map/pallas_call | solution.py:2159
  239.7 101.4 %shard_map.377 = (bf16[8,3,256,128]{3,2,1,0:T(8,128)(2,1)}, f32[64,3584]{1,0:T(8,128)}) custom-call(bf16[8,3,256,128]{3,2,1,0:T(8,128)(2,1)} %get-tuple-element.85.joint, f32[8,2048]{1,0:T(8,128)} %get-tuple-element.86.tag_ref, f32[2048,1]{1,0:T(8,128)} %get-tuple-element.87.crop_ref, f32[2048,128]{1,0:T(8,128)} %get-tuple-element.88.out_ref, ...), custom_call_target="tpu_custom_call" | custom-call | tf_op jit(solution)/shard_map/pallas_call | solution.py:1485
  341.9 1.0 pad.20.clone
  342.9 100.4 %shard_map.378 = (f32[64,3840]{1,0:T(8,128)}, bf16[4,128,128]{2,1,0:T(8,128)(2,1)}, f32[32,48,256]{2,1,0:T(8,128)}) custom-call(bf16[4,4,2,2,64,2048]{5,4,3,2,1,0:T(8,128)(2,1)} %bitcast.74, bf16[2,4,2,2,64,512]{5,4,3,2,1,0:T(8,128)(2,1)} %bitcast.80, bf16[2,2,128,128]{3,2,1,0:T(8,128)(2,1)} %bitcast.90, bf16[2,1024,512]{2,1,0:T(8,128)(2,1)} %bitcast.77, ...), custom_call_target="tpu_custom_call" | custom-call | tf_op jit(solution)/shard_map/pallas_call | solution.py:1093
  443.3 2.1 fusion.1
  445.5 0.8 maximum_bitcast_fusion
  446.3 0.8 pad_maximum_fusion.1
  447.1 0.8 slice.100
  448.3 0.7 broadcast_multiply_fusion
  449.0 0.7 fusion.2
  449.8 0.6 copy.89
  450.5 0.6 copy.77
  451.1 0.7 slice.122
  451.8 0.7 slice_reduce_fusion
  452.6 2.1 copy.75
  454.6 0.7 copy.74
  455.4 1.4 slice.117
  456.7 0.8 slice.114
  457.5 0.7 copy.78
  458.2 0.8 slice.99
  458.9 0.7 copy.76
  459.6 0.8 slice.113
  (61 shorter events, 5.8 us)
Async XLA Ops:
  0.7 8.5 %copy-start.3 = (bf16[4,128,96]{1,2,0:T(8,128)(2,1)S(1)}, bf16[4,128,96]{1,2,0:T(8,128)(2,1)}, u32[]{:S(2)}) copy-start(bf16[4,128,96]{1,2,0:T(8,128)(2,1)} %param.47) | copy-start | bytes 294916
  0.7 9.4 %copy-start.4 = (bf16[48,4,32]{0,2,1:T(8,128)(2,1)S(1)}, bf16[48,4,32]{0,2,1:T(8,128)(2,1)}, u32[]{:S(2)}) copy-start(bf16[48,4,32]{0,2,1:T(8,128)(2,1)} %param.30) | copy-start | bytes 36868
  0.7 9.5 %copy-start.13 = (bf16[2,32]{1,0:T(2,128)(2,1)S(1)}, bf16[2,32]{1,0:T(2,128)(2,1)}, u32[]{:S(2)}) copy-start(bf16[2,32]{1,0:T(2,128)(2,1)} %param.36) | copy-start | bytes 388
  0.7 9.6 %copy-start.9 = (bf16[32]{0:T(256)(128)(2,1)S(1)}, bf16[32]{0:T(256)(128)(2,1)}, u32[]{:S(2)}) copy-start(bf16[32]{0:T(256)(128)(2,1)} %param.37) | copy-start | bytes 196
  0.7 9.6 %copy-start.10 = (bf16[32]{0:T(256)(128)(2,1)S(1)}, bf16[32]{0:T(256)(128)(2,1)}, u32[]{:S(2)}) copy-start(bf16[32]{0:T(256)(128)(2,1)} %param.38) | copy-start | bytes 196
  0.7 9.6 %copy-start.11 = (bf16[32]{0:T(256)(128)(2,1)S(1)}, bf16[32]{0:T(256)(128)(2,1)}, u32[]{:S(2)}) copy-start(bf16[32]{0:T(256)(128)(2,1)} %param.41) | copy-start | bytes 196
  0.7 9.6 %copy-start.12 = (bf16[32]{0:T(256)(128)(2,1)S(1)}, bf16[32]{0:T(256)(128)(2,1)}, u32[]{:S(2)}) copy-start(bf16[32]{0:T(256)(128)(2,1)} %param.42) | copy-start | bytes 196
  0.7 9.9 %copy-start.8 = (bf16[48,32]{0,1:T(8,128)(2,1)S(1)}, bf16[48,32]{0,1:T(8,128)(2,1)}, u32[]{:S(2)}) copy-start(bf16[48,32]{0,1:T(8,128)(2,1)} %param.31) | copy-start | bytes 9220
  0.7 10.6 %copy-start.7 = (bf16[64,96]{1,0:T(8,128)(2,1)S(1)}, bf16[64,96]{1,0:T(8,128)(2,1)}, u32[]{:S(2)}) copy-start(bf16[64,96]{1,0:T(8,128)(2,1)} %param.46) | copy-start | bytes 36868
  239.7 101.5 %copy-start.6 = (f32[1,4096]{1,0:T(1,128)S(1)}, f32[1,4096]{1,0:T(1,128)}, u32[]{:S(2)}) copy-start(f32[1,4096]{1,0:T(1,128)} %get-tuple-element.84) | copy-start | bytes 49156
  443.3 2.1 copy-start.1
  445.4 2.7 copy-start.5
  445.4 7.1 %copy-start = (f32[32,48,256]{2,1,0:T(8,128)S(1)}, f32[32,48,256]{2,1,0:T(8,128)}, u32[]{:S(2)}) copy-start(f32[32,48,256]{2,1,0:T(8,128)} %get-tuple-element.96) | copy-start | bytes 4718596
  448.1 6.6 %copy-start.2 = (bf16[4,128,128]{2,1,0:T(8,128)(2,1)S(1)}, bf16[4,128,128]{2,1,0:T(8,128)(2,1)}, u32[]{:S(2)}) copy-start(bf16[4,128,128]{2,1,0:T(8,128)(2,1)} %get-tuple-element.95) | copy-start | bytes 393220
